TPU v7x, 512 devices: a whole 4x8x8 slice. The times are simulated.
512 devices in a mesh: shot: 4 (over y_hi, core), gx: 16 (over x, y_lo), gy: 8 (over z).
Axes of the slice: x: 4, y: 8 (y_hi: 2, y_lo: 4; y = y_hi * 4 + y_lo), z: 8, core: 2. Of those that a mesh axis runs over, the one named last changes fastest.
Arguments:
- mean_velocity: float32 [128, 256, 128], P('gx', 'gy'), may hold values from 0.8 to 1.2
- log_scale: float32 [128, 256, 128], P('gx', 'gy'), may hold values from -4 to -2.3
- shot_noise: float32 [4, 128, 256, 128], P('shot', 'gx', 'gy'), may hold values from -4 to 4
- checkpoint_prev: float32 [4, 128, 256, 128], P('shot', 'gx', 'gy'), may hold values from -6 to 6
- checkpoint_now: float32 [4, 128, 256, 128], P('shot', 'gx', 'gy'), may hold values from -6 to 6
- adjoint_next: float32 [4, 128, 256, 128], P('shot', 'gx', 'gy'), may hold values from -6 to 6
- adjoint_now: float32 [4, 128, 256, 128], P('shot', 'gx', 'gy'), may hold values from -6 to 6
- wavelet: float32 [4, 64], P('shot'), may hold values from -1200 to 1200
- source_column: int32 [4], P('shot'), may hold values from 0 to 32767
- receiver_column: int32 [4, 8192], P('shot'), may hold values from 0 to 32767
- observed: float32 [4, 4, 8192], P('shot', None, ('gx', 'gy')), may hold values from -10 to 10
- start_step: int32 [1], replicated, may hold values from 0 to 60
Outputs:
- grad_mean: float32 [128, 256, 128], P('gx', 'gy')
- grad_log_scale: float32 [128, 256, 128], P('gx', 'gy')
Inputs may be any that keep to these rules, and one draw needn't show every extreme that they name: `receiver_column`: column x * 256 + y of the cell column holding each receiver; receivers sit at depth 3; several receivers may share a cell. `source_column`: column x * 256 + y of each shot's source, at depth 6. The window reads wavelet samples start_step to start_step + 3.
All inputs are finite; a program needn't handle non-finite values.
Results may differ from a plain program's by a relative error of at most 0.0003.
Values sent between devices are 32-bit elements; how exact they have to be, the bound alone decides.
No kernel may reach another device: no remote copies, remote signals or barrier semaphores. Data moves between devices by JAX's collectives and lax.ppermute only.
A program may use at most 64 MiB of HBM per device.

v0:
```python
import jax
import jax.numpy as jnp
from jax import lax
from jax.sharding import PartitionSpec as P

STEPS = 4
SRC_DEPTH = 6
REC_DEPTH = 3


stencil_weights = (-205.0 / 72.0, 8.0 / 5.0, -1.0 / 5.0, 8.0 / 315.0, -1.0 / 560.0)
courant_sq = 0.0625
prior_var = 0.01


def with_halo(cells, sides, width):
    for axis, dim in sides:
        count = lax.axis_size(axis)
        ends = count - 1
        head = lax.slice_in_dim(cells, 0, width, axis=dim)
        tail = lax.slice_in_dim(cells, cells.shape[dim] - width, cells.shape[dim], axis=dim)
        cells = jnp.concatenate(
            [
                lax.ppermute(tail, axis, [(i, (i + 1) % count) for i in range(ends)]),
                cells,
                lax.ppermute(head, axis, [((i + 1) % count, i) for i in range(ends)]),
            ],
            axis=dim,
        )
    return cells


def stencil(padded, size_x, size_y):
    center = padded[4 : 4 + size_x, 4 : 4 + size_y]
    size_z = center.shape[2]
    padded_z = jnp.pad(center, ((0, 0), (0, 0), (4, 4)))
    running = 3.0 * stencil_weights[0] * center
    for offset in range(1, 5):
        beside = (
            padded[4 + offset : 4 + offset + size_x, 4 : 4 + size_y]
            + padded[4 - offset : 4 - offset + size_x, 4 : 4 + size_y]
        )
        beside = (
            beside
            + padded[4 : 4 + size_x, 4 + offset : 4 + offset + size_y]
            + padded[4 : 4 + size_x, 4 - offset : 4 - offset + size_y]
        )
        beside = (
            beside
            + padded_z[:, :, 4 + offset : 4 + offset + size_z]
            + padded_z[:, :, 4 - offset : 4 - offset + size_z]
        )
        running = running + stencil_weights[offset] * beside
    return running


def forward_laplace(wavefield):
    padded = with_halo(wavefield, (("gx", 0), ("gy", 1)), 4)
    return stencil(padded, wavefield.shape[0], wavefield.shape[1])


def adjoint_laplace(wavefield):
    padded = with_halo(wavefield, (("gx", 0), ("gy", 1)), 4)
    return stencil(padded, wavefield.shape[0], wavefield.shape[1])


def local(
    mean_velocity,
    log_scale,
    shot_noise,
    checkpoint_prev,
    checkpoint_now,
    adjoint_next,
    adjoint_now,
    wavelet,
    source_column,
    receiver_column,
    observed,
    start_step,
):
    size_x, size_y, size_z = mean_velocity.shape
    width_y = size_y * lax.axis_size("gy")
    anchor_x = lax.axis_index("gx") * size_x
    anchor_y = lax.axis_index("gy") * size_y
    noise_here = shot_noise[0]
    spread = jnp.exp(log_scale)
    velocity = mean_velocity + spread * noise_here
    coefficient = courant_sq * velocity * velocity
    row_index = lax.broadcasted_iota(jnp.int32, (size_x, size_y, size_z), 0)
    col_index = lax.broadcasted_iota(jnp.int32, (size_x, size_y, size_z), 1)
    depth_index = lax.broadcasted_iota(jnp.int32, (size_x, size_y, size_z), 2)
    src_cell = source_column[0]
    src_x = src_cell // width_y - anchor_x
    src_y = src_cell % width_y - anchor_y
    source_field = (
        (row_index == src_x) & (col_index == src_y) & (depth_index == SRC_DEPTH)
    ).astype(jnp.float32)
    rec_cols = receiver_column[0]
    rec_x = rec_cols // width_y - anchor_x
    rec_y = rec_cols % width_y - anchor_y
    owned_mask = (rec_x >= 0) & (rec_x < size_x) & (rec_y >= 0) & (rec_y < size_y)
    flat_index = jnp.where(owned_mask, (rec_x * size_y + rec_y) * size_z + REC_DEPTH, 0)
    samples = lax.dynamic_slice_in_dim(wavelet[0], start_step[0], STEPS)
    wave_prev = checkpoint_prev[0]
    wave_now = checkpoint_now[0]
    stored_laps = []
    picked_rows = []
    for step in range(STEPS):
        laplacian = forward_laplace(wave_now)
        stored_laps.append(laplacian)
        wave_next = (
            2.0 * wave_now - wave_prev + coefficient * laplacian + samples[step] * source_field
        )
        wave_prev, wave_now = (wave_now, wave_next)
        picked_rows.append(jnp.where(owned_mask, jnp.take(wave_now.reshape(-1), flat_index), 0.0))
    stored_rows = lax.psum_scatter(
        jnp.stack(picked_rows), ("gx", "gy"), scatter_dimension=1, tiled=True
    )
    residual_store = stored_rows - observed[0]
    residual = lax.all_gather(residual_store, ("gx", "gy"), axis=1, tiled=True)
    adj_later = adjoint_next[0]
    adj_now = adjoint_now[0]
    imaging = jnp.zeros_like(mean_velocity)
    for step in range(STEPS, 0, -1):
        injected = (
            jnp.zeros((size_x * size_y * size_z,), jnp.float32)
            .at[flat_index]
            .add(jnp.where(owned_mask, residual[step - 1], 0.0))
        )
        earlier = (
            2.0 * adj_now
            - adj_later
            + adjoint_laplace(coefficient * adj_now)
            + injected.reshape(size_x, size_y, size_z)
        )
        imaging = imaging + earlier * stored_laps[step - 1]
        adj_later, adj_now = (adj_now, earlier)
    velocity_grad = 2.0 * courant_sq * velocity * imaging
    weighted = velocity_grad * noise_here
    total_grad, total_weighted = lax.psum((velocity_grad, weighted), "shot")
    grad_log_scale = spread * total_weighted + jnp.exp(2.0 * log_scale) / prior_var - 1.0
    return (total_grad, grad_log_scale)


def solution(mesh):
    return jax.shard_map(
        local,
        mesh=mesh,
        in_specs=(
            P("gx", "gy", None),
            P("gx", "gy", None),
            P("shot", "gx", "gy", None),
            P("shot", "gx", "gy", None),
            P("shot", "gx", "gy", None),
            P("shot", "gx", "gy", None),
            P("shot", "gx", "gy", None),
            P("shot", None),
            P("shot"),
            P("shot", None),
            P("shot", None, ("gx", "gy")),
            P(),
        ),
        out_specs=(P("gx", "gy", None), P("gx", "gy", None)),
        check_vma=False,
    )
```

profile of v0, /device:TPU:1, one launch (start us, length us, event | category | flops | bytes accessed | tf_op | source)
XLA Modules:
  0.0 1734.1 jit_solution(18168645930462783396)
XLA Ops:
  9.5 4.7 collective-permute-start.5
  19.5 4.8 collective-permute-start.7
  31.1 4.0 collective-permute-start.9
  37.7 4.6 collective-permute-start.11
  45.8 4.3 collective-permute-start.13
  51.4 5.9 collective-permute-start.1
  58.6 4.6 collective-permute-start.15
  66.7 6.7 collective-permute-start.17
  74.7 5.8 collective-permute-start.3
  80.6 45.5 %gather_fusion = f32[8192]{0:T(1024)S(1)} fusion(f32[32768]{0:T(1024)S(1)} %bitcast.93, s32[8192]{0:T(1024)S(1)} %get-tuple-element.17), kind=kCustom, calls=%fused_computation.clone | custom fusion | bytes 98304 | tf_op jit(solution)/shard_map/jit(_take)/gather | solution.py:115
  127.5 5.5 collective-permute-start.19
  133.0 45.5 %gather_fusion.1 = f32[8192]{0:T(1024)S(1)} fusion(f32[32768]{0:T(1024)S(1)} %bitcast.94, s32[8192]{0:T(1024)S(1)} %get-tuple-element.17), kind=kCustom, calls=%fused_computation.1.clone | custom fusion | bytes 98304 | tf_op jit(solution)/shard_map/jit(_take)/gather | solution.py:115
  178.5 45.5 %gather_fusion.2 = f32[8192]{0:T(1024)S(1)} fusion(f32[32768]{0:T(1024)S(1)} %bitcast.95, s32[8192]{0:T(1024)S(1)} %get-tuple-element.17), kind=kCustom, calls=%fused_computation.2.clone | custom fusion | bytes 98304 | tf_op jit(solution)/shard_map/jit(_take)/gather | solution.py:115
  225.2 45.5 %gather_fusion.3 = f32[8192]{0:T(1024)S(1)} fusion(f32[32768]{0:T(1024)S(1)} %bitcast.96, s32[8192]{0:T(1024)S(1)} %get-tuple-element.17), kind=kCustom, calls=%fused_computation.3.clone | custom fusion | bytes 98304 | tf_op jit(solution)/shard_map/jit(_take)/gather | solution.py:115
  274.1 658.5 %reduce-scatter.4.cloned.1.call-done = f32[64,4]{1,0:T(8,128)} async-done(((f32[8192,4]{1,0:T(8,128)}), f32[64,4]{1,0:T(8,128)}) %reduce-scatter.4.cloned.1.call-update) | async-done | bytes 1040
  933.4 306.0 %all-gather = f32[128,64,4]{1,2,0:T(4,128)S(1)} all-gather(f32[1,64,4]{1,2,0:T(4,128)S(1)} %fusion.286), channel_id=1, replica_groups=mesh['shot'=4,'gx'=16,'gy'=8] {'gx','gy'}, dimensions={0}, use_global_device_ids=true | all-gather | bytes 132096 | tf_op jit(solution)/shard_map/all_gather | solution.py:120
  1239.8 56.7 %scatter_custom_fusion = f32[32768]{0:T(1024)S(1)} fusion(s32[8192]{0:T(1024)S(1)} %bitcast.115, f32[8192]{0:T(1024)S(1)} %get-tuple-element.83, f32[]{:T(128)} %constant.90.clone.1), kind=kCustom, calls=%fused_computation.516 | custom fusion | flops 8192 | bytes 131076 | tf_op jit(solution)/shard_map/scatter-add | solution.py:128
  1298.1 4.0 collective-permute-start.21
  1308.8 56.7 %scatter_custom_fusion.1 = f32[32768]{0:T(1024)S(1)} fusion(s32[8192]{0:T(1024)S(1)} %bitcast.116, f32[8192]{0:T(1024)S(1)} %get-tuple-element.85, f32[]{:T(128)} %constant.90.clone.1), kind=kCustom, calls=%fused_computation.514 | custom fusion | flops 8192 | bytes 131076 | tf_op jit(solution)/shard_map/scatter-add | solution.py:128
  1367.3 4.7 collective-permute-start.25
  1378.5 56.9 %scatter_custom_fusion.2 = f32[32768]{0:T(1024)S(1)} fusion(s32[8192]{0:T(1024)S(1)} %bitcast.117, f32[8192]{0:T(1024)S(1)} %get-tuple-element.84, f32[]{:T(128)} %constant.90.clone.1), kind=kCustom, calls=%fused_computation.512 | custom fusion | flops 8192 | bytes 131076 | tf_op jit(solution)/shard_map/scatter-add | solution.py:128
  1437.2 4.2 collective-permute-start.29
  1448.0 56.7 %scatter_custom_fusion.3 = f32[32768]{0:T(1024)S(1)} fusion(s32[8192]{0:T(1024)S(1)} %bitcast.118, f32[8192]{0:T(1024)S(1)} %get-tuple-element.86, f32[]{:T(128)} %constant.90.clone.1), kind=kCustom, calls=%fused_computation.510 | custom fusion | flops 8192 | bytes 131076 | tf_op jit(solution)/shard_map/scatter-add | solution.py:128
  1505.9 218.2 %all-reduce.11.cloned.1.call-done = (f32[8,32,128]{2,1,0:T(8,128)}, f32[8,32,128]{2,1,0:T(8,128)}) async-done(((f32[8,32,128]{2,1,0:T(8,128)}, f32[8,32,128]{2,1,0:T(8,128)}), (f32[8,32,128]{2,1,0:T(8,128)}, f32[8,32,128]{2,1,0:T(8,128)})) %all-reduce.11.cloned.1.call-update) | async-done | bytes 262160 | tf_op jit(solution)/shard_map/psum | solution.py:140
  (123 shorter events, 62.3 us)
Async XLA Ops:
  7.2 925.4 %reduce-scatter.4.cloned.1.call-start = ((), (), s32[]{:S(2)}) async-start(), calls=%async_computation.1 | async-start | bytes 4227072
  8.2 9.2 collective-permute-start.4
  9.5 7.9 collective-permute-start.5
  18.2 6.1 collective-permute-start.6
  44.5 12.8 collective-permute-start.12
  45.8 11.6 collective-permute-start.13
  50.1 23.3 %collective-permute-start = (f32[4,32,128]{2,1,0:T(8,128)S(1)}, f32[4,32,128]{2,1,0:T(8,128)S(1)}, u32[]{:S(2)}, u32[]{:S(2)}) collective-permute-start(f32[4,32,128]{2,1,0:T(8,128)S(1)} %get-tuple-element.67), channel_id=1, source_target_pairs={{8,0},{16,8},{24,16},{32,24},{40,32},{48,40},{56,48},{64,56},{72,6... | collective-permute-start | bytes 196616 | tf_op jit(solution)/shard_map/ppermute | solution.py:26
  51.4 22.0 %collective-permute-start.1 = (f32[4,32,128]{2,1,0:T(8,128)S(1)}, f32[4,32,128]{2,1,0:T(8,128)S(1)}, u32[]{:S(2)}, u32[]{:S(2)}) collective-permute-start(f32[4,32,128]{2,1,0:T(8,128)S(1)} %get-tuple-element.66), channel_id=1, source_target_pairs={{0,8},{8,16},{16,24},{24,32},{32,40},{40,48},{48,56},{56,64},{64,7... | collective-permute-start | bytes 196616 | tf_op jit(solution)/shard_map/ppermute | solution.py:24
  57.3 6.0 collective-permute-start.14
  65.4 60.7 %collective-permute-start.16 = (f32[4,32,128]{2,1,0:T(8,128)S(1)}, f32[4,32,128]{2,1,0:T(8,128)S(1)}, u32[]{:S(2)}, u32[]{:S(2)}) collective-permute-start(f32[4,32,128]{2,1,0:T(8,128)S(1)} %get-tuple-element.73), channel_id=1, source_target_pairs={{8,0},{16,8},{24,16},{32,24},{40,32},{48,40},{56,48},{64,56},{72,6... | collective-permute-start | bytes 196616 | tf_op jit(solution)/shard_map/ppermute | solution.py:26
  66.7 59.4 %collective-permute-start.17 = (f32[4,32,128]{2,1,0:T(8,128)S(1)}, f32[4,32,128]{2,1,0:T(8,128)S(1)}, u32[]{:S(2)}, u32[]{:S(2)}) collective-permute-start(f32[4,32,128]{2,1,0:T(8,128)S(1)} %get-tuple-element.72), channel_id=1, source_target_pairs={{0,8},{8,16},{16,24},{24,32},{32,40},{40,48},{48,56},{56,64},{64,7... | collective-permute-start | bytes 196616 | tf_op jit(solution)/shard_map/ppermute | solution.py:24
  73.4 200.6 %collective-permute-start.2 = (f32[16,4,128]{2,1,0:T(4,128)S(1)}, f32[16,4,128]{2,1,0:T(4,128)S(1)}, u32[]{:S(2)}, u32[]{:S(2)}) collective-permute-start(f32[16,4,128]{2,1,0:T(4,128)S(1)} %get-tuple-element.42), channel_id=1, source_target_pairs={{1,0},{2,1},{3,2},{4,3},{5,4},{6,5},{7,6},{9,8},{10,9},{11,10},{12... | collective-permute-start | bytes 98312 | tf_op jit(solution)/shard_map/ppermute | solution.py:26
  74.7 199.3 %collective-permute-start.3 = (f32[16,4,128]{2,1,0:T(4,128)S(1)}, f32[16,4,128]{2,1,0:T(4,128)S(1)}, u32[]{:S(2)}, u32[]{:S(2)}) collective-permute-start(f32[16,4,128]{2,1,0:T(4,128)S(1)} %get-tuple-element.43), channel_id=1, source_target_pairs={{0,1},{1,2},{2,3},{3,4},{4,5},{5,6},{6,7},{8,9},{9,10},{10,11},{11... | collective-permute-start | bytes 98312 | tf_op jit(solution)/shard_map/ppermute | solution.py:24
  126.2 97.9 %collective-permute-start.18 = (f32[16,4,128]{2,1,0:T(4,128)S(1)}, f32[16,4,128]{2,1,0:T(4,128)S(1)}, u32[]{:S(2)}, u32[]{:S(2)}) collective-permute-start(f32[16,4,128]{2,1,0:T(4,128)S(1)} %get-tuple-element.46), channel_id=1, source_target_pairs={{1,0},{2,1},{3,2},{4,3},{5,4},{6,5},{7,6},{9,8},{10,9},{11,10},{12... | collective-permute-start | bytes 98312 | tf_op jit(solution)/shard_map/ppermute | solution.py:26
  127.5 96.6 %collective-permute-start.19 = (f32[16,4,128]{2,1,0:T(4,128)S(1)}, f32[16,4,128]{2,1,0:T(4,128)S(1)}, u32[]{:S(2)}, u32[]{:S(2)}) collective-permute-start(f32[16,4,128]{2,1,0:T(4,128)S(1)} %get-tuple-element.47), channel_id=1, source_target_pairs={{0,1},{1,2},{2,3},{3,4},{4,5},{5,6},{6,7},{8,9},{9,10},{10,11},{11... | collective-permute-start | bytes 98312 | tf_op jit(solution)/shard_map/ppermute | solution.py:24
  273.6 1450.5 %all-reduce.11.cloned.1.call-start = ((), (), s32[]{:S(2)}) async-start(), calls=%async_computation.2 | async-start | bytes 524288 | tf_op jit(solution)/shard_map/psum | solution.py:140
  1303.5 62.0 %collective-permute-start.22 = (f32[16,4,128]{2,1,0:T(4,128)S(1)}, f32[16,4,128]{2,1,0:T(4,128)S(1)}, u32[]{:S(2)}, u32[]{:S(2)}) collective-permute-start(f32[16,4,128]{2,1,0:T(4,128)S(1)} %get-tuple-element.38), channel_id=1, source_target_pairs={{1,0},{2,1},{3,2},{4,3},{5,4},{6,5},{7,6},{9,8},{10,9},{11,10},{12... | collective-permute-start | bytes 98312 | tf_op jit(solution)/shard_map/ppermute | solution.py:26
  1304.8 60.7 %collective-permute-start.23 = (f32[16,4,128]{2,1,0:T(4,128)S(1)}, f32[16,4,128]{2,1,0:T(4,128)S(1)}, u32[]{:S(2)}, u32[]{:S(2)}) collective-permute-start(f32[16,4,128]{2,1,0:T(4,128)S(1)} %get-tuple-element.39), channel_id=1, source_target_pairs={{0,1},{1,2},{2,3},{3,4},{4,5},{5,6},{6,7},{8,9},{9,10},{10,11},{11... | collective-permute-start | bytes 98312 | tf_op jit(solution)/shard_map/ppermute | solution.py:24
  1365.9 6.0 collective-permute-start.24
  1367.3 6.0 collective-permute-start.25
  1373.2 62.2 %collective-permute-start.26 = (f32[16,4,128]{2,1,0:T(4,128)S(1)}, f32[16,4,128]{2,1,0:T(4,128)S(1)}, u32[]{:S(2)}, u32[]{:S(2)}) collective-permute-start(f32[16,4,128]{2,1,0:T(4,128)S(1)} %get-tuple-element.34), channel_id=1, source_target_pairs={{1,0},{2,1},{3,2},{4,3},{5,4},{6,5},{7,6},{9,8},{10,9},{11,10},{12... | collective-permute-start | bytes 98312 | tf_op jit(solution)/shard_map/ppermute | solution.py:26
  1374.5 60.9 %collective-permute-start.27 = (f32[16,4,128]{2,1,0:T(4,128)S(1)}, f32[16,4,128]{2,1,0:T(4,128)S(1)}, u32[]{:S(2)}, u32[]{:S(2)}) collective-permute-start(f32[16,4,128]{2,1,0:T(4,128)S(1)} %get-tuple-element.35), channel_id=1, source_target_pairs={{0,1},{1,2},{2,3},{3,4},{4,5},{5,6},{6,7},{8,9},{9,10},{10,11},{11... | collective-permute-start | bytes 98312 | tf_op jit(solution)/shard_map/ppermute | solution.py:24
  1442.7 62.0 %collective-permute-start.30 = (f32[16,4,128]{2,1,0:T(4,128)S(1)}, f32[16,4,128]{2,1,0:T(4,128)S(1)}, u32[]{:S(2)}, u32[]{:S(2)}) collective-permute-start(f32[16,4,128]{2,1,0:T(4,128)S(1)} %get-tuple-element.30), channel_id=1, source_target_pairs={{1,0},{2,1},{3,2},{4,3},{5,4},{6,5},{7,6},{9,8},{10,9},{11,10},{12... | collective-permute-start | bytes 98312 | tf_op jit(solution)/shard_map/ppermute | solution.py:26
  1444.0 60.7 %collective-permute-start.31 = (f32[16,4,128]{2,1,0:T(4,128)S(1)}, f32[16,4,128]{2,1,0:T(4,128)S(1)}, u32[]{:S(2)}, u32[]{:S(2)}) collective-permute-start(f32[16,4,128]{2,1,0:T(4,128)S(1)} %get-tuple-element.31), channel_id=1, source_target_pairs={{0,1},{1,2},{2,3},{3,4},{4,5},{5,6},{6,7},{8,9},{9,10},{10,11},{11... | collective-permute-start | bytes 98312 | tf_op jit(solution)/shard_map/ppermute | solution.py:24
  (18 other events, 3351.4 us)
Sparse Core Ops, SparseCore 0:
  273.7 658.8 reduce-scatter.3
  1506.0 218.0 all-reduce.10
where the time goes:
time: 1740 us; the launch traced here: 1730 us
  waiting for transfers between devices  885 us (51%)
  blocking collectives  306 us (18%)
  other arithmetic  241 us (14%)
  local copies, waits for them, and re-layouts  189 us (11%)
  starting transfers between devices  96.5 us (6%)
    unnamed x3, waiting for transfers between devices  659 us
    all_gather x1, blocking collectives, local(): residual = lax.all_gather(residual_store, ('gx', 'gy'), axis=1, tiled=True)  306 us
    scatter-add x4, other arithmetic, local(): injected = jnp.zeros((size_x * size_y * size_z,), jnp.float32).at[flat_in...  227 us
    psum x1, waiting for transfers between devices, local(): total_grad, total_weighted = lax.psum((velocity_grad, weighted), 'shot')  218 us
    gather x4, local copies, waits for them, and re-layouts, local(): jnp.take(wave_now.reshape(-1), flat_index)  182 us
    ppermute x16, starting transfers between devices, with_halo(): lax.ppermute(tail, axis, [(i, (i + 1) % count) for i in range(ends)])  75.8 us
  transfers between devices with their start and end apart: 34, of which 9 were waited for; matrix products, arithmetic and copies ran while one was open for 21% of the time, Pallas kernels for 0%

commit v1 on v0

v1 whole, which is shorter than its diff:
```python
import jax
import jax.numpy as jnp
from jax import lax
from jax.sharding import PartitionSpec as P

STEPS = 4
SRC_DEPTH = 6
REC_DEPTH = 3
W = 4
SLAB = 16

stencil_weights = (-205.0 / 72.0, 8.0 / 5.0, -1.0 / 5.0, 8.0 / 315.0, -1.0 / 560.0)
courant_sq = 0.0625
prior_var = 0.01


def shift(x, axis, k):
    n = lax.axis_size(axis)
    return lax.ppermute(x, axis, [(i, i + k) for i in range(n) if 0 <= i + k < n])


def swap_x(low, high):
    return shift(high, "gx", 1), shift(low, "gx", -1)


def swap_y(low, high):
    return shift(high, "gy", 1), shift(low, "gy", -1)


def star(center, pad_x, pad_y):
    nx, ny, nz = center.shape
    pad_z = jnp.pad(center, ((0, 0), (0, 0), (W, W)))
    out = 3.0 * stencil_weights[0] * center
    for k in range(1, W + 1):
        beside = pad_x[W + k : W + k + nx] + pad_x[W - k : W - k + nx]
        beside = beside + pad_y[:, W + k : W + k + ny] + pad_y[:, W - k : W - k + ny]
        beside = beside + pad_z[:, :, W + k : W + k + nz] + pad_z[:, :, W - k : W - k + nz]
        out = out + stencil_weights[k] * beside
    return out


def star_inner(block):
    return star(block[W:-W, W:-W], block[:, W:-W], block[W:-W])


def local(
    mean_velocity,
    log_scale,
    shot_noise,
    checkpoint_prev,
    checkpoint_now,
    adjoint_next,
    adjoint_now,
    wavelet,
    source_column,
    receiver_column,
    observed,
    start_step,
):
    sx, sy, sz = mean_velocity.shape
    ngx, ngy, nshot = lax.axis_size("gx"), lax.axis_size("gy"), lax.axis_size("shot")
    width_y = sy * ngy
    ix, iy = lax.axis_index("gx"), lax.axis_index("gy")
    ax, ay = ix * sx, iy * sy
    noise = shot_noise[0]
    spread = jnp.exp(log_scale)
    velocity = mean_velocity + spread * noise
    coef = courant_sq * velocity * velocity

    row = lax.broadcasted_iota(jnp.int32, (sx, sy, sz), 0)
    col = lax.broadcasted_iota(jnp.int32, (sx, sy, sz), 1)
    dep = lax.broadcasted_iota(jnp.int32, (sx, sy, sz), 2)
    src = source_column[0]
    at_source = (row == src // width_y - ax) & (col == src % width_y - ay) & (dep == SRC_DEPTH)
    samples = lax.dynamic_slice_in_dim(wavelet[0], start_step[0], STEPS)

    p_prev, p = checkpoint_prev[0], checkpoint_now[0]
    q_later, q = adjoint_next[0], adjoint_now[0]
    laps, planes, free = [], [], []

    cslab = coef[:, :, :SLAB]
    for n in range(STEPS):
        s = coef * q
        xl = [p[:W], s[:W]]
        xh = [p[sx - W :], s[sx - W :]]
        yl = [p[:, :W], s[:, :W]]
        yh = [p[:, sy - W :], s[:, sy - W :]]
        from_l, from_r = swap_x(jnp.concatenate(xl, 0), jnp.concatenate(xh, 0))
        from_d, from_u = swap_y(jnp.concatenate(yl, 1), jnp.concatenate(yh, 1))
        if n == 0:
            cd, cu = swap_y(cslab[:, :8].reshape(sx, 128), cslab[:, sy - 8 :].reshape(sx, 128))
            cd, cu = cd.reshape(sx, 8, SLAB), cu.reshape(sx, 8, SLAB)
            cy = jnp.concatenate([cd, cslab, cu], 1)
        if n == 1:
            cflat = cy.reshape(sx, -1, 128)
            cl, cr = swap_x(cflat, cflat)
            cext = jnp.concatenate([cl.reshape(cy.shape), cy, cr.reshape(cy.shape)], 0)
        lap = star(
            p,
            jnp.concatenate([from_l[:W], p, from_r[:W]], 0),
            jnp.concatenate([from_d[:, :W], p, from_u[:, :W]], 1),
        )
        lap_s = star(
            s,
            jnp.concatenate([from_l[W:], s, from_r[W:]], 0),
            jnp.concatenate([from_d[:, W:], s, from_u[:, W:]], 1),
        )
        p_next = 2.0 * p - p_prev + coef * lap + jnp.where(at_source, samples[n], 0.0)
        q_next = 2.0 * q - q_later + lap_s
        p_prev, p = p, p_next
        q_later, q = q, q_next
        laps.append(lap)
        planes.append(p[:, :, REC_DEPTH])
        free.append(q)

    mine = jnp.concatenate(
        [
            planes[3].reshape(-1),
            planes[2].reshape(-1),
            planes[1].reshape(-1),
            coef[:, :, REC_DEPTH].reshape(-1),
            observed[0].reshape(-1),
        ]
    )
    ncell = sx * sy
    everyone = lax.all_to_all(
        jnp.broadcast_to(mine[None], (ngx * ngy, mine.size)), ("gx", "gy"), 0, 0
    )
    grid = everyone[:, : 4 * ncell].reshape(ngx, ngy, 4, sx, sy)
    grid = jnp.pad(grid, ((2, 2), (1, 1), (0, 0), (0, 0), (0, 0)))
    near = lax.dynamic_slice(grid, (ix, iy, 0, 0, 0), (5, 3, 4, sx, sy))
    near = near.transpose(2, 0, 3, 1, 4).reshape(4, 5 * sx, 3 * sy)
    hx, hy = 2 * sx - 12, sy - 12
    near = near[:, hx : hx + sx + 24, hy : hy + sy + 24]
    traces = everyone[:, 4 * ncell :].reshape(ngx * ngy, STEPS, -1).transpose(1, 0, 2)
    traces = traces.reshape(STEPS, -1)
    ex, ey = sx + 24, sy + 24
    rec = receiver_column[0]
    rx = rec // width_y - ax + 12
    ry = rec % width_y - ay + 12
    hot_x = (lax.broadcasted_iota(jnp.int32, (ex, rec.size), 0) == rx[None]).astype(jnp.float32)
    hot_y = (lax.broadcasted_iota(jnp.int32, (ey, rec.size), 0) == ry[None]).astype(jnp.float32)
    values = jnp.concatenate([traces, jnp.ones((1, rec.size), jnp.float32)], 0)
    table = (values[:, None, :] * hot_x[None]).reshape(-1, rec.size)
    sums = lax.dot_general(
        table, hot_y, (((1,), (1,)), ((), ())), precision=lax.Precision.HIGHEST
    ).reshape(STEPS + 1, ex, ey)
    count = sums[STEPS]

    def lift(plane):
        return jnp.pad(plane[:, :, None], ((0, 0), (0, 0), (REC_DEPTH, SLAB - 1 - REC_DEPTH)))

    r3 = count * near[0] - sums[3]
    in2 = (count * near[1] - sums[2])[4:-4, 4:-4]
    in1 = (count * near[2] - sums[1])[8:-8, 8:-8]
    in0 = count[12:-12, 12:-12] * planes[0] - sums[0][12:-12, 12:-12]
    r3 = lift(r3)
    c3 = lift(near[3])
    r2 = 2.0 * r3[4:-4, 4:-4] + star_inner(c3 * r3) + lift(in2)
    r1 = 2.0 * r2[4:-4, 4:-4] - r3[8:-8, 8:-8] + star_inner(cext * r2) + lift(in1)
    r0 = (
        2.0 * r1[4:-4, 4:-4]
        - r2[8:-8, 8:-8]
        + star_inner(cext[4:-4, 4:-4] * r1)
        + lift(in0)
    )
    r = [r0, r1[4:-4, 4:-4], r2[8:-8, 8:-8], r3[12:-12, 12:-12]]
    imaging = jnp.zeros_like(mean_velocity)
    for n in range(STEPS):
        adj = free[STEPS - 1 - n] + jnp.pad(r[n], ((0, 0), (0, 0), (0, sz - SLAB)))
        imaging = imaging + adj * laps[n]
    velocity_grad = 2.0 * courant_sq * velocity * imaging
    both = jnp.stack([velocity_grad, velocity_grad * noise])
    parts = both.reshape(2, nshot, sx // nshot, sy, sz).transpose(1, 0, 2, 3, 4)
    quarter = lax.all_to_all(parts, "shot", 0, 0).sum(0)
    total = lax.all_gather(quarter, "shot", axis=0)
    total_grad = total[:, 0].reshape(sx, sy, sz)
    total_weighted = total[:, 1].reshape(sx, sy, sz)
    grad_log_scale = spread * total_weighted + jnp.exp(2.0 * log_scale) / prior_var - 1.0
    return (total_grad, grad_log_scale)


def solution(mesh):
    return jax.shard_map(
        local,
        mesh=mesh,
        in_specs=(
            P("gx", "gy", None),
            P("gx", "gy", None),
            P("shot", "gx", "gy", None),
            P("shot", "gx", "gy", None),
            P("shot", "gx", "gy", None),
            P("shot", "gx", "gy", None),
            P("shot", "gx", "gy", None),
            P("shot", None),
            P("shot"),
            P("shot", None),
            P("shot", None, ("gx", "gy")),
            P(),
        ),
        out_specs=(P("gx", "gy", None), P("gx", "gy", None)),
        check_vma=False,
    )
```

time: 1740 us -> 210 us (0.12)
  waiting for transfers between devices: 885 us -> 27.4 us
  blocking collectives: 306 us -> 36.5 us
  other arithmetic: 241 us -> 34 us
  local copies, waits for them, and re-layouts: 189 us -> 19.3 us
    unnamed x3 -> x0, waiting for transfers between devices: 659 us -> none
    all_gather x1, blocking collectives: 306 us -> 10.7 us  [local(): total = lax.all_gather(quarter, 'shot', axis=0)]
    scatter-add x4 -> x0, other arithmetic: 227 us -> none  [local(): injected = jnp.zeros((size_x * size_y * size_z,), jnp.float32).at[flat_in...]
    psum x1 -> x0, waiting for transfers between devices: 218 us -> none  [local(): total_grad, total_weighted = lax.psum((velocity_grad, weighted), 'shot')]
    gather x4 -> x0, local copies, waits for them, and re-layouts: 182 us -> none  [local(): jnp.take(wave_now.reshape(-1), flat_index)]
    ppermute x32 -> x20, starting transfers between devices: 96.4 us -> 58.5 us  [shift(): lax.ppermute(x, axis, [(i, i + k) for i in range(n) if 0 <= i + k < n])]
    all_to_all x0 -> x1, blocking collectives: none -> 25.8 us  [local(): quarter = lax.all_to_all(parts, 'shot', 0, 0).sum(0)]
    all_to_all x0 -> x1, starting transfers between devices: none -> 25.7 us  [local(): lax.all_to_all(jnp.broadcast_to(mine[None], (ngx * ngy, mine.size)), ('gx...]
  transfers between devices with their start and end apart: 34 -> 21, of which waited for: 9 -> 7; matrix products, arithmetic and copies ran while one was open for 21% -> 12% of each run, Pallas kernels for 0% -> 0%
where the time goes in v1:
time: 210 us; the launch traced here: 208 us
  starting transfers between devices  84.3 us (40%)
  blocking collectives  36.5 us (17%)
  other arithmetic  34 us (16%)
  waiting for transfers between devices  27.4 us (13%)
  local copies, waits for them, and re-layouts  19.3 us (9%)
  between operations  3.26 us (2%)
  matrix products  3.09 us (1%)
    ppermute x20, starting transfers between devices, shift(): lax.ppermute(x, axis, [(i, i + k) for i in range(n) if 0 <= i + k < n])  58.5 us
    all_to_all x1, blocking collectives, local(): quarter = lax.all_to_all(parts, 'shot', 0, 0).sum(0)  25.8 us
    all_to_all x1, starting transfers between devices, local(): lax.all_to_all(jnp.broadcast_to(mine[None], (ngx * ngy, mine.size)), ('gx...  25.7 us
    ppermute x20, waiting for transfers between devices, shift(): lax.ppermute(x, axis, [(i, i + k) for i in range(n) if 0 <= i + k < n])  14.6 us
    all_to_all x1, waiting for transfers between devices, local(): lax.all_to_all(jnp.broadcast_to(mine[None], (ngx * ngy, mine.size)), ('gx...  12.8 us
    all_gather x1, blocking collectives, local(): total = lax.all_gather(quarter, 'shot', axis=0)  10.7 us
    mul x1, other arithmetic, local(): cext * r2  10.5 us
    add x3, other arithmetic, local(): 2.0 * p - p_prev + coef * lap + jnp.where(at_source, samples[n], 0.0)  8.74 us
  transfers between devices with their start and end apart: 21, of which 7 were waited for; matrix products, arithmetic and copies ran while one was open for 12% of the time, Pallas kernels for 0%

profile of v1, /device:TPU:1, one launch (start us, length us, event | category | flops | bytes accessed | tf_op | source)
XLA Modules:
  0.0 207.9 jit_solution(4654134795834043210)
XLA Ops:
  4.0 5.5 %collective-permute-start.3 = (f32[8,8,128]{2,1,0:T(8,128)S(1)}, f32[8,8,128]{2,1,0:T(8,128)S(1)}, u32[]{:S(2)}, u32[]{:S(2)}) collective-permute-start(f32[8,8,128]{2,1,0:T(8,128)S(1)} %pad_maximum_fusion.43), channel_id=1, source_target_pairs={{0,1},{1,2},{2,3},{3,4},{4,5},{5,6},{6,7},{8,9},{9,10},{10,11},{11... | collective-permute-start | bytes 98312 | tf_op jit(solution)/shard_map/ppermute | solution.py:19
  11.8 4.0 %collective-permute-start.16 = (f32[8,128]{1,0:T(8,128)S(1)}, f32[8,128]{1,0:T(8,128)S(1)}, u32[]{:S(2)}, u32[]{:S(2)}) collective-permute-start(f32[8,128]{1,0:T(8,128)S(1)} %reshape.100), channel_id=1, source_target_pairs={{0,1},{1,2},{2,3},{3,4},{4,5},{5,6},{6,7},{8,9},{9,10},{10,11},{11... | collective-permute-start | bytes 12296 | tf_op jit(solution)/shard_map/ppermute | solution.py:19
  22.5 4.0 %collective-permute-start.1 = (f32[8,32,128]{2,1,0:T(8,128)S(1)}, f32[8,32,128]{2,1,0:T(8,128)S(1)}, u32[]{:S(2)}, u32[]{:S(2)}) collective-permute-start(f32[8,32,128]{2,1,0:T(8,128)S(1)} %pad_maximum_fusion.35), channel_id=1, source_target_pairs={{0,8},{8,16},{16,24},{24,32},{32,40},{40,48},{48,56},{56,64},{64,7... | collective-permute-start | bytes 393224 | tf_op jit(solution)/shard_map/ppermute | solution.py:19
  26.8 3.2 %collective-permute-start.18 = (f32[8,6,128]{2,1,0:T(8,128)S(1)}, f32[8,6,128]{2,1,0:T(8,128)S(1)}, u32[]{:S(2)}, u32[]{:S(2)}) collective-permute-start(f32[8,6,128]{2,1,0:T(8,128)S(1)} %reshape.104), channel_id=1, source_target_pairs={{0,8},{8,16},{16,24},{24,32},{32,40},{40,48},{48,56},{56,64},{64,7... | collective-permute-start | bytes 73736 | tf_op jit(solution)/shard_map/ppermute | solution.py:19
  32.8 4.3 %fusion.419 = (f32[8,32,128]{2,1,0:T(8,128)S(1)}, f32[8,32,128]{2,1,0:T(8,128)S(1)}) fusion(f32[1,8,32,128]{3,2,1,0:T(8,128)} %param.15, f32[8,32,128]{2,1,0:T(8,128)S(1)} %get-tuple-element.35, f32[]{:T(128)} %bitcast.9, f32[1,8,32,128]{3,2,1,0:T(8,128)} %param.16, pred[128]{0:T(512)(128)(4,1)S(1)} %iota_compare_fusion.3, ...), kind=kLoop, calls=%fused_computation.783 | loop fusion | flops 1736704 | bytes 950444 | tf_op jit(solution)/shard_map/add | solution.py:108
  38.5 4.6 %collective-permute-start.5 = (f32[8,32,128]{2,1,0:T(8,128)S(1)}, f32[8,32,128]{2,1,0:T(8,128)S(1)}, u32[]{:S(2)}, u32[]{:S(2)}) collective-permute-start(f32[8,32,128]{2,1,0:T(8,128)S(1)} %pad_maximum_fusion.37), channel_id=1, source_target_pairs={{0,8},{8,16},{16,24},{24,32},{32,40},{40,48},{48,56},{56,64},{64,7... | collective-permute-start | bytes 393224 | tf_op jit(solution)/shard_map/ppermute | solution.py:19
  44.5 4.6 %collective-permute-done.6 = f32[8,8,128]{2,1,0:T(8,128)S(1)} collective-permute-done((f32[8,8,128]{2,1,0:T(8,128)S(1)}, f32[8,8,128]{2,1,0:T(8,128)S(1)}, u32[]{:S(2)}, u32[]{:S(2)}) %collective-permute-start.6) | collective-permute-done | bytes 32800 | tf_op jit(solution)/shard_map/ppermute | solution.py:19
  49.1 5.2 %collective-permute-start.7 = (f32[8,8,128]{2,1,0:T(8,128)S(1)}, f32[8,8,128]{2,1,0:T(8,128)S(1)}, u32[]{:S(2)}, u32[]{:S(2)}) collective-permute-start(f32[8,8,128]{2,1,0:T(8,128)S(1)} %pad_maximum_fusion.45), channel_id=1, source_target_pairs={{0,1},{1,2},{2,3},{3,4},{4,5},{5,6},{6,7},{8,9},{9,10},{10,11},{11... | collective-permute-start | bytes 98312 | tf_op jit(solution)/shard_map/ppermute | solution.py:19
  58.8 6.4 %collective-permute-start.9 = (f32[8,32,128]{2,1,0:T(8,128)S(1)}, f32[8,32,128]{2,1,0:T(8,128)S(1)}, u32[]{:S(2)}, u32[]{:S(2)}) collective-permute-start(f32[8,32,128]{2,1,0:T(8,128)S(1)} %pad_maximum_fusion.39), channel_id=1, source_target_pairs={{0,8},{8,16},{16,24},{24,32},{32,40},{40,48},{48,56},{56,64},{64,7... | collective-permute-start | bytes 393224 | tf_op jit(solution)/shard_map/ppermute | solution.py:19
  66.5 3.6 %collective-permute-done.10 = f32[8,8,128]{2,1,0:T(8,128)S(1)} collective-permute-done((f32[8,8,128]{2,1,0:T(8,128)S(1)}, f32[8,8,128]{2,1,0:T(8,128)S(1)}, u32[]{:S(2)}, u32[]{:S(2)}) %collective-permute-start.10) | collective-permute-done | bytes 32800 | tf_op jit(solution)/shard_map/ppermute | solution.py:19
  70.1 4.3 %collective-permute-start.11 = (f32[8,8,128]{2,1,0:T(8,128)S(1)}, f32[8,8,128]{2,1,0:T(8,128)S(1)}, u32[]{:S(2)}, u32[]{:S(2)}) collective-permute-start(f32[8,8,128]{2,1,0:T(8,128)S(1)} %pad_maximum_fusion.47), channel_id=1, source_target_pairs={{0,1},{1,2},{2,3},{3,4},{4,5},{5,6},{6,7},{8,9},{9,10},{10,11},{11... | collective-permute-start | bytes 98312 | tf_op jit(solution)/shard_map/ppermute | solution.py:19
  77.1 2.9 %select_add_fusion = (f32[8,32,128]{2,1,0:T(8,128)S(1)}, f32[8,32,128]{2,1,0:T(8,128)}) fusion(f32[8,32,128]{2,1,0:T(8,128)S(1)} %get-tuple-element.35, f32[8,32,128]{2,1,0:T(8,128)S(1)} %get-tuple-element.27, f32[]{:T(128)} %bitcast.11, f32[]{:T(128)} %bitcast.10, f32[8,32,128]{2,1,0:T(8,128)S(1)} %get-tuple-element.31, ...), kind=kLoop, calls=%fused_computation.791 | loop fusion | flops 2129920 | bytes 1212596 | tf_op jit(solution)/shard_map/add | solution.py:108
  81.3 4.0 %collective-permute-start.13 = (f32[8,32,128]{2,1,0:T(8,128)S(1)}, f32[8,32,128]{2,1,0:T(8,128)S(1)}, u32[]{:S(2)}, u32[]{:S(2)}) collective-permute-start(f32[8,32,128]{2,1,0:T(8,128)S(1)} %pad_maximum_fusion.41), channel_id=1, source_target_pairs={{0,8},{8,16},{16,24},{24,32},{32,40},{40,48},{48,56},{56,64},{64,7... | collective-permute-start | bytes 393224 | tf_op jit(solution)/shard_map/ppermute | solution.py:19
  86.7 3.9 %collective-permute-done.14 = f32[8,8,128]{2,1,0:T(8,128)S(1)} collective-permute-done((f32[8,8,128]{2,1,0:T(8,128)S(1)}, f32[8,8,128]{2,1,0:T(8,128)S(1)}, u32[]{:S(2)}, u32[]{:S(2)}) %collective-permute-start.14) | collective-permute-done | bytes 32800 | tf_op jit(solution)/shard_map/ppermute | solution.py:19
  90.6 4.6 %collective-permute-start.15 = (f32[8,8,128]{2,1,0:T(8,128)S(1)}, f32[8,8,128]{2,1,0:T(8,128)S(1)}, u32[]{:S(2)}, u32[]{:S(2)}) collective-permute-start(f32[8,8,128]{2,1,0:T(8,128)S(1)} %pad_maximum_fusion.49), channel_id=1, source_target_pairs={{0,1},{1,2},{2,3},{3,4},{4,5},{5,6},{6,7},{8,9},{9,10},{10,11},{11... | collective-permute-start | bytes 98312 | tf_op jit(solution)/shard_map/ppermute | solution.py:19
  100.9 25.7 %all-to-all-start = ((f32[128,1,1280]{2,1,0:T(1,128)}), f32[128,1,1280]{2,1,0:T(1,128)S(1)}, u32[]{:S(2)}, u32[]{:S(2)}) async-start(f32[128,1,1280]{2,1,0:T(1,128)} %broadcast_in_dim.48), calls=%async_computation | async-start | bytes 1310720 | tf_op jit(solution)/shard_map/all_to_all | solution.py:126
  129.3 12.8 %all-to-all-done = f32[128,1,1280]{2,1,0:T(1,128)S(1)} async-done(((f32[128,1,1280]{2,1,0:T(1,128)}), f32[128,1,1280]{2,1,0:T(1,128)S(1)}, u32[]{:S(2)}, u32[]{:S(2)}) %all-to-all-start) | async-done | bytes 655392 | tf_op jit(solution)/shard_map/all_to_all | solution.py:126
  143.9 1.7 reshape.98
  147.0 3.1 %fusion = f32[160,56]{0,1:T(8,128)S(1)} fusion(f32[160,8192]{1,0:T(8,128)S(1)} %bitcast.98, s32[8192]{0:T(1024)S(1)} %bitcast.109), kind=kOutput, calls=%fused_computation.3 | convolution fusion | flops 881262592 | bytes 5311488 | tf_op jit(solution)/shard_map/dot_general | solution.py:145
  154.7 10.5 %fusion.427 = (f32[24,48,16]{2,1,0:T(8,128)S(1)}, f32[24,48,16]{2,1,0:T(8,128)S(1)}, f32[24,48,16]{2,1,0:T(8,128)S(1)}) fusion(f32[8,48,16]{2,1,0:T(8,128)} %reshape.106, f32[8,8,16]{2,1,0:T(8,128)S(1)} %copy-done.21, f32[8,32,16]{2,1,0:T(8,128)S(1)} %bitcast.100, f32[8,8,16]{2,1,0:T(8,128)S(1)} %copy-done.19, f32[8,48,16]{2,1,0:T(8,128)} %reshape.105, ...), kind=kLoop, calls=%fused_computation.838 | loop fusion | flops 976896 | bytes 387584 | tf_op jit(solution)/shard_map/mul | solution.py:160
  165.3 2.1 slice_multiply_fusion
  168.3 1.6 bitcast_multiply_fusion.3
  170.0 25.8 %all_to_all.14 = f32[4,2,2,32,128]{4,3,2,1,0:T(8,128)S(1)} all-to-all(f32[4,2,2,32,128]{4,3,2,1,0:T(8,128)S(1)} %copy.1065), channel_id=1, replica_groups=mesh['shot'=4,'gx'=16,'gy'=8] {'shot'}, dimensions={0} | all-to-all | bytes 524288 | tf_op jit(solution)/shard_map/all_to_all | solution.py:175
  195.8 10.7 %all-gather = f32[8,2,32,128]{3,2,1,0:T(8,128)S(1)} all-gather(f32[2,2,32,128]{3,2,1,0:T(8,128)S(1)} %reduce_sum.9), channel_id=2, replica_groups=mesh['shot'=4,'gx'=16,'gy'=8] {'shot'}, dimensions={0}, use_global_device_ids=true | all-gather | bytes 327680 | tf_op jit(solution)/shard_map/all_gather | solution.py:176
  (202 shorter events, 45.6 us)
Async XLA Ops:
  0.7 55.1 %copy-start.1 = (f32[1,8,32,128]{3,2,1,0:T(8,128)S(1)}, f32[1,8,32,128]{3,2,1,0:T(8,128)}, u32[]{:S(2)}) copy-start(f32[1,8,32,128]{3,2,1,0:T(8,128)} %param.16) | copy-start | bytes 393220
  0.7 55.1 %copy-start.16 = (f32[1,8,32,128]{3,2,1,0:T(8,128)S(1)}, f32[1,8,32,128]{3,2,1,0:T(8,128)}, u32[]{:S(2)}) copy-start(f32[1,8,32,128]{3,2,1,0:T(8,128)} %param.15) | copy-start | bytes 393220
  2.7 27.4 %collective-permute-start.2 = (f32[8,8,128]{2,1,0:T(8,128)S(1)}, f32[8,8,128]{2,1,0:T(8,128)S(1)}, u32[]{:S(2)}, u32[]{:S(2)}) collective-permute-start(f32[8,8,128]{2,1,0:T(8,128)S(1)} %pad_maximum_fusion.42), channel_id=1, source_target_pairs={{1,0},{2,1},{3,2},{4,3},{5,4},{6,5},{7,6},{9,8},{10,9},{11,10},{12... | collective-permute-start | bytes 98312 | tf_op jit(solution)/shard_map/ppermute | solution.py:19
  4.0 27.4 %collective-permute-start.3 = (f32[8,8,128]{2,1,0:T(8,128)S(1)}, f32[8,8,128]{2,1,0:T(8,128)S(1)}, u32[]{:S(2)}, u32[]{:S(2)}) collective-permute-start(f32[8,8,128]{2,1,0:T(8,128)S(1)} %pad_maximum_fusion.43), channel_id=1, source_target_pairs={{0,1},{1,2},{2,3},{3,4},{4,5},{5,6},{6,7},{8,9},{9,10},{10,11},{11... | collective-permute-start | bytes 98312 | tf_op jit(solution)/shard_map/ppermute | solution.py:19
  10.4 21.0 %collective-permute-start = (f32[8,32,128]{2,1,0:T(8,128)S(1)}, f32[8,32,128]{2,1,0:T(8,128)S(1)}, u32[]{:S(2)}, u32[]{:S(2)}) collective-permute-start(f32[8,32,128]{2,1,0:T(8,128)S(1)} %pad_maximum_fusion.34), channel_id=1, source_target_pairs={{8,0},{16,8},{24,16},{32,24},{40,32},{48,40},{56,48},{64,56},{72,6... | collective-permute-start | bytes 393224 | tf_op jit(solution)/shard_map/ppermute | solution.py:19
  11.8 10.8 %collective-permute-start.16 = (f32[8,128]{1,0:T(8,128)S(1)}, f32[8,128]{1,0:T(8,128)S(1)}, u32[]{:S(2)}, u32[]{:S(2)}) collective-permute-start(f32[8,128]{1,0:T(8,128)S(1)} %reshape.100), channel_id=1, source_target_pairs={{0,1},{1,2},{2,3},{3,4},{4,5},{5,6},{6,7},{8,9},{9,10},{10,11},{11... | collective-permute-start | bytes 12296 | tf_op jit(solution)/shard_map/ppermute | solution.py:19
  15.9 10.8 %collective-permute-start.17 = (f32[8,128]{1,0:T(8,128)S(1)}, f32[8,128]{1,0:T(8,128)S(1)}, u32[]{:S(2)}, u32[]{:S(2)}) collective-permute-start(f32[8,128]{1,0:T(8,128)S(1)} %reshape.102), channel_id=1, source_target_pairs={{1,0},{2,1},{3,2},{4,3},{5,4},{6,5},{7,6},{9,8},{10,9},{11,10},{12... | collective-permute-start | bytes 12296 | tf_op jit(solution)/shard_map/ppermute | solution.py:19
  22.5 8.9 %collective-permute-start.1 = (f32[8,32,128]{2,1,0:T(8,128)S(1)}, f32[8,32,128]{2,1,0:T(8,128)S(1)}, u32[]{:S(2)}, u32[]{:S(2)}) collective-permute-start(f32[8,32,128]{2,1,0:T(8,128)S(1)} %pad_maximum_fusion.35), channel_id=1, source_target_pairs={{0,8},{8,16},{16,24},{24,32},{32,40},{40,48},{48,56},{56,64},{64,7... | collective-permute-start | bytes 393224 | tf_op jit(solution)/shard_map/ppermute | solution.py:19
  26.8 99.9 %collective-permute-start.18 = (f32[8,6,128]{2,1,0:T(8,128)S(1)}, f32[8,6,128]{2,1,0:T(8,128)S(1)}, u32[]{:S(2)}, u32[]{:S(2)}) collective-permute-start(f32[8,6,128]{2,1,0:T(8,128)S(1)} %reshape.104), channel_id=1, source_target_pairs={{0,8},{8,16},{16,24},{24,32},{32,40},{40,48},{48,56},{56,64},{64,7... | collective-permute-start | bytes 73736 | tf_op jit(solution)/shard_map/ppermute | solution.py:19
  30.1 97.5 %collective-permute-start.19 = (f32[8,6,128]{2,1,0:T(8,128)S(1)}, f32[8,6,128]{2,1,0:T(8,128)S(1)}, u32[]{:S(2)}, u32[]{:S(2)}) collective-permute-start(f32[8,6,128]{2,1,0:T(8,128)S(1)} %reshape.104), channel_id=1, source_target_pairs={{8,0},{16,8},{24,16},{32,24},{40,32},{48,40},{56,48},{64,56},{72,6... | collective-permute-start | bytes 73736 | tf_op jit(solution)/shard_map/ppermute | solution.py:19
  37.1 61.3 %copy-start.4 = (f32[8,32,128]{2,1,0:T(8,128)}, f32[8,32,128]{2,1,0:T(8,128)S(1)}, u32[]{:S(2)}) copy-start(f32[8,32,128]{2,1,0:T(8,128)S(1)} %get-tuple-element.31) | copy-start | bytes 393220
  37.2 18.1 %collective-permute-start.4 = (f32[8,32,128]{2,1,0:T(8,128)S(1)}, f32[8,32,128]{2,1,0:T(8,128)S(1)}, u32[]{:S(2)}, u32[]{:S(2)}) collective-permute-start(f32[8,32,128]{2,1,0:T(8,128)S(1)} %pad_maximum_fusion.36), channel_id=1, source_target_pairs={{8,0},{16,8},{24,16},{32,24},{40,32},{48,40},{56,48},{64,56},{72,6... | collective-permute-start | bytes 393224 | tf_op jit(solution)/shard_map/ppermute | solution.py:19
  38.5 16.8 %collective-permute-start.5 = (f32[8,32,128]{2,1,0:T(8,128)S(1)}, f32[8,32,128]{2,1,0:T(8,128)S(1)}, u32[]{:S(2)}, u32[]{:S(2)}) collective-permute-start(f32[8,32,128]{2,1,0:T(8,128)S(1)} %pad_maximum_fusion.37), channel_id=1, source_target_pairs={{0,8},{8,16},{16,24},{24,32},{32,40},{40,48},{48,56},{56,64},{64,7... | collective-permute-start | bytes 393224 | tf_op jit(solution)/shard_map/ppermute | solution.py:19
  43.1 5.9 %collective-permute-start.6 = (f32[8,8,128]{2,1,0:T(8,128)S(1)}, f32[8,8,128]{2,1,0:T(8,128)S(1)}, u32[]{:S(2)}, u32[]{:S(2)}) collective-permute-start(f32[8,8,128]{2,1,0:T(8,128)S(1)} %pad_maximum_fusion.44), channel_id=1, source_target_pairs={{1,0},{2,1},{3,2},{4,3},{5,4},{6,5},{7,6},{9,8},{10,9},{11,10},{12... | collective-permute-start | bytes 98312 | tf_op jit(solution)/shard_map/ppermute | solution.py:19
  49.1 6.2 %collective-permute-start.7 = (f32[8,8,128]{2,1,0:T(8,128)S(1)}, f32[8,8,128]{2,1,0:T(8,128)S(1)}, u32[]{:S(2)}, u32[]{:S(2)}) collective-permute-start(f32[8,8,128]{2,1,0:T(8,128)S(1)} %pad_maximum_fusion.45), channel_id=1, source_target_pairs={{0,1},{1,2},{2,3},{3,4},{4,5},{5,6},{6,7},{8,9},{9,10},{10,11},{11... | collective-permute-start | bytes 98312 | tf_op jit(solution)/shard_map/ppermute | solution.py:19
  57.4 18.0 %collective-permute-start.8 = (f32[8,32,128]{2,1,0:T(8,128)S(1)}, f32[8,32,128]{2,1,0:T(8,128)S(1)}, u32[]{:S(2)}, u32[]{:S(2)}) collective-permute-start(f32[8,32,128]{2,1,0:T(8,128)S(1)} %pad_maximum_fusion.38), channel_id=1, source_target_pairs={{8,0},{16,8},{24,16},{32,24},{40,32},{48,40},{56,48},{64,56},{72,6... | collective-permute-start | bytes 393224 | tf_op jit(solution)/shard_map/ppermute | solution.py:19
  58.8 16.7 %collective-permute-start.9 = (f32[8,32,128]{2,1,0:T(8,128)S(1)}, f32[8,32,128]{2,1,0:T(8,128)S(1)}, u32[]{:S(2)}, u32[]{:S(2)}) collective-permute-start(f32[8,32,128]{2,1,0:T(8,128)S(1)} %pad_maximum_fusion.39), channel_id=1, source_target_pairs={{0,8},{8,16},{16,24},{24,32},{32,40},{40,48},{48,56},{56,64},{64,7... | collective-permute-start | bytes 393224 | tf_op jit(solution)/shard_map/ppermute | solution.py:19
  65.2 4.9 %collective-permute-start.10 = (f32[8,8,128]{2,1,0:T(8,128)S(1)}, f32[8,8,128]{2,1,0:T(8,128)S(1)}, u32[]{:S(2)}, u32[]{:S(2)}) collective-permute-start(f32[8,8,128]{2,1,0:T(8,128)S(1)} %pad_maximum_fusion.46), channel_id=1, source_target_pairs={{1,0},{2,1},{3,2},{4,3},{5,4},{6,5},{7,6},{9,8},{10,9},{11,10},{12... | collective-permute-start | bytes 98312 | tf_op jit(solution)/shard_map/ppermute | solution.py:19
  70.1 5.3 %collective-permute-start.11 = (f32[8,8,128]{2,1,0:T(8,128)S(1)}, f32[8,8,128]{2,1,0:T(8,128)S(1)}, u32[]{:S(2)}, u32[]{:S(2)}) collective-permute-start(f32[8,8,128]{2,1,0:T(8,128)S(1)} %pad_maximum_fusion.47), channel_id=1, source_target_pairs={{0,1},{1,2},{2,3},{3,4},{4,5},{5,6},{6,7},{8,9},{9,10},{10,11},{11... | collective-permute-start | bytes 98312 | tf_op jit(solution)/shard_map/ppermute | solution.py:19
  80.0 16.8 %collective-permute-start.12 = (f32[8,32,128]{2,1,0:T(8,128)S(1)}, f32[8,32,128]{2,1,0:T(8,128)S(1)}, u32[]{:S(2)}, u32[]{:S(2)}) collective-permute-start(f32[8,32,128]{2,1,0:T(8,128)S(1)} %pad_maximum_fusion.40), channel_id=1, source_target_pairs={{8,0},{16,8},{24,16},{32,24},{40,32},{48,40},{56,48},{64,56},{72,6... | collective-permute-start | bytes 393224 | tf_op jit(solution)/shard_map/ppermute | solution.py:19
  81.3 16.1 %collective-permute-start.13 = (f32[8,32,128]{2,1,0:T(8,128)S(1)}, f32[8,32,128]{2,1,0:T(8,128)S(1)}, u32[]{:S(2)}, u32[]{:S(2)}) collective-permute-start(f32[8,32,128]{2,1,0:T(8,128)S(1)} %pad_maximum_fusion.41), channel_id=1, source_target_pairs={{0,8},{8,16},{16,24},{24,32},{32,40},{40,48},{48,56},{56,64},{64,7... | collective-permute-start | bytes 393224 | tf_op jit(solution)/shard_map/ppermute | solution.py:19
  85.3 5.2 %collective-permute-start.14 = (f32[8,8,128]{2,1,0:T(8,128)S(1)}, f32[8,8,128]{2,1,0:T(8,128)S(1)}, u32[]{:S(2)}, u32[]{:S(2)}) collective-permute-start(f32[8,8,128]{2,1,0:T(8,128)S(1)} %pad_maximum_fusion.48), channel_id=1, source_target_pairs={{1,0},{2,1},{3,2},{4,3},{5,4},{6,5},{7,6},{9,8},{10,9},{11,10},{12... | collective-permute-start | bytes 98312 | tf_op jit(solution)/shard_map/ppermute | solution.py:19
  90.6 5.6 %collective-permute-start.15 = (f32[8,8,128]{2,1,0:T(8,128)S(1)}, f32[8,8,128]{2,1,0:T(8,128)S(1)}, u32[]{:S(2)}, u32[]{:S(2)}) collective-permute-start(f32[8,8,128]{2,1,0:T(8,128)S(1)} %pad_maximum_fusion.49), channel_id=1, source_target_pairs={{0,1},{1,2},{2,3},{3,4},{4,5},{5,6},{6,7},{8,9},{9,10},{10,11},{11... | collective-permute-start | bytes 98312 | tf_op jit(solution)/shard_map/ppermute | solution.py:19
  100.9 41.1 %all-to-all-start = ((f32[128,1,1280]{2,1,0:T(1,128)}), f32[128,1,1280]{2,1,0:T(1,128)S(1)}, u32[]{:S(2)}, u32[]{:S(2)}) async-start(f32[128,1,1280]{2,1,0:T(1,128)} %broadcast_in_dim.48), calls=%async_computation | async-start | bytes 1310720 | tf_op jit(solution)/shard_map/all_to_all | solution.py:126
  (24 other events, 403.5 us)

commit v2 on v1

v2 whole, which is shorter than its diff:
```python
import functools

import jax
import jax.numpy as jnp
from jax import lax
from jax.experimental import pallas as pl
from jax.experimental.pallas import tpu as pltpu
from jax.sharding import PartitionSpec as P

STEPS = 4
SRC_DEPTH = 6
REC_DEPTH = 3
NX, NY, NZ = 8, 32, 128
W = 4
SLAB = 16

C0, C1, C2, C3, C4 = (-205.0 / 72.0, 8.0 / 5.0, -1.0 / 5.0, 8.0 / 315.0, -1.0 / 560.0)
CK = (C0, C1, C2, C3, C4)
courant_sq = 0.0625
prior_var = 0.01

f32 = jnp.float32
VM = pl.BlockSpec(memory_space=pltpu.VMEM)
SM = pl.BlockSpec(memory_space=pltpu.SMEM)


def sds(*shape):
    return jax.ShapeDtypeStruct(shape, f32)


def lanes(rows=1):
    return lax.broadcasted_iota(jnp.int32, (rows, 128), 1)


def roll(x, k):
    k = k % 128
    return x if k == 0 else pltpu.roll(x, k, 1)


def pack(rows):
    part = lanes() // SLAB
    out = jnp.where(part == 0, rows[0], 0.0)
    for x in range(1, NX):
        out = jnp.where(part == x, roll(rows[x], SLAB * x), out)
    return out


def put_strips(i, p, s, xlo, xhi, ylo, yhi):
    out, j = (xlo, i) if i < W else (xhi, i - W)
    out[NY * j : NY * (j + 1)] = p
    out[NY * (W + j) : NY * (W + j + 1)] = s
    ylo[8 * i : 8 * i + 4] = p[:W]
    ylo[8 * i + 4 : 8 * i + 8] = s[:W]
    yhi[8 * i : 8 * i + 4] = p[NY - W :]
    yhi[8 * i + 4 : 8 * i + 8] = s[NY - W :]


def first_kernel(mean, logs, noise, p, q, obs, c_out, xlo, xhi, ylo, yhi, cpk):
    rows = []
    for i in range(NX):
        vel = mean[i] + jnp.exp(logs[i]) * noise[i]
        c = courant_sq * vel * vel
        c_out[i] = c
        put_strips(i, p[i], c * q[i], xlo, xhi, ylo, yhi)
        rows.append(c)
    slab = pack(rows)
    cpk[...] = slab
    ylo[64:80] = slab[:16]
    yhi[64:80] = slab[16:]
    ylo[80:88] = obs[...]
    yhi[80:88] = obs[...]


def fill(buf, field, rows_l, rows_r, md, mu, at, keep_d, keep_u):
    for i in range(NX):
        buf[W + i, 8:40] = field[i]
        buf[W + i, 4:8] = jnp.where(keep_d, md[8 * i + at : 8 * i + at + 4], 0.0)
        buf[W + i, 40:44] = jnp.where(keep_u, mu[8 * i + at : 8 * i + at + 4], 0.0)
    for j in range(W):
        buf[j, 8:40] = rows_l[j]
        buf[W + NX + j, 8:40] = rows_r[j]


def laplace(buf, i, wz):
    here = buf[W + i, 8:40]
    out = (3.0 * C0) * here
    for k in range(1, W + 1):
        beside = buf[W + i + k, 8:40] + buf[W + i - k, 8:40]
        beside = beside + buf[W + i, 8 + k : 40 + k] + buf[W + i, 8 - k : 40 - k]
        out = out + CK[k] * beside
        out = out + wz[k][0] * roll(here, -k) + wz[k][1] * roll(here, k)
    return out


def step_kernel(n, meta, samples, c, p, pp, q, ql, ml, mr, md, mu, oc, *rest):
    rest = list(rest)
    bufp, bufs = rest[-2:]
    rest = rest[:-2]
    take = lambda: rest.pop(0)
    cpk = cl = cr = lap_other = q3 = img = None
    if n == 1:
        cext = take()
    if n == 2:
        lap_other = take()
    if n == 3:
        lap_other, q3, img = take(), take(), take()
    lpk, oc_out, qn = take(), take(), take()
    if n < 3:
        pn, xlo, xhi, ylo, yhi = take(), take(), take(), take(), take()
    else:
        pn = take()
    if n == 0:
        lap_out, cext = take(), take()
    if n == 1:
        lap_out = take()
    if n == 2:
        img_out = take()
    if n == 3:
        img_out, mat = take(), take()

    keep_d, keep_u = meta[3] > 0, meta[4] > 0
    lane = lanes()
    wz = [None] + [
        (jnp.where(lane < NZ - k, CK[k], 0.0), jnp.where(lane >= k, CK[k], 0.0))
        for k in range(1, W + 1)
    ]

    def strip(m, at):
        return [m[at + NY * j : at + NY * (j + 1)] for j in range(W)]

    fill(bufp, p, strip(ml, 0), strip(mr, 0), md, mu, 0, keep_d, keep_u)
    s = [c[i] * q[i] for i in range(NX)]
    fill(bufs, s, strip(ml, 128), strip(mr, 128), md, mu, 4, keep_d, keep_u)
    slab = jnp.zeros((NY, NZ), f32)
    for i in range(NX):
        lap = laplace(bufp, i, wz)
        slab = jnp.where(lane // SLAB == i, roll(lap, SLAB * i), slab)
        pn[i] = 2.0 * p[i] - pp[i] + c[i] * lap
        q_new = 2.0 * q[i] - ql[i] + laplace(bufs, i, wz)
        qn[i] = q_new
        if n < 2:
            lap_out[i] = lap
        if n == 2:
            img_out[i] = lap * q[i] + q_new * lap_other[i]
        if n == 3:
            img_out[i] = img[i] + lap * q3[i] + q_new * lap_other[i]
    lpk[...] = slab

    sx, sy = meta[0], meta[1]

    @pl.when((sx >= 0) & (sx < NX) & (sy >= 0) & (sy < NY))
    def _():
        row = pn[sx, pl.ds(sy, 1), :]
        pn[sx, pl.ds(sy, 1), :] = row + jnp.where(lane == SRC_DEPTH, samples[n], 0.0)

    at = 80 if n == 0 else 64
    got_d, got_u = md[at : at + 8], mu[at : at + 8]
    oc_out[...] = oc[...]
    up, turn_u, down, turn_d = ((0, 64, 12, 64), (4, 0, 12, 0), (4, 64, 8, 64), (8, 0, None, 0))[n]
    oc_out[up : up + 4] = oc_out[up : up + 4] + roll(got_u, turn_u)[:4]
    if down is not None:
        oc_out[down : down + 4] = oc_out[down : down + 4] + roll(got_d, turn_d)[:4]

    if n < 3:
        for i in range(NX):
            put_strips(i, pn[i], c[i] * qn[i], xlo, xhi, ylo, yhi)
        ylo[64:72] = got_u
        yhi[64:72] = got_d
    if n == 0:
        cext[0:16] = jnp.where(keep_d, md[64:80], 0.0)
        cext[16:48] = pack([c[i] for i in range(NX)])
        cext[48:64] = jnp.where(keep_u, mu[64:80], 0.0)
        xlo[256:320] = cext[...]
        xhi[256:320] = cext[...]
    if n == 1:
        xlo[256:288] = mr[272:304]
        xhi[256:288] = ml[272:304]
    if n == 3:
        out = jnp.zeros((NY, NZ), f32)
        for i in range(NX):
            for t, row in ((1, None), (2, pp[i]), (3, p[i]), (4, pn[i])):
                if row is not None:
                    to = 4 * i + t - 1
                    out = jnp.where(lane == to, roll(row, to - REC_DEPTH), out)
        mat[...] = out


def chunk_kernel(mat, got_d, got_u, p1, oc, out):
    m = mat[...]
    lane = lanes()
    for i in range(NX):
        m = jnp.where(lane == 4 * i, roll(p1[i], 4 * i - REC_DEPTH), m)
    packed = got_d[...] + roll(m[:16], 32) + roll(m[16:], 64) + roll(got_u[...], 96)
    for g in range(out.shape[0]):
        out[g, 0:16] = oc[...]
        out[g, 16:32] = packed


def lap_packed(buf, g, lo, hi, wz):
    lane = lanes()
    here = buf[g, lo:hi]
    before, after = buf[g - 1, lo:hi], buf[g + 1, lo:hi]
    out = (3.0 * C0) * here
    for k in range(1, W + 1):
        t = SLAB * k
        beside = jnp.where(lane < 128 - t, roll(here, -t), roll(after, -t))
        beside = beside + jnp.where(lane >= t, roll(here, t), roll(before, t))
        beside = beside + buf[g, lo + k : hi + k] + buf[g, lo - k : hi - k]
        out = out + CK[k] * beside
        out = out + wz[k][0] * roll(here, -k) + wz[k][1] * roll(here, k)
    return out


def last_kernel(
    meta, got, keyx, keyy, cext, c1l, c1r, c2l, c2r, lp0, lp1, lp2, lp3, img, mean, logs, noise,
    out, table, hoty, x, r3, r2, r1, inj,
):
    ngx = got.shape[0]
    lane = lanes()
    ix = meta[2]
    bf = jnp.bfloat16

    row4 = lax.broadcasted_iota(jnp.int32, (160, 128), 0) // 4
    coly = lax.broadcasted_iota(jnp.int32, (64, 128), 0)

    def build(g, carry):
        for rp in range(4):
            kx = keyx[pl.ds(4 * g + rp, 1), :]
            ky = keyy[pl.ds(4 * g + rp, 1), :]
            at = pl.ds(pl.multiple_of((4 * g + rp) * 128, 128), 128)
            val = got[g, 4 * rp : 4 * rp + 4, :]
            hi = val.astype(bf).astype(f32)
            mid = (val - hi).astype(bf).astype(f32)
            low = val - hi - mid
            hot = row4 == kx
            for part, v in enumerate((hi, mid, low)):
                v8 = jnp.concatenate([v, v], 0)
                v160 = jnp.concatenate([v8] * 20, 0)
                table[160 * part : 160 * (part + 1), at] = jnp.where(hot, v160, 0.0).astype(bf)
            table[480:640, at] = jnp.where(hot, 1.0, 0.0).astype(bf)
            hoty[:, at] = jnp.where(coly == ky, 1.0, 0.0).astype(bf)
        return carry

    lax.fori_loop(0, ngx, build, 0)
    sums = lax.dot_general(
        table[...], hoty[...], (((1,), (1,)), ((), ())), preferred_element_type=f32
    )
    seen = sums[0:160] + sums[160:320] + sums[320:480]
    count = sums[480:640]
    zero = jnp.zeros((96, 64), f32)
    seen = jnp.concatenate([seen, zero], 0)
    count = jnp.concatenate([count, zero], 0)
    both = jnp.concatenate([seen, count], 1)
    tr = [both[:128].T, both[128:].T]

    k_in = lax.broadcasted_iota(jnp.int32, (128, 512), 0)
    k_out = lax.broadcasted_iota(jnp.int32, (128, 512), 1)
    spread_to = jnp.where(
        (k_in < 32) & (k_out == (k_in % 4) * 128 + (k_in // 4) * SLAB + REC_DEPTH), 1.0, 0.0
    )
    dense = []
    for g in range(5):
        src = ix + (g - 2)
        ok = (src >= 0) & (src < ngx)
        blk = got[jnp.clip(src, 0, ngx - 1), 16:32, :]
        m = jnp.concatenate([roll(blk, -32 * t) for t in range(4)], 0)
        m = jnp.where(ok, m, 0.0)
        t = tr[g // 4]
        s_g = roll(t[:64], -32 * (g % 4))
        n_g = roll(t[64:], -32 * (g % 4))
        dense.append(n_g * m - s_g)
    inj[...] = jnp.dot(
        jnp.concatenate(dense, 0), spread_to,
        precision=lax.Precision.HIGHEST, preferred_element_type=f32,
    )

    def j(n, g, lo, hi):
        return inj[64 * g + lo : 64 * g + hi, 128 * n : 128 * (n + 1)]

    d = lane % SLAB
    wz = [None] + [
        (jnp.where(d < SLAB - k, CK[k], 0.0), jnp.where(d >= k, CK[k], 0.0))
        for k in range(1, W + 1)
    ]
    coef = {1: c1l, 2: cext, 3: c1r}
    pad = jnp.zeros((16, 128), f32)
    for g in range(5):
        r3[g] = j(3, g, 0, 64)
        if g in coef:
            x[g] = coef[g][...] * r3[g]
    for g, far in ((0, c2l), (4, c2r)):
        x[g, 0:16] = pad
        x[g, 16:48] = far[...] * r3[g, 16:48]
        x[g, 48:64] = pad
    for g in (1, 2, 3):
        r2[g] = 2.0 * r3[g, 8:56] + lap_packed(x, g, 8, 56, wz) + j(2, g, 8, 56)
    x[0] = jnp.zeros((64, 128), f32)
    x[4] = jnp.zeros((64, 128), f32)
    for g in (1, 2, 3):
        x[g, 0:8] = pad[:8]
        x[g, 8:56] = coef[g][8:56] * r2[g]
        x[g, 56:64] = pad[:8]
    for g in (1, 2, 3):
        r1[g] = 2.0 * r2[g] - r3[g, 8:56] + lap_packed(x, g, 8, 56, wz) + j(1, g, 8, 56)
    for g in (1, 2, 3):
        x[g, 8:56] = coef[g][8:56] * r1[g]
    r0 = 2.0 * r1[2, 8:40] - r2[2, 8:40] + lap_packed(x, 2, 16, 48, wz) + j(0, 2, 16, 48)
    corr = r0 * lp0[...] + r1[2, 8:40] * lp1[...] + r2[2, 8:40] * lp2[...]
    corr = corr + r3[2, 16:48] * lp3[...]

    per = NX // out.shape[0]
    for i in range(NX):
        image = img[i] + jnp.where(lane < SLAB, roll(corr, -SLAB * i), 0.0)
        z = noise[i]
        vel = mean[i] + jnp.exp(logs[i]) * z
        grad = (2.0 * courant_sq) * vel * image
        out[i // per, 0, i % per] = grad
        out[i // per, 1, i % per] = grad * z


def call(kernel, outs, scratch=(), smem=0):
    def go(*args):
        return pl.pallas_call(
            kernel,
            out_shape=outs,
            in_specs=[SM] * smem + [VM] * (len(args) - smem),
            out_specs=jax.tree.map(lambda _: VM, outs),
            scratch_shapes=list(scratch),
            compiler_params=pltpu.CompilerParams(vmem_limit_bytes=48 * 2**20),
        )(*args)

    return go


def shift(x, axis, k, wrap=False):
    n = lax.axis_size(axis)
    return lax.ppermute(x, axis, [(i, (i + k) % n) for i in range(n) if wrap or 0 <= i + k < n])


def local(
    mean_velocity,
    log_scale,
    shot_noise,
    checkpoint_prev,
    checkpoint_now,
    adjoint_next,
    adjoint_now,
    wavelet,
    source_column,
    receiver_column,
    observed,
    start_step,
):
    ngx, ngy, nshot = lax.axis_size("gx"), lax.axis_size("gy"), lax.axis_size("shot")
    width_y = NY * ngy
    ix, iy = lax.axis_index("gx"), lax.axis_index("gy")
    noise = shot_noise[0]
    src = source_column[0]
    meta = jnp.stack(
        [
            src // width_y - ix * NX,
            src % width_y - iy * NY,
            ix,
            (iy > 0).astype(jnp.int32),
            (iy < ngy - 1).astype(jnp.int32),
        ]
    ).astype(jnp.int32)
    samples = lax.dynamic_slice_in_dim(wavelet[0], start_step[0], STEPS)
    obs = jnp.pad(observed[0], ((0, 4), (0, 64)))
    rec = receiver_column[0].reshape(ngx, ngy, -1)
    rec = lax.dynamic_slice_in_dim(jnp.concatenate([rec, rec], 1), iy, ngy, 1).reshape(-1, 128)
    keyx = rec // width_y - ix * NX + 16
    keyy = rec % width_y - iy * NY + 16

    p_prev, p = checkpoint_prev[0], checkpoint_now[0]
    q_later, q = adjoint_next[0], adjoint_now[0]
    F = sds(NX, NY, NZ)
    coef, xlo, xhi, ylo, yhi, cpk = call(
        first_kernel, (F, sds(256, 128), sds(256, 128), sds(88, 128), sds(88, 128), sds(NY, NZ))
    )(mean_velocity, log_scale, noise, p, q, obs)
    oc = jnp.pad(observed[0], ((0, 12), (0, 64)))
    buf = pltpu.VMEM((NX + 2 * W, 48, NZ), f32)
    slabs, keep = [], {}
    for n in range(STEPS):
        ml, mr = shift(xhi, "gx", 1), shift(xlo, "gx", -1)
        md, mu = shift(yhi, "gy", 1, True), shift(ylo, "gy", -1, True)
        extra = ()
        if n == 1:
            extra = (keep["cext"],)
        if n == 2:
            extra = (keep["lap1"],)
        if n == 3:
            extra = (keep["lap0"], keep["q3"], keep["img"])
        outs = [sds(NY, NZ), sds(16, 128), F, F]
        if n < 3:
            rows = (320, 288, 256)[n]
            outs += [sds(rows, 128), sds(rows, 128), sds(72, 128), sds(72, 128)]
        outs += {0: [F, sds(64, 128)], 1: [F], 2: [F], 3: [F, sds(NY, NZ)]}[n]
        res = call(functools.partial(step_kernel, n), tuple(outs), (buf, buf), smem=2)(
            meta, samples, coef, p, p_prev, q, q_later, ml, mr, md, mu, oc, *extra
        )
        lpk, oc, q_next, p_next = res[:4]
        slabs.append(lpk)
        if n < 3:
            xlo, xhi, ylo, yhi = res[4:8]
        if n == 0:
            keep["lap0"], keep["cext"], keep["q3"], keep["p1"] = res[8], res[9], q_next, p_next
        if n == 1:
            keep["lap1"] = res[8]
            c1l, c1r = ml[256:320], mr[256:320]
        if n == 2:
            keep["img"] = res[8]
            c2l, c2r = ml[256:288], mr[256:288]
        if n == 3:
            img, mat = res[4], res[5]
        p_prev, p = p, p_next
        q_later, q = q, q_next

    mat_d, mat_u = shift(mat[16:], "gy", 1), shift(mat[:16], "gy", -1)
    chunk = call(chunk_kernel, sds(ngx, 32, 128))(mat, mat_d, mat_u, keep["p1"], oc)
    got = lax.all_to_all(chunk, "gx", 0, 0)
    nrec = receiver_column.shape[1]
    g5 = pltpu.VMEM((5, 64, 128), f32)
    g48 = pltpu.VMEM((5, 48, 128), f32)
    parts = call(
        last_kernel,
        sds(nshot, 2, NX // nshot, NY, NZ),
        (
            pltpu.VMEM((640, nrec), jnp.bfloat16),
            pltpu.VMEM((64, nrec), jnp.bfloat16),
            g5,
            g5,
            g48,
            g48,
            pltpu.VMEM((320, 512), f32),
        ),
        smem=1,
    )(
        meta, got, keyx, keyy, keep["cext"], c1l, c1r, c2l, c2r, *slabs, img,
        mean_velocity, log_scale, noise,
    )
    quarter = lax.all_to_all(parts, "shot", 0, 0).sum(0)
    total = lax.all_gather(quarter, "shot", axis=0)
    total_grad = total[:, 0].reshape(NX, NY, NZ)
    total_weighted = total[:, 1].reshape(NX, NY, NZ)
    spread = jnp.exp(log_scale)
    grad_log_scale = spread * total_weighted + jnp.exp(2.0 * log_scale) / prior_var - 1.0
    return (total_grad, grad_log_scale)


def solution(mesh):
    return jax.shard_map(
        local,
        mesh=mesh,
        in_specs=(
            P("gx", "gy", None),
            P("gx", "gy", None),
            P("shot", "gx", "gy", None),
            P("shot", "gx", "gy", None),
            P("shot", "gx", "gy", None),
            P("shot", "gx", "gy", None),
            P("shot", "gx", "gy", None),
            P("shot", None),
            P("shot"),
            P("shot", None),
            P("shot", None, ("gx", "gy")),
            P(),
        ),
        out_specs=(P("gx", "gy", None), P("gx", "gy", None)),
        check_vma=False,
    )
```

time: 210 us -> 156 us (0.74)
  other arithmetic: 34 us -> 1.51 us
  Pallas kernels: 0 us -> 19.5 us
  waiting for transfers between devices: 27.4 us -> 10.3 us
  local copies, waits for them, and re-layouts: 19.3 us -> 7.44 us
  starting transfers between devices: 84.3 us -> 74.9 us
  matrix products: 3.09 us -> 0 us
    mul x9 -> x0, other arithmetic: 19.8 us -> none  [the longest x1 10.5 us: local(): cext * r2]
    pallas_call x0 -> x7, Pallas kernels: none -> 19.5 us  [go(): pl.pallas_call(kernel, out_shape=outs, in_specs=[SM] * smem + [VM] * (len...]
    add x7 -> x1, other arithmetic: 11.8 us -> 0.04 us  [local(): keyy = rec % width_y - iy * NY + 16]
    ppermute x20 -> x18, waiting for transfers between devices: 14.6 us -> 3.89 us  [shift(): lax.ppermute(x, axis, [(i, (i + k) % n) for i in range(n) if wrap or 0 <=...]
    all_to_all x1, starting transfers between devices: 25.7 us -> 15.8 us  [local(): got = lax.all_to_all(chunk, 'gx', 0, 0)]
    slice x43 -> x6, local copies, waits for them, and re-layouts: 7.76 us -> 0.69 us  [the longest x1 0.67 us: local(): total_weighted = total[:, 1].reshape(NX, NY, NZ)]
    all_to_all x1, waiting for transfers between devices: 12.8 us -> 6.46 us  [local(): got = lax.all_to_all(chunk, 'gx', 0, 0)]
    unnamed x61 -> x31, local copies, waits for them, and re-layouts: 0.97 us -> 5.74 us
  transfers between devices with their start and end apart: 21 -> 19, of which waited for: 7 -> 5; matrix products, arithmetic and copies ran while one was open for 12% -> 1% of each run, Pallas kernels for 0% -> 0%
where the time goes in v2:
time: 156 us; the launch traced here: 153 us
  starting transfers between devices  74.9 us (48%)
  blocking collectives  37.1 us (24%)
  Pallas kernels  19.5 us (12%)
  waiting for transfers between devices  10.3 us (7%)
  local copies, waits for them, and re-layouts  7.44 us (5%)
  between operations  2.31 us (1%)
    ppermute x18, starting transfers between devices, shift(): lax.ppermute(x, axis, [(i, (i + k) % n) for i in range(n) if wrap or 0 <=...  59.1 us
    all_to_all x1, blocking collectives, local(): quarter = lax.all_to_all(parts, 'shot', 0, 0).sum(0)  26.4 us
    pallas_call x7, Pallas kernels, go(): pl.pallas_call(kernel, out_shape=outs, in_specs=[SM] * smem + [VM] * (len...  19.5 us
    all_to_all x1, starting transfers between devices, local(): got = lax.all_to_all(chunk, 'gx', 0, 0)  15.8 us
    all_gather x1, blocking collectives, local(): total = lax.all_gather(quarter, 'shot', axis=0)  10.7 us
    all_to_all x1, waiting for transfers between devices, local(): got = lax.all_to_all(chunk, 'gx', 0, 0)  6.46 us
    unnamed x31, local copies, waits for them, and re-layouts  5.74 us
    ppermute x18, waiting for transfers between devices, shift(): lax.ppermute(x, axis, [(i, (i + k) % n) for i in range(n) if wrap or 0 <=...  3.89 us
  transfers between devices with their start and end apart: 19, of which 5 were waited for; matrix products, arithmetic and copies ran while one was open for 1% of the time, Pallas kernels for 0%

profile of v2, /device:TPU:1, one launch (start us, length us, event | category | flops | bytes accessed | tf_op | source)
XLA Modules:
  0.0 153.1 jit_solution(3909163620716595286)
XLA Ops:
  6.6 4.0 %collective-permute-start = (f32[256,128]{1,0:T(8,128)S(1)}, f32[256,128]{1,0:T(8,128)S(1)}, u32[]{:S(2)}, u32[]{:S(2)}) collective-permute-start(f32[256,128]{1,0:T(8,128)S(1)} %get-tuple-element.40), channel_id=1, source_target_pairs={{0,8},{8,16},{16,24},{24,32},{32,40},{40,48},{48,56},{56,64},{64,7... | collective-permute-start | bytes 393224 | tf_op jit(solution)/shard_map/ppermute | solution.py:337
  10.6 1.3 collective-permute-start.1
  11.9 4.0 %collective-permute-start.2 = (f32[88,128]{1,0:T(8,128)S(1)}, f32[88,128]{1,0:T(8,128)S(1)}, u32[]{:S(2)}, u32[]{:S(2)}) collective-permute-start(f32[88,128]{1,0:T(8,128)S(1)} %get-tuple-element.42), channel_id=1, source_target_pairs={{0,1},{1,2},{2,3},{3,4},{4,5},{5,6},{6,7},{7,0},{8,9},{9,10},{10,1... | collective-permute-start | bytes 135176 | tf_op jit(solution)/shard_map/ppermute | solution.py:337
  15.9 8.6 %collective-permute-start.3 = (f32[88,128]{1,0:T(8,128)S(1)}, f32[88,128]{1,0:T(8,128)S(1)}, u32[]{:S(2)}, u32[]{:S(2)}) collective-permute-start(f32[88,128]{1,0:T(8,128)S(1)} %get-tuple-element.43), channel_id=1, source_target_pairs={{0,7},{1,0},{2,1},{3,2},{4,3},{5,4},{6,5},{7,6},{8,15},{9,8},{10,9... | collective-permute-start | bytes 135176 | tf_op jit(solution)/shard_map/ppermute | solution.py:337
  26.8 1.7 %shard_map.132 = (f32[32,128]{1,0:T(8,128)S(1)}, f32[16,128]{1,0:T(8,128)S(1)}, f32[8,32,128]{2,1,0:T(8,128)S(1)}, f32[8,32,128]{2,1,0:T(8,128)S(1)}, f32[320,12...) custom-call(s32[5]{0:T(128)S(1)} %stack.31.meta, ...), custom_call_target="tpu_custom_call" | custom-call | tf_op jit(solution)/shard_map/pallas_call | solution.py:323
  28.5 4.0 %collective-permute-start.4 = (f32[320,128]{1,0:T(8,128)S(1)}, f32[320,128]{1,0:T(8,128)S(1)}, u32[]{:S(2)}, u32[]{:S(2)}) collective-permute-start(f32[320,128]{1,0:T(8,128)S(1)} %get-tuple-element.46), channel_id=1, source_target_pairs={{0,8},{8,16},{16,24},{24,32},{32,40},{40,48},{48,56},{56,64},{64,7... | collective-permute-start | bytes 491528 | tf_op jit(solution)/shard_map/ppermute | solution.py:337
  33.8 1.9 %collective-permute-start.6 = (f32[72,128]{1,0:T(8,128)S(1)}, f32[72,128]{1,0:T(8,128)S(1)}, u32[]{:S(2)}, u32[]{:S(2)}) collective-permute-start(f32[72,128]{1,0:T(8,128)S(1)} %get-tuple-element.48), channel_id=1, source_target_pairs={{0,1},{1,2},{2,3},{3,4},{4,5},{5,6},{6,7},{7,0},{8,9},{9,10},{10,1... | collective-permute-start | bytes 110600 | tf_op jit(solution)/shard_map/ppermute | solution.py:337
  35.7 4.6 %collective-permute-start.7 = (f32[72,128]{1,0:T(8,128)S(1)}, f32[72,128]{1,0:T(8,128)S(1)}, u32[]{:S(2)}, u32[]{:S(2)}) collective-permute-start(f32[72,128]{1,0:T(8,128)S(1)} %get-tuple-element.49), channel_id=1, source_target_pairs={{0,7},{1,0},{2,1},{3,2},{4,3},{5,4},{6,5},{7,6},{8,15},{9,8},{10,9... | collective-permute-start | bytes 110600 | tf_op jit(solution)/shard_map/ppermute | solution.py:337
  41.4 1.6 %shard_map.133 = (f32[32,128]{1,0:T(8,128)S(1)}, f32[16,128]{1,0:T(8,128)S(1)}, f32[8,32,128]{2,1,0:T(8,128)S(1)}, f32[8,32,128]{2,1,0:T(8,128)S(1)}, f32[288,12...) custom-call(s32[5]{0:T(128)S(1)} %stack.31.meta, ...), custom_call_target="tpu_custom_call" | custom-call | tf_op jit(solution)/shard_map/pallas_call | solution.py:323
  43.0 4.0 %collective-permute-start.8 = (f32[288,128]{1,0:T(8,128)S(1)}, f32[288,128]{1,0:T(8,128)S(1)}, u32[]{:S(2)}, u32[]{:S(2)}) collective-permute-start(f32[288,128]{1,0:T(8,128)S(1)} %get-tuple-element.54), channel_id=1, source_target_pairs={{0,8},{8,16},{16,24},{24,32},{32,40},{40,48},{48,56},{56,64},{64,7... | collective-permute-start | bytes 442376 | tf_op jit(solution)/shard_map/ppermute | solution.py:337
  48.3 2.2 %collective-permute-start.10 = (f32[72,128]{1,0:T(8,128)S(1)}, f32[72,128]{1,0:T(8,128)S(1)}, u32[]{:S(2)}, u32[]{:S(2)}) collective-permute-start(f32[72,128]{1,0:T(8,128)S(1)} %get-tuple-element.56), channel_id=1, source_target_pairs={{0,1},{1,2},{2,3},{3,4},{4,5},{5,6},{6,7},{7,0},{8,9},{9,10},{10,1... | collective-permute-start | bytes 110600 | tf_op jit(solution)/shard_map/ppermute | solution.py:337
  50.5 4.6 %collective-permute-start.11 = (f32[72,128]{1,0:T(8,128)S(1)}, f32[72,128]{1,0:T(8,128)S(1)}, u32[]{:S(2)}, u32[]{:S(2)}) collective-permute-start(f32[72,128]{1,0:T(8,128)S(1)} %get-tuple-element.57), channel_id=1, source_target_pairs={{0,7},{1,0},{2,1},{3,2},{4,3},{5,4},{6,5},{7,6},{8,15},{9,8},{10,9... | collective-permute-start | bytes 110600 | tf_op jit(solution)/shard_map/ppermute | solution.py:337
  56.2 1.7 %shard_map.134 = (f32[32,128]{1,0:T(8,128)S(1)}, f32[16,128]{1,0:T(8,128)S(1)}, f32[8,32,128]{2,1,0:T(8,128)S(1)}, f32[8,32,128]{2,1,0:T(8,128)S(1)}, f32[256,12...) custom-call(s32[5]{0:T(128)S(1)} %stack.31.meta, ...), custom_call_target="tpu_custom_call" | custom-call | tf_op jit(solution)/shard_map/pallas_call | solution.py:323
  57.9 4.0 %collective-permute-start.12 = (f32[256,128]{1,0:T(8,128)S(1)}, f32[256,128]{1,0:T(8,128)S(1)}, u32[]{:S(2)}, u32[]{:S(2)}) collective-permute-start(f32[256,128]{1,0:T(8,128)S(1)} %get-tuple-element.62), channel_id=1, source_target_pairs={{0,8},{8,16},{16,24},{24,32},{32,40},{40,48},{48,56},{56,64},{64,7... | collective-permute-start | bytes 393224 | tf_op jit(solution)/shard_map/ppermute | solution.py:337
  61.8 1.3 collective-permute-start.13
  63.1 3.0 %collective-permute-start.14 = (f32[72,128]{1,0:T(8,128)S(1)}, f32[72,128]{1,0:T(8,128)S(1)}, u32[]{:S(2)}, u32[]{:S(2)}) collective-permute-start(f32[72,128]{1,0:T(8,128)S(1)} %get-tuple-element.64), channel_id=1, source_target_pairs={{0,1},{1,2},{2,3},{3,4},{4,5},{5,6},{6,7},{7,0},{8,9},{9,10},{10,1... | collective-permute-start | bytes 110600 | tf_op jit(solution)/shard_map/ppermute | solution.py:337
  66.1 3.8 %collective-permute-start.15 = (f32[72,128]{1,0:T(8,128)S(1)}, f32[72,128]{1,0:T(8,128)S(1)}, u32[]{:S(2)}, u32[]{:S(2)}) collective-permute-start(f32[72,128]{1,0:T(8,128)S(1)} %get-tuple-element.65), channel_id=1, source_target_pairs={{0,7},{1,0},{2,1},{3,2},{4,3},{5,4},{6,5},{7,6},{8,15},{9,8},{10,9... | collective-permute-start | bytes 110600 | tf_op jit(solution)/shard_map/ppermute | solution.py:337
  71.0 2.4 %shard_map.135 = (f32[32,128]{1,0:T(8,128)S(1)}, f32[16,128]{1,0:T(8,128)S(1)}, f32[8,32,128]{2,1,0:T(8,128)}, f32[8,32,128]{2,1,0:T(8,128)}, f32[8,32,128]{2,1,0:T(8,128)S(1)}, /*index=5*/f32[32,128]{1,0:T(8,128)S(1)}) custom-call(s32[5]{0:T(128)S(1)} %stack.31.meta, f32[4]{0:T(128)S(1)} %fusion.9.samples, f32[8,32,128]{2,1,0:T(8,128)S(1)} %get-tuple-element.39.c, ...), custom_call_target="tpu_custom_call" | custom-call | tf_op jit(solution)/shard_map/pallas_call | solution.py:323
  74.7 4.0 %collective-permute-start.16 = (f32[16,128]{1,0:T(8,128)S(1)}, f32[16,128]{1,0:T(8,128)S(1)}, u32[]{:S(2)}, u32[]{:S(2)}) collective-permute-start(f32[16,128]{1,0:T(8,128)S(1)} %get-tuple-element.81), channel_id=1, source_target_pairs={{0,1},{1,2},{2,3},{3,4},{4,5},{5,6},{6,7},{8,9},{9,10},{10,11},{11... | collective-permute-start | bytes 24584 | tf_op jit(solution)/shard_map/ppermute | solution.py:337
  80.3 15.8 %all-to-all-start = ((f32[16,32,128]{2,1,0:T(8,128)}), f32[16,32,128]{2,1,0:T(8,128)S(1)}, u32[]{:S(2)}, u32[]{:S(2)}) async-start(f32[16,32,128]{2,1,0:T(8,128)} %shard_map.136), calls=%async_computation | async-start | bytes 524288 | tf_op jit(solution)/shard_map/all_to_all | solution.py:421
  97.7 6.5 %all-to-all-done.got = f32[16,32,128]{2,1,0:T(8,128)S(1)} async-done(((f32[16,32,128]{2,1,0:T(8,128)}), f32[16,32,128]{2,1,0:T(8,128)S(1)}, u32[]{:S(2)}, u32[]{:S(2)}) %all-to-all-start) | async-done | bytes 262176 | tf_op jit(solution)/shard_map/all_to_all | solution.py:421
  104.2 10.5 %shard_map.137 = f32[4,2,2,32,128]{4,3,2,1,0:T(8,128)S(1)} custom-call(s32[5]{0:T(128)S(1)} %stack.31.meta, f32[16,32,128]{2,1,0:T(8,128)S(1)} %all-to-all-done.got, s32[64,128]{1,0:T(8,128)S(1)} %get-tuple-element.79.keyx, s32[64,128]{1,0:T(8,128)S(1)} %get-tuple-element.78.keyy, f32[64,128]{1,0:T(8,128)S(1)} %get-tuple-element.51.rest_0_.cext, ...), custom_call_target="tpu_custom_call" | custom-call | tf_op jit(solution)/shard_map/pallas_call | solution.py:323
  114.6 26.4 %all_to_all.10 = f32[4,2,2,32,128]{4,3,2,1,0:T(8,128)S(1)} all-to-all(f32[4,2,2,32,128]{4,3,2,1,0:T(8,128)S(1)} %shard_map.137), channel_id=1, replica_groups=mesh['shot'=4,'gx'=16,'gy'=8] {'shot'}, dimensions={0} | all-to-all | bytes 524288 | tf_op jit(solution)/shard_map/all_to_all | solution.py:442
  141.1 10.7 %all-gather = f32[8,2,32,128]{3,2,1,0:T(8,128)S(1)} all-gather(f32[2,2,32,128]{3,2,1,0:T(8,128)S(1)} %reduce_sum.9), channel_id=2, replica_groups=mesh['shot'=4,'gx'=16,'gy'=8] {'shot'}, dimensions={0}, use_global_device_ids=true | all-gather | bytes 327680 | tf_op jit(solution)/shard_map/all_gather | solution.py:443
  (71 shorter events, 18.3 us)
Async XLA Ops:
  0.6 24.6 %copy-start = (f32[1,64]{1,0:T(1,128)S(1)}, f32[1,64]{1,0:T(1,128)}, u32[]{:S(2)}) copy-start(f32[1,64]{1,0:T(1,128)} %param.19) | copy-start | bytes 772
  5.9 20.9 %copy-start.2 = (f32[1,8,32,128]{3,2,1,0:T(8,128)S(1)}, f32[1,8,32,128]{3,2,1,0:T(8,128)}, u32[]{:S(2)}) copy-start(f32[1,8,32,128]{3,2,1,0:T(8,128)} %param.16) | copy-start | bytes 393220
  5.9 20.9 %copy-start.4 = (f32[1,8,32,128]{3,2,1,0:T(8,128)S(1)}, f32[1,8,32,128]{3,2,1,0:T(8,128)}, u32[]{:S(2)}) copy-start(f32[1,8,32,128]{3,2,1,0:T(8,128)} %param.18) | copy-start | bytes 393220
  5.9 20.9 %copy-start.11 = (f32[1,8,32,128]{3,2,1,0:T(8,128)S(1)}, f32[1,8,32,128]{3,2,1,0:T(8,128)}, u32[]{:S(2)}) copy-start(f32[1,8,32,128]{3,2,1,0:T(8,128)} %param.15) | copy-start | bytes 393220
  5.9 20.9 %copy-start.12 = (f32[1,8,32,128]{3,2,1,0:T(8,128)S(1)}, f32[1,8,32,128]{3,2,1,0:T(8,128)}, u32[]{:S(2)}) copy-start(f32[1,8,32,128]{3,2,1,0:T(8,128)} %param.17) | copy-start | bytes 393220
  6.6 20.1 %collective-permute-start = (f32[256,128]{1,0:T(8,128)S(1)}, f32[256,128]{1,0:T(8,128)S(1)}, u32[]{:S(2)}, u32[]{:S(2)}) collective-permute-start(f32[256,128]{1,0:T(8,128)S(1)} %get-tuple-element.40), channel_id=1, source_target_pairs={{0,8},{8,16},{16,24},{24,32},{32,40},{40,48},{48,56},{56,64},{64,7... | collective-permute-start | bytes 393224 | tf_op jit(solution)/shard_map/ppermute | solution.py:337
  10.6 16.1 %collective-permute-start.1 = (f32[256,128]{1,0:T(8,128)S(1)}, f32[256,128]{1,0:T(8,128)S(1)}, u32[]{:S(2)}, u32[]{:S(2)}) collective-permute-start(f32[256,128]{1,0:T(8,128)S(1)} %get-tuple-element.41), channel_id=1, source_target_pairs={{8,0},{16,8},{24,16},{32,24},{40,32},{48,40},{56,48},{64,56},{72,6... | collective-permute-start | bytes 393224 | tf_op jit(solution)/shard_map/ppermute | solution.py:337
  11.9 14.8 %collective-permute-start.2 = (f32[88,128]{1,0:T(8,128)S(1)}, f32[88,128]{1,0:T(8,128)S(1)}, u32[]{:S(2)}, u32[]{:S(2)}) collective-permute-start(f32[88,128]{1,0:T(8,128)S(1)} %get-tuple-element.42), channel_id=1, source_target_pairs={{0,1},{1,2},{2,3},{3,4},{4,5},{5,6},{6,7},{7,0},{8,9},{9,10},{10,1... | collective-permute-start | bytes 135176 | tf_op jit(solution)/shard_map/ppermute | solution.py:337
  15.9 10.8 %collective-permute-start.3 = (f32[88,128]{1,0:T(8,128)S(1)}, f32[88,128]{1,0:T(8,128)S(1)}, u32[]{:S(2)}, u32[]{:S(2)}) collective-permute-start(f32[88,128]{1,0:T(8,128)S(1)} %get-tuple-element.43), channel_id=1, source_target_pairs={{0,7},{1,0},{2,1},{3,2},{4,3},{5,4},{6,5},{7,6},{8,15},{9,8},{10,9... | collective-permute-start | bytes 135176 | tf_op jit(solution)/shard_map/ppermute | solution.py:337
  28.5 12.9 %collective-permute-start.4 = (f32[320,128]{1,0:T(8,128)S(1)}, f32[320,128]{1,0:T(8,128)S(1)}, u32[]{:S(2)}, u32[]{:S(2)}) collective-permute-start(f32[320,128]{1,0:T(8,128)S(1)} %get-tuple-element.46), channel_id=1, source_target_pairs={{0,8},{8,16},{16,24},{24,32},{32,40},{40,48},{48,56},{56,64},{64,7... | collective-permute-start | bytes 491528 | tf_op jit(solution)/shard_map/ppermute | solution.py:337
  32.5 8.9 %collective-permute-start.5 = (f32[320,128]{1,0:T(8,128)S(1)}, f32[320,128]{1,0:T(8,128)S(1)}, u32[]{:S(2)}, u32[]{:S(2)}) collective-permute-start(f32[320,128]{1,0:T(8,128)S(1)} %get-tuple-element.47), channel_id=1, source_target_pairs={{8,0},{16,8},{24,16},{32,24},{40,32},{48,40},{56,48},{64,56},{72,6... | collective-permute-start | bytes 491528 | tf_op jit(solution)/shard_map/ppermute | solution.py:337
  33.8 6.5 %collective-permute-start.6 = (f32[72,128]{1,0:T(8,128)S(1)}, f32[72,128]{1,0:T(8,128)S(1)}, u32[]{:S(2)}, u32[]{:S(2)}) collective-permute-start(f32[72,128]{1,0:T(8,128)S(1)} %get-tuple-element.48), channel_id=1, source_target_pairs={{0,1},{1,2},{2,3},{3,4},{4,5},{5,6},{6,7},{7,0},{8,9},{9,10},{10,1... | collective-permute-start | bytes 110600 | tf_op jit(solution)/shard_map/ppermute | solution.py:337
  35.7 5.6 %collective-permute-start.7 = (f32[72,128]{1,0:T(8,128)S(1)}, f32[72,128]{1,0:T(8,128)S(1)}, u32[]{:S(2)}, u32[]{:S(2)}) collective-permute-start(f32[72,128]{1,0:T(8,128)S(1)} %get-tuple-element.49), channel_id=1, source_target_pairs={{0,7},{1,0},{2,1},{3,2},{4,3},{5,4},{6,5},{7,6},{8,15},{9,8},{10,9... | collective-permute-start | bytes 110600 | tf_op jit(solution)/shard_map/ppermute | solution.py:337
  43.0 13.1 %collective-permute-start.8 = (f32[288,128]{1,0:T(8,128)S(1)}, f32[288,128]{1,0:T(8,128)S(1)}, u32[]{:S(2)}, u32[]{:S(2)}) collective-permute-start(f32[288,128]{1,0:T(8,128)S(1)} %get-tuple-element.54), channel_id=1, source_target_pairs={{0,8},{8,16},{16,24},{24,32},{32,40},{40,48},{48,56},{56,64},{64,7... | collective-permute-start | bytes 442376 | tf_op jit(solution)/shard_map/ppermute | solution.py:337
  47.0 9.1 %collective-permute-start.9 = (f32[288,128]{1,0:T(8,128)S(1)}, f32[288,128]{1,0:T(8,128)S(1)}, u32[]{:S(2)}, u32[]{:S(2)}) collective-permute-start(f32[288,128]{1,0:T(8,128)S(1)} %get-tuple-element.55), channel_id=1, source_target_pairs={{8,0},{16,8},{24,16},{32,24},{40,32},{48,40},{56,48},{64,56},{72,6... | collective-permute-start | bytes 442376 | tf_op jit(solution)/shard_map/ppermute | solution.py:337
  48.3 6.8 %collective-permute-start.10 = (f32[72,128]{1,0:T(8,128)S(1)}, f32[72,128]{1,0:T(8,128)S(1)}, u32[]{:S(2)}, u32[]{:S(2)}) collective-permute-start(f32[72,128]{1,0:T(8,128)S(1)} %get-tuple-element.56), channel_id=1, source_target_pairs={{0,1},{1,2},{2,3},{3,4},{4,5},{5,6},{6,7},{7,0},{8,9},{9,10},{10,1... | collective-permute-start | bytes 110600 | tf_op jit(solution)/shard_map/ppermute | solution.py:337
  50.5 5.6 %collective-permute-start.11 = (f32[72,128]{1,0:T(8,128)S(1)}, f32[72,128]{1,0:T(8,128)S(1)}, u32[]{:S(2)}, u32[]{:S(2)}) collective-permute-start(f32[72,128]{1,0:T(8,128)S(1)} %get-tuple-element.57), channel_id=1, source_target_pairs={{0,7},{1,0},{2,1},{3,2},{4,3},{5,4},{6,5},{7,6},{8,15},{9,8},{10,9... | collective-permute-start | bytes 110600 | tf_op jit(solution)/shard_map/ppermute | solution.py:337
  57.9 13.1 %collective-permute-start.12 = (f32[256,128]{1,0:T(8,128)S(1)}, f32[256,128]{1,0:T(8,128)S(1)}, u32[]{:S(2)}, u32[]{:S(2)}) collective-permute-start(f32[256,128]{1,0:T(8,128)S(1)} %get-tuple-element.62), channel_id=1, source_target_pairs={{0,8},{8,16},{16,24},{24,32},{32,40},{40,48},{48,56},{56,64},{64,7... | collective-permute-start | bytes 393224 | tf_op jit(solution)/shard_map/ppermute | solution.py:337
  61.8 9.1 %collective-permute-start.13 = (f32[256,128]{1,0:T(8,128)S(1)}, f32[256,128]{1,0:T(8,128)S(1)}, u32[]{:S(2)}, u32[]{:S(2)}) collective-permute-start(f32[256,128]{1,0:T(8,128)S(1)} %get-tuple-element.63), channel_id=1, source_target_pairs={{8,0},{16,8},{24,16},{32,24},{40,32},{48,40},{56,48},{64,56},{72,6... | collective-permute-start | bytes 393224 | tf_op jit(solution)/shard_map/ppermute | solution.py:337
  63.1 6.8 %collective-permute-start.14 = (f32[72,128]{1,0:T(8,128)S(1)}, f32[72,128]{1,0:T(8,128)S(1)}, u32[]{:S(2)}, u32[]{:S(2)}) collective-permute-start(f32[72,128]{1,0:T(8,128)S(1)} %get-tuple-element.64), channel_id=1, source_target_pairs={{0,1},{1,2},{2,3},{3,4},{4,5},{5,6},{6,7},{7,0},{8,9},{9,10},{10,1... | collective-permute-start | bytes 110600 | tf_op jit(solution)/shard_map/ppermute | solution.py:337
  66.1 4.8 %collective-permute-start.15 = (f32[72,128]{1,0:T(8,128)S(1)}, f32[72,128]{1,0:T(8,128)S(1)}, u32[]{:S(2)}, u32[]{:S(2)}) collective-permute-start(f32[72,128]{1,0:T(8,128)S(1)} %get-tuple-element.65), channel_id=1, source_target_pairs={{0,7},{1,0},{2,1},{3,2},{4,3},{5,4},{6,5},{7,6},{8,15},{9,8},{10,9... | collective-permute-start | bytes 110600 | tf_op jit(solution)/shard_map/ppermute | solution.py:337
  73.4 5.3 %collective-permute-start.17 = (f32[16,128]{1,0:T(8,128)S(1)}, f32[16,128]{1,0:T(8,128)S(1)}, u32[]{:S(2)}, u32[]{:S(2)}) collective-permute-start(f32[16,128]{1,0:T(8,128)S(1)} %get-tuple-element.80), channel_id=1, source_target_pairs={{1,0},{2,1},{3,2},{4,3},{5,4},{6,5},{7,6},{9,8},{10,9},{11,10},{12... | collective-permute-start | bytes 24584 | tf_op jit(solution)/shard_map/ppermute | solution.py:337
  74.7 4.8 %collective-permute-start.16 = (f32[16,128]{1,0:T(8,128)S(1)}, f32[16,128]{1,0:T(8,128)S(1)}, u32[]{:S(2)}, u32[]{:S(2)}) collective-permute-start(f32[16,128]{1,0:T(8,128)S(1)} %get-tuple-element.81), channel_id=1, source_target_pairs={{0,1},{1,2},{2,3},{3,4},{4,5},{5,6},{6,7},{8,9},{9,10},{10,11},{11... | collective-permute-start | bytes 24584 | tf_op jit(solution)/shard_map/ppermute | solution.py:337
  80.3 23.8 %all-to-all-start = ((f32[16,32,128]{2,1,0:T(8,128)}), f32[16,32,128]{2,1,0:T(8,128)S(1)}, u32[]{:S(2)}, u32[]{:S(2)}) async-start(f32[16,32,128]{2,1,0:T(8,128)} %shard_map.136), calls=%async_computation | async-start | bytes 524288 | tf_op jit(solution)/shard_map/all_to_all | solution.py:421
  (10 other events, 41.3 us)

commit v3 on v2

--- a/solution.py
+++ b/solution.py
@@ -55,11 +55,19 @@
     yhi[8 * i + 4 : 8 * i + 8] = s[NY - W :]
 
 
-def first_kernel(mean, logs, noise, p, q, obs, c_out, xlo, xhi, ylo, yhi, cpk):
+def first_kernel(
+    mean, logs, noise, p, q, obs, c_out, v_out, xlo, xhi, ylo, yhi, cpk, oc
+):
+    oc[...] = jnp.zeros((16, 128), f32)
+    oc[0:4, 0:64] = obs[...]
+    for y in (ylo, yhi):
+        y[80:88] = jnp.zeros((8, 128), f32)
+        y[80:84, 0:64] = obs[...]
     rows = []
     for i in range(NX):
         vel = mean[i] + jnp.exp(logs[i]) * noise[i]
         c = courant_sq * vel * vel
+        v_out[i] = vel
         c_out[i] = c
         put_strips(i, p[i], c * q[i], xlo, xhi, ylo, yhi)
         rows.append(c)
@@ -67,8 +75,6 @@
     cpk[...] = slab
     ylo[64:80] = slab[:16]
     yhi[64:80] = slab[16:]
-    ylo[80:88] = obs[...]
-    yhi[80:88] = obs[...]
 
 
 def fill(buf, field, rows_l, rows_r, md, mu, at, keep_d, keep_u):
@@ -92,18 +98,18 @@
     return out
 
 
-def step_kernel(n, meta, samples, c, p, pp, q, ql, ml, mr, md, mu, oc, *rest):
+def step_kernel(n, source, start, wavelet, c, p, pp, q, ql, ml, mr, md, mu, oc, *rest):
+    ix, iy, ngy = lax.axis_index("gx"), lax.axis_index("gy"), lax.axis_size("gy")
     rest = list(rest)
     bufp, bufs = rest[-2:]
     rest = rest[:-2]
     take = lambda: rest.pop(0)
-    cpk = cl = cr = lap_other = q3 = img = None
     if n == 1:
         cext = take()
     if n == 2:
         lap_other = take()
     if n == 3:
-        lap_other, q3, img = take(), take(), take()
+        lap_other, q3, img, vel, noise = take(), take(), take(), take(), take()
     lpk, oc_out, qn = take(), take(), take()
     if n < 3:
         pn, xlo, xhi, ylo, yhi = take(), take(), take(), take(), take()
@@ -116,9 +122,9 @@
     if n == 2:
         img_out = take()
     if n == 3:
-        img_out, mat = take(), take()
-
-    keep_d, keep_u = meta[3] > 0, meta[4] > 0
+        mat, mat_lo, mat_hi, own, sent = take(), take(), take(), take(), take()
+
+    keep_d, keep_u = iy > 0, iy < ngy - 1
     lane = lanes()
     wz = [None] + [
         (jnp.where(lane < NZ - k, CK[k], 0.0), jnp.where(lane >= k, CK[k], 0.0))
@@ -143,15 +149,21 @@
         if n == 2:
             img_out[i] = lap * q[i] + q_new * lap_other[i]
         if n == 3:
-            img_out[i] = img[i] + lap * q3[i] + q_new * lap_other[i]
+            image = img[i] + lap * q3[i] + q_new * lap_other[i]
+            grad = (2.0 * courant_sq) * vel[i] * image
+            weighted = grad * noise[i]
+            first = lax.axis_index("shot") % 2 == 0
+            own[i] = jnp.where(first, grad, weighted)
+            sent[i] = jnp.where(first, weighted, grad)
     lpk[...] = slab
 
-    sx, sy = meta[0], meta[1]
+    sx = source[0] // (NY * ngy) - ix * NX
+    sy = source[0] % (NY * ngy) - iy * NY
 
     @pl.when((sx >= 0) & (sx < NX) & (sy >= 0) & (sy < NY))
     def _():
         row = pn[sx, pl.ds(sy, 1), :]
-        pn[sx, pl.ds(sy, 1), :] = row + jnp.where(lane == SRC_DEPTH, samples[n], 0.0)
+        pn[sx, pl.ds(sy, 1), :] = row + jnp.where(lane == SRC_DEPTH, wavelet[0, start[0] + n], 0.0)
 
     at = 80 if n == 0 else 64
     got_d, got_u = md[at : at + 8], mu[at : at + 8]
@@ -178,11 +190,12 @@
     if n == 3:
         out = jnp.zeros((NY, NZ), f32)
         for i in range(NX):
-            for t, row in ((1, None), (2, pp[i]), (3, p[i]), (4, pn[i])):
-                if row is not None:
-                    to = 4 * i + t - 1
-                    out = jnp.where(lane == to, roll(row, to - REC_DEPTH), out)
+            for t, row in ((2, pp[i]), (3, p[i]), (4, pn[i])):
+                to = 4 * i + t - 1
+                out = jnp.where(lane == to, roll(row, to - REC_DEPTH), out)
         mat[...] = out
+        mat_lo[...] = out[:16]
+        mat_hi[...] = out[16:]
 
 
 def chunk_kernel(mat, got_d, got_u, p1, oc, out):
@@ -211,34 +224,63 @@
     return out
 
 
+def table_kernel(rec, vel, noise, keyx, hoty, count, vpk, zpk, hot):
+    ix, iy, ngy = lax.axis_index("gx"), lax.axis_index("gy"), lax.axis_size("gy")
+    half = ngy // 2
+    odd = iy % 2 == 1
+    lane = lanes()
+    bf = jnp.bfloat16
+    row4 = lax.broadcasted_iota(jnp.int32, (160, 128), 0) // 4
+    coly = lax.broadcasted_iota(jnp.int32, (64, 128), 0)
+
+    def build(g, carry):
+        at = pl.ds(pl.multiple_of(g * 128, 128), 128)
+        first = (iy + 2 * (g % half)) % ngy
+        second = (first + 1) % ngy
+        row_a = rec[pl.ds((g // half) * half + first // 2, 1), :]
+        row_b = rec[pl.ds((g // half) * half + second // 2, 1), :]
+        row = jnp.where(odd, jnp.where(lane < 64, roll(row_a, 64), roll(row_b, 64)), row_a)
+        kx = row // (NY * ngy) - ix * NX + 16
+        ky = row % (NY * ngy) - iy * NY + 16
+        keyx[pl.ds(g, 1), :] = kx
+        hot[:, at] = jnp.where(row4 == kx, 1.0, 0.0).astype(bf)
+        hoty[:, at] = jnp.where(coly == ky, 1.0, 0.0).astype(bf)
+        return carry
+
+    lax.fori_loop(0, rec.shape[0], build, 0)
+    count[...] = lax.dot_general(
+        hot[...], hoty[...], (((1,), (1,)), ((), ())), preferred_element_type=f32
+    )
+    vpk[...] = pack([vel[i] for i in range(NX)])
+    zpk[...] = pack([noise[i] for i in range(NX)])
+
+
 def last_kernel(
-    meta, got, keyx, keyy, cext, c1l, c1r, c2l, c2r, lp0, lp1, lp2, lp3, img, mean, logs, noise,
-    out, table, hoty, x, r3, r2, r1, inj,
+    got, keyx, hoty, cnt, cext, ml1, mr1, ml2, mr2, lp0, lp1, lp2, lp3, vpk, zpk, own, other,
+    out, table, x, r3, r2, r1, inj,
 ):
     ngx = got.shape[0]
     lane = lanes()
-    ix = meta[2]
+    ix = lax.axis_index("gx")
+    c1l, c1r = ml1.at[256:320], mr1.at[256:320]
+    c2l, c2r = ml2.at[256:288], mr2.at[256:288]
     bf = jnp.bfloat16
-
-    row4 = lax.broadcasted_iota(jnp.int32, (160, 128), 0) // 4
-    coly = lax.broadcasted_iota(jnp.int32, (64, 128), 0)
+    row4 = (lax.broadcasted_iota(jnp.int32, (160, 128), 0) // 4).astype(f32).astype(bf)
+    none = jnp.zeros((), bf)
 
     def build(g, carry):
         for rp in range(4):
-            kx = keyx[pl.ds(4 * g + rp, 1), :]
-            ky = keyy[pl.ds(4 * g + rp, 1), :]
             at = pl.ds(pl.multiple_of((4 * g + rp) * 128, 128), 128)
             val = got[g, 4 * rp : 4 * rp + 4, :]
             hi = val.astype(bf).astype(f32)
             mid = (val - hi).astype(bf).astype(f32)
             low = val - hi - mid
-            hot = row4 == kx
+            kx = jnp.clip(keyx[pl.ds(4 * g + rp, 1), :], -1, 40).astype(f32).astype(bf)
+            here = row4 == kx
             for part, v in enumerate((hi, mid, low)):
-                v8 = jnp.concatenate([v, v], 0)
-                v160 = jnp.concatenate([v8] * 20, 0)
-                table[160 * part : 160 * (part + 1), at] = jnp.where(hot, v160, 0.0).astype(bf)
-            table[480:640, at] = jnp.where(hot, 1.0, 0.0).astype(bf)
-            hoty[:, at] = jnp.where(coly == ky, 1.0, 0.0).astype(bf)
+                v16 = jnp.concatenate([v, v, v, v], 0).astype(bf)
+                v160 = jnp.concatenate([v16] * 10, 0)
+                table[160 * part : 160 * (part + 1), at] = jnp.where(here, v160, none)
         return carry
 
     lax.fori_loop(0, ngx, build, 0)
@@ -246,10 +288,9 @@
         table[...], hoty[...], (((1,), (1,)), ((), ())), preferred_element_type=f32
     )
     seen = sums[0:160] + sums[160:320] + sums[320:480]
-    count = sums[480:640]
     zero = jnp.zeros((96, 64), f32)
     seen = jnp.concatenate([seen, zero], 0)
-    count = jnp.concatenate([count, zero], 0)
+    count = jnp.concatenate([cnt[...], zero], 0)
     both = jnp.concatenate([seen, count], 1)
     tr = [both[:128].T, both[128:].T]
 
@@ -308,17 +349,34 @@
     corr = r0 * lp0[...] + r1[2, 8:40] * lp1[...] + r2[2, 8:40] * lp2[...]
     corr = corr + r3[2, 16:48] * lp3[...]
 
-    per = NX // out.shape[0]
+    cells = NX * NY
     for i in range(NX):
-        image = img[i] + jnp.where(lane < SLAB, roll(corr, -SLAB * i), 0.0)
-        z = noise[i]
-        vel = mean[i] + jnp.exp(logs[i]) * z
-        grad = (2.0 * courant_sq) * vel * image
-        out[i // per, 0, i % per] = grad
-        out[i // per, 1, i % per] = grad * z
-
-
-def call(kernel, outs, scratch=(), smem=0):
+        out[NY * i : NY * (i + 1)] = own[i] + other[i]
+    grad = (2.0 * courant_sq) * vpk[...] * corr
+    out[cells : cells + NY] = grad
+    out[cells + NY : cells + 2 * NY] = grad * zpk[...]
+
+
+def sum_kernel(every, logs, grad_mean, grad_logs):
+    lane = lanes()
+    cells = NX * NY
+
+    def packed(at):
+        rows = slice(at, at + NY)
+        return (every[0, rows] + every[1, rows]) + (every[2, rows] + every[3, rows])
+
+    grad_in, weighted_in = packed(cells), packed(cells + NY)
+    for i in range(NX):
+        rows = slice(NY * i, NY * (i + 1))
+        grad = every[0, rows] + every[2, rows]
+        grad_mean[i] = grad + jnp.where(lane < SLAB, roll(grad_in, -SLAB * i), 0.0)
+        weighted = every[1, rows] + every[3, rows]
+        weighted = weighted + jnp.where(lane < SLAB, roll(weighted_in, -SLAB * i), 0.0)
+        spread = jnp.exp(logs[i])
+        grad_logs[i] = spread * weighted + jnp.exp(2.0 * logs[i]) / prior_var - 1.0
+
+
+def call(kernel, outs, scratch=(), smem=0, mib=4):
     def go(*args):
         return pl.pallas_call(
             kernel,
@@ -326,7 +384,7 @@
             in_specs=[SM] * smem + [VM] * (len(args) - smem),
             out_specs=jax.tree.map(lambda _: VM, outs),
             scratch_shapes=list(scratch),
-            compiler_params=pltpu.CompilerParams(vmem_limit_bytes=48 * 2**20),
+            compiler_params=pltpu.CompilerParams(vmem_limit_bytes=mib * 2**20),
         )(*args)
 
     return go
@@ -352,33 +410,17 @@
     start_step,
 ):
     ngx, ngy, nshot = lax.axis_size("gx"), lax.axis_size("gy"), lax.axis_size("shot")
-    width_y = NY * ngy
-    ix, iy = lax.axis_index("gx"), lax.axis_index("gy")
     noise = shot_noise[0]
-    src = source_column[0]
-    meta = jnp.stack(
-        [
-            src // width_y - ix * NX,
-            src % width_y - iy * NY,
-            ix,
-            (iy > 0).astype(jnp.int32),
-            (iy < ngy - 1).astype(jnp.int32),
-        ]
-    ).astype(jnp.int32)
-    samples = lax.dynamic_slice_in_dim(wavelet[0], start_step[0], STEPS)
-    obs = jnp.pad(observed[0], ((0, 4), (0, 64)))
-    rec = receiver_column[0].reshape(ngx, ngy, -1)
-    rec = lax.dynamic_slice_in_dim(jnp.concatenate([rec, rec], 1), iy, ngy, 1).reshape(-1, 128)
-    keyx = rec // width_y - ix * NX + 16
-    keyy = rec % width_y - iy * NY + 16
-
     p_prev, p = checkpoint_prev[0], checkpoint_now[0]
     q_later, q = adjoint_next[0], adjoint_now[0]
     F = sds(NX, NY, NZ)
-    coef, xlo, xhi, ylo, yhi, cpk = call(
-        first_kernel, (F, sds(256, 128), sds(256, 128), sds(88, 128), sds(88, 128), sds(NY, NZ))
-    )(mean_velocity, log_scale, noise, p, q, obs)
-    oc = jnp.pad(observed[0], ((0, 12), (0, 64)))
+    coef, vel, xlo, xhi, ylo, yhi, _, oc = call(
+        first_kernel,
+        (
+            F, F, sds(256, 128), sds(256, 128), sds(88, 128), sds(88, 128), sds(NY, NZ),
+            sds(16, 128),
+        ),
+    )(mean_velocity, log_scale, noise, p, q, observed[0])
     buf = pltpu.VMEM((NX + 2 * W, 48, NZ), f32)
     slabs, keep = [], {}
     for n in range(STEPS):
@@ -390,14 +432,14 @@
         if n == 2:
             extra = (keep["lap1"],)
         if n == 3:
-            extra = (keep["lap0"], keep["q3"], keep["img"])
+            extra = (keep["lap0"], keep["q3"], keep["img"], vel, noise)
         outs = [sds(NY, NZ), sds(16, 128), F, F]
         if n < 3:
             rows = (320, 288, 256)[n]
             outs += [sds(rows, 128), sds(rows, 128), sds(72, 128), sds(72, 128)]
-        outs += {0: [F, sds(64, 128)], 1: [F], 2: [F], 3: [F, sds(NY, NZ)]}[n]
-        res = call(functools.partial(step_kernel, n), tuple(outs), (buf, buf), smem=2)(
-            meta, samples, coef, p, p_prev, q, q_later, ml, mr, md, mu, oc, *extra
+        outs += {0: [F, sds(64, 128)], 1: [F], 2: [F], 3: [sds(NY, NZ), sds(16, NZ), sds(16, NZ), F, F]}[n]
+        res = call(functools.partial(step_kernel, n), tuple(outs), (buf, buf), smem=3)(
+            source_column, start_step, wavelet, coef, p, p_prev, q, q_later, ml, mr, md, mu, oc, *extra
         )
         lpk, oc, q_next, p_next = res[:4]
         slabs.append(lpk)
@@ -407,45 +449,43 @@
             keep["lap0"], keep["cext"], keep["q3"], keep["p1"] = res[8], res[9], q_next, p_next
         if n == 1:
             keep["lap1"] = res[8]
-            c1l, c1r = ml[256:320], mr[256:320]
+            keep["c"] = [ml, mr]
         if n == 2:
             keep["img"] = res[8]
-            c2l, c2r = ml[256:288], mr[256:288]
+            keep["c"] += [ml, mr]
         if n == 3:
-            img, mat = res[4], res[5]
+            mat, mat_lo, mat_hi, own, sent = res[4:9]
         p_prev, p = p, p_next
         q_later, q = q, q_next
 
-    mat_d, mat_u = shift(mat[16:], "gy", 1), shift(mat[:16], "gy", -1)
+    mat_d, mat_u = shift(mat_hi, "gy", 1), shift(mat_lo, "gy", -1)
+    other = lax.ppermute(sent, "shot", [(i, i ^ 1) for i in range(nshot)])
+    nrec = receiver_column.shape[1]
+    bf = jnp.bfloat16
+    keyx, hoty, count, vpk, zpk = call(
+        table_kernel,
+        (
+            jax.ShapeDtypeStruct((nrec // 128, 128), jnp.int32),
+            jax.ShapeDtypeStruct((64, nrec), bf),
+            sds(160, 64),
+            sds(NY, NZ),
+            sds(NY, NZ),
+        ),
+        [pltpu.VMEM((160, nrec), bf)],
+        mib=16,
+    )(receiver_column.reshape(-1, 128), vel, noise)
     chunk = call(chunk_kernel, sds(ngx, 32, 128))(mat, mat_d, mat_u, keep["p1"], oc)
     got = lax.all_to_all(chunk, "gx", 0, 0)
-    nrec = receiver_column.shape[1]
     g5 = pltpu.VMEM((5, 64, 128), f32)
     g48 = pltpu.VMEM((5, 48, 128), f32)
-    parts = call(
+    part = call(
         last_kernel,
-        sds(nshot, 2, NX // nshot, NY, NZ),
-        (
-            pltpu.VMEM((640, nrec), jnp.bfloat16),
-            pltpu.VMEM((64, nrec), jnp.bfloat16),
-            g5,
-            g5,
-            g48,
-            g48,
-            pltpu.VMEM((320, 512), f32),
-        ),
-        smem=1,
-    )(
-        meta, got, keyx, keyy, keep["cext"], c1l, c1r, c2l, c2r, *slabs, img,
-        mean_velocity, log_scale, noise,
-    )
-    quarter = lax.all_to_all(parts, "shot", 0, 0).sum(0)
-    total = lax.all_gather(quarter, "shot", axis=0)
-    total_grad = total[:, 0].reshape(NX, NY, NZ)
-    total_weighted = total[:, 1].reshape(NX, NY, NZ)
-    spread = jnp.exp(log_scale)
-    grad_log_scale = spread * total_weighted + jnp.exp(2.0 * log_scale) / prior_var - 1.0
-    return (total_grad, grad_log_scale)
+        sds(NX * NY + 2 * NY, NZ),
+        (pltpu.VMEM((480, nrec), bf), g5, g5, g48, g48, pltpu.VMEM((320, 512), f32)),
+        mib=24,
+    )(got, keyx, hoty, count, keep["cext"], *keep["c"], *slabs, vpk, zpk, own, other)
+    every = lax.all_gather(part, "shot", axis=0)
+    return call(sum_kernel, (F, F))(every, log_scale)
 
 
 def solution(mesh):

time: 156 us -> 144 us (0.923)
  the two profiles are of different devices: /device:TPU:1 before, /device:TPU:53 now
where the time goes in v3:
time: 144 us; the launch traced here: 143 us
  starting transfers between devices  86.7 us (60%)
  Pallas kernels  25.5 us (18%)
  blocking collectives  15.5 us (11%)
  waiting for transfers between devices  7.12 us (5%)
  local copies, waits for them, and re-layouts  5.83 us (4%)
  between operations  2.27 us (2%)
    ppermute x18, starting transfers between devices, shift(): lax.ppermute(x, axis, [(i, (i + k) % n) for i in range(n) if wrap or 0 <=...  63.7 us
    pallas_call x9, Pallas kernels, go(): pl.pallas_call(kernel, out_shape=outs, in_specs=[SM] * smem + [VM] * (len...  25.5 us
    all_gather x1, blocking collectives, local(): every = lax.all_gather(part, 'shot', axis=0)  15.5 us
    ppermute x1, starting transfers between devices, local(): other = lax.ppermute(sent, 'shot', [(i, i ^ 1) for i in range(nshot)])  12.1 us
    all_to_all x1, starting transfers between devices, local(): got = lax.all_to_all(chunk, 'gx', 0, 0)  10.9 us
    ppermute x18, waiting for transfers between devices, shift(): lax.ppermute(x, axis, [(i, (i + k) % n) for i in range(n) if wrap or 0 <=...  7.12 us
    unnamed x28, local copies, waits for them, and re-layouts  5.83 us
  transfers between devices with their start and end apart: 20, of which 5 were waited for; matrix products, arithmetic and copies ran while one was open for 0% of the time, Pallas kernels for 6%

profile of v3, /device:TPU:53, one launch (start us, length us, event | category | flops | bytes accessed | tf_op | source)
XLA Modules:
  0.0 142.9 jit_solution(13994248170612834815)
XLA Ops:
  6.6 2.3 %collective-permute-start = (f32[256,128]{1,0:T(8,128)S(1)}, f32[256,128]{1,0:T(8,128)S(1)}, u32[]{:S(2)}, u32[]{:S(2)}) collective-permute-start(f32[256,128]{1,0:T(8,128)S(1)} %get-tuple-element.50), channel_id=1, source_target_pairs={{0,8},{8,16},{16,24},{24,32},{32,40},{40,48},{48,56},{56,64},{64,7... | collective-permute-start | bytes 393224 | tf_op jit(solution)/shard_map/ppermute | solution.py:395
  8.9 3.0 %collective-permute-start.1 = (f32[256,128]{1,0:T(8,128)S(1)}, f32[256,128]{1,0:T(8,128)S(1)}, u32[]{:S(2)}, u32[]{:S(2)}) collective-permute-start(f32[256,128]{1,0:T(8,128)S(1)} %get-tuple-element.51), channel_id=1, source_target_pairs={{8,0},{16,8},{24,16},{32,24},{40,32},{48,40},{56,48},{64,56},{72,6... | collective-permute-start | bytes 393224 | tf_op jit(solution)/shard_map/ppermute | solution.py:395
  11.9 4.0 %collective-permute-start.2 = (f32[88,128]{1,0:T(8,128)S(1)}, f32[88,128]{1,0:T(8,128)S(1)}, u32[]{:S(2)}, u32[]{:S(2)}) collective-permute-start(f32[88,128]{1,0:T(8,128)S(1)} %get-tuple-element.52), channel_id=1, source_target_pairs={{0,1},{1,2},{2,3},{3,4},{4,5},{5,6},{6,7},{7,0},{8,9},{9,10},{10,1... | collective-permute-start | bytes 135176 | tf_op jit(solution)/shard_map/ppermute | solution.py:395
  15.9 8.6 %collective-permute-start.3 = (f32[88,128]{1,0:T(8,128)S(1)}, f32[88,128]{1,0:T(8,128)S(1)}, u32[]{:S(2)}, u32[]{:S(2)}) collective-permute-start(f32[88,128]{1,0:T(8,128)S(1)} %get-tuple-element.53), channel_id=1, source_target_pairs={{0,7},{1,0},{2,1},{3,2},{4,3},{5,4},{6,5},{7,6},{8,15},{9,8},{10,9... | collective-permute-start | bytes 135176 | tf_op jit(solution)/shard_map/ppermute | solution.py:395
  28.2 4.1 %collective-permute-start.4 = (f32[320,128]{1,0:T(8,128)S(1)}, f32[320,128]{1,0:T(8,128)S(1)}, u32[]{:S(2)}, u32[]{:S(2)}) collective-permute-start(f32[320,128]{1,0:T(8,128)S(1)} %get-tuple-element.57), channel_id=1, source_target_pairs={{0,8},{8,16},{16,24},{24,32},{32,40},{40,48},{48,56},{56,64},{64,7... | collective-permute-start | bytes 491528 | tf_op jit(solution)/shard_map/ppermute | solution.py:395
  32.3 1.9 %collective-permute-start.5 = (f32[320,128]{1,0:T(8,128)S(1)}, f32[320,128]{1,0:T(8,128)S(1)}, u32[]{:S(2)}, u32[]{:S(2)}) collective-permute-start(f32[320,128]{1,0:T(8,128)S(1)} %get-tuple-element.58), channel_id=1, source_target_pairs={{8,0},{16,8},{24,16},{32,24},{40,32},{48,40},{56,48},{64,56},{72,6... | collective-permute-start | bytes 491528 | tf_op jit(solution)/shard_map/ppermute | solution.py:395
  34.2 1.9 %collective-permute-start.6 = (f32[72,128]{1,0:T(8,128)S(1)}, f32[72,128]{1,0:T(8,128)S(1)}, u32[]{:S(2)}, u32[]{:S(2)}) collective-permute-start(f32[72,128]{1,0:T(8,128)S(1)} %get-tuple-element.59), channel_id=1, source_target_pairs={{0,1},{1,2},{2,3},{3,4},{4,5},{5,6},{6,7},{7,0},{8,9},{9,10},{10,1... | collective-permute-start | bytes 110600 | tf_op jit(solution)/shard_map/ppermute | solution.py:395
  36.2 4.9 %collective-permute-start.7 = (f32[72,128]{1,0:T(8,128)S(1)}, f32[72,128]{1,0:T(8,128)S(1)}, u32[]{:S(2)}, u32[]{:S(2)}) collective-permute-start(f32[72,128]{1,0:T(8,128)S(1)} %get-tuple-element.60), channel_id=1, source_target_pairs={{0,7},{1,0},{2,1},{3,2},{4,3},{5,4},{6,5},{7,6},{8,15},{9,8},{10,9... | collective-permute-start | bytes 110600 | tf_op jit(solution)/shard_map/ppermute | solution.py:395
  44.4 5.1 %collective-permute-start.8 = (f32[288,128]{1,0:T(8,128)S(1)}, f32[288,128]{1,0:T(8,128)S(1)}, u32[]{:S(2)}, u32[]{:S(2)}) collective-permute-start(f32[288,128]{1,0:T(8,128)S(1)} %get-tuple-element.65), channel_id=1, source_target_pairs={{0,8},{8,16},{16,24},{24,32},{32,40},{40,48},{48,56},{56,64},{64,7... | collective-permute-start | bytes 442376 | tf_op jit(solution)/shard_map/ppermute | solution.py:395
  49.6 1.9 %collective-permute-start.9 = (f32[288,128]{1,0:T(8,128)S(1)}, f32[288,128]{1,0:T(8,128)S(1)}, u32[]{:S(2)}, u32[]{:S(2)}) collective-permute-start(f32[288,128]{1,0:T(8,128)S(1)} %get-tuple-element.66), channel_id=1, source_target_pairs={{8,0},{16,8},{24,16},{32,24},{40,32},{48,40},{56,48},{64,56},{72,6... | collective-permute-start | bytes 442376 | tf_op jit(solution)/shard_map/ppermute | solution.py:395
  51.5 3.0 %collective-permute-start.10 = (f32[72,128]{1,0:T(8,128)S(1)}, f32[72,128]{1,0:T(8,128)S(1)}, u32[]{:S(2)}, u32[]{:S(2)}) collective-permute-start(f32[72,128]{1,0:T(8,128)S(1)} %get-tuple-element.67), channel_id=1, source_target_pairs={{0,1},{1,2},{2,3},{3,4},{4,5},{5,6},{6,7},{7,0},{8,9},{9,10},{10,1... | collective-permute-start | bytes 110600 | tf_op jit(solution)/shard_map/ppermute | solution.py:395
  54.5 3.8 %collective-permute-start.11 = (f32[72,128]{1,0:T(8,128)S(1)}, f32[72,128]{1,0:T(8,128)S(1)}, u32[]{:S(2)}, u32[]{:S(2)}) collective-permute-start(f32[72,128]{1,0:T(8,128)S(1)} %get-tuple-element.68), channel_id=1, source_target_pairs={{0,7},{1,0},{2,1},{3,2},{4,3},{5,4},{6,5},{7,6},{8,15},{9,8},{10,9... | collective-permute-start | bytes 110600 | tf_op jit(solution)/shard_map/ppermute | solution.py:395
  61.2 5.9 %collective-permute-start.12 = (f32[256,128]{1,0:T(8,128)S(1)}, f32[256,128]{1,0:T(8,128)S(1)}, u32[]{:S(2)}, u32[]{:S(2)}) collective-permute-start(f32[256,128]{1,0:T(8,128)S(1)} %get-tuple-element.73), channel_id=1, source_target_pairs={{0,8},{8,16},{16,24},{24,32},{32,40},{40,48},{48,56},{56,64},{64,7... | collective-permute-start | bytes 393224 | tf_op jit(solution)/shard_map/ppermute | solution.py:395
  67.1 1.9 %collective-permute-start.13 = (f32[256,128]{1,0:T(8,128)S(1)}, f32[256,128]{1,0:T(8,128)S(1)}, u32[]{:S(2)}, u32[]{:S(2)}) collective-permute-start(f32[256,128]{1,0:T(8,128)S(1)} %get-tuple-element.74), channel_id=1, source_target_pairs={{8,0},{16,8},{24,16},{32,24},{40,32},{48,40},{56,48},{64,56},{72,6... | collective-permute-start | bytes 393224 | tf_op jit(solution)/shard_map/ppermute | solution.py:395
  69.1 3.2 %collective-permute-start.14 = (f32[72,128]{1,0:T(8,128)S(1)}, f32[72,128]{1,0:T(8,128)S(1)}, u32[]{:S(2)}, u32[]{:S(2)}) collective-permute-start(f32[72,128]{1,0:T(8,128)S(1)} %get-tuple-element.75), channel_id=1, source_target_pairs={{0,1},{1,2},{2,3},{3,4},{4,5},{5,6},{6,7},{7,0},{8,9},{9,10},{10,1... | collective-permute-start | bytes 110600 | tf_op jit(solution)/shard_map/ppermute | solution.py:395
  72.3 3.6 %collective-permute-start.15 = (f32[72,128]{1,0:T(8,128)S(1)}, f32[72,128]{1,0:T(8,128)S(1)}, u32[]{:S(2)}, u32[]{:S(2)}) collective-permute-start(f32[72,128]{1,0:T(8,128)S(1)} %get-tuple-element.76), channel_id=1, source_target_pairs={{0,7},{1,0},{2,1},{3,2},{4,3},{5,4},{6,5},{7,6},{8,15},{9,8},{10,9... | collective-permute-start | bytes 110600 | tf_op jit(solution)/shard_map/ppermute | solution.py:395
  77.0 2.4 %shard_map.135 = (f32[32,128]{1,0:T(8,128)S(1)}, f32[16,128]{1,0:T(8,128)S(1)}, f32[8,32,128]{2,1,0:T(8,128)}, f32[8,32,128]{2,1,0:T(8,128)}, f32[32,128]{1,0:T(...) custom-call(s32[1]{0:T(128)S(6)} %copy.14.source, ...), custom_call_target="tpu_custom_call" | custom-call | tf_op jit(solution)/shard_map/pallas_call | solution.py:381
  79.4 3.2 %collective-permute-start.16 = (f32[16,128]{1,0:T(8,128)S(1)}, f32[16,128]{1,0:T(8,128)S(1)}, u32[]{:S(2)}, u32[]{:S(2)}) collective-permute-start(f32[16,128]{1,0:T(8,128)S(1)} %get-tuple-element.82), channel_id=1, source_target_pairs={{0,1},{1,2},{2,3},{3,4},{4,5},{5,6},{6,7},{8,9},{9,10},{10,11},{11... | collective-permute-start | bytes 24584 | tf_op jit(solution)/shard_map/ppermute | solution.py:395
  83.9 3.1 %collective-permute-done.17.got_u = f32[16,128]{1,0:T(8,128)S(1)} collective-permute-done((f32[16,128]{1,0:T(8,128)S(1)}, f32[16,128]{1,0:T(8,128)S(1)}, u32[]{:S(2)}, u32[]{:S(2)}) %collective-permute-start.17) | collective-permute-done | bytes 8224 | tf_op jit(solution)/shard_map/ppermute | solution.py:395
  87.9 10.9 %all-to-all-start = ((f32[16,32,128]{2,1,0:T(8,128)}), f32[16,32,128]{2,1,0:T(8,128)S(1)}, u32[]{:S(2)}, u32[]{:S(2)}) async-start(f32[16,32,128]{2,1,0:T(8,128)} %shard_map.136), calls=%async_computation | async-start | bytes 524288 | tf_op jit(solution)/shard_map/all_to_all | solution.py:478
  98.8 12.1 %collective-permute-start.18 = (f32[8,32,128]{2,1,0:T(8,128)S(1)}, f32[8,32,128]{2,1,0:T(8,128)S(1)}, u32[]{:S(2)}, u32[]{:S(2)}) collective-permute-start(f32[8,32,128]{2,1,0:T(8,128)S(1)} %get-tuple-element.95), channel_id=1, source_target_pairs={{0,128},{128,0},{256,384},{384,256},{1,129},{129,1},{257,385},{385... | collective-permute-start | bytes 393224 | tf_op jit(solution)/shard_map/ppermute | solution.py:462
  110.9 8.2 %shard_map.137 = (s32[64,128]{1,0:T(8,128)S(1)}, bf16[64,8192]{1,0:T(8,128)(2,1)S(1)}, f32[160,64]{1,0:T(8,128)S(1)}, f32[32,128]{1,0:T(8,128)S(1)}, f32[32,128]{1,0:T(8,128)S(1)}) custom-call(s32[64,128]{1,0:T(8,128)S(1)} %bitcast.20, f32[8,32,128]{2,1,0:T(8,128)S(1)} %get-tuple-element.80.rest_3_.vel, f32[8,32,128]{2,1,0:T(8,128)S(1)} %bitcast.17), custom_call_target="tpu_custom_call" | custom-call | tf_op jit(solution)/shard_map/pallas_call | solution.py:381
  119.1 7.4 %shard_map.138 = f32[320,128]{1,0:T(8,128)S(1)} custom-call(f32[16,32,128]{2,1,0:T(8,128)S(1)} %all-to-all-done.got, s32[64,128]{1,0:T(8,128)S(1)} %get-tuple-element.85.keyx, bf16[64,8192]{1,0:T(8,128)(2,1)S(1)} %get-tuple-element.86.hoty, f32[160,64]{1,0:T(8,128)S(1)} %get-tuple-element.87.cnt, f32[64,128]{1,0:T(8,128)S(1)} %get-tuple-element.62.rest_0_.cext, ...), custom_call_target="tpu_custom_call" | custom-call | tf_op jit(solution)/shard_map/pallas_call | solution.py:381
  126.5 15.5 %all-gather = f32[1280,128]{1,0:T(8,128)S(1)} all-gather(f32[320,128]{1,0:T(8,128)S(1)} %shard_map.138), channel_id=2, replica_groups=mesh['shot'=4,'gx'=16,'gy'=8] {'shot'}, dimensions={0}, use_global_device_ids=true | all-gather | bytes 819200 | tf_op jit(solution)/shard_map/all_gather | solution.py:487
  (54 shorter events, 18.6 us)
Async XLA Ops:
  5.8 20.0 %copy-start.3 = (f32[1,8,32,128]{3,2,1,0:T(8,128)S(1)}, f32[1,8,32,128]{3,2,1,0:T(8,128)}, u32[]{:S(2)}) copy-start(f32[1,8,32,128]{3,2,1,0:T(8,128)} %param.18) | copy-start | bytes 393220
  5.8 20.0 %copy-start.9 = (f32[1,8,32,128]{3,2,1,0:T(8,128)S(1)}, f32[1,8,32,128]{3,2,1,0:T(8,128)}, u32[]{:S(2)}) copy-start(f32[1,8,32,128]{3,2,1,0:T(8,128)} %param.15) | copy-start | bytes 393220
  5.8 20.0 %copy-start.10 = (f32[1,8,32,128]{3,2,1,0:T(8,128)S(1)}, f32[1,8,32,128]{3,2,1,0:T(8,128)}, u32[]{:S(2)}) copy-start(f32[1,8,32,128]{3,2,1,0:T(8,128)} %param.17) | copy-start | bytes 393220
  6.6 19.2 %collective-permute-start = (f32[256,128]{1,0:T(8,128)S(1)}, f32[256,128]{1,0:T(8,128)S(1)}, u32[]{:S(2)}, u32[]{:S(2)}) collective-permute-start(f32[256,128]{1,0:T(8,128)S(1)} %get-tuple-element.50), channel_id=1, source_target_pairs={{0,8},{8,16},{16,24},{24,32},{32,40},{40,48},{48,56},{56,64},{64,7... | collective-permute-start | bytes 393224 | tf_op jit(solution)/shard_map/ppermute | solution.py:395
  8.9 16.9 %collective-permute-start.1 = (f32[256,128]{1,0:T(8,128)S(1)}, f32[256,128]{1,0:T(8,128)S(1)}, u32[]{:S(2)}, u32[]{:S(2)}) collective-permute-start(f32[256,128]{1,0:T(8,128)S(1)} %get-tuple-element.51), channel_id=1, source_target_pairs={{8,0},{16,8},{24,16},{32,24},{40,32},{48,40},{56,48},{64,56},{72,6... | collective-permute-start | bytes 393224 | tf_op jit(solution)/shard_map/ppermute | solution.py:395
  11.9 13.9 %collective-permute-start.2 = (f32[88,128]{1,0:T(8,128)S(1)}, f32[88,128]{1,0:T(8,128)S(1)}, u32[]{:S(2)}, u32[]{:S(2)}) collective-permute-start(f32[88,128]{1,0:T(8,128)S(1)} %get-tuple-element.52), channel_id=1, source_target_pairs={{0,1},{1,2},{2,3},{3,4},{4,5},{5,6},{6,7},{7,0},{8,9},{9,10},{10,1... | collective-permute-start | bytes 135176 | tf_op jit(solution)/shard_map/ppermute | solution.py:395
  15.9 9.9 %collective-permute-start.3 = (f32[88,128]{1,0:T(8,128)S(1)}, f32[88,128]{1,0:T(8,128)S(1)}, u32[]{:S(2)}, u32[]{:S(2)}) collective-permute-start(f32[88,128]{1,0:T(8,128)S(1)} %get-tuple-element.53), channel_id=1, source_target_pairs={{0,7},{1,0},{2,1},{3,2},{4,3},{5,4},{6,5},{7,6},{8,15},{9,8},{10,9... | collective-permute-start | bytes 135176 | tf_op jit(solution)/shard_map/ppermute | solution.py:395
  28.2 14.0 %collective-permute-start.4 = (f32[320,128]{1,0:T(8,128)S(1)}, f32[320,128]{1,0:T(8,128)S(1)}, u32[]{:S(2)}, u32[]{:S(2)}) collective-permute-start(f32[320,128]{1,0:T(8,128)S(1)} %get-tuple-element.57), channel_id=1, source_target_pairs={{0,8},{8,16},{16,24},{24,32},{32,40},{40,48},{48,56},{56,64},{64,7... | collective-permute-start | bytes 491528 | tf_op jit(solution)/shard_map/ppermute | solution.py:395
  32.3 10.5 %collective-permute-start.5 = (f32[320,128]{1,0:T(8,128)S(1)}, f32[320,128]{1,0:T(8,128)S(1)}, u32[]{:S(2)}, u32[]{:S(2)}) collective-permute-start(f32[320,128]{1,0:T(8,128)S(1)} %get-tuple-element.58), channel_id=1, source_target_pairs={{8,0},{16,8},{24,16},{32,24},{40,32},{48,40},{56,48},{64,56},{72,6... | collective-permute-start | bytes 491528 | tf_op jit(solution)/shard_map/ppermute | solution.py:395
  34.2 6.9 %collective-permute-start.6 = (f32[72,128]{1,0:T(8,128)S(1)}, f32[72,128]{1,0:T(8,128)S(1)}, u32[]{:S(2)}, u32[]{:S(2)}) collective-permute-start(f32[72,128]{1,0:T(8,128)S(1)} %get-tuple-element.59), channel_id=1, source_target_pairs={{0,1},{1,2},{2,3},{3,4},{4,5},{5,6},{6,7},{7,0},{8,9},{9,10},{10,1... | collective-permute-start | bytes 110600 | tf_op jit(solution)/shard_map/ppermute | solution.py:395
  36.2 6.0 %collective-permute-start.7 = (f32[72,128]{1,0:T(8,128)S(1)}, f32[72,128]{1,0:T(8,128)S(1)}, u32[]{:S(2)}, u32[]{:S(2)}) collective-permute-start(f32[72,128]{1,0:T(8,128)S(1)} %get-tuple-element.60), channel_id=1, source_target_pairs={{0,7},{1,0},{2,1},{3,2},{4,3},{5,4},{6,5},{7,6},{8,15},{9,8},{10,9... | collective-permute-start | bytes 110600 | tf_op jit(solution)/shard_map/ppermute | solution.py:395
  44.4 15.1 %collective-permute-start.8 = (f32[288,128]{1,0:T(8,128)S(1)}, f32[288,128]{1,0:T(8,128)S(1)}, u32[]{:S(2)}, u32[]{:S(2)}) collective-permute-start(f32[288,128]{1,0:T(8,128)S(1)} %get-tuple-element.65), channel_id=1, source_target_pairs={{0,8},{8,16},{16,24},{24,32},{32,40},{40,48},{48,56},{56,64},{64,7... | collective-permute-start | bytes 442376 | tf_op jit(solution)/shard_map/ppermute | solution.py:395
  49.6 9.9 %collective-permute-start.9 = (f32[288,128]{1,0:T(8,128)S(1)}, f32[288,128]{1,0:T(8,128)S(1)}, u32[]{:S(2)}, u32[]{:S(2)}) collective-permute-start(f32[288,128]{1,0:T(8,128)S(1)} %get-tuple-element.66), channel_id=1, source_target_pairs={{8,0},{16,8},{24,16},{32,24},{40,32},{48,40},{56,48},{64,56},{72,6... | collective-permute-start | bytes 442376 | tf_op jit(solution)/shard_map/ppermute | solution.py:395
  51.5 6.8 %collective-permute-start.10 = (f32[72,128]{1,0:T(8,128)S(1)}, f32[72,128]{1,0:T(8,128)S(1)}, u32[]{:S(2)}, u32[]{:S(2)}) collective-permute-start(f32[72,128]{1,0:T(8,128)S(1)} %get-tuple-element.67), channel_id=1, source_target_pairs={{0,1},{1,2},{2,3},{3,4},{4,5},{5,6},{6,7},{7,0},{8,9},{9,10},{10,1... | collective-permute-start | bytes 110600 | tf_op jit(solution)/shard_map/ppermute | solution.py:395
  54.5 5.0 %collective-permute-start.11 = (f32[72,128]{1,0:T(8,128)S(1)}, f32[72,128]{1,0:T(8,128)S(1)}, u32[]{:S(2)}, u32[]{:S(2)}) collective-permute-start(f32[72,128]{1,0:T(8,128)S(1)} %get-tuple-element.68), channel_id=1, source_target_pairs={{0,7},{1,0},{2,1},{3,2},{4,3},{5,4},{6,5},{7,6},{8,15},{9,8},{10,9... | collective-permute-start | bytes 110600 | tf_op jit(solution)/shard_map/ppermute | solution.py:395
  61.2 15.8 %collective-permute-start.12 = (f32[256,128]{1,0:T(8,128)S(1)}, f32[256,128]{1,0:T(8,128)S(1)}, u32[]{:S(2)}, u32[]{:S(2)}) collective-permute-start(f32[256,128]{1,0:T(8,128)S(1)} %get-tuple-element.73), channel_id=1, source_target_pairs={{0,8},{8,16},{16,24},{24,32},{32,40},{40,48},{48,56},{56,64},{64,7... | collective-permute-start | bytes 393224 | tf_op jit(solution)/shard_map/ppermute | solution.py:395
  67.1 9.9 %collective-permute-start.13 = (f32[256,128]{1,0:T(8,128)S(1)}, f32[256,128]{1,0:T(8,128)S(1)}, u32[]{:S(2)}, u32[]{:S(2)}) collective-permute-start(f32[256,128]{1,0:T(8,128)S(1)} %get-tuple-element.74), channel_id=1, source_target_pairs={{8,0},{16,8},{24,16},{32,24},{40,32},{48,40},{56,48},{64,56},{72,6... | collective-permute-start | bytes 393224 | tf_op jit(solution)/shard_map/ppermute | solution.py:395
  69.1 6.8 %collective-permute-start.14 = (f32[72,128]{1,0:T(8,128)S(1)}, f32[72,128]{1,0:T(8,128)S(1)}, u32[]{:S(2)}, u32[]{:S(2)}) collective-permute-start(f32[72,128]{1,0:T(8,128)S(1)} %get-tuple-element.75), channel_id=1, source_target_pairs={{0,1},{1,2},{2,3},{3,4},{4,5},{5,6},{6,7},{7,0},{8,9},{9,10},{10,1... | collective-permute-start | bytes 110600 | tf_op jit(solution)/shard_map/ppermute | solution.py:395
  72.3 4.7 %collective-permute-start.15 = (f32[72,128]{1,0:T(8,128)S(1)}, f32[72,128]{1,0:T(8,128)S(1)}, u32[]{:S(2)}, u32[]{:S(2)}) collective-permute-start(f32[72,128]{1,0:T(8,128)S(1)} %get-tuple-element.76), channel_id=1, source_target_pairs={{0,7},{1,0},{2,1},{3,2},{4,3},{5,4},{6,5},{7,6},{8,15},{9,8},{10,9... | collective-permute-start | bytes 110600 | tf_op jit(solution)/shard_map/ppermute | solution.py:395
  79.4 4.5 %collective-permute-start.16 = (f32[16,128]{1,0:T(8,128)S(1)}, f32[16,128]{1,0:T(8,128)S(1)}, u32[]{:S(2)}, u32[]{:S(2)}) collective-permute-start(f32[16,128]{1,0:T(8,128)S(1)} %get-tuple-element.82), channel_id=1, source_target_pairs={{0,1},{1,2},{2,3},{3,4},{4,5},{5,6},{6,7},{8,9},{9,10},{10,11},{11... | collective-permute-start | bytes 24584 | tf_op jit(solution)/shard_map/ppermute | solution.py:395
  82.6 4.4 %collective-permute-start.17 = (f32[16,128]{1,0:T(8,128)S(1)}, f32[16,128]{1,0:T(8,128)S(1)}, u32[]{:S(2)}, u32[]{:S(2)}) collective-permute-start(f32[16,128]{1,0:T(8,128)S(1)} %get-tuple-element.83), channel_id=1, source_target_pairs={{1,0},{2,1},{3,2},{4,3},{5,4},{6,5},{7,6},{9,8},{10,9},{11,10},{12... | collective-permute-start | bytes 24584 | tf_op jit(solution)/shard_map/ppermute | solution.py:395
  87.9 23.0 %copy-start.11 = (s32[1,8192]{1,0:T(1,128)S(1)}, s32[1,8192]{1,0:T(1,128)}, u32[]{:S(2)}) copy-start(s32[1,8192]{1,0:T(1,128)} %param.21) | copy-start | bytes 98308
  87.9 31.2 %all-to-all-start = ((f32[16,32,128]{2,1,0:T(8,128)}), f32[16,32,128]{2,1,0:T(8,128)S(1)}, u32[]{:S(2)}, u32[]{:S(2)}) async-start(f32[16,32,128]{2,1,0:T(8,128)} %shard_map.136), calls=%async_computation | async-start | bytes 524288 | tf_op jit(solution)/shard_map/all_to_all | solution.py:478
  98.8 20.3 %collective-permute-start.18 = (f32[8,32,128]{2,1,0:T(8,128)S(1)}, f32[8,32,128]{2,1,0:T(8,128)S(1)}, u32[]{:S(2)}, u32[]{:S(2)}) collective-permute-start(f32[8,32,128]{2,1,0:T(8,128)S(1)} %get-tuple-element.95), channel_id=1, source_target_pairs={{0,128},{128,0},{256,384},{384,256},{1,129},{129,1},{257,385},{385... | collective-permute-start | bytes 393224 | tf_op jit(solution)/shard_map/ppermute | solution.py:462
  (10 other events, 58.8 us)

commit v4 on v3

--- a/solution.py
+++ b/solution.py
@@ -45,167 +45,240 @@
     return out
 
 
-def put_strips(i, p, s, xlo, xhi, ylo, yhi):
+def put_rows(i, p, s, xlo, xhi):
     out, j = (xlo, i) if i < W else (xhi, i - W)
     out[NY * j : NY * (j + 1)] = p
     out[NY * (W + j) : NY * (W + j + 1)] = s
-    ylo[8 * i : 8 * i + 4] = p[:W]
-    ylo[8 * i + 4 : 8 * i + 8] = s[:W]
-    yhi[8 * i : 8 * i + 4] = p[NY - W :]
-    yhi[8 * i + 4 : 8 * i + 8] = s[NY - W :]
-
-
-def first_kernel(
-    mean, logs, noise, p, q, obs, c_out, v_out, xlo, xhi, ylo, yhi, cpk, oc
-):
+
+
+def put_pair(i, section, a, b, ylo, yhi, far=0):
+    at = 64 * section + 8 * i
+    lo, hi = slice(far, far + W), slice(NY - W - far, NY - far)
+    if a is not None:
+        ylo[at : at + 4] = a[lo]
+        yhi[at : at + 4] = a[hi]
+    ylo[at + 4 : at + 8] = b[lo]
+    yhi[at + 4 : at + 8] = b[hi]
+
+
+def put_columns(i, p, s, ylo, yhi):
+    put_pair(i, 0, p, s, ylo, yhi)
+    put_pair(i, 1, p, s, ylo, yhi, W)
+
+
+def first_kernel(mean, logs, noise, p, q, pp, ql, obs, c_out, v_out, xlo, xhi, ylo, yhi, oc, ob):
     oc[...] = jnp.zeros((16, 128), f32)
     oc[0:4, 0:64] = obs[...]
-    for y in (ylo, yhi):
-        y[80:88] = jnp.zeros((8, 128), f32)
-        y[80:84, 0:64] = obs[...]
+    ob[...] = jnp.zeros((8, 128), f32)
+    ob[0:4, 0:64] = obs[...]
     rows = []
     for i in range(NX):
         vel = mean[i] + jnp.exp(logs[i]) * noise[i]
         c = courant_sq * vel * vel
+        s = c * q[i]
         v_out[i] = vel
         c_out[i] = c
-        put_strips(i, p[i], c * q[i], xlo, xhi, ylo, yhi)
+        put_rows(i, p[i], s, xlo, xhi)
+        put_columns(i, p[i], s, ylo, yhi)
+        put_pair(i, 2, pp[i], q[i], ylo, yhi)
+        put_pair(i, 3, ql[i], c, ylo, yhi)
         rows.append(c)
     slab = pack(rows)
-    cpk[...] = slab
-    ylo[64:80] = slab[:16]
-    yhi[64:80] = slab[16:]
-
-
-def fill(buf, field, rows_l, rows_r, md, mu, at, keep_d, keep_u):
-    for i in range(NX):
-        buf[W + i, 8:40] = field[i]
-        buf[W + i, 4:8] = jnp.where(keep_d, md[8 * i + at : 8 * i + at + 4], 0.0)
-        buf[W + i, 40:44] = jnp.where(keep_u, mu[8 * i + at : 8 * i + at + 4], 0.0)
-    for j in range(W):
-        buf[j, 8:40] = rows_l[j]
-        buf[W + NX + j, 8:40] = rows_r[j]
-
-
-def laplace(buf, i, wz):
-    here = buf[W + i, 8:40]
+    ylo[256:272] = slab[:16]
+    yhi[256:272] = slab[16:]
+    for y in (ylo, yhi):
+        y[272:280] = ob[...]
+
+
+def join_kernel(xlo, xhi, md, mu, lo, hi):
+    n = xlo.shape[0]
+    lo[:n] = xlo[...]
+    lo[n : n + 32] = md[:32]
+    lo[n + 32 :] = mu[:32]
+    hi[:n] = xhi[...]
+    hi[n : n + 32] = md[32:64]
+    hi[n + 32 :] = mu[32:64]
+
+
+def edges():
+    iy = lax.axis_index("gy")
+    return iy > 0, iy < lax.axis_size("gy") - 1
+
+
+def depth_weights():
+    lane = lanes()
+    return [None] + [
+        (jnp.where(lane < NZ - k, CK[k], 0.0), jnp.where(lane >= k, CK[k], 0.0))
+        for k in range(1, W + 1)
+    ]
+
+
+def laplace(buf, i, lo, hi, wz):
+    here = buf[W + i, lo:hi]
     out = (3.0 * C0) * here
     for k in range(1, W + 1):
-        beside = buf[W + i + k, 8:40] + buf[W + i - k, 8:40]
-        beside = beside + buf[W + i, 8 + k : 40 + k] + buf[W + i, 8 - k : 40 - k]
+        beside = buf[W + i + k, lo:hi] + buf[W + i - k, lo:hi]
+        beside = beside + buf[W + i, lo + k : hi + k] + buf[W + i, lo - k : hi - k]
         out = out + CK[k] * beside
         out = out + wz[k][0] * roll(here, -k) + wz[k][1] * roll(here, k)
     return out
 
 
-def step_kernel(n, source, start, wavelet, c, p, pp, q, ql, ml, mr, md, mu, oc, *rest):
-    ix, iy, ngy = lax.axis_index("gx"), lax.axis_index("gy"), lax.axis_size("gy")
-    rest = list(rest)
-    bufp, bufs = rest[-2:]
-    rest = rest[:-2]
-    take = lambda: rest.pop(0)
+def add_source(n, source, start, wavelet, field, margin, reach):
+    ix, iy, width = lax.axis_index("gx"), lax.axis_index("gy"), NY * lax.axis_size("gy")
+    sx = source[0] // width - ix * NX
+    sy = source[0] % width - iy * NY
+
+    @pl.when((sx >= 0) & (sx < NX) & (sy >= -reach) & (sy < NY + reach))
+    def _():
+        at = pl.ds(sy + margin, 1)
+        row = field[sx, at, :]
+        field[sx, at, :] = row + jnp.where(lanes() == SRC_DEPTH, wavelet[0, start[0] + n], 0.0)
+
+
+def even_kernel(n, source, start, wavelet, c, p, pp, q, ql, ml, mr, md, mu, oc, *rest):
+    if n == 0:
+        lpk, oc_out, fwd, pe, qe, xlo, xhi, lap_out, ce, cext, bufp, bufs, qn, ppe, qle = rest
+    else:
+        lap1, lpk, oc_out, fwd, pe, qe, xlo, xhi, img, bufp, bufs, qn = rest
+    keep_d, keep_u = edges()
+    lane = lanes()
+    wz = depth_weights()
+
+    def part(m, keep, at):
+        return jnp.where(keep, m[at : at + 4], 0.0)
+
+    def extend(ext, field, section, half):
+        for i in range(NX):
+            at = 64 * section + 8 * i + half
+            ext[i, 8:40] = field[i]
+            ext[i, 4:8] = part(md, keep_d, at)
+            ext[i, 40:44] = part(mu, keep_u, at)
+
+    extend(qn, q, 2, 4)
+    if n == 0:
+        extend(ppe, pp, 2, 0)
+        extend(qle, ql, 3, 0)
+        extend(ce, c, 3, 4)
+    else:
+        ce, ppe, qle = c, pp, ql
+    corner = 256 if n == 0 else 288
+    for buf, half in ((bufp, 0), (bufs, 4)):
+        for i in range(NX):
+            row = p[i] if half == 0 else ce[i, 8:40] * q[i]
+            buf[W + i, 16:48] = row
+            near, far = 8 * i + half, 64 + 8 * i + half
+            buf[W + i, 8:12] = part(md, keep_d, far)
+            buf[W + i, 12:16] = part(md, keep_d, near)
+            buf[W + i, 48:52] = part(mu, keep_u, near)
+            buf[W + i, 52:56] = part(mu, keep_u, far)
+        for j in range(W):
+            at = 32 * half + NY * j
+            for m, row in ((ml, j), (mr, W + NX + j)):
+                buf[row, 16:48] = m[at : at + NY]
+                buf[row, 12:16] = part(m, keep_d, corner + 8 * j + half)
+                buf[row, 48:52] = part(m, keep_u, corner + 32 + 8 * j + half)
+    slab = jnp.zeros((NY, NZ), f32)
+    for i in range(NX):
+        lap_e = laplace(bufp, i, 8, 56, wz)
+        lap = lap_e[8:40]
+        slab = jnp.where(lane // SLAB == i, roll(lap, SLAB * i), slab)
+        pe[i] = 2.0 * bufp[W + i, 8:56] - ppe[i] + ce[i] * lap_e
+        q_new = 2.0 * qn[i] - qle[i] + laplace(bufs, i, 8, 56, wz)
+        qe[i] = q_new
+        if n == 0:
+            lap_out[i] = lap
+        else:
+            img[i] = lap * q[i] + q_new[8:40] * lap1[i]
+    lpk[...] = slab
+    add_source(n, source, start, wavelet, pe, 8, W)
+
+    at = 272 if n == 0 else 192
+    got_d, got_u = md[at : at + 8], mu[at : at + 8]
+    fwd[0:8] = got_d
+    fwd[8:16] = got_u
+    oc_out[...] = oc[...]
+    up, turn = (0, 64) if n == 0 else (4, 0)
+    oc_out[up : up + 4] = oc_out[up : up + 4] + roll(got_u, turn)[:4]
+    oc_out[12:16] = oc_out[12:16] + roll(got_d, turn)[:4]
+
+    for i in range(NX):
+        put_rows(i, pe[i, 8:40], ce[i, 8:40] * qe[i, 8:40], xlo, xhi)
+    if n == 0:
+        cext[0:16] = jnp.where(keep_d, md[256:272], 0.0)
+        cext[16:48] = pack([c[i] for i in range(NX)])
+        cext[48:64] = jnp.where(keep_u, mu[256:272], 0.0)
+        xlo[256:320] = cext[...]
+        xhi[256:320] = cext[...]
+
+
+def odd_kernel(n, source, start, wavelet, ce, pe, pp, qe, ql, ml, mr, fwd, *rest):
     if n == 1:
-        cext = take()
-    if n == 2:
-        lap_other = take()
-    if n == 3:
-        lap_other, q3, img, vel, noise = take(), take(), take(), take(), take()
-    lpk, oc_out, qn = take(), take(), take()
-    if n < 3:
-        pn, xlo, xhi, ylo, yhi = take(), take(), take(), take(), take()
+        lpk, qn, pn, xlo, xhi, ylo, yhi, lap_out, bufp, bufs = rest
     else:
-        pn = take()
-    if n == 0:
-        lap_out, cext = take(), take()
-    if n == 1:
-        lap_out = take()
-    if n == 2:
-        img_out = take()
-    if n == 3:
-        mat, mat_lo, mat_hi, own, sent = take(), take(), take(), take(), take()
-
-    keep_d, keep_u = iy > 0, iy < ngy - 1
-    lane = lanes()
-    wz = [None] + [
-        (jnp.where(lane < NZ - k, CK[k], 0.0), jnp.where(lane >= k, CK[k], 0.0))
-        for k in range(1, W + 1)
-    ]
-
-    def strip(m, at):
-        return [m[at + NY * j : at + NY * (j + 1)] for j in range(W)]
-
-    fill(bufp, p, strip(ml, 0), strip(mr, 0), md, mu, 0, keep_d, keep_u)
-    s = [c[i] * q[i] for i in range(NX)]
-    fill(bufs, s, strip(ml, 128), strip(mr, 128), md, mu, 4, keep_d, keep_u)
+        (lap0, q3, img, vel, noise, lpk, mat, mat_lo, mat_hi, own, sent, bufp, bufs, pn) = rest
+    lane = lanes()
+    wz = depth_weights()
+    for i in range(NX):
+        bufp[W + i, 12:52] = pe[i, 4:44]
+        bufs[W + i, 12:52] = ce[i, 4:44] * qe[i, 4:44]
+    for j in range(W):
+        for m, row in ((ml, j), (mr, W + NX + j)):
+            bufp[row, 16:48] = m[NY * j : NY * (j + 1)]
+            bufs[row, 16:48] = m[128 + NY * j : 128 + NY * (j + 1)]
     slab = jnp.zeros((NY, NZ), f32)
     for i in range(NX):
-        lap = laplace(bufp, i, wz)
+        lap = laplace(bufp, i, 16, 48, wz)
         slab = jnp.where(lane // SLAB == i, roll(lap, SLAB * i), slab)
-        pn[i] = 2.0 * p[i] - pp[i] + c[i] * lap
-        q_new = 2.0 * q[i] - ql[i] + laplace(bufs, i, wz)
-        qn[i] = q_new
-        if n < 2:
+        pn[i] = 2.0 * pe[i, 8:40] - pp[i] + ce[i, 8:40] * lap
+        q_new = 2.0 * qe[i, 8:40] - ql[i] + laplace(bufs, i, 16, 48, wz)
+        if n == 1:
+            qn[i] = q_new
             lap_out[i] = lap
-        if n == 2:
-            img_out[i] = lap * q[i] + q_new * lap_other[i]
-        if n == 3:
-            image = img[i] + lap * q3[i] + q_new * lap_other[i]
+        else:
+            image = img[i] + lap * q3[i, 8:40] + q_new * lap0[i]
             grad = (2.0 * courant_sq) * vel[i] * image
             weighted = grad * noise[i]
             first = lax.axis_index("shot") % 2 == 0
             own[i] = jnp.where(first, grad, weighted)
             sent[i] = jnp.where(first, weighted, grad)
     lpk[...] = slab
-
-    sx = source[0] // (NY * ngy) - ix * NX
-    sy = source[0] % (NY * ngy) - iy * NY
-
-    @pl.when((sx >= 0) & (sx < NX) & (sy >= 0) & (sy < NY))
-    def _():
-        row = pn[sx, pl.ds(sy, 1), :]
-        pn[sx, pl.ds(sy, 1), :] = row + jnp.where(lane == SRC_DEPTH, wavelet[0, start[0] + n], 0.0)
-
-    at = 80 if n == 0 else 64
-    got_d, got_u = md[at : at + 8], mu[at : at + 8]
-    oc_out[...] = oc[...]
-    up, turn_u, down, turn_d = ((0, 64, 12, 64), (4, 0, 12, 0), (4, 64, 8, 64), (8, 0, None, 0))[n]
-    oc_out[up : up + 4] = oc_out[up : up + 4] + roll(got_u, turn_u)[:4]
-    if down is not None:
-        oc_out[down : down + 4] = oc_out[down : down + 4] + roll(got_d, turn_d)[:4]
-
-    if n < 3:
+    add_source(n, source, start, wavelet, pn, 0, 0)
+    if n == 1:
         for i in range(NX):
-            put_strips(i, pn[i], c[i] * qn[i], xlo, xhi, ylo, yhi)
-        ylo[64:72] = got_u
-        yhi[64:72] = got_d
-    if n == 0:
-        cext[0:16] = jnp.where(keep_d, md[64:80], 0.0)
-        cext[16:48] = pack([c[i] for i in range(NX)])
-        cext[48:64] = jnp.where(keep_u, mu[64:80], 0.0)
-        xlo[256:320] = cext[...]
-        xhi[256:320] = cext[...]
-    if n == 1:
+            s = ce[i, 8:40] * qn[i]
+            put_rows(i, pn[i], s, xlo, xhi)
+            put_columns(i, pn[i], s, ylo, yhi)
+            put_pair(i, 2, None, qn[i], ylo, yhi)
         xlo[256:288] = mr[272:304]
         xhi[256:288] = ml[272:304]
-    if n == 3:
+        ylo[192:200] = fwd[8:16]
+        yhi[192:200] = fwd[0:8]
+    else:
         out = jnp.zeros((NY, NZ), f32)
         for i in range(NX):
-            for t, row in ((2, pp[i]), (3, p[i]), (4, pn[i])):
+            for t, row in ((2, pp[i]), (3, pe[i, 8:40]), (4, pn[i])):
                 to = 4 * i + t - 1
                 out = jnp.where(lane == to, roll(row, to - REC_DEPTH), out)
         mat[...] = out
-        mat_lo[...] = out[:16]
-        mat_hi[...] = out[16:]
-
-
-def chunk_kernel(mat, got_d, got_u, p1, oc, out):
+        mat_lo[0:16] = out[:16]
+        mat_hi[0:16] = out[16:]
+        mat_lo[16:24] = fwd[8:16]
+        mat_hi[16:24] = fwd[0:8]
+
+
+def chunk_kernel(mat, got_d, got_u, far, p1, oc, out):
     m = mat[...]
     lane = lanes()
     for i in range(NX):
-        m = jnp.where(lane == 4 * i, roll(p1[i], 4 * i - REC_DEPTH), m)
-    packed = got_d[...] + roll(m[:16], 32) + roll(m[16:], 64) + roll(got_u[...], 96)
+        m = jnp.where(lane == 4 * i, roll(p1[i, 8:40], 4 * i - REC_DEPTH), m)
+    packed = got_d[:16] + roll(m[:16], 32) + roll(m[16:], 64) + roll(got_u[:16], 96)
+    third_u, third_d = roll(got_u[16:24], 64)[:4], roll(got_d[16:24], 64)[:4]
     for g in range(out.shape[0]):
-        out[g, 0:16] = oc[...]
+        out[g, 0:4] = oc[0:4]
+        out[g, 4:8] = oc[4:8] + third_u
+        out[g, 8:12] = oc[8:12] + third_d + far[:4]
+        out[g, 12:16] = oc[12:16]
         out[g, 16:32] = packed
 
 
@@ -228,6 +301,8 @@
     ix, iy, ngy = lax.axis_index("gx"), lax.axis_index("gy"), lax.axis_size("gy")
     half = ngy // 2
     odd = iy % 2 == 1
+    bits = (NY * ngy).bit_length() - 1
+    assert 2**bits == NY * ngy
     lane = lanes()
     bf = jnp.bfloat16
     row4 = lax.broadcasted_iota(jnp.int32, (160, 128), 0) // 4
@@ -240,8 +315,8 @@
         row_a = rec[pl.ds((g // half) * half + first // 2, 1), :]
         row_b = rec[pl.ds((g // half) * half + second // 2, 1), :]
         row = jnp.where(odd, jnp.where(lane < 64, roll(row_a, 64), roll(row_b, 64)), row_a)
-        kx = row // (NY * ngy) - ix * NX + 16
-        ky = row % (NY * ngy) - iy * NY + 16
+        kx = (row >> bits) - ix * NX + 16
+        ky = (row & (NY * ngy - 1)) - iy * NY + 16
         keyx[pl.ds(g, 1), :] = kx
         hot[:, at] = jnp.where(row4 == kx, 1.0, 0.0).astype(bf)
         hoty[:, at] = jnp.where(coly == ky, 1.0, 0.0).astype(bf)
@@ -414,51 +489,62 @@
     p_prev, p = checkpoint_prev[0], checkpoint_now[0]
     q_later, q = adjoint_next[0], adjoint_now[0]
     F = sds(NX, NY, NZ)
-    coef, vel, xlo, xhi, ylo, yhi, _, oc = call(
+    E = sds(NX, NY + 16, NZ)
+    coef, vel, xlo, xhi, ylo, yhi, oc, ob = call(
         first_kernel,
         (
-            F, F, sds(256, 128), sds(256, 128), sds(88, 128), sds(88, 128), sds(NY, NZ),
-            sds(16, 128),
+            F, F, sds(256, 128), sds(256, 128), sds(280, 128), sds(280, 128), sds(16, 128),
+            sds(8, 128),
         ),
-    )(mean_velocity, log_scale, noise, p, q, observed[0])
-    buf = pltpu.VMEM((NX + 2 * W, 48, NZ), f32)
-    slabs, keep = [], {}
-    for n in range(STEPS):
-        ml, mr = shift(xhi, "gx", 1), shift(xlo, "gx", -1)
-        md, mu = shift(yhi, "gy", 1, True), shift(ylo, "gy", -1, True)
-        extra = ()
-        if n == 1:
-            extra = (keep["cext"],)
-        if n == 2:
-            extra = (keep["lap1"],)
-        if n == 3:
-            extra = (keep["lap0"], keep["q3"], keep["img"], vel, noise)
-        outs = [sds(NY, NZ), sds(16, 128), F, F]
-        if n < 3:
-            rows = (320, 288, 256)[n]
-            outs += [sds(rows, 128), sds(rows, 128), sds(72, 128), sds(72, 128)]
-        outs += {0: [F, sds(64, 128)], 1: [F], 2: [F], 3: [sds(NY, NZ), sds(16, NZ), sds(16, NZ), F, F]}[n]
-        res = call(functools.partial(step_kernel, n), tuple(outs), (buf, buf), smem=3)(
-            source_column, start_step, wavelet, coef, p, p_prev, q, q_later, ml, mr, md, mu, oc, *extra
-        )
-        lpk, oc, q_next, p_next = res[:4]
-        slabs.append(lpk)
-        if n < 3:
-            xlo, xhi, ylo, yhi = res[4:8]
-        if n == 0:
-            keep["lap0"], keep["cext"], keep["q3"], keep["p1"] = res[8], res[9], q_next, p_next
-        if n == 1:
-            keep["lap1"] = res[8]
-            keep["c"] = [ml, mr]
-        if n == 2:
-            keep["img"] = res[8]
-            keep["c"] += [ml, mr]
-        if n == 3:
-            mat, mat_lo, mat_hi, own, sent = res[4:9]
-        p_prev, p = p, p_next
-        q_later, q = q, q_next
-
-    mat_d, mat_u = shift(mat_hi, "gy", 1), shift(mat_lo, "gy", -1)
+    )(mean_velocity, log_scale, noise, p, q, p_prev, q_later, observed[0])
+    buf = pltpu.VMEM((NX + 2 * W, 64, NZ), f32)
+    ext = pltpu.VMEM((NX, NY + 16, NZ), f32)
+    own_block = pltpu.VMEM((NX, NY, NZ), f32)
+    scalars = (source_column, start_step, wavelet)
+
+    def to_y(lo, hi):
+        return shift(hi, "gy", 1, True), shift(lo, "gy", -1, True)
+
+    def to_x(lo, hi):
+        return shift(hi, "gx", 1), shift(lo, "gx", -1)
+
+    def join(xlo, xhi, md, mu):
+        out = sds(xlo.shape[0] + 64, 128)
+        return call(join_kernel, (out, out))(xlo, xhi, md, mu)
+
+    step = lambda kernel, n, outs, scratch: call(
+        functools.partial(kernel, n), tuple(outs), scratch, smem=3
+    )
+    head = [sds(NY, NZ), sds(16, 128), sds(16, 128), E, E]
+
+    md, mu = to_y(ylo, yhi)
+    far = shift(ob, "gy", ngy // 2, True)
+    ml, mr = to_x(*join(xlo, xhi, md, mu))
+    lp0, oc, fwd, p1, q3, xlo, xhi, lap0, cext_f, cext = step(
+        even_kernel, 0, head + [sds(320, 128), sds(320, 128), F, E, sds(64, 128)],
+        (buf, buf, ext, ext, ext),
+    )(*scalars, coef, p, p_prev, q, q_later, ml, mr, md, mu, oc)
+
+    ml1, mr1 = to_x(xlo, xhi)
+    lp1, q2, p2, xlo, xhi, ylo, yhi, lap1 = step(
+        odd_kernel, 1,
+        [sds(NY, NZ), F, F, sds(288, 128), sds(288, 128), sds(200, 128), sds(200, 128), F],
+        (buf, buf),
+    )(*scalars, cext_f, p1, p, q3, q, ml1, mr1, fwd)
+
+    md, mu = to_y(ylo, yhi)
+    ml2, mr2 = to_x(*join(xlo, xhi, md, mu))
+    lp2, oc, fwd, p3, q1, xlo, xhi, img = step(
+        even_kernel, 2, head + [sds(256, 128), sds(256, 128), F], (buf, buf, ext)
+    )(*scalars, cext_f, p2, p1, q2, q3, ml2, mr2, md, mu, oc, lap1)
+
+    ml, mr = to_x(xlo, xhi)
+    lp3, mat, mat_lo, mat_hi, own, sent = step(
+        odd_kernel, 3, [sds(NY, NZ), sds(NY, NZ), sds(24, NZ), sds(24, NZ), F, F],
+        (buf, buf, own_block),
+    )(*scalars, cext_f, p3, p2, q1, q2, ml, mr, fwd, lap0, q3, img, vel, noise)
+
+    mat_d, mat_u = shift(mat_hi, "gy", 1, True), shift(mat_lo, "gy", -1, True)
     other = lax.ppermute(sent, "shot", [(i, i ^ 1) for i in range(nshot)])
     nrec = receiver_column.shape[1]
     bf = jnp.bfloat16
@@ -474,7 +560,7 @@
         [pltpu.VMEM((160, nrec), bf)],
         mib=16,
     )(receiver_column.reshape(-1, 128), vel, noise)
-    chunk = call(chunk_kernel, sds(ngx, 32, 128))(mat, mat_d, mat_u, keep["p1"], oc)
+    chunk = call(chunk_kernel, sds(ngx, 32, 128))(mat, mat_d, mat_u, far, p1, oc)
     got = lax.all_to_all(chunk, "gx", 0, 0)
     g5 = pltpu.VMEM((5, 64, 128), f32)
     g48 = pltpu.VMEM((5, 48, 128), f32)
@@ -483,7 +569,9 @@
         sds(NX * NY + 2 * NY, NZ),
         (pltpu.VMEM((480, nrec), bf), g5, g5, g48, g48, pltpu.VMEM((320, 512), f32)),
         mib=24,
-    )(got, keyx, hoty, count, keep["cext"], *keep["c"], *slabs, vpk, zpk, own, other)
+    )(
+        got, keyx, hoty, count, cext, ml1, mr1, ml2, mr2, lp0, lp1, lp2, lp3, vpk, zpk, own, other
+    )
     every = lax.all_gather(part, "shot", axis=0)
     return call(sum_kernel, (F, F))(every, log_scale)
 

time: 144 us -> 153 us (1.062)
  waiting for transfers between devices: 7.12 us -> 26.7 us
  starting transfers between devices: 86.7 us -> 75.3 us
  local copies, waits for them, and re-layouts: 5.83 us -> 7.66 us
    ppermute x18 -> x15, waiting for transfers between devices: 7.12 us -> 26.7 us  [shift(): lax.ppermute(x, axis, [(i, (i + k) % n) for i in range(n) if wrap or 0 <=...]
    ppermute x18 -> x15, starting transfers between devices: 63.7 us -> 55.4 us  [shift(): lax.ppermute(x, axis, [(i, (i + k) % n) for i in range(n) if wrap or 0 <=...]
    ppermute x1, starting transfers between devices: 12.1 us -> 8.98 us  [local(): other = lax.ppermute(sent, 'shot', [(i, i ^ 1) for i in range(nshot)])]
    unnamed x28 -> x32, local copies, waits for them, and re-layouts: 5.83 us -> 7.66 us
    pallas_call x9 -> x11, Pallas kernels: 25.5 us -> 24.5 us  [go(): pl.pallas_call(kernel, out_shape=outs, in_specs=[SM] * smem + [VM] * (len...]
  transfers between devices with their start and end apart: 20 -> 17, of which waited for: 5 -> 11; matrix products, arithmetic and copies ran while one was open for 0% -> 0% of each run, Pallas kernels for 6% -> 5%
where the time goes in v4:
time: 153 us; the launch traced here: 152 us
  starting transfers between devices  75.3 us (49%)
  waiting for transfers between devices  26.7 us (17%)
  Pallas kernels  24.5 us (16%)
  blocking collectives  15.5 us (10%)
  local copies, waits for them, and re-layouts  7.66 us (5%)
  between operations  2.18 us (1%)
    ppermute x15, starting transfers between devices, shift(): lax.ppermute(x, axis, [(i, (i + k) % n) for i in range(n) if wrap or 0 <=...  55.4 us
    ppermute x15, waiting for transfers between devices, shift(): lax.ppermute(x, axis, [(i, (i + k) % n) for i in range(n) if wrap or 0 <=...  26.7 us
    pallas_call x11, Pallas kernels, go(): pl.pallas_call(kernel, out_shape=outs, in_specs=[SM] * smem + [VM] * (len...  24.5 us
    all_gather x1, blocking collectives, local(): every = lax.all_gather(part, 'shot', axis=0)  15.5 us
    all_to_all x1, starting transfers between devices, local(): got = lax.all_to_all(chunk, 'gx', 0, 0)  10.9 us
    ppermute x1, starting transfers between devices, local(): other = lax.ppermute(sent, 'shot', [(i, i ^ 1) for i in range(nshot)])  8.98 us
    unnamed x32, local copies, waits for them, and re-layouts  7.66 us
  transfers between devices with their start and end apart: 17, of which 11 were waited for; matrix products, arithmetic and copies ran while one was open for 0% of the time, Pallas kernels for 5%

profile of v4, /device:TPU:53, one launch (start us, length us, event | category | flops | bytes accessed | tf_op | source)
XLA Modules:
  0.0 151.9 jit_solution(6829215971468009400)
XLA Ops:
  7.8 4.0 %collective-permute-start = (f32[280,128]{1,0:T(8,128)S(1)}, f32[280,128]{1,0:T(8,128)S(1)}, u32[]{:S(2)}, u32[]{:S(2)}) collective-permute-start(f32[280,128]{1,0:T(8,128)S(1)} %get-tuple-element.54), channel_id=1, source_target_pairs={{0,1},{1,2},{2,3},{3,4},{4,5},{5,6},{6,7},{7,0},{8,9},{9,10},{10,1... | collective-permute-start | bytes 430088 | tf_op jit(solution)/shard_map/ppermute | solution.py:470
  11.8 8.6 %collective-permute-start.1 = (f32[280,128]{1,0:T(8,128)S(1)}, f32[280,128]{1,0:T(8,128)S(1)}, u32[]{:S(2)}, u32[]{:S(2)}) collective-permute-start(f32[280,128]{1,0:T(8,128)S(1)} %get-tuple-element.55), channel_id=1, source_target_pairs={{0,7},{1,0},{2,1},{3,2},{4,3},{5,4},{6,5},{7,6},{8,15},{9,8},{10,9... | collective-permute-start | bytes 430088 | tf_op jit(solution)/shard_map/ppermute | solution.py:470
  22.8 2.4 %collective-permute-start.2 = (f32[320,128]{1,0:T(8,128)S(1)}, f32[320,128]{1,0:T(8,128)S(1)}, u32[]{:S(2)}, u32[]{:S(2)}) collective-permute-start(f32[320,128]{1,0:T(8,128)S(1)} %get-tuple-element.56), channel_id=1, source_target_pairs={{0,8},{8,16},{16,24},{24,32},{32,40},{40,48},{48,56},{56,64},{64,7... | collective-permute-start | bytes 491528 | tf_op jit(solution)/shard_map/ppermute | solution.py:470
  25.3 3.0 %collective-permute-start.3 = (f32[320,128]{1,0:T(8,128)S(1)}, f32[320,128]{1,0:T(8,128)S(1)}, u32[]{:S(2)}, u32[]{:S(2)}) collective-permute-start(f32[320,128]{1,0:T(8,128)S(1)} %get-tuple-element.57), channel_id=1, source_target_pairs={{8,0},{16,8},{24,16},{32,24},{40,32},{48,40},{56,48},{64,56},{72,6... | collective-permute-start | bytes 491528 | tf_op jit(solution)/shard_map/ppermute | solution.py:470
  29.6 5.7 %collective-permute-done.3.mr = f32[320,128]{1,0:T(8,128)S(1)} collective-permute-done((f32[320,128]{1,0:T(8,128)S(1)}, f32[320,128]{1,0:T(8,128)S(1)}, u32[]{:S(2)}, u32[]{:S(2)}) %collective-permute-start.3) | collective-permute-done | bytes 163872 | tf_op jit(solution)/shard_map/ppermute | solution.py:470
  36.0 2.1 %shard_map.133 = (f32[32,128]{1,0:T(8,128)S(1)}, f32[16,128]{1,0:T(8,128)S(1)}, f32[16,128]{1,0:T(8,128)S(1)}, f32[8,48,128]{2,1,0:T(8,128)S(1)}, f32[8,48,128]{...) custom-call(s32[1]{0:T(128)S(6)} %copy.14.source, ...), custom_call_target="tpu_custom_call" | custom-call | tf_op jit(solution)/shard_map/pallas_call | solution.py:456
  38.0 3.9 %collective-permute-start.4 = (f32[320,128]{1,0:T(8,128)S(1)}, f32[320,128]{1,0:T(8,128)S(1)}, u32[]{:S(2)}, u32[]{:S(2)}) collective-permute-start(f32[320,128]{1,0:T(8,128)S(1)} %get-tuple-element.62), channel_id=1, source_target_pairs={{0,8},{8,16},{16,24},{24,32},{32,40},{40,48},{48,56},{56,64},{64,7... | collective-permute-start | bytes 491528 | tf_op jit(solution)/shard_map/ppermute | solution.py:470
  41.9 2.1 %collective-permute-start.5 = (f32[320,128]{1,0:T(8,128)S(1)}, f32[320,128]{1,0:T(8,128)S(1)}, u32[]{:S(2)}, u32[]{:S(2)}) collective-permute-start(f32[320,128]{1,0:T(8,128)S(1)} %get-tuple-element.63), channel_id=1, source_target_pairs={{8,0},{16,8},{24,16},{32,24},{40,32},{48,40},{56,48},{64,56},{72,6... | collective-permute-start | bytes 491528 | tf_op jit(solution)/shard_map/ppermute | solution.py:470
  44.8 4.8 %collective-permute-done.5.mr.mr1 = f32[320,128]{1,0:T(8,128)S(1)} collective-permute-done((f32[320,128]{1,0:T(8,128)S(1)}, f32[320,128]{1,0:T(8,128)S(1)}, u32[]{:S(2)}, u32[]{:S(2)}) %collective-permute-start.5) | collective-permute-done | bytes 163872 | tf_op jit(solution)/shard_map/ppermute | solution.py:470
  53.2 5.3 %collective-permute-start.7 = (f32[200,128]{1,0:T(8,128)S(1)}, f32[200,128]{1,0:T(8,128)S(1)}, u32[]{:S(2)}, u32[]{:S(2)}) collective-permute-start(f32[200,128]{1,0:T(8,128)S(1)} %get-tuple-element.70), channel_id=1, source_target_pairs={{0,7},{1,0},{2,1},{3,2},{4,3},{5,4},{6,5},{7,6},{8,15},{9,8},{10,9... | collective-permute-start | bytes 307208 | tf_op jit(solution)/shard_map/ppermute | solution.py:470
  60.2 3.0 %collective-permute-start.8 = (f32[352,128]{1,0:T(8,128)S(1)}, f32[352,128]{1,0:T(8,128)S(1)}, u32[]{:S(2)}, u32[]{:S(2)}) collective-permute-start(f32[352,128]{1,0:T(8,128)S(1)} %get-tuple-element.71), channel_id=1, source_target_pairs={{0,8},{8,16},{16,24},{24,32},{32,40},{40,48},{48,56},{56,64},{64,7... | collective-permute-start | bytes 540680 | tf_op jit(solution)/shard_map/ppermute | solution.py:470
  63.2 2.3 %collective-permute-start.9 = (f32[352,128]{1,0:T(8,128)S(1)}, f32[352,128]{1,0:T(8,128)S(1)}, u32[]{:S(2)}, u32[]{:S(2)}) collective-permute-start(f32[352,128]{1,0:T(8,128)S(1)} %get-tuple-element.72), channel_id=1, source_target_pairs={{8,0},{16,8},{24,16},{32,24},{40,32},{48,40},{56,48},{64,56},{72,6... | collective-permute-start | bytes 540680 | tf_op jit(solution)/shard_map/ppermute | solution.py:470
  66.4 3.3 %collective-permute-done.9.mr.mr2 = f32[352,128]{1,0:T(8,128)S(1)} collective-permute-done((f32[352,128]{1,0:T(8,128)S(1)}, f32[352,128]{1,0:T(8,128)S(1)}, u32[]{:S(2)}, u32[]{:S(2)}) %collective-permute-start.9) | collective-permute-done | bytes 180256 | tf_op jit(solution)/shard_map/ppermute | solution.py:470
  71.7 4.8 %collective-permute-start.10 = (f32[256,128]{1,0:T(8,128)S(1)}, f32[256,128]{1,0:T(8,128)S(1)}, u32[]{:S(2)}, u32[]{:S(2)}) collective-permute-start(f32[256,128]{1,0:T(8,128)S(1)} %get-tuple-element.77), channel_id=1, source_target_pairs={{0,8},{8,16},{16,24},{24,32},{32,40},{40,48},{48,56},{56,64},{64,7... | collective-permute-start | bytes 393224 | tf_op jit(solution)/shard_map/ppermute | solution.py:470
  78.5 3.8 %collective-permute-done.11.mr = f32[256,128]{1,0:T(8,128)S(1)} collective-permute-done((f32[256,128]{1,0:T(8,128)S(1)}, f32[256,128]{1,0:T(8,128)S(1)}, u32[]{:S(2)}, u32[]{:S(2)}) %collective-permute-start.11) | collective-permute-done | bytes 131104 | tf_op jit(solution)/shard_map/ppermute | solution.py:470
  84.1 3.5 %collective-permute-start.12 = (f32[24,128]{1,0:T(8,128)S(1)}, f32[24,128]{1,0:T(8,128)S(1)}, u32[]{:S(2)}, u32[]{:S(2)}) collective-permute-start(f32[24,128]{1,0:T(8,128)S(1)} %get-tuple-element.84), channel_id=1, source_target_pairs={{0,1},{1,2},{2,3},{3,4},{4,5},{5,6},{6,7},{7,0},{8,9},{9,10},{10,1... | collective-permute-start | bytes 36872 | tf_op jit(solution)/shard_map/ppermute | solution.py:470
  87.7 3.7 %collective-permute-start.13 = (f32[24,128]{1,0:T(8,128)S(1)}, f32[24,128]{1,0:T(8,128)S(1)}, u32[]{:S(2)}, u32[]{:S(2)}) collective-permute-start(f32[24,128]{1,0:T(8,128)S(1)} %get-tuple-element.85), channel_id=1, source_target_pairs={{0,7},{1,0},{2,1},{3,2},{4,3},{5,4},{6,5},{7,6},{8,15},{9,8},{10,9... | collective-permute-start | bytes 36872 | tf_op jit(solution)/shard_map/ppermute | solution.py:470
  91.3 4.9 %collective-permute-start.14 = (f32[8,128]{1,0:T(8,128)S(1)}, f32[8,128]{1,0:T(8,128)S(1)}, u32[]{:S(2)}, u32[]{:S(2)}) collective-permute-start(f32[8,128]{1,0:T(8,128)S(1)} %get-tuple-element.86), channel_id=1, source_target_pairs={{0,4},{1,5},{2,6},{3,7},{4,0},{5,1},{6,2},{7,3},{8,12},{9,13},{10,... | collective-permute-start | bytes 12296 | tf_op jit(solution)/shard_map/ppermute | solution.py:470
  96.3 3.3 %collective-permute-done.14.far = f32[8,128]{1,0:T(8,128)S(1)} collective-permute-done((f32[8,128]{1,0:T(8,128)S(1)}, f32[8,128]{1,0:T(8,128)S(1)}, u32[]{:S(2)}, u32[]{:S(2)}) %collective-permute-start.14) | collective-permute-done | bytes 4128 | tf_op jit(solution)/shard_map/ppermute | solution.py:470
  100.5 10.9 %all-to-all-start = ((f32[16,32,128]{2,1,0:T(8,128)}), f32[16,32,128]{2,1,0:T(8,128)S(1)}, u32[]{:S(2)}, u32[]{:S(2)}) async-start(f32[16,32,128]{2,1,0:T(8,128)} %shard_map.138), calls=%async_computation | async-start | bytes 524288 | tf_op jit(solution)/shard_map/all_to_all | solution.py:564
  111.4 9.0 %collective-permute-start.15 = (f32[8,32,128]{2,1,0:T(8,128)S(1)}, f32[8,32,128]{2,1,0:T(8,128)S(1)}, u32[]{:S(2)}, u32[]{:S(2)}) collective-permute-start(f32[8,32,128]{2,1,0:T(8,128)S(1)} %get-tuple-element.99), channel_id=1, source_target_pairs={{0,128},{128,0},{256,384},{384,256},{1,129},{129,1},{257,385},{385... | collective-permute-start | bytes 393224 | tf_op jit(solution)/shard_map/ppermute | solution.py:548
  120.4 7.8 %shard_map.139 = (s32[64,128]{1,0:T(8,128)S(1)}, bf16[64,8192]{1,0:T(8,128)(2,1)S(1)}, f32[160,64]{1,0:T(8,128)S(1)}, f32[32,128]{1,0:T(8,128)S(1)}, f32[32,128]{1,0:T(8,128)S(1)}) custom-call(s32[64,128]{1,0:T(8,128)S(1)} %bitcast.22, f32[8,32,128]{2,1,0:T(8,128)S(1)} %get-tuple-element.82.rest_3_.vel, f32[8,32,128]{2,1,0:T(8,128)S(1)} %bitcast.17), custom_call_target="tpu_custom_call" | custom-call | tf_op jit(solution)/shard_map/pallas_call | solution.py:456
  128.2 7.4 %shard_map.140 = f32[320,128]{1,0:T(8,128)S(1)} custom-call(f32[16,32,128]{2,1,0:T(8,128)S(1)} %all-to-all-done.got, s32[64,128]{1,0:T(8,128)S(1)} %get-tuple-element.88.keyx, bf16[64,8192]{1,0:T(8,128)(2,1)S(1)} %get-tuple-element.89.hoty, f32[160,64]{1,0:T(8,128)S(1)} %get-tuple-element.90.cnt, f32[64,128]{1,0:T(8,128)S(1)} %get-tuple-element.91.cext, ...), custom_call_target="tpu_custom_call" | custom-call | tf_op jit(solution)/shard_map/pallas_call | solution.py:456
  135.6 15.5 %all-gather = f32[1280,128]{1,0:T(8,128)S(1)} all-gather(f32[320,128]{1,0:T(8,128)S(1)} %shard_map.140), channel_id=2, replica_groups=mesh['shot'=4,'gx'=16,'gy'=8] {'shot'}, dimensions={0}, use_global_device_ids=true | all-gather | bytes 819200 | tf_op jit(solution)/shard_map/all_gather | solution.py:575
  (54 shorter events, 24.6 us)
Async XLA Ops:
  7.8 14.1 %collective-permute-start = (f32[280,128]{1,0:T(8,128)S(1)}, f32[280,128]{1,0:T(8,128)S(1)}, u32[]{:S(2)}, u32[]{:S(2)}) collective-permute-start(f32[280,128]{1,0:T(8,128)S(1)} %get-tuple-element.54), channel_id=1, source_target_pairs={{0,1},{1,2},{2,3},{3,4},{4,5},{5,6},{6,7},{7,0},{8,9},{9,10},{10,1... | collective-permute-start | bytes 430088 | tf_op jit(solution)/shard_map/ppermute | solution.py:470
  11.8 11.0 %collective-permute-start.1 = (f32[280,128]{1,0:T(8,128)S(1)}, f32[280,128]{1,0:T(8,128)S(1)}, u32[]{:S(2)}, u32[]{:S(2)}) collective-permute-start(f32[280,128]{1,0:T(8,128)S(1)} %get-tuple-element.55), channel_id=1, source_target_pairs={{0,7},{1,0},{2,1},{3,2},{4,3},{5,4},{6,5},{7,6},{8,15},{9,8},{10,9... | collective-permute-start | bytes 430088 | tf_op jit(solution)/shard_map/ppermute | solution.py:470
  22.8 12.5 %copy-start.1 = (f32[1,8,32,128]{3,2,1,0:T(8,128)S(1)}, f32[1,8,32,128]{3,2,1,0:T(8,128)}, u32[]{:S(2)}) copy-start(f32[1,8,32,128]{3,2,1,0:T(8,128)} %param.16) | copy-start | bytes 393220
  22.8 12.5 %copy-start.3 = (f32[1,8,32,128]{3,2,1,0:T(8,128)S(1)}, f32[1,8,32,128]{3,2,1,0:T(8,128)}, u32[]{:S(2)}) copy-start(f32[1,8,32,128]{3,2,1,0:T(8,128)} %param.18) | copy-start | bytes 393220
  22.8 12.5 %copy-start.9 = (f32[1,8,32,128]{3,2,1,0:T(8,128)S(1)}, f32[1,8,32,128]{3,2,1,0:T(8,128)}, u32[]{:S(2)}) copy-start(f32[1,8,32,128]{3,2,1,0:T(8,128)} %param.15) | copy-start | bytes 393220
  22.8 12.5 %copy-start.11 = (f32[1,8,32,128]{3,2,1,0:T(8,128)S(1)}, f32[1,8,32,128]{3,2,1,0:T(8,128)}, u32[]{:S(2)}) copy-start(f32[1,8,32,128]{3,2,1,0:T(8,128)} %param.17) | copy-start | bytes 393220
  22.8 6.7 %collective-permute-start.2 = (f32[320,128]{1,0:T(8,128)S(1)}, f32[320,128]{1,0:T(8,128)S(1)}, u32[]{:S(2)}, u32[]{:S(2)}) collective-permute-start(f32[320,128]{1,0:T(8,128)S(1)} %get-tuple-element.56), channel_id=1, source_target_pairs={{0,8},{8,16},{16,24},{24,32},{32,40},{40,48},{48,56},{56,64},{64,7... | collective-permute-start | bytes 491528 | tf_op jit(solution)/shard_map/ppermute | solution.py:470
  25.3 10.0 %collective-permute-start.3 = (f32[320,128]{1,0:T(8,128)S(1)}, f32[320,128]{1,0:T(8,128)S(1)}, u32[]{:S(2)}, u32[]{:S(2)}) collective-permute-start(f32[320,128]{1,0:T(8,128)S(1)} %get-tuple-element.57), channel_id=1, source_target_pairs={{8,0},{16,8},{24,16},{32,24},{40,32},{48,40},{56,48},{64,56},{72,6... | collective-permute-start | bytes 491528 | tf_op jit(solution)/shard_map/ppermute | solution.py:470
  38.0 6.8 %collective-permute-start.4 = (f32[320,128]{1,0:T(8,128)S(1)}, f32[320,128]{1,0:T(8,128)S(1)}, u32[]{:S(2)}, u32[]{:S(2)}) collective-permute-start(f32[320,128]{1,0:T(8,128)S(1)} %get-tuple-element.62), channel_id=1, source_target_pairs={{0,8},{8,16},{16,24},{24,32},{32,40},{40,48},{48,56},{56,64},{64,7... | collective-permute-start | bytes 491528 | tf_op jit(solution)/shard_map/ppermute | solution.py:470
  41.9 7.7 %collective-permute-start.5 = (f32[320,128]{1,0:T(8,128)S(1)}, f32[320,128]{1,0:T(8,128)S(1)}, u32[]{:S(2)}, u32[]{:S(2)}) collective-permute-start(f32[320,128]{1,0:T(8,128)S(1)} %get-tuple-element.63), channel_id=1, source_target_pairs={{8,0},{16,8},{24,16},{32,24},{40,32},{48,40},{56,48},{64,56},{72,6... | collective-permute-start | bytes 491528 | tf_op jit(solution)/shard_map/ppermute | solution.py:470
  51.3 7.4 %collective-permute-start.6 = (f32[200,128]{1,0:T(8,128)S(1)}, f32[200,128]{1,0:T(8,128)S(1)}, u32[]{:S(2)}, u32[]{:S(2)}) collective-permute-start(f32[200,128]{1,0:T(8,128)S(1)} %get-tuple-element.69), channel_id=1, source_target_pairs={{0,1},{1,2},{2,3},{3,4},{4,5},{5,6},{6,7},{7,0},{8,9},{9,10},{10,1... | collective-permute-start | bytes 307208 | tf_op jit(solution)/shard_map/ppermute | solution.py:470
  53.2 7.0 %collective-permute-start.7 = (f32[200,128]{1,0:T(8,128)S(1)}, f32[200,128]{1,0:T(8,128)S(1)}, u32[]{:S(2)}, u32[]{:S(2)}) collective-permute-start(f32[200,128]{1,0:T(8,128)S(1)} %get-tuple-element.70), channel_id=1, source_target_pairs={{0,7},{1,0},{2,1},{3,2},{4,3},{5,4},{6,5},{7,6},{8,15},{9,8},{10,9... | collective-permute-start | bytes 307208 | tf_op jit(solution)/shard_map/ppermute | solution.py:470
  60.2 6.2 %collective-permute-start.8 = (f32[352,128]{1,0:T(8,128)S(1)}, f32[352,128]{1,0:T(8,128)S(1)}, u32[]{:S(2)}, u32[]{:S(2)}) collective-permute-start(f32[352,128]{1,0:T(8,128)S(1)} %get-tuple-element.71), channel_id=1, source_target_pairs={{0,8},{8,16},{16,24},{24,32},{32,40},{40,48},{48,56},{56,64},{64,7... | collective-permute-start | bytes 540680 | tf_op jit(solution)/shard_map/ppermute | solution.py:470
  63.2 6.5 %collective-permute-start.9 = (f32[352,128]{1,0:T(8,128)S(1)}, f32[352,128]{1,0:T(8,128)S(1)}, u32[]{:S(2)}, u32[]{:S(2)}) collective-permute-start(f32[352,128]{1,0:T(8,128)S(1)} %get-tuple-element.72), channel_id=1, source_target_pairs={{8,0},{16,8},{24,16},{32,24},{40,32},{48,40},{56,48},{64,56},{72,6... | collective-permute-start | bytes 540680 | tf_op jit(solution)/shard_map/ppermute | solution.py:470
  69.8 12.5 %copy-start.5 = (f32[1,8,32,128]{3,2,1,0:T(8,128)S(1)}, f32[1,8,32,128]{3,2,1,0:T(8,128)}, u32[]{:S(2)}) copy-start(f32[1,8,32,128]{3,2,1,0:T(8,128)} %param.14) | copy-start | bytes 393220
  71.7 6.8 %collective-permute-start.10 = (f32[256,128]{1,0:T(8,128)S(1)}, f32[256,128]{1,0:T(8,128)S(1)}, u32[]{:S(2)}, u32[]{:S(2)}) collective-permute-start(f32[256,128]{1,0:T(8,128)S(1)} %get-tuple-element.77), channel_id=1, source_target_pairs={{0,8},{8,16},{16,24},{24,32},{32,40},{40,48},{48,56},{56,64},{64,7... | collective-permute-start | bytes 393224 | tf_op jit(solution)/shard_map/ppermute | solution.py:470
  76.6 5.7 %collective-permute-start.11 = (f32[256,128]{1,0:T(8,128)S(1)}, f32[256,128]{1,0:T(8,128)S(1)}, u32[]{:S(2)}, u32[]{:S(2)}) collective-permute-start(f32[256,128]{1,0:T(8,128)S(1)} %get-tuple-element.78), channel_id=1, source_target_pairs={{8,0},{16,8},{24,16},{32,24},{40,32},{48,40},{56,48},{64,56},{72,6... | collective-permute-start | bytes 393224 | tf_op jit(solution)/shard_map/ppermute | solution.py:470
  84.1 15.5 %collective-permute-start.12 = (f32[24,128]{1,0:T(8,128)S(1)}, f32[24,128]{1,0:T(8,128)S(1)}, u32[]{:S(2)}, u32[]{:S(2)}) collective-permute-start(f32[24,128]{1,0:T(8,128)S(1)} %get-tuple-element.84), channel_id=1, source_target_pairs={{0,1},{1,2},{2,3},{3,4},{4,5},{5,6},{6,7},{7,0},{8,9},{9,10},{10,1... | collective-permute-start | bytes 36872 | tf_op jit(solution)/shard_map/ppermute | solution.py:470
  87.7 11.9 %collective-permute-start.13 = (f32[24,128]{1,0:T(8,128)S(1)}, f32[24,128]{1,0:T(8,128)S(1)}, u32[]{:S(2)}, u32[]{:S(2)}) collective-permute-start(f32[24,128]{1,0:T(8,128)S(1)} %get-tuple-element.85), channel_id=1, source_target_pairs={{0,7},{1,0},{2,1},{3,2},{4,3},{5,4},{6,5},{7,6},{8,15},{9,8},{10,9... | collective-permute-start | bytes 36872 | tf_op jit(solution)/shard_map/ppermute | solution.py:470
  91.3 8.3 %collective-permute-start.14 = (f32[8,128]{1,0:T(8,128)S(1)}, f32[8,128]{1,0:T(8,128)S(1)}, u32[]{:S(2)}, u32[]{:S(2)}) collective-permute-start(f32[8,128]{1,0:T(8,128)S(1)} %get-tuple-element.86), channel_id=1, source_target_pairs={{0,4},{1,5},{2,6},{3,7},{4,0},{5,1},{6,2},{7,3},{8,12},{9,13},{10,... | collective-permute-start | bytes 12296 | tf_op jit(solution)/shard_map/ppermute | solution.py:470
  100.5 19.9 %copy-start.13 = (s32[1,8192]{1,0:T(1,128)S(1)}, s32[1,8192]{1,0:T(1,128)}, u32[]{:S(2)}) copy-start(s32[1,8192]{1,0:T(1,128)} %param.21) | copy-start | bytes 98308
  100.5 27.7 %all-to-all-start = ((f32[16,32,128]{2,1,0:T(8,128)}), f32[16,32,128]{2,1,0:T(8,128)S(1)}, u32[]{:S(2)}, u32[]{:S(2)}) async-start(f32[16,32,128]{2,1,0:T(8,128)} %shard_map.138), calls=%async_computation | async-start | bytes 524288 | tf_op jit(solution)/shard_map/all_to_all | solution.py:564
  111.4 16.8 %collective-permute-start.15 = (f32[8,32,128]{2,1,0:T(8,128)S(1)}, f32[8,32,128]{2,1,0:T(8,128)S(1)}, u32[]{:S(2)}, u32[]{:S(2)}) collective-permute-start(f32[8,32,128]{2,1,0:T(8,128)S(1)} %get-tuple-element.99), channel_id=1, source_target_pairs={{0,128},{128,0},{256,384},{384,256},{1,129},{129,1},{257,385},{385... | collective-permute-start | bytes 393224 | tf_op jit(solution)/shard_map/ppermute | solution.py:548
  135.6 15.5 %copy-start.7 = (f32[8,32,128]{2,1,0:T(8,128)S(1)}, f32[8,32,128]{2,1,0:T(8,128)}, u32[]{:S(2)}) copy-start(f32[8,32,128]{2,1,0:T(8,128)} %logs.3) | copy-start | bytes 393220
  (9 other events, 7.7 us)

commit v5 on v3

--- a/solution.py
+++ b/solution.py
@@ -55,24 +55,15 @@
     yhi[8 * i + 4 : 8 * i + 8] = s[NY - W :]
 
 
-def first_kernel(
-    mean, logs, noise, p, q, obs, c_out, v_out, xlo, xhi, ylo, yhi, cpk, oc
-):
+def first_kernel(c, s, p, obs, xlo, xhi, ylo, yhi, oc):
     oc[...] = jnp.zeros((16, 128), f32)
     oc[0:4, 0:64] = obs[...]
     for y in (ylo, yhi):
         y[80:88] = jnp.zeros((8, 128), f32)
         y[80:84, 0:64] = obs[...]
-    rows = []
-    for i in range(NX):
-        vel = mean[i] + jnp.exp(logs[i]) * noise[i]
-        c = courant_sq * vel * vel
-        v_out[i] = vel
-        c_out[i] = c
-        put_strips(i, p[i], c * q[i], xlo, xhi, ylo, yhi)
-        rows.append(c)
-    slab = pack(rows)
-    cpk[...] = slab
+    for i in range(NX):
+        put_strips(i, p[i], s[i], xlo, xhi, ylo, yhi)
+    slab = pack([c[i] for i in range(NX)])
     ylo[64:80] = slab[:16]
     yhi[64:80] = slab[16:]
 
@@ -224,39 +215,33 @@
     return out
 
 
-def table_kernel(rec, vel, noise, keyx, hoty, count, vpk, zpk, hot):
+def table_kernel(rec, vel, noise, keyx, hoty, vpk, zpk, cols, rows):
     ix, iy, ngy = lax.axis_index("gx"), lax.axis_index("gy"), lax.axis_size("gy")
     half = ngy // 2
+    bits = (NY * ngy).bit_length() - 1
+    assert 2**bits == NY * ngy
     odd = iy % 2 == 1
-    lane = lanes()
+    low = lanes() < 64
     bf = jnp.bfloat16
-    row4 = lax.broadcasted_iota(jnp.int32, (160, 128), 0) // 4
-    coly = lax.broadcasted_iota(jnp.int32, (64, 128), 0)
-
-    def build(g, carry):
-        at = pl.ds(pl.multiple_of(g * 128, 128), 128)
+    coly = lax.broadcasted_iota(jnp.int32, (64, 128), 0).astype(f32).astype(bf)
+    one, none = jnp.ones((), bf), jnp.zeros((), bf)
+    kx = jnp.clip((rec[...] >> bits) - ix * NX + 16, -1, 40).astype(f32)
+    ky = jnp.clip((rec[...] & (NY * ngy - 1)) - iy * NY + 16, -1, 64).astype(f32)
+    for ref, k in ((rows, kx), (cols, ky)):
+        ref[0] = jnp.where(odd, roll(k, 64), k)
+    for g in range(rec.shape[0]):
         first = (iy + 2 * (g % half)) % ngy
-        second = (first + 1) % ngy
-        row_a = rec[pl.ds((g // half) * half + first // 2, 1), :]
-        row_b = rec[pl.ds((g // half) * half + second // 2, 1), :]
-        row = jnp.where(odd, jnp.where(lane < 64, roll(row_a, 64), roll(row_b, 64)), row_a)
-        kx = row // (NY * ngy) - ix * NX + 16
-        ky = row % (NY * ngy) - iy * NY + 16
-        keyx[pl.ds(g, 1), :] = kx
-        hot[:, at] = jnp.where(row4 == kx, 1.0, 0.0).astype(bf)
-        hoty[:, at] = jnp.where(coly == ky, 1.0, 0.0).astype(bf)
-        return carry
-
-    lax.fori_loop(0, rec.shape[0], build, 0)
-    count[...] = lax.dot_general(
-        hot[...], hoty[...], (((1,), (1,)), ((), ())), preferred_element_type=f32
-    )
+        a = pl.ds((g // half) * half + first // 2, 1)
+        b = pl.ds((g // half) * half + ((first + 1) % ngy) // 2, 1)
+        keyx[g : g + 1] = jnp.where(low, rows[0, a, :], rows[0, b, :])
+        here = jnp.where(low, cols[0, a, :], cols[0, b, :]).astype(bf)
+        hoty[:, 128 * g : 128 * (g + 1)] = jnp.where(coly == here, one, none)
     vpk[...] = pack([vel[i] for i in range(NX)])
     zpk[...] = pack([noise[i] for i in range(NX)])
 
 
 def last_kernel(
-    got, keyx, hoty, cnt, cext, ml1, mr1, ml2, mr2, lp0, lp1, lp2, lp3, vpk, zpk, own, other,
+    got, keyx, hoty, cext, ml1, mr1, ml2, mr2, lp0, lp1, lp2, lp3, vpk, zpk, own, other,
     out, table, x, r3, r2, r1, inj,
 ):
     ngx = got.shape[0]
@@ -266,7 +251,7 @@
     c2l, c2r = ml2.at[256:288], mr2.at[256:288]
     bf = jnp.bfloat16
     row4 = (lax.broadcasted_iota(jnp.int32, (160, 128), 0) // 4).astype(f32).astype(bf)
-    none = jnp.zeros((), bf)
+    one, none = jnp.ones((), bf), jnp.zeros((), bf)
 
     def build(g, carry):
         for rp in range(4):
@@ -275,22 +260,22 @@
             hi = val.astype(bf).astype(f32)
             mid = (val - hi).astype(bf).astype(f32)
             low = val - hi - mid
-            kx = jnp.clip(keyx[pl.ds(4 * g + rp, 1), :], -1, 40).astype(f32).astype(bf)
-            here = row4 == kx
+            here = row4 == keyx[pl.ds(4 * g + rp, 1), :].astype(bf)
             for part, v in enumerate((hi, mid, low)):
                 v16 = jnp.concatenate([v, v, v, v], 0).astype(bf)
                 v160 = jnp.concatenate([v16] * 10, 0)
                 table[160 * part : 160 * (part + 1), at] = jnp.where(here, v160, none)
+            table[480:640, at] = jnp.where(here, one, none)
         return carry
 
-    lax.fori_loop(0, ngx, build, 0)
+    lax.fori_loop(0, ngx, build, 0, unroll=2)
     sums = lax.dot_general(
         table[...], hoty[...], (((1,), (1,)), ((), ())), preferred_element_type=f32
     )
     seen = sums[0:160] + sums[160:320] + sums[320:480]
     zero = jnp.zeros((96, 64), f32)
     seen = jnp.concatenate([seen, zero], 0)
-    count = jnp.concatenate([cnt[...], zero], 0)
+    count = jnp.concatenate([sums[480:640], zero], 0)
     both = jnp.concatenate([seen, count], 1)
     tr = [both[:128].T, both[128:].T]
 
@@ -414,13 +399,12 @@
     p_prev, p = checkpoint_prev[0], checkpoint_now[0]
     q_later, q = adjoint_next[0], adjoint_now[0]
     F = sds(NX, NY, NZ)
-    coef, vel, xlo, xhi, ylo, yhi, _, oc = call(
+    vel = mean_velocity + jnp.exp(log_scale) * noise
+    coef = courant_sq * vel * vel
+    xlo, xhi, ylo, yhi, oc = call(
         first_kernel,
-        (
-            F, F, sds(256, 128), sds(256, 128), sds(88, 128), sds(88, 128), sds(NY, NZ),
-            sds(16, 128),
-        ),
-    )(mean_velocity, log_scale, noise, p, q, observed[0])
+        (sds(256, 128), sds(256, 128), sds(88, 128), sds(88, 128), sds(16, 128)),
+    )(coef, coef * q, p, observed[0])
     buf = pltpu.VMEM((NX + 2 * W, 48, NZ), f32)
     slabs, keep = [], {}
     for n in range(STEPS):
@@ -462,17 +446,16 @@
     other = lax.ppermute(sent, "shot", [(i, i ^ 1) for i in range(nshot)])
     nrec = receiver_column.shape[1]
     bf = jnp.bfloat16
-    keyx, hoty, count, vpk, zpk = call(
+    keyx, hoty, vpk, zpk = call(
         table_kernel,
         (
-            jax.ShapeDtypeStruct((nrec // 128, 128), jnp.int32),
+            sds(nrec // 128, 128),
             jax.ShapeDtypeStruct((64, nrec), bf),
-            sds(160, 64),
             sds(NY, NZ),
             sds(NY, NZ),
         ),
-        [pltpu.VMEM((160, nrec), bf)],
-        mib=16,
+        [pltpu.VMEM((1, nrec // 128, 128), f32)] * 2,
+        mib=8,
     )(receiver_column.reshape(-1, 128), vel, noise)
     chunk = call(chunk_kernel, sds(ngx, 32, 128))(mat, mat_d, mat_u, keep["p1"], oc)
     got = lax.all_to_all(chunk, "gx", 0, 0)
@@ -481,9 +464,9 @@
     part = call(
         last_kernel,
         sds(NX * NY + 2 * NY, NZ),
-        (pltpu.VMEM((480, nrec), bf), g5, g5, g48, g48, pltpu.VMEM((320, 512), f32)),
+        (pltpu.VMEM((640, nrec), bf), g5, g5, g48, g48, pltpu.VMEM((320, 512), f32)),
         mib=24,
-    )(got, keyx, hoty, count, keep["cext"], *keep["c"], *slabs, vpk, zpk, own, other)
+    )(got, keyx, hoty, keep["cext"], *keep["c"], *slabs, vpk, zpk, own, other)
     every = lax.all_gather(part, "shot", axis=0)
     return call(sum_kernel, (F, F))(every, log_scale)
 

time: 144 us -> 139 us (0.965)
  the two profiles are of different devices: /device:TPU:53 before, /device:TPU:1 now
where the time goes in v5:
time: 139 us
  starting transfers between devices  85.8 us (62%)
  blocking collectives  21.6 us (16%)
  Pallas kernels  18.6 us (13%)
  waiting for transfers between devices  7.57 us (5%)
  between operations  2.26 us (2%)
  local copies, waits for them, and re-layouts  1.52 us (1%)
    ppermute x18, starting transfers between devices, shift(): lax.ppermute(x, axis, [(i, (i + k) % n) for i in range(n) if wrap or 0 <=...  57.9 us
    all_gather x1, blocking collectives, local(): every = lax.all_gather(part, 'shot', axis=0)  21.6 us
    pallas_call x9, Pallas kernels, go(): pl.pallas_call(kernel, out_shape=outs, in_specs=[SM] * smem + [VM] * (len...  18.6 us
    all_to_all x1, starting transfers between devices, local(): got = lax.all_to_all(chunk, 'gx', 0, 0)  16.1 us
    ppermute x1, starting transfers between devices, local(): other = lax.ppermute(sent, 'shot', [(i, i ^ 1) for i in range(nshot)])  11.9 us
    ppermute x18, waiting for transfers between devices, shift(): lax.ppermute(x, axis, [(i, (i + k) % n) for i in range(n) if wrap or 0 <=...  6.96 us
  transfers between devices with their start and end apart: 20, of which 5 were waited for; matrix products, arithmetic and copies ran while one was open for 0% of the time, Pallas kernels for 0%

profile of v5, /device:TPU:1, one launch (start us, length us, event | category | flops | bytes accessed | tf_op | source)
XLA Modules:
  0.0 138.5 jit_solution(11434587287055159027)
XLA Ops:
  2.8 4.2 %collective-permute-start = (f32[256,128]{1,0:T(8,128)S(1)}, f32[256,128]{1,0:T(8,128)S(1)}, u32[]{:S(2)}, u32[]{:S(2)}) collective-permute-start(f32[256,128]{1,0:T(8,128)S(1)} %get-tuple-element.46), channel_id=1, source_target_pairs={{0,8},{8,16},{16,24},{24,32},{32,40},{40,48},{48,56},{56,64},{64,7... | collective-permute-start | bytes 393224 | tf_op jit(solution)/shard_map/ppermute | solution.py:380
  8.3 4.0 %collective-permute-start.2 = (f32[88,128]{1,0:T(8,128)S(1)}, f32[88,128]{1,0:T(8,128)S(1)}, u32[]{:S(2)}, u32[]{:S(2)}) collective-permute-start(f32[88,128]{1,0:T(8,128)S(1)} %get-tuple-element.48), channel_id=1, source_target_pairs={{0,1},{1,2},{2,3},{3,4},{4,5},{5,6},{6,7},{7,0},{8,9},{9,10},{10,1... | collective-permute-start | bytes 135176 | tf_op jit(solution)/shard_map/ppermute | solution.py:380
  12.3 8.6 %collective-permute-start.3 = (f32[88,128]{1,0:T(8,128)S(1)}, f32[88,128]{1,0:T(8,128)S(1)}, u32[]{:S(2)}, u32[]{:S(2)}) collective-permute-start(f32[88,128]{1,0:T(8,128)S(1)} %get-tuple-element.49), channel_id=1, source_target_pairs={{0,7},{1,0},{2,1},{3,2},{4,3},{5,4},{6,5},{7,6},{8,15},{9,8},{10,9... | collective-permute-start | bytes 135176 | tf_op jit(solution)/shard_map/ppermute | solution.py:380
  22.9 1.7 %shard_map.132 = (f32[32,128]{1,0:T(8,128)S(1)}, f32[16,128]{1,0:T(8,128)S(1)}, f32[8,32,128]{2,1,0:T(8,128)S(1)}, f32[8,32,128]{2,1,0:T(8,128)S(1)}, f32[320,12...) custom-call(s32[1]{0:T(128)S(6)} %copy.14.source, ...), custom_call_target="tpu_custom_call" | custom-call | tf_op jit(solution)/shard_map/pallas_call | solution.py:366
  24.6 4.0 %collective-permute-start.4 = (f32[320,128]{1,0:T(8,128)S(1)}, f32[320,128]{1,0:T(8,128)S(1)}, u32[]{:S(2)}, u32[]{:S(2)}) collective-permute-start(f32[320,128]{1,0:T(8,128)S(1)} %get-tuple-element.53), channel_id=1, source_target_pairs={{0,8},{8,16},{16,24},{24,32},{32,40},{40,48},{48,56},{56,64},{64,7... | collective-permute-start | bytes 491528 | tf_op jit(solution)/shard_map/ppermute | solution.py:380
  29.9 1.9 %collective-permute-start.6 = (f32[72,128]{1,0:T(8,128)S(1)}, f32[72,128]{1,0:T(8,128)S(1)}, u32[]{:S(2)}, u32[]{:S(2)}) collective-permute-start(f32[72,128]{1,0:T(8,128)S(1)} %get-tuple-element.55), channel_id=1, source_target_pairs={{0,1},{1,2},{2,3},{3,4},{4,5},{5,6},{6,7},{7,0},{8,9},{9,10},{10,1... | collective-permute-start | bytes 110600 | tf_op jit(solution)/shard_map/ppermute | solution.py:380
  31.8 4.7 %collective-permute-start.7 = (f32[72,128]{1,0:T(8,128)S(1)}, f32[72,128]{1,0:T(8,128)S(1)}, u32[]{:S(2)}, u32[]{:S(2)}) collective-permute-start(f32[72,128]{1,0:T(8,128)S(1)} %get-tuple-element.56), channel_id=1, source_target_pairs={{0,7},{1,0},{2,1},{3,2},{4,3},{5,4},{6,5},{7,6},{8,15},{9,8},{10,9... | collective-permute-start | bytes 110600 | tf_op jit(solution)/shard_map/ppermute | solution.py:380
  37.5 1.6 %shard_map.133 = (f32[32,128]{1,0:T(8,128)S(1)}, f32[16,128]{1,0:T(8,128)S(1)}, f32[8,32,128]{2,1,0:T(8,128)S(1)}, f32[8,32,128]{2,1,0:T(8,128)S(1)}, f32[288,12...) custom-call(s32[1]{0:T(128)S(6)} %copy.14.source, ...), custom_call_target="tpu_custom_call" | custom-call | tf_op jit(solution)/shard_map/pallas_call | solution.py:366
  39.2 4.0 %collective-permute-start.8 = (f32[288,128]{1,0:T(8,128)S(1)}, f32[288,128]{1,0:T(8,128)S(1)}, u32[]{:S(2)}, u32[]{:S(2)}) collective-permute-start(f32[288,128]{1,0:T(8,128)S(1)} %get-tuple-element.61), channel_id=1, source_target_pairs={{0,8},{8,16},{16,24},{24,32},{32,40},{40,48},{48,56},{56,64},{64,7... | collective-permute-start | bytes 442376 | tf_op jit(solution)/shard_map/ppermute | solution.py:380
  44.5 3.0 %collective-permute-start.10 = (f32[72,128]{1,0:T(8,128)S(1)}, f32[72,128]{1,0:T(8,128)S(1)}, u32[]{:S(2)}, u32[]{:S(2)}) collective-permute-start(f32[72,128]{1,0:T(8,128)S(1)} %get-tuple-element.63), channel_id=1, source_target_pairs={{0,1},{1,2},{2,3},{3,4},{4,5},{5,6},{6,7},{7,0},{8,9},{9,10},{10,1... | collective-permute-start | bytes 110600 | tf_op jit(solution)/shard_map/ppermute | solution.py:380
  47.5 3.8 %collective-permute-start.11 = (f32[72,128]{1,0:T(8,128)S(1)}, f32[72,128]{1,0:T(8,128)S(1)}, u32[]{:S(2)}, u32[]{:S(2)}) collective-permute-start(f32[72,128]{1,0:T(8,128)S(1)} %get-tuple-element.64), channel_id=1, source_target_pairs={{0,7},{1,0},{2,1},{3,2},{4,3},{5,4},{6,5},{7,6},{8,15},{9,8},{10,9... | collective-permute-start | bytes 110600 | tf_op jit(solution)/shard_map/ppermute | solution.py:380
  51.3 1.4 %collective-permute-done.11.mu = f32[72,128]{1,0:T(8,128)S(1)} collective-permute-done((f32[72,128]{1,0:T(8,128)S(1)}, f32[72,128]{1,0:T(8,128)S(1)}, u32[]{:S(2)}, u32[]{:S(2)}) %collective-permute-start.11) | collective-permute-done | bytes 36896 | tf_op jit(solution)/shard_map/ppermute | solution.py:380
  52.7 1.7 %shard_map.134 = (f32[32,128]{1,0:T(8,128)S(1)}, f32[16,128]{1,0:T(8,128)S(1)}, f32[8,32,128]{2,1,0:T(8,128)S(1)}, f32[8,32,128]{2,1,0:T(8,128)S(1)}, f32[256,12...) custom-call(s32[1]{0:T(128)S(6)} %copy.14.source, ...), custom_call_target="tpu_custom_call" | custom-call | tf_op jit(solution)/shard_map/pallas_call | solution.py:366
  54.4 3.7 %collective-permute-start.12 = (f32[256,128]{1,0:T(8,128)S(1)}, f32[256,128]{1,0:T(8,128)S(1)}, u32[]{:S(2)}, u32[]{:S(2)}) collective-permute-start(f32[256,128]{1,0:T(8,128)S(1)} %get-tuple-element.69), channel_id=1, source_target_pairs={{0,8},{8,16},{16,24},{24,32},{32,40},{40,48},{48,56},{56,64},{64,7... | collective-permute-start | bytes 393224 | tf_op jit(solution)/shard_map/ppermute | solution.py:380
  59.4 3.4 %collective-permute-start.14 = (f32[72,128]{1,0:T(8,128)S(1)}, f32[72,128]{1,0:T(8,128)S(1)}, u32[]{:S(2)}, u32[]{:S(2)}) collective-permute-start(f32[72,128]{1,0:T(8,128)S(1)} %get-tuple-element.71), channel_id=1, source_target_pairs={{0,1},{1,2},{2,3},{3,4},{4,5},{5,6},{6,7},{7,0},{8,9},{9,10},{10,1... | collective-permute-start | bytes 110600 | tf_op jit(solution)/shard_map/ppermute | solution.py:380
  62.8 3.3 %collective-permute-start.15 = (f32[72,128]{1,0:T(8,128)S(1)}, f32[72,128]{1,0:T(8,128)S(1)}, u32[]{:S(2)}, u32[]{:S(2)}) collective-permute-start(f32[72,128]{1,0:T(8,128)S(1)} %get-tuple-element.72), channel_id=1, source_target_pairs={{0,7},{1,0},{2,1},{3,2},{4,3},{5,4},{6,5},{7,6},{8,15},{9,8},{10,9... | collective-permute-start | bytes 110600 | tf_op jit(solution)/shard_map/ppermute | solution.py:380
  66.1 1.4 collective-permute-done.15.mu
  67.5 2.4 %shard_map.135 = (f32[32,128]{1,0:T(8,128)S(1)}, f32[16,128]{1,0:T(8,128)S(1)}, f32[8,32,128]{2,1,0:T(8,128)}, f32[8,32,128]{2,1,0:T(8,128)}, f32[32,128]{1,0:T(...) custom-call(s32[1]{0:T(128)S(6)} %copy.14.source, ...), custom_call_target="tpu_custom_call" | custom-call | tf_op jit(solution)/shard_map/pallas_call | solution.py:366
  69.9 2.9 %collective-permute-start.16 = (f32[16,128]{1,0:T(8,128)S(1)}, f32[16,128]{1,0:T(8,128)S(1)}, u32[]{:S(2)}, u32[]{:S(2)}) collective-permute-start(f32[16,128]{1,0:T(8,128)S(1)} %get-tuple-element.77), channel_id=1, source_target_pairs={{0,1},{1,2},{2,3},{3,4},{4,5},{5,6},{6,7},{8,9},{9,10},{10,11},{11... | collective-permute-start | bytes 24584 | tf_op jit(solution)/shard_map/ppermute | solution.py:380
  74.2 3.1 %collective-permute-done.17.got_u = f32[16,128]{1,0:T(8,128)S(1)} collective-permute-done((f32[16,128]{1,0:T(8,128)S(1)}, f32[16,128]{1,0:T(8,128)S(1)}, u32[]{:S(2)}, u32[]{:S(2)}) %collective-permute-start.17) | collective-permute-done | bytes 8224 | tf_op jit(solution)/shard_map/ppermute | solution.py:380
  78.2 16.1 %all-to-all-start = ((f32[16,32,128]{2,1,0:T(8,128)}), f32[16,32,128]{2,1,0:T(8,128)S(1)}, u32[]{:S(2)}, u32[]{:S(2)}) async-start(f32[16,32,128]{2,1,0:T(8,128)} %shard_map.136), calls=%async_computation | async-start | bytes 524288 | tf_op jit(solution)/shard_map/all_to_all | solution.py:461
  94.3 11.9 %collective-permute-start.18 = (f32[8,32,128]{2,1,0:T(8,128)S(1)}, f32[8,32,128]{2,1,0:T(8,128)S(1)}, u32[]{:S(2)}, u32[]{:S(2)}) collective-permute-start(f32[8,32,128]{2,1,0:T(8,128)S(1)} %get-tuple-element.89), channel_id=1, source_target_pairs={{0,128},{128,0},{256,384},{384,256},{1,129},{129,1},{257,385},{385... | collective-permute-start | bytes 393224 | tf_op jit(solution)/shard_map/ppermute | solution.py:446
  107.1 9.0 %shard_map.138 = f32[320,128]{1,0:T(8,128)S(1)} custom-call(f32[16,32,128]{2,1,0:T(8,128)S(1)} %all-to-all-done.got, f32[64,128]{1,0:T(8,128)S(1)} %get-tuple-element.80.keyx, bf16[64,8192]{1,0:T(8,128)(2,1)S(1)} %get-tuple-element.81.hoty, f32[64,128]{1,0:T(8,128)S(1)} %get-tuple-element.58.rest_0_.cext, f32[320,128]{1,0:T(8,128)S(1)} %collective-permute-done.4.ml.ml1, ...), custom_call_target="tpu_custom_call" | custom-call | tf_op jit(solution)/shard_map/pallas_call | solution.py:366
  116.1 21.6 %all-gather = f32[1280,128]{1,0:T(8,128)S(1)} all-gather(f32[320,128]{1,0:T(8,128)S(1)} %shard_map.138), channel_id=2, replica_groups=mesh['shot'=4,'gx'=16,'gy'=8] {'shot'}, dimensions={0}, use_global_device_ids=true | all-gather | bytes 819200 | tf_op jit(solution)/shard_map/all_gather | solution.py:470
  (46 shorter events, 12.9 us)
Async XLA Ops:
  2.7 19.5 %copy-start.4 = (f32[1,8,32,128]{3,2,1,0:T(8,128)S(1)}, f32[1,8,32,128]{3,2,1,0:T(8,128)}, u32[]{:S(2)}) copy-start(f32[1,8,32,128]{3,2,1,0:T(8,128)} %param.15) | copy-start | bytes 393220
  2.7 19.6 %copy-start.5 = (f32[1,8,32,128]{3,2,1,0:T(8,128)S(1)}, f32[1,8,32,128]{3,2,1,0:T(8,128)}, u32[]{:S(2)}) copy-start(f32[1,8,32,128]{3,2,1,0:T(8,128)} %param.17) | copy-start | bytes 393220
  2.8 19.4 %collective-permute-start = (f32[256,128]{1,0:T(8,128)S(1)}, f32[256,128]{1,0:T(8,128)S(1)}, u32[]{:S(2)}, u32[]{:S(2)}) collective-permute-start(f32[256,128]{1,0:T(8,128)S(1)} %get-tuple-element.46), channel_id=1, source_target_pairs={{0,8},{8,16},{16,24},{24,32},{32,40},{40,48},{48,56},{56,64},{64,7... | collective-permute-start | bytes 393224 | tf_op jit(solution)/shard_map/ppermute | solution.py:380
  7.0 15.2 %collective-permute-start.1 = (f32[256,128]{1,0:T(8,128)S(1)}, f32[256,128]{1,0:T(8,128)S(1)}, u32[]{:S(2)}, u32[]{:S(2)}) collective-permute-start(f32[256,128]{1,0:T(8,128)S(1)} %get-tuple-element.47), channel_id=1, source_target_pairs={{8,0},{16,8},{24,16},{32,24},{40,32},{48,40},{56,48},{64,56},{72,6... | collective-permute-start | bytes 393224 | tf_op jit(solution)/shard_map/ppermute | solution.py:380
  8.3 13.9 %collective-permute-start.2 = (f32[88,128]{1,0:T(8,128)S(1)}, f32[88,128]{1,0:T(8,128)S(1)}, u32[]{:S(2)}, u32[]{:S(2)}) collective-permute-start(f32[88,128]{1,0:T(8,128)S(1)} %get-tuple-element.48), channel_id=1, source_target_pairs={{0,1},{1,2},{2,3},{3,4},{4,5},{5,6},{6,7},{7,0},{8,9},{9,10},{10,1... | collective-permute-start | bytes 135176 | tf_op jit(solution)/shard_map/ppermute | solution.py:380
  12.3 9.9 %collective-permute-start.3 = (f32[88,128]{1,0:T(8,128)S(1)}, f32[88,128]{1,0:T(8,128)S(1)}, u32[]{:S(2)}, u32[]{:S(2)}) collective-permute-start(f32[88,128]{1,0:T(8,128)S(1)} %get-tuple-element.49), channel_id=1, source_target_pairs={{0,7},{1,0},{2,1},{3,2},{4,3},{5,4},{6,5},{7,6},{8,15},{9,8},{10,9... | collective-permute-start | bytes 135176 | tf_op jit(solution)/shard_map/ppermute | solution.py:380
  24.6 12.9 %collective-permute-start.4 = (f32[320,128]{1,0:T(8,128)S(1)}, f32[320,128]{1,0:T(8,128)S(1)}, u32[]{:S(2)}, u32[]{:S(2)}) collective-permute-start(f32[320,128]{1,0:T(8,128)S(1)} %get-tuple-element.53), channel_id=1, source_target_pairs={{0,8},{8,16},{16,24},{24,32},{32,40},{40,48},{48,56},{56,64},{64,7... | collective-permute-start | bytes 491528 | tf_op jit(solution)/shard_map/ppermute | solution.py:380
  28.6 8.9 %collective-permute-start.5 = (f32[320,128]{1,0:T(8,128)S(1)}, f32[320,128]{1,0:T(8,128)S(1)}, u32[]{:S(2)}, u32[]{:S(2)}) collective-permute-start(f32[320,128]{1,0:T(8,128)S(1)} %get-tuple-element.54), channel_id=1, source_target_pairs={{8,0},{16,8},{24,16},{32,24},{40,32},{48,40},{56,48},{64,56},{72,6... | collective-permute-start | bytes 491528 | tf_op jit(solution)/shard_map/ppermute | solution.py:380
  29.9 6.6 %collective-permute-start.6 = (f32[72,128]{1,0:T(8,128)S(1)}, f32[72,128]{1,0:T(8,128)S(1)}, u32[]{:S(2)}, u32[]{:S(2)}) collective-permute-start(f32[72,128]{1,0:T(8,128)S(1)} %get-tuple-element.55), channel_id=1, source_target_pairs={{0,1},{1,2},{2,3},{3,4},{4,5},{5,6},{6,7},{7,0},{8,9},{9,10},{10,1... | collective-permute-start | bytes 110600 | tf_op jit(solution)/shard_map/ppermute | solution.py:380
  31.8 5.7 %collective-permute-start.7 = (f32[72,128]{1,0:T(8,128)S(1)}, f32[72,128]{1,0:T(8,128)S(1)}, u32[]{:S(2)}, u32[]{:S(2)}) collective-permute-start(f32[72,128]{1,0:T(8,128)S(1)} %get-tuple-element.56), channel_id=1, source_target_pairs={{0,7},{1,0},{2,1},{3,2},{4,3},{5,4},{6,5},{7,6},{8,15},{9,8},{10,9... | collective-permute-start | bytes 110600 | tf_op jit(solution)/shard_map/ppermute | solution.py:380
  39.2 13.6 %collective-permute-start.8 = (f32[288,128]{1,0:T(8,128)S(1)}, f32[288,128]{1,0:T(8,128)S(1)}, u32[]{:S(2)}, u32[]{:S(2)}) collective-permute-start(f32[288,128]{1,0:T(8,128)S(1)} %get-tuple-element.61), channel_id=1, source_target_pairs={{0,8},{8,16},{16,24},{24,32},{32,40},{40,48},{48,56},{56,64},{64,7... | collective-permute-start | bytes 442376 | tf_op jit(solution)/shard_map/ppermute | solution.py:380
  43.2 9.6 %collective-permute-start.9 = (f32[288,128]{1,0:T(8,128)S(1)}, f32[288,128]{1,0:T(8,128)S(1)}, u32[]{:S(2)}, u32[]{:S(2)}) collective-permute-start(f32[288,128]{1,0:T(8,128)S(1)} %get-tuple-element.62), channel_id=1, source_target_pairs={{8,0},{16,8},{24,16},{32,24},{40,32},{48,40},{56,48},{64,56},{72,6... | collective-permute-start | bytes 442376 | tf_op jit(solution)/shard_map/ppermute | solution.py:380
  44.5 6.8 %collective-permute-start.10 = (f32[72,128]{1,0:T(8,128)S(1)}, f32[72,128]{1,0:T(8,128)S(1)}, u32[]{:S(2)}, u32[]{:S(2)}) collective-permute-start(f32[72,128]{1,0:T(8,128)S(1)} %get-tuple-element.63), channel_id=1, source_target_pairs={{0,1},{1,2},{2,3},{3,4},{4,5},{5,6},{6,7},{7,0},{8,9},{9,10},{10,1... | collective-permute-start | bytes 110600 | tf_op jit(solution)/shard_map/ppermute | solution.py:380
  47.5 5.2 %collective-permute-start.11 = (f32[72,128]{1,0:T(8,128)S(1)}, f32[72,128]{1,0:T(8,128)S(1)}, u32[]{:S(2)}, u32[]{:S(2)}) collective-permute-start(f32[72,128]{1,0:T(8,128)S(1)} %get-tuple-element.64), channel_id=1, source_target_pairs={{0,7},{1,0},{2,1},{3,2},{4,3},{5,4},{6,5},{7,6},{8,15},{9,8},{10,9... | collective-permute-start | bytes 110600 | tf_op jit(solution)/shard_map/ppermute | solution.py:380
  54.4 13.1 %collective-permute-start.12 = (f32[256,128]{1,0:T(8,128)S(1)}, f32[256,128]{1,0:T(8,128)S(1)}, u32[]{:S(2)}, u32[]{:S(2)}) collective-permute-start(f32[256,128]{1,0:T(8,128)S(1)} %get-tuple-element.69), channel_id=1, source_target_pairs={{0,8},{8,16},{16,24},{24,32},{32,40},{40,48},{48,56},{56,64},{64,7... | collective-permute-start | bytes 393224 | tf_op jit(solution)/shard_map/ppermute | solution.py:380
  58.1 9.4 %collective-permute-start.13 = (f32[256,128]{1,0:T(8,128)S(1)}, f32[256,128]{1,0:T(8,128)S(1)}, u32[]{:S(2)}, u32[]{:S(2)}) collective-permute-start(f32[256,128]{1,0:T(8,128)S(1)} %get-tuple-element.70), channel_id=1, source_target_pairs={{8,0},{16,8},{24,16},{32,24},{40,32},{48,40},{56,48},{64,56},{72,6... | collective-permute-start | bytes 393224 | tf_op jit(solution)/shard_map/ppermute | solution.py:380
  59.4 6.7 %collective-permute-start.14 = (f32[72,128]{1,0:T(8,128)S(1)}, f32[72,128]{1,0:T(8,128)S(1)}, u32[]{:S(2)}, u32[]{:S(2)}) collective-permute-start(f32[72,128]{1,0:T(8,128)S(1)} %get-tuple-element.71), channel_id=1, source_target_pairs={{0,1},{1,2},{2,3},{3,4},{4,5},{5,6},{6,7},{7,0},{8,9},{9,10},{10,1... | collective-permute-start | bytes 110600 | tf_op jit(solution)/shard_map/ppermute | solution.py:380
  62.8 4.7 %collective-permute-start.15 = (f32[72,128]{1,0:T(8,128)S(1)}, f32[72,128]{1,0:T(8,128)S(1)}, u32[]{:S(2)}, u32[]{:S(2)}) collective-permute-start(f32[72,128]{1,0:T(8,128)S(1)} %get-tuple-element.72), channel_id=1, source_target_pairs={{0,7},{1,0},{2,1},{3,2},{4,3},{5,4},{6,5},{7,6},{8,15},{9,8},{10,9... | collective-permute-start | bytes 110600 | tf_op jit(solution)/shard_map/ppermute | solution.py:380
  69.9 4.2 %collective-permute-start.16 = (f32[16,128]{1,0:T(8,128)S(1)}, f32[16,128]{1,0:T(8,128)S(1)}, u32[]{:S(2)}, u32[]{:S(2)}) collective-permute-start(f32[16,128]{1,0:T(8,128)S(1)} %get-tuple-element.77), channel_id=1, source_target_pairs={{0,1},{1,2},{2,3},{3,4},{4,5},{5,6},{6,7},{8,9},{9,10},{10,11},{11... | collective-permute-start | bytes 24584 | tf_op jit(solution)/shard_map/ppermute | solution.py:380
  72.9 4.4 %collective-permute-start.17 = (f32[16,128]{1,0:T(8,128)S(1)}, f32[16,128]{1,0:T(8,128)S(1)}, u32[]{:S(2)}, u32[]{:S(2)}) collective-permute-start(f32[16,128]{1,0:T(8,128)S(1)} %get-tuple-element.78), channel_id=1, source_target_pairs={{1,0},{2,1},{3,2},{4,3},{5,4},{6,5},{7,6},{9,8},{10,9},{11,10},{12... | collective-permute-start | bytes 24584 | tf_op jit(solution)/shard_map/ppermute | solution.py:380
  78.2 28.0 %copy-start.6 = (s32[1,8192]{1,0:T(1,128)S(1)}, s32[1,8192]{1,0:T(1,128)}, u32[]{:S(2)}) copy-start(s32[1,8192]{1,0:T(1,128)} %param.21) | copy-start | bytes 98308
  78.2 29.0 %all-to-all-start = ((f32[16,32,128]{2,1,0:T(8,128)}), f32[16,32,128]{2,1,0:T(8,128)S(1)}, u32[]{:S(2)}, u32[]{:S(2)}) async-start(f32[16,32,128]{2,1,0:T(8,128)} %shard_map.136), calls=%async_computation | async-start | bytes 524288 | tf_op jit(solution)/shard_map/all_to_all | solution.py:461
  94.3 12.8 %collective-permute-start.18 = (f32[8,32,128]{2,1,0:T(8,128)S(1)}, f32[8,32,128]{2,1,0:T(8,128)S(1)}, u32[]{:S(2)}, u32[]{:S(2)}) collective-permute-start(f32[8,32,128]{2,1,0:T(8,128)S(1)} %get-tuple-element.89), channel_id=1, source_target_pairs={{0,128},{128,0},{256,384},{384,256},{1,129},{129,1},{257,385},{385... | collective-permute-start | bytes 393224 | tf_op jit(solution)/shard_map/ppermute | solution.py:446
  116.1 21.6 %copy-start.3 = (f32[8,32,128]{2,1,0:T(8,128)S(1)}, f32[8,32,128]{2,1,0:T(8,128)}, u32[]{:S(2)}) copy-start(f32[8,32,128]{2,1,0:T(8,128)} %logs.1) | copy-start | bytes 393220
  (5 other events, 36.8 us)

commit v6 on v5

--- a/solution.py
+++ b/solution.py
@@ -89,42 +89,56 @@
     return out
 
 
-def step_kernel(n, source, start, wavelet, c, p, pp, q, ql, ml, mr, md, mu, oc, *rest):
-    ix, iy, ngy = lax.axis_index("gx"), lax.axis_index("gy"), lax.axis_size("gy")
-    rest = list(rest)
-    bufp, bufs = rest[-2:]
-    rest = rest[:-2]
-    take = lambda: rest.pop(0)
-    if n == 1:
-        cext = take()
-    if n == 2:
-        lap_other = take()
-    if n == 3:
-        lap_other, q3, img, vel, noise = take(), take(), take(), take(), take()
-    lpk, oc_out, qn = take(), take(), take()
-    if n < 3:
-        pn, xlo, xhi, ylo, yhi = take(), take(), take(), take(), take()
-    else:
-        pn = take()
-    if n == 0:
-        lap_out, cext = take(), take()
-    if n == 1:
-        lap_out = take()
-    if n == 2:
-        img_out = take()
-    if n == 3:
-        mat, mat_lo, mat_hi, own, sent = take(), take(), take(), take(), take()
-
-    keep_d, keep_u = iy > 0, iy < ngy - 1
-    lane = lanes()
-    wz = [None] + [
+def depth_weights():
+    lane = lanes()
+    return [None] + [
         (jnp.where(lane < NZ - k, CK[k], 0.0), jnp.where(lane >= k, CK[k], 0.0))
         for k in range(1, W + 1)
     ]
 
-    def strip(m, at):
-        return [m[at + NY * j : at + NY * (j + 1)] for j in range(W)]
-
+
+def edges():
+    iy = lax.axis_index("gy")
+    return iy > 0, iy < lax.axis_size("gy") - 1
+
+
+def strip(m, at):
+    return [m[at + NY * j : at + NY * (j + 1)] for j in range(W)]
+
+
+def add_source(n, source, start, wavelet, field):
+    width = NY * lax.axis_size("gy")
+    sx = source[0] // width - lax.axis_index("gx") * NX
+    sy = source[0] % width - lax.axis_index("gy") * NY
+
+    @pl.when((sx >= 0) & (sx < NX) & (sy >= 0) & (sy < NY))
+    def _():
+        row = field[sx, pl.ds(sy, 1), :]
+        add = jnp.where(lanes() == SRC_DEPTH, wavelet[0, start[0] + n], 0.0)
+        field[sx, pl.ds(sy, 1), :] = row + add
+
+
+def collect(n, md, mu, oc, oc_out):
+    at = 80 if n == 0 else 64
+    got_d, got_u = md[at : at + 8], mu[at : at + 8]
+    oc_out[...] = oc[...]
+    up, turn_u, down, turn_d = ((0, 64, 12, 64), (4, 0, 12, 0), (4, 64, 8, 64), (8, 0, None, 0))[n]
+    oc_out[up : up + 4] = oc_out[up : up + 4] + roll(got_u, turn_u)[:4]
+    if down is not None:
+        oc_out[down : down + 4] = oc_out[down : down + 4] + roll(got_d, turn_d)[:4]
+    return got_d, got_u
+
+
+def step_kernel(n, source, start, wavelet, c, p, pp, q, ql, ml, mr, md, mu, oc, *rest):
+    if n == 0:
+        lpk, oc_out, qn, pn, xlo, xhi, ylo, yhi, lap_out, cext, bufp, bufs = rest
+    if n == 1:
+        cext, lpk, oc_out, qn, pn, xlo, xhi, ylo, yhi, lap_out, bufp, bufs = rest
+    if n == 2:
+        lap_other, lpk, oc_out, qn, pn, xlo, xhi, ylo, yhi, img_out, bufp, bufs = rest
+    keep_d, keep_u = edges()
+    lane = lanes()
+    wz = depth_weights()
     fill(bufp, p, strip(ml, 0), strip(mr, 0), md, mu, 0, keep_d, keep_u)
     s = [c[i] * q[i] for i in range(NX)]
     fill(bufs, s, strip(ml, 128), strip(mr, 128), md, mu, 4, keep_d, keep_u)
@@ -137,38 +151,15 @@
         qn[i] = q_new
         if n < 2:
             lap_out[i] = lap
-        if n == 2:
+        else:
             img_out[i] = lap * q[i] + q_new * lap_other[i]
-        if n == 3:
-            image = img[i] + lap * q3[i] + q_new * lap_other[i]
-            grad = (2.0 * courant_sq) * vel[i] * image
-            weighted = grad * noise[i]
-            first = lax.axis_index("shot") % 2 == 0
-            own[i] = jnp.where(first, grad, weighted)
-            sent[i] = jnp.where(first, weighted, grad)
     lpk[...] = slab
-
-    sx = source[0] // (NY * ngy) - ix * NX
-    sy = source[0] % (NY * ngy) - iy * NY
-
-    @pl.when((sx >= 0) & (sx < NX) & (sy >= 0) & (sy < NY))
-    def _():
-        row = pn[sx, pl.ds(sy, 1), :]
-        pn[sx, pl.ds(sy, 1), :] = row + jnp.where(lane == SRC_DEPTH, wavelet[0, start[0] + n], 0.0)
-
-    at = 80 if n == 0 else 64
-    got_d, got_u = md[at : at + 8], mu[at : at + 8]
-    oc_out[...] = oc[...]
-    up, turn_u, down, turn_d = ((0, 64, 12, 64), (4, 0, 12, 0), (4, 64, 8, 64), (8, 0, None, 0))[n]
-    oc_out[up : up + 4] = oc_out[up : up + 4] + roll(got_u, turn_u)[:4]
-    if down is not None:
-        oc_out[down : down + 4] = oc_out[down : down + 4] + roll(got_d, turn_d)[:4]
-
-    if n < 3:
-        for i in range(NX):
-            put_strips(i, pn[i], c[i] * qn[i], xlo, xhi, ylo, yhi)
-        ylo[64:72] = got_u
-        yhi[64:72] = got_d
+    add_source(n, source, start, wavelet, pn)
+    got_d, got_u = collect(n, md, mu, oc, oc_out)
+    for i in range(NX):
+        put_strips(i, pn[i], c[i] * qn[i], xlo, xhi, ylo, yhi)
+    ylo[64:72] = got_u
+    yhi[64:72] = got_d
     if n == 0:
         cext[0:16] = jnp.where(keep_d, md[64:80], 0.0)
         cext[16:48] = pack([c[i] for i in range(NX)])
@@ -178,23 +169,58 @@
     if n == 1:
         xlo[256:288] = mr[272:304]
         xhi[256:288] = ml[272:304]
-    if n == 3:
-        out = jnp.zeros((NY, NZ), f32)
-        for i in range(NX):
-            for t, row in ((2, pp[i]), (3, p[i]), (4, pn[i])):
-                to = 4 * i + t - 1
-                out = jnp.where(lane == to, roll(row, to - REC_DEPTH), out)
-        mat[...] = out
-        mat_lo[...] = out[:16]
-        mat_hi[...] = out[16:]
-
-
-def chunk_kernel(mat, got_d, got_u, p1, oc, out):
+
+
+def plane_kernel(
+    source, start, wavelet, c, p, pp, ml, mr, md, mu, oc,
+    lpk, oc_out, lap_out, mat, mat_lo, mat_hi, bufp, pn,
+):
+    keep_d, keep_u = edges()
+    lane = lanes()
+    wz = depth_weights()
+    fill(bufp, p, strip(ml, 0), strip(mr, 0), md, mu, 0, keep_d, keep_u)
+    slab = jnp.zeros((NY, NZ), f32)
+    for i in range(NX):
+        lap = laplace(bufp, i, wz)
+        slab = jnp.where(lane // SLAB == i, roll(lap, SLAB * i), slab)
+        lap_out[i] = lap
+        pn[i] = 2.0 * p[i] - pp[i] + c[i] * lap
+    lpk[...] = slab
+    add_source(3, source, start, wavelet, pn)
+    collect(3, md, mu, oc, oc_out)
+    out = jnp.zeros((NY, NZ), f32)
+    for i in range(NX):
+        for t, row in ((2, pp[i]), (3, p[i]), (4, pn[i])):
+            to = 4 * i + t - 1
+            out = jnp.where(lane == to, roll(row, to - REC_DEPTH), out)
+    mat[...] = out
+    mat_lo[...] = out[:16]
+    mat_hi[...] = out[16:]
+
+
+def adjoint_kernel(
+    c, q, ql, ml, mr, md, mu, lap3, lap0, q3, img, vel, noise, mat, p1, own, sent, base, bufs
+):
+    keep_d, keep_u = edges()
+    lane = lanes()
+    wz = depth_weights()
+    first = lax.axis_index("shot") % 2 == 0
+    s = [c[i] * q[i] for i in range(NX)]
+    fill(bufs, s, strip(ml, 128), strip(mr, 128), md, mu, 4, keep_d, keep_u)
     m = mat[...]
-    lane = lanes()
-    for i in range(NX):
+    for i in range(NX):
+        q_new = 2.0 * q[i] - ql[i] + laplace(bufs, i, wz)
+        image = img[i] + lap3[i] * q3[i] + q_new * lap0[i]
+        grad = (2.0 * courant_sq) * vel[i] * image
+        weighted = grad * noise[i]
+        own[i] = jnp.where(first, grad, weighted)
+        sent[i] = jnp.where(first, weighted, grad)
         m = jnp.where(lane == 4 * i, roll(p1[i], 4 * i - REC_DEPTH), m)
-    packed = got_d[...] + roll(m[:16], 32) + roll(m[16:], 64) + roll(got_u[...], 96)
+    base[...] = roll(m[:16], 32) + roll(m[16:], 64)
+
+
+def chunk_kernel(base, got_d, got_u, oc, out):
+    packed = base[...] + got_d[...] + roll(got_u[...], 96)
     for g in range(out.shape[0]):
         out[g, 0:16] = oc[...]
         out[g, 16:32] = packed
@@ -215,7 +241,7 @@
     return out
 
 
-def table_kernel(rec, vel, noise, keyx, hoty, vpk, zpk, cols, rows):
+def table_kernel(rec, vel, noise, keyx, hoty, count, vpk, zpk, cols, rows, hot):
     ix, iy, ngy = lax.axis_index("gx"), lax.axis_index("gy"), lax.axis_size("gy")
     half = ngy // 2
     bits = (NY * ngy).bit_length() - 1
@@ -224,8 +250,9 @@
     low = lanes() < 64
     bf = jnp.bfloat16
     coly = lax.broadcasted_iota(jnp.int32, (64, 128), 0).astype(f32).astype(bf)
+    row4 = (lax.broadcasted_iota(jnp.int32, (128, 128), 0) // 4).astype(f32).astype(bf)
     one, none = jnp.ones((), bf), jnp.zeros((), bf)
-    kx = jnp.clip((rec[...] >> bits) - ix * NX + 16, -1, 40).astype(f32)
+    kx = jnp.clip((rec[...] >> bits) - ix * NX + 12, -1, 32).astype(f32)
     ky = jnp.clip((rec[...] & (NY * ngy - 1)) - iy * NY + 16, -1, 64).astype(f32)
     for ref, k in ((rows, kx), (cols, ky)):
         ref[0] = jnp.where(odd, roll(k, 64), k)
@@ -233,15 +260,20 @@
         first = (iy + 2 * (g % half)) % ngy
         a = pl.ds((g // half) * half + first // 2, 1)
         b = pl.ds((g // half) * half + ((first + 1) % ngy) // 2, 1)
-        keyx[g : g + 1] = jnp.where(low, rows[0, a, :], rows[0, b, :])
+        key = jnp.where(low, rows[0, a, :], rows[0, b, :])
+        keyx[g : g + 1] = key
+        hot[:, 128 * g : 128 * (g + 1)] = jnp.where(row4 == key.astype(bf), one, none)
         here = jnp.where(low, cols[0, a, :], cols[0, b, :]).astype(bf)
         hoty[:, 128 * g : 128 * (g + 1)] = jnp.where(coly == here, one, none)
+    count[...] = lax.dot_general(
+        hot[...], hoty[...], (((1,), (1,)), ((), ())), preferred_element_type=f32
+    )
     vpk[...] = pack([vel[i] for i in range(NX)])
     zpk[...] = pack([noise[i] for i in range(NX)])
 
 
 def last_kernel(
-    got, keyx, hoty, cext, ml1, mr1, ml2, mr2, lp0, lp1, lp2, lp3, vpk, zpk, own, other,
+    got, keyx, hoty, count, cext, ml1, mr1, ml2, mr2, lp0, lp1, lp2, lp3, vpk, zpk, own, other,
     out, table, x, r3, r2, r1, inj,
 ):
     ngx = got.shape[0]
@@ -250,8 +282,8 @@
     c1l, c1r = ml1.at[256:320], mr1.at[256:320]
     c2l, c2r = ml2.at[256:288], mr2.at[256:288]
     bf = jnp.bfloat16
-    row4 = (lax.broadcasted_iota(jnp.int32, (160, 128), 0) // 4).astype(f32).astype(bf)
-    one, none = jnp.ones((), bf), jnp.zeros((), bf)
+    row4 = (lax.broadcasted_iota(jnp.int32, (128, 128), 0) // 4).astype(f32).astype(bf)
+    none = jnp.zeros((), bf)
 
     def build(g, carry):
         for rp in range(4):
@@ -263,21 +295,16 @@
             here = row4 == keyx[pl.ds(4 * g + rp, 1), :].astype(bf)
             for part, v in enumerate((hi, mid, low)):
                 v16 = jnp.concatenate([v, v, v, v], 0).astype(bf)
-                v160 = jnp.concatenate([v16] * 10, 0)
-                table[160 * part : 160 * (part + 1), at] = jnp.where(here, v160, none)
-            table[480:640, at] = jnp.where(here, one, none)
+                v128 = jnp.concatenate([v16] * 8, 0)
+                table[128 * part : 128 * (part + 1), at] = jnp.where(here, v128, none)
         return carry
 
     lax.fori_loop(0, ngx, build, 0, unroll=2)
     sums = lax.dot_general(
         table[...], hoty[...], (((1,), (1,)), ((), ())), preferred_element_type=f32
     )
-    seen = sums[0:160] + sums[160:320] + sums[320:480]
-    zero = jnp.zeros((96, 64), f32)
-    seen = jnp.concatenate([seen, zero], 0)
-    count = jnp.concatenate([sums[480:640], zero], 0)
-    both = jnp.concatenate([seen, count], 1)
-    tr = [both[:128].T, both[128:].T]
+    seen = sums[0:128] + sums[128:256] + sums[256:384]
+    tr = jnp.concatenate([seen, count[...]], 1).T
 
     k_in = lax.broadcasted_iota(jnp.int32, (128, 512), 0)
     k_out = lax.broadcasted_iota(jnp.int32, (128, 512), 1)
@@ -291,9 +318,8 @@
         blk = got[jnp.clip(src, 0, ngx - 1), 16:32, :]
         m = jnp.concatenate([roll(blk, -32 * t) for t in range(4)], 0)
         m = jnp.where(ok, m, 0.0)
-        t = tr[g // 4]
-        s_g = roll(t[:64], -32 * (g % 4))
-        n_g = roll(t[64:], -32 * (g % 4))
+        s_g = roll(tr[:64], 16 - 32 * g)
+        n_g = roll(tr[64:], 16 - 32 * g)
         dense.append(n_g * m - s_g)
     inj[...] = jnp.dot(
         jnp.concatenate(dense, 0), spread_to,
@@ -361,7 +387,7 @@
         grad_logs[i] = spread * weighted + jnp.exp(2.0 * logs[i]) / prior_var - 1.0
 
 
-def call(kernel, outs, scratch=(), smem=0, mib=4):
+def call(kernel, outs, scratch=(), smem=0, mib=4, cost=None):
     def go(*args):
         return pl.pallas_call(
             kernel,
@@ -369,6 +395,9 @@
             in_specs=[SM] * smem + [VM] * (len(args) - smem),
             out_specs=jax.tree.map(lambda _: VM, outs),
             scratch_shapes=list(scratch),
+            cost_estimate=cost and pl.CostEstimate(
+                flops=cost[0], bytes_accessed=cost[1], transcendentals=0
+            ),
             compiler_params=pltpu.CompilerParams(vmem_limit_bytes=mib * 2**20),
         )(*args)
 
@@ -410,63 +439,68 @@
     for n in range(STEPS):
         ml, mr = shift(xhi, "gx", 1), shift(xlo, "gx", -1)
         md, mu = shift(yhi, "gy", 1, True), shift(ylo, "gy", -1, True)
-        extra = ()
-        if n == 1:
-            extra = (keep["cext"],)
-        if n == 2:
-            extra = (keep["lap1"],)
-        if n == 3:
-            extra = (keep["lap0"], keep["q3"], keep["img"], vel, noise)
+        halos = (ml, mr, md, mu)
+        if n == STEPS - 1:
+            break
+        extra = {1: (keep.get("cext"),), 2: (keep.get("lap1"),)}.get(n, ())
+        rows = (320, 288, 256)[n]
         outs = [sds(NY, NZ), sds(16, 128), F, F]
-        if n < 3:
-            rows = (320, 288, 256)[n]
-            outs += [sds(rows, 128), sds(rows, 128), sds(72, 128), sds(72, 128)]
-        outs += {0: [F, sds(64, 128)], 1: [F], 2: [F], 3: [sds(NY, NZ), sds(16, NZ), sds(16, NZ), F, F]}[n]
+        outs += [sds(rows, 128), sds(rows, 128), sds(72, 128), sds(72, 128), F]
+        if n == 0:
+            outs.append(sds(64, 128))
         res = call(functools.partial(step_kernel, n), tuple(outs), (buf, buf), smem=3)(
-            source_column, start_step, wavelet, coef, p, p_prev, q, q_later, ml, mr, md, mu, oc, *extra
+            source_column, start_step, wavelet, coef, p, p_prev, q, q_later, *halos, oc, *extra
         )
-        lpk, oc, q_next, p_next = res[:4]
+        lpk, oc, q_next, p_next, xlo, xhi, ylo, yhi = res[:8]
         slabs.append(lpk)
-        if n < 3:
-            xlo, xhi, ylo, yhi = res[4:8]
         if n == 0:
             keep["lap0"], keep["cext"], keep["q3"], keep["p1"] = res[8], res[9], q_next, p_next
         if n == 1:
-            keep["lap1"] = res[8]
-            keep["c"] = [ml, mr]
+            keep["lap1"], keep["c"] = res[8], [ml, mr]
         if n == 2:
-            keep["img"] = res[8]
+            img = res[8]
             keep["c"] += [ml, mr]
-        if n == 3:
-            mat, mat_lo, mat_hi, own, sent = res[4:9]
         p_prev, p = p, p_next
         q_later, q = q, q_next
 
+    lpk, oc, lap3, mat, mat_lo, mat_hi = call(
+        plane_kernel,
+        (sds(NY, NZ), sds(16, 128), F, sds(NY, NZ), sds(16, NZ), sds(16, NZ)),
+        (buf, pltpu.VMEM((NX, NY, NZ), f32)),
+        smem=3,
+    )(source_column, start_step, wavelet, coef, p, p_prev, *halos, oc)
+    slabs.append(lpk)
     mat_d, mat_u = shift(mat_hi, "gy", 1), shift(mat_lo, "gy", -1)
+    own, sent, base = call(
+        adjoint_kernel, (F, F, sds(16, NZ)), (buf,), cost=(2_000_000, 2_000_000)
+    )(
+        coef, q, q_later, *halos, lap3, keep["lap0"], keep["q3"], img, vel, noise, mat, keep["p1"]
+    )
     other = lax.ppermute(sent, "shot", [(i, i ^ 1) for i in range(nshot)])
     nrec = receiver_column.shape[1]
     bf = jnp.bfloat16
-    keyx, hoty, vpk, zpk = call(
+    keyx, hoty, count, vpk, zpk = call(
         table_kernel,
         (
             sds(nrec // 128, 128),
             jax.ShapeDtypeStruct((64, nrec), bf),
+            sds(128, 64),
             sds(NY, NZ),
             sds(NY, NZ),
         ),
-        [pltpu.VMEM((1, nrec // 128, 128), f32)] * 2,
-        mib=8,
+        [pltpu.VMEM((1, nrec // 128, 128), f32)] * 2 + [pltpu.VMEM((128, nrec), bf)],
+        mib=12,
     )(receiver_column.reshape(-1, 128), vel, noise)
-    chunk = call(chunk_kernel, sds(ngx, 32, 128))(mat, mat_d, mat_u, keep["p1"], oc)
+    chunk = call(chunk_kernel, sds(ngx, 32, 128))(base, mat_d, mat_u, oc)
     got = lax.all_to_all(chunk, "gx", 0, 0)
     g5 = pltpu.VMEM((5, 64, 128), f32)
     g48 = pltpu.VMEM((5, 48, 128), f32)
     part = call(
         last_kernel,
         sds(NX * NY + 2 * NY, NZ),
-        (pltpu.VMEM((640, nrec), bf), g5, g5, g48, g48, pltpu.VMEM((320, 512), f32)),
+        (pltpu.VMEM((384, nrec), bf), g5, g5, g48, g48, pltpu.VMEM((320, 512), f32)),
         mib=24,
-    )(got, keyx, hoty, keep["cext"], *keep["c"], *slabs, vpk, zpk, own, other)
+    )(got, keyx, hoty, count, keep["cext"], *keep["c"], *slabs, vpk, zpk, own, other)
     every = lax.all_gather(part, "shot", axis=0)
     return call(sum_kernel, (F, F))(every, log_scale)
 

time: 139 us -> 136 us (0.978)
  Pallas kernels: 18.6 us -> 16.2 us
    pallas_call x9 -> x10, Pallas kernels: 18.6 us -> 16.2 us  [go(): pl.pallas_call(kernel, out_shape=outs, in_specs=[SM] * smem + [VM] * (len...]
  transfers between devices with their start and end apart: 20 -> 20, of which waited for: 5 -> 4; matrix products, arithmetic and copies ran while one was open for 0% -> 0% of each run, Pallas kernels for 0% -> 1%
where the time goes in v6:
time: 136 us; the launch traced here: 135 us
  starting transfers between devices  85.9 us (63%)
  blocking collectives  21.7 us (16%)
  Pallas kernels  16.2 us (12%)
  waiting for transfers between devices  6.54 us (5%)
  between operations  2.3 us (2%)
  local copies, waits for them, and re-layouts  1.52 us (1%)
    ppermute x18, starting transfers between devices, shift(): lax.ppermute(x, axis, [(i, (i + k) % n) for i in range(n) if wrap or 0 <=...  57.9 us
    all_gather x1, blocking collectives, local(): every = lax.all_gather(part, 'shot', axis=0)  21.7 us
    pallas_call x10, Pallas kernels, go(): pl.pallas_call(kernel, out_shape=outs, in_specs=[SM] * smem + [VM] * (len...  16.2 us
    all_to_all x1, starting transfers between devices, local(): got = lax.all_to_all(chunk, 'gx', 0, 0)  16.1 us
    ppermute x1, starting transfers between devices, local(): other = lax.ppermute(sent, 'shot', [(i, i ^ 1) for i in range(nshot)])  11.9 us
    ppermute x18, waiting for transfers between devices, shift(): lax.ppermute(x, axis, [(i, (i + k) % n) for i in range(n) if wrap or 0 <=...  6.54 us
  transfers between devices with their start and end apart: 20, of which 4 were waited for; matrix products, arithmetic and copies ran while one was open for 0% of the time, Pallas kernels for 1%

profile of v6, /device:TPU:1, one launch (start us, length us, event | category | flops | bytes accessed | tf_op | source)
XLA Modules:
  0.0 135.2 jit_solution(11662203029145668985)
XLA Ops:
  2.8 4.2 %collective-permute-start = (f32[256,128]{1,0:T(8,128)S(1)}, f32[256,128]{1,0:T(8,128)S(1)}, u32[]{:S(2)}, u32[]{:S(2)}) collective-permute-start(f32[256,128]{1,0:T(8,128)S(1)} %get-tuple-element.49), channel_id=1, source_target_pairs={{0,8},{8,16},{16,24},{24,32},{32,40},{40,48},{48,56},{56,64},{64,7... | collective-permute-start | bytes 393224 | tf_op jit(solution)/shard_map/ppermute | solution.py:409
  8.3 4.0 %collective-permute-start.2 = (f32[88,128]{1,0:T(8,128)S(1)}, f32[88,128]{1,0:T(8,128)S(1)}, u32[]{:S(2)}, u32[]{:S(2)}) collective-permute-start(f32[88,128]{1,0:T(8,128)S(1)} %get-tuple-element.51), channel_id=1, source_target_pairs={{0,1},{1,2},{2,3},{3,4},{4,5},{5,6},{6,7},{7,0},{8,9},{9,10},{10,1... | collective-permute-start | bytes 135176 | tf_op jit(solution)/shard_map/ppermute | solution.py:409
  12.3 8.6 %collective-permute-start.3 = (f32[88,128]{1,0:T(8,128)S(1)}, f32[88,128]{1,0:T(8,128)S(1)}, u32[]{:S(2)}, u32[]{:S(2)}) collective-permute-start(f32[88,128]{1,0:T(8,128)S(1)} %get-tuple-element.52), channel_id=1, source_target_pairs={{0,7},{1,0},{2,1},{3,2},{4,3},{5,4},{6,5},{7,6},{8,15},{9,8},{10,9... | collective-permute-start | bytes 135176 | tf_op jit(solution)/shard_map/ppermute | solution.py:409
  22.9 1.7 %shard_map.132 = (f32[32,128]{1,0:T(8,128)S(1)}, f32[16,128]{1,0:T(8,128)S(1)}, f32[8,32,128]{2,1,0:T(8,128)S(1)}, f32[8,32,128]{2,1,0:T(8,128)S(1)}, f32[320,12...) custom-call(s32[1]{0:T(128)S(6)} %copy.14.source, ...), custom_call_target="tpu_custom_call" | custom-call | tf_op jit(solution)/shard_map/pallas_call | solution.py:392
  24.6 4.0 %collective-permute-start.4 = (f32[320,128]{1,0:T(8,128)S(1)}, f32[320,128]{1,0:T(8,128)S(1)}, u32[]{:S(2)}, u32[]{:S(2)}) collective-permute-start(f32[320,128]{1,0:T(8,128)S(1)} %get-tuple-element.56), channel_id=1, source_target_pairs={{0,8},{8,16},{16,24},{24,32},{32,40},{40,48},{48,56},{56,64},{64,7... | collective-permute-start | bytes 491528 | tf_op jit(solution)/shard_map/ppermute | solution.py:409
  29.9 1.9 %collective-permute-start.6 = (f32[72,128]{1,0:T(8,128)S(1)}, f32[72,128]{1,0:T(8,128)S(1)}, u32[]{:S(2)}, u32[]{:S(2)}) collective-permute-start(f32[72,128]{1,0:T(8,128)S(1)} %get-tuple-element.58), channel_id=1, source_target_pairs={{0,1},{1,2},{2,3},{3,4},{4,5},{5,6},{6,7},{7,0},{8,9},{9,10},{10,1... | collective-permute-start | bytes 110600 | tf_op jit(solution)/shard_map/ppermute | solution.py:409
  31.8 4.7 %collective-permute-start.7 = (f32[72,128]{1,0:T(8,128)S(1)}, f32[72,128]{1,0:T(8,128)S(1)}, u32[]{:S(2)}, u32[]{:S(2)}) collective-permute-start(f32[72,128]{1,0:T(8,128)S(1)} %get-tuple-element.59), channel_id=1, source_target_pairs={{0,7},{1,0},{2,1},{3,2},{4,3},{5,4},{6,5},{7,6},{8,15},{9,8},{10,9... | collective-permute-start | bytes 110600 | tf_op jit(solution)/shard_map/ppermute | solution.py:409
  37.5 1.6 %shard_map.133 = (f32[32,128]{1,0:T(8,128)S(1)}, f32[16,128]{1,0:T(8,128)S(1)}, f32[8,32,128]{2,1,0:T(8,128)S(1)}, f32[8,32,128]{2,1,0:T(8,128)S(1)}, f32[288,12...) custom-call(s32[1]{0:T(128)S(6)} %copy.14.source, ...), custom_call_target="tpu_custom_call" | custom-call | tf_op jit(solution)/shard_map/pallas_call | solution.py:392
  39.2 4.0 %collective-permute-start.8 = (f32[288,128]{1,0:T(8,128)S(1)}, f32[288,128]{1,0:T(8,128)S(1)}, u32[]{:S(2)}, u32[]{:S(2)}) collective-permute-start(f32[288,128]{1,0:T(8,128)S(1)} %get-tuple-element.64), channel_id=1, source_target_pairs={{0,8},{8,16},{16,24},{24,32},{32,40},{40,48},{48,56},{56,64},{64,7... | collective-permute-start | bytes 442376 | tf_op jit(solution)/shard_map/ppermute | solution.py:409
  44.5 3.0 %collective-permute-start.10 = (f32[72,128]{1,0:T(8,128)S(1)}, f32[72,128]{1,0:T(8,128)S(1)}, u32[]{:S(2)}, u32[]{:S(2)}) collective-permute-start(f32[72,128]{1,0:T(8,128)S(1)} %get-tuple-element.66), channel_id=1, source_target_pairs={{0,1},{1,2},{2,3},{3,4},{4,5},{5,6},{6,7},{7,0},{8,9},{9,10},{10,1... | collective-permute-start | bytes 110600 | tf_op jit(solution)/shard_map/ppermute | solution.py:409
  47.5 3.8 %collective-permute-start.11 = (f32[72,128]{1,0:T(8,128)S(1)}, f32[72,128]{1,0:T(8,128)S(1)}, u32[]{:S(2)}, u32[]{:S(2)}) collective-permute-start(f32[72,128]{1,0:T(8,128)S(1)} %get-tuple-element.67), channel_id=1, source_target_pairs={{0,7},{1,0},{2,1},{3,2},{4,3},{5,4},{6,5},{7,6},{8,15},{9,8},{10,9... | collective-permute-start | bytes 110600 | tf_op jit(solution)/shard_map/ppermute | solution.py:409
  51.3 1.4 %collective-permute-done.11.mu = f32[72,128]{1,0:T(8,128)S(1)} collective-permute-done((f32[72,128]{1,0:T(8,128)S(1)}, f32[72,128]{1,0:T(8,128)S(1)}, u32[]{:S(2)}, u32[]{:S(2)}) %collective-permute-start.11) | collective-permute-done | bytes 36896 | tf_op jit(solution)/shard_map/ppermute | solution.py:409
  52.7 1.7 %shard_map.134 = (f32[32,128]{1,0:T(8,128)S(1)}, f32[16,128]{1,0:T(8,128)S(1)}, f32[8,32,128]{2,1,0:T(8,128)S(1)}, f32[8,32,128]{2,1,0:T(8,128)S(1)}, f32[256,12...) custom-call(s32[1]{0:T(128)S(6)} %copy.14.source, ...), custom_call_target="tpu_custom_call" | custom-call | tf_op jit(solution)/shard_map/pallas_call | solution.py:392
  54.4 3.7 %collective-permute-start.12 = (f32[256,128]{1,0:T(8,128)S(1)}, f32[256,128]{1,0:T(8,128)S(1)}, u32[]{:S(2)}, u32[]{:S(2)}) collective-permute-start(f32[256,128]{1,0:T(8,128)S(1)} %get-tuple-element.71), channel_id=1, source_target_pairs={{0,8},{8,16},{16,24},{24,32},{32,40},{40,48},{48,56},{56,64},{64,7... | collective-permute-start | bytes 393224 | tf_op jit(solution)/shard_map/ppermute | solution.py:409
  59.4 3.4 %collective-permute-start.14 = (f32[72,128]{1,0:T(8,128)S(1)}, f32[72,128]{1,0:T(8,128)S(1)}, u32[]{:S(2)}, u32[]{:S(2)}) collective-permute-start(f32[72,128]{1,0:T(8,128)S(1)} %get-tuple-element.73), channel_id=1, source_target_pairs={{0,1},{1,2},{2,3},{3,4},{4,5},{5,6},{6,7},{7,0},{8,9},{9,10},{10,1... | collective-permute-start | bytes 110600 | tf_op jit(solution)/shard_map/ppermute | solution.py:409
  62.8 3.3 %collective-permute-start.15 = (f32[72,128]{1,0:T(8,128)S(1)}, f32[72,128]{1,0:T(8,128)S(1)}, u32[]{:S(2)}, u32[]{:S(2)}) collective-permute-start(f32[72,128]{1,0:T(8,128)S(1)} %get-tuple-element.74), channel_id=1, source_target_pairs={{0,7},{1,0},{2,1},{3,2},{4,3},{5,4},{6,5},{7,6},{8,15},{9,8},{10,9... | collective-permute-start | bytes 110600 | tf_op jit(solution)/shard_map/ppermute | solution.py:409
  66.1 1.4 %collective-permute-done.15.mu = f32[72,128]{1,0:T(8,128)S(1)} collective-permute-done((f32[72,128]{1,0:T(8,128)S(1)}, f32[72,128]{1,0:T(8,128)S(1)}, u32[]{:S(2)}, u32[]{:S(2)}) %collective-permute-start.15) | collective-permute-done | bytes 36896 | tf_op jit(solution)/shard_map/ppermute | solution.py:409
  67.5 1.4 %shard_map.135 = (f32[32,128]{1,0:T(8,128)S(1)}, f32[16,128]{1,0:T(8,128)S(1)}, f32[8,32,128]{2,1,0:T(8,128)S(1)}, f32[32,128]{1,0:T(8,128)S(1)}, f32[16,128]{1,0:T(8,128)S(1)}, /*index=5*/f32[16,128]{1,0:T(8,128)S(1)}) custom-call(s32[1]{0:T(128)S(6)} %copy.14.source, s32[1]{0:T(128)S(6)} %copy.15.start, f32[1,64]{1,0:T(1,128)S(1)} %copy-done.7, ...), custom_call_target="tpu_custom_call" | custom-call | tf_op jit(solution)/shard_map/pallas_call | solution.py:392
  68.9 2.9 %collective-permute-start.16 = (f32[16,128]{1,0:T(8,128)S(1)}, f32[16,128]{1,0:T(8,128)S(1)}, u32[]{:S(2)}, u32[]{:S(2)}) collective-permute-start(f32[16,128]{1,0:T(8,128)S(1)} %get-tuple-element.82), channel_id=1, source_target_pairs={{0,1},{1,2},{2,3},{3,4},{4,5},{5,6},{6,7},{8,9},{9,10},{10,11},{11... | collective-permute-start | bytes 24584 | tf_op jit(solution)/shard_map/ppermute | solution.py:409
  73.6 2.7 %collective-permute-done.17.got_u = f32[16,128]{1,0:T(8,128)S(1)} collective-permute-done((f32[16,128]{1,0:T(8,128)S(1)}, f32[16,128]{1,0:T(8,128)S(1)}, u32[]{:S(2)}, u32[]{:S(2)}) %collective-permute-start.17) | collective-permute-done | bytes 8224 | tf_op jit(solution)/shard_map/ppermute | solution.py:409
  77.0 16.1 %all-to-all-start = ((f32[16,32,128]{2,1,0:T(8,128)}), f32[16,32,128]{2,1,0:T(8,128)S(1)}, u32[]{:S(2)}, u32[]{:S(2)}) async-start(f32[16,32,128]{2,1,0:T(8,128)} %shard_map.137), calls=%async_computation | async-start | bytes 524288 | tf_op jit(solution)/shard_map/all_to_all | solution.py:495
  93.1 11.9 %collective-permute-start.18 = (f32[8,32,128]{2,1,0:T(8,128)S(1)}, f32[8,32,128]{2,1,0:T(8,128)S(1)}, u32[]{:S(2)}, u32[]{:S(2)}) collective-permute-start(f32[8,32,128]{2,1,0:T(8,128)S(1)} %get-tuple-element.95), channel_id=1, source_target_pairs={{0,128},{128,0},{256,384},{384,256},{1,129},{129,1},{257,385},{385... | collective-permute-start | bytes 393224 | tf_op jit(solution)/shard_map/ppermute | solution.py:479
  106.2 6.5 %shard_map.139 = f32[320,128]{1,0:T(8,128)S(1)} custom-call(f32[16,32,128]{2,1,0:T(8,128)S(1)} %all-to-all-done.got, f32[64,128]{1,0:T(8,128)S(1)} %get-tuple-element.85.keyx, bf16[64,8192]{1,0:T(8,128)(2,1)S(1)} %get-tuple-element.86.hoty, f32[128,64]{1,0:T(8,128)S(1)} %get-tuple-element.87.count, f32[64,128]{1,0:T(8,128)S(1)} %get-tuple-element.61.rest_0_.cext, ...), custom_call_target="tpu_custom_call" | custom-call | tf_op jit(solution)/shard_map/pallas_call | solution.py:392
  112.7 21.7 %all-gather = f32[1280,128]{1,0:T(8,128)S(1)} all-gather(f32[320,128]{1,0:T(8,128)S(1)} %shard_map.139), channel_id=2, replica_groups=mesh['shot'=4,'gx'=16,'gy'=8] {'shot'}, dimensions={0}, use_global_device_ids=true | all-gather | bytes 819200 | tf_op jit(solution)/shard_map/all_gather | solution.py:504
  (47 shorter events, 13.4 us)
Async XLA Ops:
  2.7 19.5 %copy-start.4 = (f32[1,8,32,128]{3,2,1,0:T(8,128)S(1)}, f32[1,8,32,128]{3,2,1,0:T(8,128)}, u32[]{:S(2)}) copy-start(f32[1,8,32,128]{3,2,1,0:T(8,128)} %param.15) | copy-start | bytes 393220
  2.7 19.6 %copy-start.5 = (f32[1,8,32,128]{3,2,1,0:T(8,128)S(1)}, f32[1,8,32,128]{3,2,1,0:T(8,128)}, u32[]{:S(2)}) copy-start(f32[1,8,32,128]{3,2,1,0:T(8,128)} %param.17) | copy-start | bytes 393220
  2.8 19.4 %collective-permute-start = (f32[256,128]{1,0:T(8,128)S(1)}, f32[256,128]{1,0:T(8,128)S(1)}, u32[]{:S(2)}, u32[]{:S(2)}) collective-permute-start(f32[256,128]{1,0:T(8,128)S(1)} %get-tuple-element.49), channel_id=1, source_target_pairs={{0,8},{8,16},{16,24},{24,32},{32,40},{40,48},{48,56},{56,64},{64,7... | collective-permute-start | bytes 393224 | tf_op jit(solution)/shard_map/ppermute | solution.py:409
  7.0 15.2 %collective-permute-start.1 = (f32[256,128]{1,0:T(8,128)S(1)}, f32[256,128]{1,0:T(8,128)S(1)}, u32[]{:S(2)}, u32[]{:S(2)}) collective-permute-start(f32[256,128]{1,0:T(8,128)S(1)} %get-tuple-element.50), channel_id=1, source_target_pairs={{8,0},{16,8},{24,16},{32,24},{40,32},{48,40},{56,48},{64,56},{72,6... | collective-permute-start | bytes 393224 | tf_op jit(solution)/shard_map/ppermute | solution.py:409
  8.3 13.9 %collective-permute-start.2 = (f32[88,128]{1,0:T(8,128)S(1)}, f32[88,128]{1,0:T(8,128)S(1)}, u32[]{:S(2)}, u32[]{:S(2)}) collective-permute-start(f32[88,128]{1,0:T(8,128)S(1)} %get-tuple-element.51), channel_id=1, source_target_pairs={{0,1},{1,2},{2,3},{3,4},{4,5},{5,6},{6,7},{7,0},{8,9},{9,10},{10,1... | collective-permute-start | bytes 135176 | tf_op jit(solution)/shard_map/ppermute | solution.py:409
  12.3 9.9 %collective-permute-start.3 = (f32[88,128]{1,0:T(8,128)S(1)}, f32[88,128]{1,0:T(8,128)S(1)}, u32[]{:S(2)}, u32[]{:S(2)}) collective-permute-start(f32[88,128]{1,0:T(8,128)S(1)} %get-tuple-element.52), channel_id=1, source_target_pairs={{0,7},{1,0},{2,1},{3,2},{4,3},{5,4},{6,5},{7,6},{8,15},{9,8},{10,9... | collective-permute-start | bytes 135176 | tf_op jit(solution)/shard_map/ppermute | solution.py:409
  24.6 12.9 %collective-permute-start.4 = (f32[320,128]{1,0:T(8,128)S(1)}, f32[320,128]{1,0:T(8,128)S(1)}, u32[]{:S(2)}, u32[]{:S(2)}) collective-permute-start(f32[320,128]{1,0:T(8,128)S(1)} %get-tuple-element.56), channel_id=1, source_target_pairs={{0,8},{8,16},{16,24},{24,32},{32,40},{40,48},{48,56},{56,64},{64,7... | collective-permute-start | bytes 491528 | tf_op jit(solution)/shard_map/ppermute | solution.py:409
  28.6 8.9 %collective-permute-start.5 = (f32[320,128]{1,0:T(8,128)S(1)}, f32[320,128]{1,0:T(8,128)S(1)}, u32[]{:S(2)}, u32[]{:S(2)}) collective-permute-start(f32[320,128]{1,0:T(8,128)S(1)} %get-tuple-element.57), channel_id=1, source_target_pairs={{8,0},{16,8},{24,16},{32,24},{40,32},{48,40},{56,48},{64,56},{72,6... | collective-permute-start | bytes 491528 | tf_op jit(solution)/shard_map/ppermute | solution.py:409
  29.9 6.6 %collective-permute-start.6 = (f32[72,128]{1,0:T(8,128)S(1)}, f32[72,128]{1,0:T(8,128)S(1)}, u32[]{:S(2)}, u32[]{:S(2)}) collective-permute-start(f32[72,128]{1,0:T(8,128)S(1)} %get-tuple-element.58), channel_id=1, source_target_pairs={{0,1},{1,2},{2,3},{3,4},{4,5},{5,6},{6,7},{7,0},{8,9},{9,10},{10,1... | collective-permute-start | bytes 110600 | tf_op jit(solution)/shard_map/ppermute | solution.py:409
  31.8 5.7 %collective-permute-start.7 = (f32[72,128]{1,0:T(8,128)S(1)}, f32[72,128]{1,0:T(8,128)S(1)}, u32[]{:S(2)}, u32[]{:S(2)}) collective-permute-start(f32[72,128]{1,0:T(8,128)S(1)} %get-tuple-element.59), channel_id=1, source_target_pairs={{0,7},{1,0},{2,1},{3,2},{4,3},{5,4},{6,5},{7,6},{8,15},{9,8},{10,9... | collective-permute-start | bytes 110600 | tf_op jit(solution)/shard_map/ppermute | solution.py:409
  39.2 13.6 %collective-permute-start.8 = (f32[288,128]{1,0:T(8,128)S(1)}, f32[288,128]{1,0:T(8,128)S(1)}, u32[]{:S(2)}, u32[]{:S(2)}) collective-permute-start(f32[288,128]{1,0:T(8,128)S(1)} %get-tuple-element.64), channel_id=1, source_target_pairs={{0,8},{8,16},{16,24},{24,32},{32,40},{40,48},{48,56},{56,64},{64,7... | collective-permute-start | bytes 442376 | tf_op jit(solution)/shard_map/ppermute | solution.py:409
  43.2 9.6 %collective-permute-start.9 = (f32[288,128]{1,0:T(8,128)S(1)}, f32[288,128]{1,0:T(8,128)S(1)}, u32[]{:S(2)}, u32[]{:S(2)}) collective-permute-start(f32[288,128]{1,0:T(8,128)S(1)} %get-tuple-element.65), channel_id=1, source_target_pairs={{8,0},{16,8},{24,16},{32,24},{40,32},{48,40},{56,48},{64,56},{72,6... | collective-permute-start | bytes 442376 | tf_op jit(solution)/shard_map/ppermute | solution.py:409
  44.5 6.8 %collective-permute-start.10 = (f32[72,128]{1,0:T(8,128)S(1)}, f32[72,128]{1,0:T(8,128)S(1)}, u32[]{:S(2)}, u32[]{:S(2)}) collective-permute-start(f32[72,128]{1,0:T(8,128)S(1)} %get-tuple-element.66), channel_id=1, source_target_pairs={{0,1},{1,2},{2,3},{3,4},{4,5},{5,6},{6,7},{7,0},{8,9},{9,10},{10,1... | collective-permute-start | bytes 110600 | tf_op jit(solution)/shard_map/ppermute | solution.py:409
  47.5 5.2 %collective-permute-start.11 = (f32[72,128]{1,0:T(8,128)S(1)}, f32[72,128]{1,0:T(8,128)S(1)}, u32[]{:S(2)}, u32[]{:S(2)}) collective-permute-start(f32[72,128]{1,0:T(8,128)S(1)} %get-tuple-element.67), channel_id=1, source_target_pairs={{0,7},{1,0},{2,1},{3,2},{4,3},{5,4},{6,5},{7,6},{8,15},{9,8},{10,9... | collective-permute-start | bytes 110600 | tf_op jit(solution)/shard_map/ppermute | solution.py:409
  54.4 13.1 %collective-permute-start.12 = (f32[256,128]{1,0:T(8,128)S(1)}, f32[256,128]{1,0:T(8,128)S(1)}, u32[]{:S(2)}, u32[]{:S(2)}) collective-permute-start(f32[256,128]{1,0:T(8,128)S(1)} %get-tuple-element.71), channel_id=1, source_target_pairs={{0,8},{8,16},{16,24},{24,32},{32,40},{40,48},{48,56},{56,64},{64,7... | collective-permute-start | bytes 393224 | tf_op jit(solution)/shard_map/ppermute | solution.py:409
  58.1 9.4 %collective-permute-start.13 = (f32[256,128]{1,0:T(8,128)S(1)}, f32[256,128]{1,0:T(8,128)S(1)}, u32[]{:S(2)}, u32[]{:S(2)}) collective-permute-start(f32[256,128]{1,0:T(8,128)S(1)} %get-tuple-element.72), channel_id=1, source_target_pairs={{8,0},{16,8},{24,16},{32,24},{40,32},{48,40},{56,48},{64,56},{72,6... | collective-permute-start | bytes 393224 | tf_op jit(solution)/shard_map/ppermute | solution.py:409
  59.4 6.7 %collective-permute-start.14 = (f32[72,128]{1,0:T(8,128)S(1)}, f32[72,128]{1,0:T(8,128)S(1)}, u32[]{:S(2)}, u32[]{:S(2)}) collective-permute-start(f32[72,128]{1,0:T(8,128)S(1)} %get-tuple-element.73), channel_id=1, source_target_pairs={{0,1},{1,2},{2,3},{3,4},{4,5},{5,6},{6,7},{7,0},{8,9},{9,10},{10,1... | collective-permute-start | bytes 110600 | tf_op jit(solution)/shard_map/ppermute | solution.py:409
  62.8 4.7 %collective-permute-start.15 = (f32[72,128]{1,0:T(8,128)S(1)}, f32[72,128]{1,0:T(8,128)S(1)}, u32[]{:S(2)}, u32[]{:S(2)}) collective-permute-start(f32[72,128]{1,0:T(8,128)S(1)} %get-tuple-element.74), channel_id=1, source_target_pairs={{0,7},{1,0},{2,1},{3,2},{4,3},{5,4},{6,5},{7,6},{8,15},{9,8},{10,9... | collective-permute-start | bytes 110600 | tf_op jit(solution)/shard_map/ppermute | solution.py:409
  68.9 4.7 %collective-permute-start.16 = (f32[16,128]{1,0:T(8,128)S(1)}, f32[16,128]{1,0:T(8,128)S(1)}, u32[]{:S(2)}, u32[]{:S(2)}) collective-permute-start(f32[16,128]{1,0:T(8,128)S(1)} %get-tuple-element.82), channel_id=1, source_target_pairs={{0,1},{1,2},{2,3},{3,4},{4,5},{5,6},{6,7},{8,9},{9,10},{10,11},{11... | collective-permute-start | bytes 24584 | tf_op jit(solution)/shard_map/ppermute | solution.py:409
  71.9 4.4 %collective-permute-start.17 = (f32[16,128]{1,0:T(8,128)S(1)}, f32[16,128]{1,0:T(8,128)S(1)}, u32[]{:S(2)}, u32[]{:S(2)}) collective-permute-start(f32[16,128]{1,0:T(8,128)S(1)} %get-tuple-element.83), channel_id=1, source_target_pairs={{1,0},{2,1},{3,2},{4,3},{5,4},{6,5},{7,6},{9,8},{10,9},{11,10},{12... | collective-permute-start | bytes 24584 | tf_op jit(solution)/shard_map/ppermute | solution.py:409
  77.0 28.0 %copy-start.6 = (s32[1,8192]{1,0:T(1,128)S(1)}, s32[1,8192]{1,0:T(1,128)}, u32[]{:S(2)}) copy-start(s32[1,8192]{1,0:T(1,128)} %param.21) | copy-start | bytes 98308
  77.0 29.2 %all-to-all-start = ((f32[16,32,128]{2,1,0:T(8,128)}), f32[16,32,128]{2,1,0:T(8,128)S(1)}, u32[]{:S(2)}, u32[]{:S(2)}) async-start(f32[16,32,128]{2,1,0:T(8,128)} %shard_map.137), calls=%async_computation | async-start | bytes 524288 | tf_op jit(solution)/shard_map/all_to_all | solution.py:495
  93.1 13.0 %collective-permute-start.18 = (f32[8,32,128]{2,1,0:T(8,128)S(1)}, f32[8,32,128]{2,1,0:T(8,128)S(1)}, u32[]{:S(2)}, u32[]{:S(2)}) collective-permute-start(f32[8,32,128]{2,1,0:T(8,128)S(1)} %get-tuple-element.95), channel_id=1, source_target_pairs={{0,128},{128,0},{256,384},{384,256},{1,129},{129,1},{257,385},{385... | collective-permute-start | bytes 393224 | tf_op jit(solution)/shard_map/ppermute | solution.py:479
  112.7 21.7 %copy-start.3 = (f32[8,32,128]{2,1,0:T(8,128)S(1)}, f32[8,32,128]{2,1,0:T(8,128)}, u32[]{:S(2)}) copy-start(f32[8,32,128]{2,1,0:T(8,128)} %logs.1) | copy-start | bytes 393220
  (5 other events, 27.6 us)

commit v7 on v6

--- a/solution.py
+++ b/solution.py
@@ -135,7 +135,7 @@
     if n == 1:
         cext, lpk, oc_out, qn, pn, xlo, xhi, ylo, yhi, lap_out, bufp, bufs = rest
     if n == 2:
-        lap_other, lpk, oc_out, qn, pn, xlo, xhi, ylo, yhi, img_out, bufp, bufs = rest
+        lap_other, lpk, oc_out, qn, pn, xlo, xhi, ylo, yhi, img_out, mat, bufp, bufs = rest
     keep_d, keep_u = edges()
     lane = lanes()
     wz = depth_weights()
@@ -166,63 +166,61 @@
         cext[48:64] = jnp.where(keep_u, mu[64:80], 0.0)
         xlo[256:320] = cext[...]
         xhi[256:320] = cext[...]
+    if n == 2:
+        new = [pn[i] for i in range(NX)]
+        slab = pack(new)
+        d = lane % SLAB
+        deep = (3.0 * C0) * slab
+        for k in range(1, W + 1):
+            deep = deep + jnp.where(d < SLAB - k, CK[k], 0.0) * roll(slab, -k)
+            deep = deep + jnp.where(d >= k, CK[k], 0.0) * roll(slab, k)
+        out = jnp.zeros((NY, NZ), f32)
+        for i in range(NX):
+            for t, row, at in (
+                (0, pp[i], REC_DEPTH),
+                (1, p[i], REC_DEPTH),
+                (2, new[i], REC_DEPTH),
+                (3, deep, SLAB * i + REC_DEPTH),
+            ):
+                out = jnp.where(lane == 4 * i + t, roll(row, 4 * i + t - at), out)
+        mat[...] = out
+        ylo[72:88] = out[:16]
+        yhi[72:88] = out[16:]
     if n == 1:
         xlo[256:288] = mr[272:304]
         xhi[256:288] = ml[272:304]
 
 
-def plane_kernel(
-    source, start, wavelet, c, p, pp, ml, mr, md, mu, oc,
-    lpk, oc_out, lap_out, mat, mat_lo, mat_hi, bufp, pn,
-):
-    keep_d, keep_u = edges()
-    lane = lanes()
-    wz = depth_weights()
-    fill(bufp, p, strip(ml, 0), strip(mr, 0), md, mu, 0, keep_d, keep_u)
-    slab = jnp.zeros((NY, NZ), f32)
-    for i in range(NX):
-        lap = laplace(bufp, i, wz)
-        slab = jnp.where(lane // SLAB == i, roll(lap, SLAB * i), slab)
-        lap_out[i] = lap
-        pn[i] = 2.0 * p[i] - pp[i] + c[i] * lap
-    lpk[...] = slab
-    add_source(3, source, start, wavelet, pn)
-    collect(3, md, mu, oc, oc_out)
-    out = jnp.zeros((NY, NZ), f32)
-    for i in range(NX):
-        for t, row in ((2, pp[i]), (3, p[i]), (4, pn[i])):
-            to = 4 * i + t - 1
-            out = jnp.where(lane == to, roll(row, to - REC_DEPTH), out)
-    mat[...] = out
-    mat_lo[...] = out[:16]
-    mat_hi[...] = out[16:]
-
-
-def adjoint_kernel(
-    c, q, ql, ml, mr, md, mu, lap3, lap0, q3, img, vel, noise, mat, p1, own, sent, base, bufs
+def final_kernel(
+    c, p, q, ql, ml, mr, md, mu, lap0, q3, img, vel, noise, lpk, own, sent, bufp, bufs
 ):
     keep_d, keep_u = edges()
     lane = lanes()
     wz = depth_weights()
     first = lax.axis_index("shot") % 2 == 0
+    fill(bufp, p, strip(ml, 0), strip(mr, 0), md, mu, 0, keep_d, keep_u)
     s = [c[i] * q[i] for i in range(NX)]
     fill(bufs, s, strip(ml, 128), strip(mr, 128), md, mu, 4, keep_d, keep_u)
-    m = mat[...]
-    for i in range(NX):
+    slab = jnp.zeros((NY, NZ), f32)
+    for i in range(NX):
+        lap = laplace(bufp, i, wz)
+        slab = jnp.where(lane // SLAB == i, roll(lap, SLAB * i), slab)
         q_new = 2.0 * q[i] - ql[i] + laplace(bufs, i, wz)
-        image = img[i] + lap3[i] * q3[i] + q_new * lap0[i]
+        image = img[i] + lap * q3[i] + q_new * lap0[i]
         grad = (2.0 * courant_sq) * vel[i] * image
         weighted = grad * noise[i]
         own[i] = jnp.where(first, grad, weighted)
         sent[i] = jnp.where(first, weighted, grad)
-        m = jnp.where(lane == 4 * i, roll(p1[i], 4 * i - REC_DEPTH), m)
-    base[...] = roll(m[:16], 32) + roll(m[16:], 64)
-
-
-def chunk_kernel(base, got_d, got_u, oc, out):
-    packed = base[...] + got_d[...] + roll(got_u[...], 96)
+    lpk[...] = slab
+
+
+def chunk_kernel(mat, md, mu, oc, out, traces):
+    keep_d, keep_u = edges()
+    collect(3, md, mu, oc, traces)
+    packed = jnp.where(keep_d, md[72:88], 0.0) + roll(jnp.where(keep_u, mu[72:88], 0.0), 96)
+    packed = packed + roll(mat[0:16], 32) + roll(mat[16:32], 64)
     for g in range(out.shape[0]):
-        out[g, 0:16] = oc[...]
+        out[g, 0:16] = traces[...]
         out[g, 16:32] = packed
 
 
@@ -297,12 +295,12 @@
                 v16 = jnp.concatenate([v, v, v, v], 0).astype(bf)
                 v128 = jnp.concatenate([v16] * 8, 0)
                 table[128 * part : 128 * (part + 1), at] = jnp.where(here, v128, none)
-        return carry
-
-    lax.fori_loop(0, ngx, build, 0, unroll=2)
-    sums = lax.dot_general(
-        table[...], hoty[...], (((1,), (1,)), ((), ())), preferred_element_type=f32
-    )
+        at = pl.ds(pl.multiple_of(g * 512, 512), 512)
+        return carry + lax.dot_general(
+            table[:, at], hoty[:, at], (((1,), (1,)), ((), ())), preferred_element_type=f32
+        )
+
+    sums = lax.fori_loop(0, ngx, build, jnp.zeros((384, 64), f32), unroll=ngx)
     seen = sums[0:128] + sums[128:256] + sums[256:384]
     tr = jnp.concatenate([seen, count[...]], 1).T
 
@@ -311,7 +309,7 @@
     spread_to = jnp.where(
         (k_in < 32) & (k_out == (k_in % 4) * 128 + (k_in // 4) * SLAB + REC_DEPTH), 1.0, 0.0
     )
-    dense = []
+    dense, raw = [], []
     for g in range(5):
         src = ix + (g - 2)
         ok = (src >= 0) & (src < ngx)
@@ -320,26 +318,45 @@
         m = jnp.where(ok, m, 0.0)
         s_g = roll(tr[:64], 16 - 32 * g)
         n_g = roll(tr[64:], 16 - 32 * g)
-        dense.append(n_g * m - s_g)
+        dense.append(jnp.where(lane % 4 == 3, 0.0, n_g * m) - s_g)
+        raw.append(jnp.where(lane % 4 == 0, n_g, m))
     inj[...] = jnp.dot(
-        jnp.concatenate(dense, 0), spread_to,
+        jnp.concatenate(dense + raw, 0), spread_to,
         precision=lax.Precision.HIGHEST, preferred_element_type=f32,
     )
 
     def j(n, g, lo, hi):
         return inj[64 * g + lo : 64 * g + hi, 128 * n : 128 * (n + 1)]
+
+    coef = {1: c1l, 2: cext, 3: c1r}
+    pad = jnp.zeros((16, 128), f32)
+    plane = [j(2, 5 + g, 0, 64) for g in range(5)]
+    for g in range(5):
+        x[g] = plane[g]
+    for g in range(5):
+        lo, hi = (16, 48) if g in (0, 4) else (4, 60)
+        part = j(3, 5 + g, lo, hi)
+        for k in range(1, W + 1):
+            t = SLAB * k
+            here = x[g, lo:hi]
+            after = x[g + 1, lo:hi] if g < 4 else jnp.zeros_like(here)
+            before = x[g - 1, lo:hi] if g > 0 else jnp.zeros_like(here)
+            beside = jnp.where(lane < 128 - t, roll(here, -t), roll(after, -t))
+            beside = beside + jnp.where(lane >= t, roll(here, t), roll(before, t))
+            beside = beside + x[g, lo + k : hi + k] + x[g, lo - k : hi - k]
+            part = part + CK[k] * jnp.where(lane % SLAB == REC_DEPTH, beside, 0.0)
+        c_g = (c2l, c2r)[g // 4][...] if g in (0, 4) else coef[g][lo:hi]
+        p4 = 2.0 * x[g, lo:hi] - j(1, 5 + g, lo, hi) + c_g * part
+        r3[g] = j(3, g, 0, 64)
+        r3[g, lo:hi] = r3[g, lo:hi] + j(0, 5 + g, lo, hi) * p4
 
     d = lane % SLAB
     wz = [None] + [
         (jnp.where(d < SLAB - k, CK[k], 0.0), jnp.where(d >= k, CK[k], 0.0))
         for k in range(1, W + 1)
     ]
-    coef = {1: c1l, 2: cext, 3: c1r}
-    pad = jnp.zeros((16, 128), f32)
-    for g in range(5):
-        r3[g] = j(3, g, 0, 64)
-        if g in coef:
-            x[g] = coef[g][...] * r3[g]
+    for g in coef:
+        x[g] = coef[g][...] * r3[g]
     for g, far in ((0, c2l), (4, c2r)):
         x[g, 0:16] = pad
         x[g, 16:48] = far[...] * r3[g, 16:48]
@@ -387,7 +404,7 @@
         grad_logs[i] = spread * weighted + jnp.exp(2.0 * logs[i]) / prior_var - 1.0
 
 
-def call(kernel, outs, scratch=(), smem=0, mib=4, cost=None):
+def call(kernel, outs, scratch=(), smem=0, mib=4):
     def go(*args):
         return pl.pallas_call(
             kernel,
@@ -395,9 +412,6 @@
             in_specs=[SM] * smem + [VM] * (len(args) - smem),
             out_specs=jax.tree.map(lambda _: VM, outs),
             scratch_shapes=list(scratch),
-            cost_estimate=cost and pl.CostEstimate(
-                flops=cost[0], bytes_accessed=cost[1], transcendentals=0
-            ),
             compiler_params=pltpu.CompilerParams(vmem_limit_bytes=mib * 2**20),
         )(*args)
 
@@ -445,37 +459,31 @@
         extra = {1: (keep.get("cext"),), 2: (keep.get("lap1"),)}.get(n, ())
         rows = (320, 288, 256)[n]
         outs = [sds(NY, NZ), sds(16, 128), F, F]
-        outs += [sds(rows, 128), sds(rows, 128), sds(72, 128), sds(72, 128), F]
-        if n == 0:
-            outs.append(sds(64, 128))
+        cols = (72, 72, 88)[n]
+        outs += [sds(rows, 128), sds(rows, 128), sds(cols, 128), sds(cols, 128), F]
+        if n != 1:
+            outs.append(sds(64, 128) if n == 0 else sds(NY, NZ))
         res = call(functools.partial(step_kernel, n), tuple(outs), (buf, buf), smem=3)(
             source_column, start_step, wavelet, coef, p, p_prev, q, q_later, *halos, oc, *extra
         )
         lpk, oc, q_next, p_next, xlo, xhi, ylo, yhi = res[:8]
         slabs.append(lpk)
         if n == 0:
-            keep["lap0"], keep["cext"], keep["q3"], keep["p1"] = res[8], res[9], q_next, p_next
+            keep["lap0"], keep["cext"], keep["q3"] = res[8], res[9], q_next
         if n == 1:
             keep["lap1"], keep["c"] = res[8], [ml, mr]
         if n == 2:
-            img = res[8]
+            img, mat = res[8], res[9]
             keep["c"] += [ml, mr]
         p_prev, p = p, p_next
         q_later, q = q, q_next
 
-    lpk, oc, lap3, mat, mat_lo, mat_hi = call(
-        plane_kernel,
-        (sds(NY, NZ), sds(16, 128), F, sds(NY, NZ), sds(16, NZ), sds(16, NZ)),
-        (buf, pltpu.VMEM((NX, NY, NZ), f32)),
-        smem=3,
-    )(source_column, start_step, wavelet, coef, p, p_prev, *halos, oc)
+    chunk = call(chunk_kernel, sds(ngx, 32, 128), (pltpu.VMEM((16, 128), f32),))(mat, md, mu, oc)
+    got = lax.all_to_all(chunk, "gx", 0, 0)
+    lpk, own, sent = call(final_kernel, (sds(NY, NZ), F, F), (buf, buf))(
+        coef, p, q, q_later, *halos, keep["lap0"], keep["q3"], img, vel, noise
+    )
     slabs.append(lpk)
-    mat_d, mat_u = shift(mat_hi, "gy", 1), shift(mat_lo, "gy", -1)
-    own, sent, base = call(
-        adjoint_kernel, (F, F, sds(16, NZ)), (buf,), cost=(2_000_000, 2_000_000)
-    )(
-        coef, q, q_later, *halos, lap3, keep["lap0"], keep["q3"], img, vel, noise, mat, keep["p1"]
-    )
     other = lax.ppermute(sent, "shot", [(i, i ^ 1) for i in range(nshot)])
     nrec = receiver_column.shape[1]
     bf = jnp.bfloat16
@@ -491,14 +499,12 @@
         [pltpu.VMEM((1, nrec // 128, 128), f32)] * 2 + [pltpu.VMEM((128, nrec), bf)],
         mib=12,
     )(receiver_column.reshape(-1, 128), vel, noise)
-    chunk = call(chunk_kernel, sds(ngx, 32, 128))(base, mat_d, mat_u, oc)
-    got = lax.all_to_all(chunk, "gx", 0, 0)
     g5 = pltpu.VMEM((5, 64, 128), f32)
     g48 = pltpu.VMEM((5, 48, 128), f32)
     part = call(
         last_kernel,
         sds(NX * NY + 2 * NY, NZ),
-        (pltpu.VMEM((384, nrec), bf), g5, g5, g48, g48, pltpu.VMEM((320, 512), f32)),
+        (pltpu.VMEM((384, nrec), bf), g5, g5, g48, g48, pltpu.VMEM((640, 512), f32)),
         mib=24,
     )(got, keyx, hoty, count, keep["cext"], *keep["c"], *slabs, vpk, zpk, own, other)
     every = lax.all_gather(part, "shot", axis=0)

time: 136 us -> 125 us (0.919)
  the two profiles are of different devices: /device:TPU:1 before, /device:TPU:25 now
where the time goes in v7:
time: 125 us; the launch traced here: 124 us
  starting transfers between devices  77.7 us (62%)
  Pallas kernels  15.9 us (13%)
  blocking collectives  15.9 us (13%)
  waiting for transfers between devices  9.93 us (8%)
  between operations  2.25 us (2%)
  local copies, waits for them, and re-layouts  1.52 us (1%)
    ppermute x16, starting transfers between devices, shift(): lax.ppermute(x, axis, [(i, (i + k) % n) for i in range(n) if wrap or 0 <=...  58.8 us
    pallas_call x9, Pallas kernels, go(): pl.pallas_call(kernel, out_shape=outs, in_specs=[SM] * smem + [VM] * (len...  15.9 us
    all_gather x1, blocking collectives, local(): every = lax.all_gather(part, 'shot', axis=0)  15.9 us
    ppermute x1, starting transfers between devices, local(): other = lax.ppermute(sent, 'shot', [(i, i ^ 1) for i in range(nshot)])  11.6 us
    ppermute x16, waiting for transfers between devices, shift(): lax.ppermute(x, axis, [(i, (i + k) % n) for i in range(n) if wrap or 0 <=...  9.92 us
    all_to_all x1, starting transfers between devices, local(): got = lax.all_to_all(chunk, 'gx', 0, 0)  7.39 us
  transfers between devices with their start and end apart: 18, of which 5 were waited for; matrix products, arithmetic and copies ran while one was open for 0% of the time, Pallas kernels for 2%

profile of v7, /device:TPU:25, one launch (start us, length us, event | category | flops | bytes accessed | tf_op | source)
XLA Modules:
  0.0 124.3 jit_solution(14990814624095594814)
XLA Ops:
  2.8 2.9 %collective-permute-start = (f32[256,128]{1,0:T(8,128)S(1)}, f32[256,128]{1,0:T(8,128)S(1)}, u32[]{:S(2)}, u32[]{:S(2)}) collective-permute-start(f32[256,128]{1,0:T(8,128)S(1)} %get-tuple-element.44), channel_id=1, source_target_pairs={{0,8},{8,16},{16,24},{24,32},{32,40},{40,48},{48,56},{56,64},{64,7... | collective-permute-start | bytes 393224 | tf_op jit(solution)/shard_map/ppermute | solution.py:423
  5.7 2.5 %collective-permute-start.1 = (f32[256,128]{1,0:T(8,128)S(1)}, f32[256,128]{1,0:T(8,128)S(1)}, u32[]{:S(2)}, u32[]{:S(2)}) collective-permute-start(f32[256,128]{1,0:T(8,128)S(1)} %get-tuple-element.45), channel_id=1, source_target_pairs={{8,0},{16,8},{24,16},{32,24},{40,32},{48,40},{56,48},{64,56},{72,6... | collective-permute-start | bytes 393224 | tf_op jit(solution)/shard_map/ppermute | solution.py:423
  8.2 4.0 %collective-permute-start.2 = (f32[88,128]{1,0:T(8,128)S(1)}, f32[88,128]{1,0:T(8,128)S(1)}, u32[]{:S(2)}, u32[]{:S(2)}) collective-permute-start(f32[88,128]{1,0:T(8,128)S(1)} %get-tuple-element.46), channel_id=1, source_target_pairs={{0,1},{1,2},{2,3},{3,4},{4,5},{5,6},{6,7},{7,0},{8,9},{9,10},{10,1... | collective-permute-start | bytes 135176 | tf_op jit(solution)/shard_map/ppermute | solution.py:423
  12.2 8.6 %collective-permute-start.3 = (f32[88,128]{1,0:T(8,128)S(1)}, f32[88,128]{1,0:T(8,128)S(1)}, u32[]{:S(2)}, u32[]{:S(2)}) collective-permute-start(f32[88,128]{1,0:T(8,128)S(1)} %get-tuple-element.47), channel_id=1, source_target_pairs={{0,7},{1,0},{2,1},{3,2},{4,3},{5,4},{6,5},{7,6},{8,15},{9,8},{10,9... | collective-permute-start | bytes 135176 | tf_op jit(solution)/shard_map/ppermute | solution.py:423
  22.8 1.7 %shard_map.132 = (f32[32,128]{1,0:T(8,128)S(1)}, f32[16,128]{1,0:T(8,128)S(1)}, f32[8,32,128]{2,1,0:T(8,128)S(1)}, f32[8,32,128]{2,1,0:T(8,128)S(1)}, f32[320,12...) custom-call(s32[1]{0:T(128)S(6)} %copy.14.source, ...), custom_call_target="tpu_custom_call" | custom-call | tf_op jit(solution)/shard_map/pallas_call | solution.py:409
  24.5 5.5 %collective-permute-start.4 = (f32[320,128]{1,0:T(8,128)S(1)}, f32[320,128]{1,0:T(8,128)S(1)}, u32[]{:S(2)}, u32[]{:S(2)}) collective-permute-start(f32[320,128]{1,0:T(8,128)S(1)} %get-tuple-element.51), channel_id=1, source_target_pairs={{0,8},{8,16},{16,24},{24,32},{32,40},{40,48},{48,56},{56,64},{64,7... | collective-permute-start | bytes 491528 | tf_op jit(solution)/shard_map/ppermute | solution.py:423
  30.0 1.9 %collective-permute-start.5 = (f32[320,128]{1,0:T(8,128)S(1)}, f32[320,128]{1,0:T(8,128)S(1)}, u32[]{:S(2)}, u32[]{:S(2)}) collective-permute-start(f32[320,128]{1,0:T(8,128)S(1)} %get-tuple-element.52), channel_id=1, source_target_pairs={{8,0},{16,8},{24,16},{32,24},{40,32},{48,40},{56,48},{64,56},{72,6... | collective-permute-start | bytes 491528 | tf_op jit(solution)/shard_map/ppermute | solution.py:423
  31.9 1.9 %collective-permute-start.6 = (f32[72,128]{1,0:T(8,128)S(1)}, f32[72,128]{1,0:T(8,128)S(1)}, u32[]{:S(2)}, u32[]{:S(2)}) collective-permute-start(f32[72,128]{1,0:T(8,128)S(1)} %get-tuple-element.53), channel_id=1, source_target_pairs={{0,1},{1,2},{2,3},{3,4},{4,5},{5,6},{6,7},{7,0},{8,9},{9,10},{10,1... | collective-permute-start | bytes 110600 | tf_op jit(solution)/shard_map/ppermute | solution.py:423
  33.9 4.7 %collective-permute-start.7 = (f32[72,128]{1,0:T(8,128)S(1)}, f32[72,128]{1,0:T(8,128)S(1)}, u32[]{:S(2)}, u32[]{:S(2)}) collective-permute-start(f32[72,128]{1,0:T(8,128)S(1)} %get-tuple-element.54), channel_id=1, source_target_pairs={{0,7},{1,0},{2,1},{3,2},{4,3},{5,4},{6,5},{7,6},{8,15},{9,8},{10,9... | collective-permute-start | bytes 110600 | tf_op jit(solution)/shard_map/ppermute | solution.py:423
  39.6 1.6 %shard_map.133 = (f32[32,128]{1,0:T(8,128)S(1)}, f32[16,128]{1,0:T(8,128)S(1)}, f32[8,32,128]{2,1,0:T(8,128)S(1)}, f32[8,32,128]{2,1,0:T(8,128)S(1)}, f32[288,12...) custom-call(s32[1]{0:T(128)S(6)} %copy.14.source, ...), custom_call_target="tpu_custom_call" | custom-call | tf_op jit(solution)/shard_map/pallas_call | solution.py:409
  41.2 6.1 %collective-permute-start.8 = (f32[288,128]{1,0:T(8,128)S(1)}, f32[288,128]{1,0:T(8,128)S(1)}, u32[]{:S(2)}, u32[]{:S(2)}) collective-permute-start(f32[288,128]{1,0:T(8,128)S(1)} %get-tuple-element.59), channel_id=1, source_target_pairs={{0,8},{8,16},{16,24},{24,32},{32,40},{40,48},{48,56},{56,64},{64,7... | collective-permute-start | bytes 442376 | tf_op jit(solution)/shard_map/ppermute | solution.py:423
  47.3 1.9 %collective-permute-start.9 = (f32[288,128]{1,0:T(8,128)S(1)}, f32[288,128]{1,0:T(8,128)S(1)}, u32[]{:S(2)}, u32[]{:S(2)}) collective-permute-start(f32[288,128]{1,0:T(8,128)S(1)} %get-tuple-element.60), channel_id=1, source_target_pairs={{8,0},{16,8},{24,16},{32,24},{40,32},{48,40},{56,48},{64,56},{72,6... | collective-permute-start | bytes 442376 | tf_op jit(solution)/shard_map/ppermute | solution.py:423
  49.2 3.0 %collective-permute-start.10 = (f32[72,128]{1,0:T(8,128)S(1)}, f32[72,128]{1,0:T(8,128)S(1)}, u32[]{:S(2)}, u32[]{:S(2)}) collective-permute-start(f32[72,128]{1,0:T(8,128)S(1)} %get-tuple-element.61), channel_id=1, source_target_pairs={{0,1},{1,2},{2,3},{3,4},{4,5},{5,6},{6,7},{7,0},{8,9},{9,10},{10,1... | collective-permute-start | bytes 110600 | tf_op jit(solution)/shard_map/ppermute | solution.py:423
  52.2 3.8 %collective-permute-start.11 = (f32[72,128]{1,0:T(8,128)S(1)}, f32[72,128]{1,0:T(8,128)S(1)}, u32[]{:S(2)}, u32[]{:S(2)}) collective-permute-start(f32[72,128]{1,0:T(8,128)S(1)} %get-tuple-element.62), channel_id=1, source_target_pairs={{0,7},{1,0},{2,1},{3,2},{4,3},{5,4},{6,5},{7,6},{8,15},{9,8},{10,9... | collective-permute-start | bytes 110600 | tf_op jit(solution)/shard_map/ppermute | solution.py:423
  57.1 1.9 %shard_map.134 = (f32[32,128]{1,0:T(8,128)S(1)}, f32[16,128]{1,0:T(8,128)S(1)}, f32[8,32,128]{2,1,0:T(8,128)S(1)}, f32[8,32,128]{2,1,0:T(8,128)S(1)}, f32[256,12...) custom-call(s32[1]{0:T(128)S(6)} %copy.14.source, ...), custom_call_target="tpu_custom_call" | custom-call | tf_op jit(solution)/shard_map/pallas_call | solution.py:409
  59.0 3.2 %collective-permute-start.12 = (f32[88,128]{1,0:T(8,128)S(1)}, f32[88,128]{1,0:T(8,128)S(1)}, u32[]{:S(2)}, u32[]{:S(2)}) collective-permute-start(f32[88,128]{1,0:T(8,128)S(1)} %get-tuple-element.66), channel_id=1, source_target_pairs={{0,1},{1,2},{2,3},{3,4},{4,5},{5,6},{6,7},{7,0},{8,9},{9,10},{10,1... | collective-permute-start | bytes 135176 | tf_op jit(solution)/shard_map/ppermute | solution.py:423
  62.2 3.6 %collective-permute-start.13 = (f32[88,128]{1,0:T(8,128)S(1)}, f32[88,128]{1,0:T(8,128)S(1)}, u32[]{:S(2)}, u32[]{:S(2)}) collective-permute-start(f32[88,128]{1,0:T(8,128)S(1)} %get-tuple-element.67), channel_id=1, source_target_pairs={{0,7},{1,0},{2,1},{3,2},{4,3},{5,4},{6,5},{7,6},{8,15},{9,8},{10,9... | collective-permute-start | bytes 135176 | tf_op jit(solution)/shard_map/ppermute | solution.py:423
  67.8 7.4 %all-to-all-start = ((f32[16,32,128]{2,1,0:T(8,128)}), f32[16,32,128]{2,1,0:T(8,128)S(1)}, u32[]{:S(2)}, u32[]{:S(2)}) async-start(f32[16,32,128]{2,1,0:T(8,128)} %shard_map.135), calls=%async_computation | async-start | bytes 524288 | tf_op jit(solution)/shard_map/all_to_all | solution.py:482
  75.2 3.1 %collective-permute-start.14 = (f32[256,128]{1,0:T(8,128)S(1)}, f32[256,128]{1,0:T(8,128)S(1)}, u32[]{:S(2)}, u32[]{:S(2)}) collective-permute-start(f32[256,128]{1,0:T(8,128)S(1)} %get-tuple-element.77), channel_id=1, source_target_pairs={{0,8},{8,16},{16,24},{24,32},{32,40},{40,48},{48,56},{56,64},{64,7... | collective-permute-start | bytes 393224 | tf_op jit(solution)/shard_map/ppermute | solution.py:423
  78.3 2.2 %collective-permute-start.15 = (f32[256,128]{1,0:T(8,128)S(1)}, f32[256,128]{1,0:T(8,128)S(1)}, u32[]{:S(2)}, u32[]{:S(2)}) collective-permute-start(f32[256,128]{1,0:T(8,128)S(1)} %get-tuple-element.78), channel_id=1, source_target_pairs={{8,0},{16,8},{24,16},{32,24},{40,32},{48,40},{56,48},{64,56},{72,6... | collective-permute-start | bytes 393224 | tf_op jit(solution)/shard_map/ppermute | solution.py:423
  80.9 6.2 %collective-permute-done.15.mr = f32[256,128]{1,0:T(8,128)S(1)} collective-permute-done((f32[256,128]{1,0:T(8,128)S(1)}, f32[256,128]{1,0:T(8,128)S(1)}, u32[]{:S(2)}, u32[]{:S(2)}) %collective-permute-start.15) | collective-permute-done | bytes 131104 | tf_op jit(solution)/shard_map/ppermute | solution.py:423
  88.2 11.6 %collective-permute-start.16 = (f32[8,32,128]{2,1,0:T(8,128)S(1)}, f32[8,32,128]{2,1,0:T(8,128)S(1)}, u32[]{:S(2)}, u32[]{:S(2)}) collective-permute-start(f32[8,32,128]{2,1,0:T(8,128)S(1)} %get-tuple-element.85), channel_id=1, source_target_pairs={{0,128},{128,0},{256,384},{384,256},{1,129},{129,1},{257,385},{385... | collective-permute-start | bytes 393224 | tf_op jit(solution)/shard_map/ppermute | solution.py:487
  101.0 6.7 %shard_map.138 = f32[320,128]{1,0:T(8,128)S(1)} custom-call(f32[16,32,128]{2,1,0:T(8,128)S(1)} %all-to-all-done.got, f32[64,128]{1,0:T(8,128)S(1)} %get-tuple-element.69.keyx, bf16[64,8192]{1,0:T(8,128)(2,1)S(1)} %get-tuple-element.70.hoty, f32[128,64]{1,0:T(8,128)S(1)} %get-tuple-element.71.count, f32[64,128]{1,0:T(8,128)S(1)} %get-tuple-element.56.rest_0_.cext, ...), custom_call_target="tpu_custom_call" | custom-call | tf_op jit(solution)/shard_map/pallas_call | solution.py:409
  107.7 15.9 %all-gather = f32[1280,128]{1,0:T(8,128)S(1)} all-gather(f32[320,128]{1,0:T(8,128)S(1)} %shard_map.138), channel_id=2, replica_groups=mesh['shot'=4,'gx'=16,'gy'=8] {'shot'}, dimensions={0}, use_global_device_ids=true | all-gather | bytes 819200 | tf_op jit(solution)/shard_map/all_gather | solution.py:510
  (42 shorter events, 10.3 us)
Async XLA Ops:
  2.7 19.5 %copy-start.1 = (f32[1,8,32,128]{3,2,1,0:T(8,128)S(1)}, f32[1,8,32,128]{3,2,1,0:T(8,128)}, u32[]{:S(2)}) copy-start(f32[1,8,32,128]{3,2,1,0:T(8,128)} %param.18) | copy-start | bytes 393220
  2.7 19.5 %copy-start.4 = (f32[1,8,32,128]{3,2,1,0:T(8,128)S(1)}, f32[1,8,32,128]{3,2,1,0:T(8,128)}, u32[]{:S(2)}) copy-start(f32[1,8,32,128]{3,2,1,0:T(8,128)} %param.15) | copy-start | bytes 393220
  2.7 19.5 %copy-start.5 = (f32[1,8,32,128]{3,2,1,0:T(8,128)S(1)}, f32[1,8,32,128]{3,2,1,0:T(8,128)}, u32[]{:S(2)}) copy-start(f32[1,8,32,128]{3,2,1,0:T(8,128)} %param.17) | copy-start | bytes 393220
  2.8 19.3 %collective-permute-start = (f32[256,128]{1,0:T(8,128)S(1)}, f32[256,128]{1,0:T(8,128)S(1)}, u32[]{:S(2)}, u32[]{:S(2)}) collective-permute-start(f32[256,128]{1,0:T(8,128)S(1)} %get-tuple-element.44), channel_id=1, source_target_pairs={{0,8},{8,16},{16,24},{24,32},{32,40},{40,48},{48,56},{56,64},{64,7... | collective-permute-start | bytes 393224 | tf_op jit(solution)/shard_map/ppermute | solution.py:423
  5.7 16.4 %collective-permute-start.1 = (f32[256,128]{1,0:T(8,128)S(1)}, f32[256,128]{1,0:T(8,128)S(1)}, u32[]{:S(2)}, u32[]{:S(2)}) collective-permute-start(f32[256,128]{1,0:T(8,128)S(1)} %get-tuple-element.45), channel_id=1, source_target_pairs={{8,0},{16,8},{24,16},{32,24},{40,32},{48,40},{56,48},{64,56},{72,6... | collective-permute-start | bytes 393224 | tf_op jit(solution)/shard_map/ppermute | solution.py:423
  8.2 13.9 %collective-permute-start.2 = (f32[88,128]{1,0:T(8,128)S(1)}, f32[88,128]{1,0:T(8,128)S(1)}, u32[]{:S(2)}, u32[]{:S(2)}) collective-permute-start(f32[88,128]{1,0:T(8,128)S(1)} %get-tuple-element.46), channel_id=1, source_target_pairs={{0,1},{1,2},{2,3},{3,4},{4,5},{5,6},{6,7},{7,0},{8,9},{9,10},{10,1... | collective-permute-start | bytes 135176 | tf_op jit(solution)/shard_map/ppermute | solution.py:423
  12.2 9.9 %collective-permute-start.3 = (f32[88,128]{1,0:T(8,128)S(1)}, f32[88,128]{1,0:T(8,128)S(1)}, u32[]{:S(2)}, u32[]{:S(2)}) collective-permute-start(f32[88,128]{1,0:T(8,128)S(1)} %get-tuple-element.47), channel_id=1, source_target_pairs={{0,7},{1,0},{2,1},{3,2},{4,3},{5,4},{6,5},{7,6},{8,15},{9,8},{10,9... | collective-permute-start | bytes 135176 | tf_op jit(solution)/shard_map/ppermute | solution.py:423
  24.5 15.1 %collective-permute-start.4 = (f32[320,128]{1,0:T(8,128)S(1)}, f32[320,128]{1,0:T(8,128)S(1)}, u32[]{:S(2)}, u32[]{:S(2)}) collective-permute-start(f32[320,128]{1,0:T(8,128)S(1)} %get-tuple-element.51), channel_id=1, source_target_pairs={{0,8},{8,16},{16,24},{24,32},{32,40},{40,48},{48,56},{56,64},{64,7... | collective-permute-start | bytes 491528 | tf_op jit(solution)/shard_map/ppermute | solution.py:423
  30.0 9.6 %collective-permute-start.5 = (f32[320,128]{1,0:T(8,128)S(1)}, f32[320,128]{1,0:T(8,128)S(1)}, u32[]{:S(2)}, u32[]{:S(2)}) collective-permute-start(f32[320,128]{1,0:T(8,128)S(1)} %get-tuple-element.52), channel_id=1, source_target_pairs={{8,0},{16,8},{24,16},{32,24},{40,32},{48,40},{56,48},{64,56},{72,6... | collective-permute-start | bytes 491528 | tf_op jit(solution)/shard_map/ppermute | solution.py:423
  31.9 6.6 %collective-permute-start.6 = (f32[72,128]{1,0:T(8,128)S(1)}, f32[72,128]{1,0:T(8,128)S(1)}, u32[]{:S(2)}, u32[]{:S(2)}) collective-permute-start(f32[72,128]{1,0:T(8,128)S(1)} %get-tuple-element.53), channel_id=1, source_target_pairs={{0,1},{1,2},{2,3},{3,4},{4,5},{5,6},{6,7},{7,0},{8,9},{9,10},{10,1... | collective-permute-start | bytes 110600 | tf_op jit(solution)/shard_map/ppermute | solution.py:423
  33.9 5.7 %collective-permute-start.7 = (f32[72,128]{1,0:T(8,128)S(1)}, f32[72,128]{1,0:T(8,128)S(1)}, u32[]{:S(2)}, u32[]{:S(2)}) collective-permute-start(f32[72,128]{1,0:T(8,128)S(1)} %get-tuple-element.54), channel_id=1, source_target_pairs={{0,7},{1,0},{2,1},{3,2},{4,3},{5,4},{6,5},{7,6},{8,15},{9,8},{10,9... | collective-permute-start | bytes 110600 | tf_op jit(solution)/shard_map/ppermute | solution.py:423
  41.2 15.8 %collective-permute-start.8 = (f32[288,128]{1,0:T(8,128)S(1)}, f32[288,128]{1,0:T(8,128)S(1)}, u32[]{:S(2)}, u32[]{:S(2)}) collective-permute-start(f32[288,128]{1,0:T(8,128)S(1)} %get-tuple-element.59), channel_id=1, source_target_pairs={{0,8},{8,16},{16,24},{24,32},{32,40},{40,48},{48,56},{56,64},{64,7... | collective-permute-start | bytes 442376 | tf_op jit(solution)/shard_map/ppermute | solution.py:423
  47.3 9.8 %collective-permute-start.9 = (f32[288,128]{1,0:T(8,128)S(1)}, f32[288,128]{1,0:T(8,128)S(1)}, u32[]{:S(2)}, u32[]{:S(2)}) collective-permute-start(f32[288,128]{1,0:T(8,128)S(1)} %get-tuple-element.60), channel_id=1, source_target_pairs={{8,0},{16,8},{24,16},{32,24},{40,32},{48,40},{56,48},{64,56},{72,6... | collective-permute-start | bytes 442376 | tf_op jit(solution)/shard_map/ppermute | solution.py:423
  49.2 6.8 %collective-permute-start.10 = (f32[72,128]{1,0:T(8,128)S(1)}, f32[72,128]{1,0:T(8,128)S(1)}, u32[]{:S(2)}, u32[]{:S(2)}) collective-permute-start(f32[72,128]{1,0:T(8,128)S(1)} %get-tuple-element.61), channel_id=1, source_target_pairs={{0,1},{1,2},{2,3},{3,4},{4,5},{5,6},{6,7},{7,0},{8,9},{9,10},{10,1... | collective-permute-start | bytes 110600 | tf_op jit(solution)/shard_map/ppermute | solution.py:423
  52.2 4.8 %collective-permute-start.11 = (f32[72,128]{1,0:T(8,128)S(1)}, f32[72,128]{1,0:T(8,128)S(1)}, u32[]{:S(2)}, u32[]{:S(2)}) collective-permute-start(f32[72,128]{1,0:T(8,128)S(1)} %get-tuple-element.62), channel_id=1, source_target_pairs={{0,7},{1,0},{2,1},{3,2},{4,3},{5,4},{6,5},{7,6},{8,15},{9,8},{10,9... | collective-permute-start | bytes 110600 | tf_op jit(solution)/shard_map/ppermute | solution.py:423
  59.0 6.8 %collective-permute-start.12 = (f32[88,128]{1,0:T(8,128)S(1)}, f32[88,128]{1,0:T(8,128)S(1)}, u32[]{:S(2)}, u32[]{:S(2)}) collective-permute-start(f32[88,128]{1,0:T(8,128)S(1)} %get-tuple-element.66), channel_id=1, source_target_pairs={{0,1},{1,2},{2,3},{3,4},{4,5},{5,6},{6,7},{7,0},{8,9},{9,10},{10,1... | collective-permute-start | bytes 135176 | tf_op jit(solution)/shard_map/ppermute | solution.py:423
  62.2 4.8 %collective-permute-start.13 = (f32[88,128]{1,0:T(8,128)S(1)}, f32[88,128]{1,0:T(8,128)S(1)}, u32[]{:S(2)}, u32[]{:S(2)}) collective-permute-start(f32[88,128]{1,0:T(8,128)S(1)} %get-tuple-element.67), channel_id=1, source_target_pairs={{0,7},{1,0},{2,1},{3,2},{4,3},{5,4},{6,5},{7,6},{8,15},{9,8},{10,9... | collective-permute-start | bytes 135176 | tf_op jit(solution)/shard_map/ppermute | solution.py:423
  67.8 19.3 %copy-start.2 = (f32[1,8,32,128]{3,2,1,0:T(8,128)S(1)}, f32[1,8,32,128]{3,2,1,0:T(8,128)}, u32[]{:S(2)}) copy-start(f32[1,8,32,128]{3,2,1,0:T(8,128)} %param.14) | copy-start | bytes 393220
  67.8 33.1 %all-to-all-start = ((f32[16,32,128]{2,1,0:T(8,128)}), f32[16,32,128]{2,1,0:T(8,128)S(1)}, u32[]{:S(2)}, u32[]{:S(2)}) async-start(f32[16,32,128]{2,1,0:T(8,128)} %shard_map.135), calls=%async_computation | async-start | bytes 524288 | tf_op jit(solution)/shard_map/all_to_all | solution.py:482
  75.2 5.7 %collective-permute-start.14 = (f32[256,128]{1,0:T(8,128)S(1)}, f32[256,128]{1,0:T(8,128)S(1)}, u32[]{:S(2)}, u32[]{:S(2)}) collective-permute-start(f32[256,128]{1,0:T(8,128)S(1)} %get-tuple-element.77), channel_id=1, source_target_pairs={{0,8},{8,16},{16,24},{24,32},{32,40},{40,48},{48,56},{56,64},{64,7... | collective-permute-start | bytes 393224 | tf_op jit(solution)/shard_map/ppermute | solution.py:423
  78.3 8.8 %collective-permute-start.15 = (f32[256,128]{1,0:T(8,128)S(1)}, f32[256,128]{1,0:T(8,128)S(1)}, u32[]{:S(2)}, u32[]{:S(2)}) collective-permute-start(f32[256,128]{1,0:T(8,128)S(1)} %get-tuple-element.78), channel_id=1, source_target_pairs={{8,0},{16,8},{24,16},{32,24},{40,32},{48,40},{56,48},{64,56},{72,6... | collective-permute-start | bytes 393224 | tf_op jit(solution)/shard_map/ppermute | solution.py:423
  87.1 12.7 %copy-start.6 = (s32[1,8192]{1,0:T(1,128)S(1)}, s32[1,8192]{1,0:T(1,128)}, u32[]{:S(2)}) copy-start(s32[1,8192]{1,0:T(1,128)} %param.21) | copy-start | bytes 98308
  88.2 12.7 %collective-permute-start.16 = (f32[8,32,128]{2,1,0:T(8,128)S(1)}, f32[8,32,128]{2,1,0:T(8,128)S(1)}, u32[]{:S(2)}, u32[]{:S(2)}) collective-permute-start(f32[8,32,128]{2,1,0:T(8,128)S(1)} %get-tuple-element.85), channel_id=1, source_target_pairs={{0,128},{128,0},{256,384},{384,256},{1,129},{129,1},{257,385},{385... | collective-permute-start | bytes 393224 | tf_op jit(solution)/shard_map/ppermute | solution.py:487
  107.6 15.9 %copy-start.3 = (f32[8,32,128]{2,1,0:T(8,128)S(1)}, f32[8,32,128]{2,1,0:T(8,128)}, u32[]{:S(2)}) copy-start(f32[8,32,128]{2,1,0:T(8,128)} %logs.1) | copy-start | bytes 393220
  (3 other events, 2.4 us)

commit v8 on v7

--- a/solution.py
+++ b/solution.py
@@ -192,7 +192,8 @@
 
 
 def final_kernel(
-    c, p, q, ql, ml, mr, md, mu, lap0, q3, img, vel, noise, lpk, own, sent, bufp, bufs
+    c, p, q, ql, ml, mr, md, mu, lap0, q3, img, vel, noise, image_in, driven, vpk, zpk,
+    own, sent, part, bufp, bufs,
 ):
     keep_d, keep_u = edges()
     lane = lanes()
@@ -211,7 +212,9 @@
         weighted = grad * noise[i]
         own[i] = jnp.where(first, grad, weighted)
         sent[i] = jnp.where(first, weighted, grad)
-    lpk[...] = slab
+    grad = (2.0 * courant_sq) * vpk[...] * (image_in[...] + driven[...] * slab)
+    part[0:NY] = grad
+    part[NY : 2 * NY] = grad * zpk[...]
 
 
 def chunk_kernel(mat, md, mu, oc, out, traces):
@@ -239,7 +242,7 @@
     return out
 
 
-def table_kernel(rec, vel, noise, keyx, hoty, count, vpk, zpk, cols, rows, hot):
+def table_kernel(rec, vel, noise, keyx, keyy, count, vpk, zpk, cols, rows, hot, hoty):
     ix, iy, ngy = lax.axis_index("gx"), lax.axis_index("gy"), lax.axis_size("gy")
     half = ngy // 2
     bits = (NY * ngy).bit_length() - 1
@@ -261,8 +264,9 @@
         key = jnp.where(low, rows[0, a, :], rows[0, b, :])
         keyx[g : g + 1] = key
         hot[:, 128 * g : 128 * (g + 1)] = jnp.where(row4 == key.astype(bf), one, none)
-        here = jnp.where(low, cols[0, a, :], cols[0, b, :]).astype(bf)
-        hoty[:, 128 * g : 128 * (g + 1)] = jnp.where(coly == here, one, none)
+        key = jnp.where(low, cols[0, a, :], cols[0, b, :])
+        keyy[g : g + 1] = key
+        hoty[:, 128 * g : 128 * (g + 1)] = jnp.where(coly == key.astype(bf), one, none)
     count[...] = lax.dot_general(
         hot[...], hoty[...], (((1,), (1,)), ((), ())), preferred_element_type=f32
     )
@@ -271,8 +275,7 @@
 
 
 def last_kernel(
-    got, keyx, hoty, count, cext, ml1, mr1, ml2, mr2, lp0, lp1, lp2, lp3, vpk, zpk, own, other,
-    out, table, x, r3, r2, r1, inj,
+    got, keyx, keyy, count, cext, ml1, mr1, ml2, mr2, lp0, lp1, lp2, image, driven, table, hoty, x, r3, r2, r1, inj,
 ):
     ngx = got.shape[0]
     lane = lanes()
@@ -281,7 +284,8 @@
     c2l, c2r = ml2.at[256:288], mr2.at[256:288]
     bf = jnp.bfloat16
     row4 = (lax.broadcasted_iota(jnp.int32, (128, 128), 0) // 4).astype(f32).astype(bf)
-    none = jnp.zeros((), bf)
+    coly = lax.broadcasted_iota(jnp.int32, (64, 128), 0).astype(f32).astype(bf)
+    one, none = jnp.ones((), bf), jnp.zeros((), bf)
 
     def build(g, carry):
         for rp in range(4):
@@ -291,6 +295,7 @@
             mid = (val - hi).astype(bf).astype(f32)
             low = val - hi - mid
             here = row4 == keyx[pl.ds(4 * g + rp, 1), :].astype(bf)
+            hoty[:, at] = jnp.where(coly == keyy[pl.ds(4 * g + rp, 1), :].astype(bf), one, none)
             for part, v in enumerate((hi, mid, low)):
                 v16 = jnp.concatenate([v, v, v, v], 0).astype(bf)
                 v128 = jnp.concatenate([v16] * 8, 0)
@@ -374,15 +379,15 @@
     for g in (1, 2, 3):
         x[g, 8:56] = coef[g][8:56] * r1[g]
     r0 = 2.0 * r1[2, 8:40] - r2[2, 8:40] + lap_packed(x, 2, 16, 48, wz) + j(0, 2, 16, 48)
-    corr = r0 * lp0[...] + r1[2, 8:40] * lp1[...] + r2[2, 8:40] * lp2[...]
-    corr = corr + r3[2, 16:48] * lp3[...]
-
+    image[...] = r0 * lp0[...] + r1[2, 8:40] * lp1[...] + r2[2, 8:40] * lp2[...]
+    driven[...] = r3[2, 16:48]
+
+
+def tail_kernel(own, other, part, out):
     cells = NX * NY
     for i in range(NX):
         out[NY * i : NY * (i + 1)] = own[i] + other[i]
-    grad = (2.0 * courant_sq) * vpk[...] * corr
-    out[cells : cells + NY] = grad
-    out[cells + NY : cells + 2 * NY] = grad * zpk[...]
+    out[cells : cells + 2 * NY] = part[...]
 
 
 def sum_kernel(every, logs, grad_mean, grad_logs):
@@ -480,33 +485,35 @@
 
     chunk = call(chunk_kernel, sds(ngx, 32, 128), (pltpu.VMEM((16, 128), f32),))(mat, md, mu, oc)
     got = lax.all_to_all(chunk, "gx", 0, 0)
-    lpk, own, sent = call(final_kernel, (sds(NY, NZ), F, F), (buf, buf))(
-        coef, p, q, q_later, *halos, keep["lap0"], keep["q3"], img, vel, noise
-    )
-    slabs.append(lpk)
-    other = lax.ppermute(sent, "shot", [(i, i ^ 1) for i in range(nshot)])
     nrec = receiver_column.shape[1]
     bf = jnp.bfloat16
-    keyx, hoty, count, vpk, zpk = call(
+    keyx, keyy, count, vpk, zpk = call(
         table_kernel,
         (
             sds(nrec // 128, 128),
-            jax.ShapeDtypeStruct((64, nrec), bf),
+            sds(nrec // 128, 128),
             sds(128, 64),
             sds(NY, NZ),
             sds(NY, NZ),
         ),
-        [pltpu.VMEM((1, nrec // 128, 128), f32)] * 2 + [pltpu.VMEM((128, nrec), bf)],
+        [pltpu.VMEM((1, nrec // 128, 128), f32)] * 2
+        + [pltpu.VMEM((128, nrec), bf), pltpu.VMEM((64, nrec), bf)],
         mib=12,
     )(receiver_column.reshape(-1, 128), vel, noise)
     g5 = pltpu.VMEM((5, 64, 128), f32)
     g48 = pltpu.VMEM((5, 48, 128), f32)
-    part = call(
+    image_in, driven = call(
         last_kernel,
-        sds(NX * NY + 2 * NY, NZ),
-        (pltpu.VMEM((384, nrec), bf), g5, g5, g48, g48, pltpu.VMEM((640, 512), f32)),
+        (sds(NY, NZ), sds(NY, NZ)),
+        (pltpu.VMEM((384, nrec), bf), pltpu.VMEM((64, nrec), bf), g5, g5, g48, g48, pltpu.VMEM((640, 512), f32)),
         mib=24,
-    )(got, keyx, hoty, count, keep["cext"], *keep["c"], *slabs, vpk, zpk, own, other)
+    )(got, keyx, keyy, count, keep["cext"], *keep["c"], *slabs)
+    own, sent, part = call(final_kernel, (F, F, sds(2 * NY, NZ)), (buf, buf))(
+        coef, p, q, q_later, *halos, keep["lap0"], keep["q3"], img, vel, noise,
+        image_in, driven, vpk, zpk,
+    )
+    other = lax.ppermute(sent, "shot", [(i, i ^ 1) for i in range(nshot)])
+    part = call(tail_kernel, sds(NX * NY + 2 * NY, NZ))(own, other, part)
     every = lax.all_gather(part, "shot", axis=0)
     return call(sum_kernel, (F, F))(every, log_scale)
 

time: 125 us -> 122 us (0.976)
  the two profiles are of different devices: /device:TPU:25 before, /device:TPU:3 now
where the time goes in v8:
time: 122 us; the launch traced here: 121 us
  starting transfers between devices  80.3 us (66%)
  Pallas kernels  16.1 us (13%)
  blocking collectives  15.4 us (13%)
  waiting for transfers between devices  4.27 us (3%)
  between operations  2.27 us (2%)
  local copies, waits for them, and re-layouts  1.52 us (1%)
    ppermute x16, starting transfers between devices, shift(): lax.ppermute(x, axis, [(i, (i + k) % n) for i in range(n) if wrap or 0 <=...  64.8 us
    pallas_call x10, Pallas kernels, go(): pl.pallas_call(kernel, out_shape=outs, in_specs=[SM] * smem + [VM] * (len...  16.1 us
    all_gather x1, blocking collectives, local(): every = lax.all_gather(part, 'shot', axis=0)  15.4 us
    ppermute x1, starting transfers between devices, local(): other = lax.ppermute(sent, 'shot', [(i, i ^ 1) for i in range(nshot)])  11.1 us
    all_to_all x1, starting transfers between devices, local(): got = lax.all_to_all(chunk, 'gx', 0, 0)  4.42 us
    ppermute x16, waiting for transfers between devices, shift(): lax.ppermute(x, axis, [(i, (i + k) % n) for i in range(n) if wrap or 0 <=...  3.31 us
  transfers between devices with their start and end apart: 18, of which 4 were waited for; matrix products, arithmetic and copies ran while one was open for 0% of the time, Pallas kernels for 7%

profile of v8, /device:TPU:3, one launch (start us, length us, event | category | flops | bytes accessed | tf_op | source)
XLA Modules:
  0.0 121.0 jit_solution(4346843149799297094)
XLA Ops:
  2.8 3.3 %collective-permute-start = (f32[256,128]{1,0:T(8,128)S(1)}, f32[256,128]{1,0:T(8,128)S(1)}, u32[]{:S(2)}, u32[]{:S(2)}) collective-permute-start(f32[256,128]{1,0:T(8,128)S(1)} %get-tuple-element.46), channel_id=1, source_target_pairs={{0,8},{8,16},{16,24},{24,32},{32,40},{40,48},{48,56},{56,64},{64,7... | collective-permute-start | bytes 393224 | tf_op jit(solution)/shard_map/ppermute | solution.py:428
  6.1 4.8 %collective-permute-start.1 = (f32[256,128]{1,0:T(8,128)S(1)}, f32[256,128]{1,0:T(8,128)S(1)}, u32[]{:S(2)}, u32[]{:S(2)}) collective-permute-start(f32[256,128]{1,0:T(8,128)S(1)} %get-tuple-element.47), channel_id=1, source_target_pairs={{8,0},{16,8},{24,16},{32,24},{40,32},{48,40},{56,48},{64,56},{72,6... | collective-permute-start | bytes 393224 | tf_op jit(solution)/shard_map/ppermute | solution.py:428
  10.9 4.0 %collective-permute-start.2 = (f32[88,128]{1,0:T(8,128)S(1)}, f32[88,128]{1,0:T(8,128)S(1)}, u32[]{:S(2)}, u32[]{:S(2)}) collective-permute-start(f32[88,128]{1,0:T(8,128)S(1)} %get-tuple-element.48), channel_id=1, source_target_pairs={{0,1},{1,2},{2,3},{3,4},{4,5},{5,6},{6,7},{7,0},{8,9},{9,10},{10,1... | collective-permute-start | bytes 135176 | tf_op jit(solution)/shard_map/ppermute | solution.py:428
  14.9 8.6 %collective-permute-start.3 = (f32[88,128]{1,0:T(8,128)S(1)}, f32[88,128]{1,0:T(8,128)S(1)}, u32[]{:S(2)}, u32[]{:S(2)}) collective-permute-start(f32[88,128]{1,0:T(8,128)S(1)} %get-tuple-element.49), channel_id=1, source_target_pairs={{0,7},{1,0},{2,1},{3,2},{4,3},{5,4},{6,5},{7,6},{8,15},{9,8},{10,9... | collective-permute-start | bytes 135176 | tf_op jit(solution)/shard_map/ppermute | solution.py:428
  25.5 1.7 %shard_map.132 = (f32[32,128]{1,0:T(8,128)S(1)}, f32[16,128]{1,0:T(8,128)S(1)}, f32[8,32,128]{2,1,0:T(8,128)S(1)}, f32[8,32,128]{2,1,0:T(8,128)S(1)}, f32[320,12...) custom-call(s32[1]{0:T(128)S(6)} %copy.14.source, ...), custom_call_target="tpu_custom_call" | custom-call | tf_op jit(solution)/shard_map/pallas_call | solution.py:414
  27.2 1.9 %collective-permute-start.4 = (f32[320,128]{1,0:T(8,128)S(1)}, f32[320,128]{1,0:T(8,128)S(1)}, u32[]{:S(2)}, u32[]{:S(2)}) collective-permute-start(f32[320,128]{1,0:T(8,128)S(1)} %get-tuple-element.53), channel_id=1, source_target_pairs={{0,8},{8,16},{16,24},{24,32},{32,40},{40,48},{48,56},{56,64},{64,7... | collective-permute-start | bytes 491528 | tf_op jit(solution)/shard_map/ppermute | solution.py:428
  29.2 6.1 %collective-permute-start.5 = (f32[320,128]{1,0:T(8,128)S(1)}, f32[320,128]{1,0:T(8,128)S(1)}, u32[]{:S(2)}, u32[]{:S(2)}) collective-permute-start(f32[320,128]{1,0:T(8,128)S(1)} %get-tuple-element.54), channel_id=1, source_target_pairs={{8,0},{16,8},{24,16},{32,24},{40,32},{48,40},{56,48},{64,56},{72,6... | collective-permute-start | bytes 491528 | tf_op jit(solution)/shard_map/ppermute | solution.py:428
  35.2 1.9 %collective-permute-start.6 = (f32[72,128]{1,0:T(8,128)S(1)}, f32[72,128]{1,0:T(8,128)S(1)}, u32[]{:S(2)}, u32[]{:S(2)}) collective-permute-start(f32[72,128]{1,0:T(8,128)S(1)} %get-tuple-element.55), channel_id=1, source_target_pairs={{0,1},{1,2},{2,3},{3,4},{4,5},{5,6},{6,7},{7,0},{8,9},{9,10},{10,1... | collective-permute-start | bytes 110600 | tf_op jit(solution)/shard_map/ppermute | solution.py:428
  37.1 4.7 %collective-permute-start.7 = (f32[72,128]{1,0:T(8,128)S(1)}, f32[72,128]{1,0:T(8,128)S(1)}, u32[]{:S(2)}, u32[]{:S(2)}) collective-permute-start(f32[72,128]{1,0:T(8,128)S(1)} %get-tuple-element.56), channel_id=1, source_target_pairs={{0,7},{1,0},{2,1},{3,2},{4,3},{5,4},{6,5},{7,6},{8,15},{9,8},{10,9... | collective-permute-start | bytes 110600 | tf_op jit(solution)/shard_map/ppermute | solution.py:428
  42.9 1.6 %shard_map.133 = (f32[32,128]{1,0:T(8,128)S(1)}, f32[16,128]{1,0:T(8,128)S(1)}, f32[8,32,128]{2,1,0:T(8,128)S(1)}, f32[8,32,128]{2,1,0:T(8,128)S(1)}, f32[288,12...) custom-call(s32[1]{0:T(128)S(6)} %copy.14.source, ...), custom_call_target="tpu_custom_call" | custom-call | tf_op jit(solution)/shard_map/pallas_call | solution.py:414
  44.5 1.9 %collective-permute-start.8 = (f32[288,128]{1,0:T(8,128)S(1)}, f32[288,128]{1,0:T(8,128)S(1)}, u32[]{:S(2)}, u32[]{:S(2)}) collective-permute-start(f32[288,128]{1,0:T(8,128)S(1)} %get-tuple-element.61), channel_id=1, source_target_pairs={{0,8},{8,16},{16,24},{24,32},{32,40},{40,48},{48,56},{56,64},{64,7... | collective-permute-start | bytes 442376 | tf_op jit(solution)/shard_map/ppermute | solution.py:428
  46.4 6.1 %collective-permute-start.9 = (f32[288,128]{1,0:T(8,128)S(1)}, f32[288,128]{1,0:T(8,128)S(1)}, u32[]{:S(2)}, u32[]{:S(2)}) collective-permute-start(f32[288,128]{1,0:T(8,128)S(1)} %get-tuple-element.62), channel_id=1, source_target_pairs={{8,0},{16,8},{24,16},{32,24},{40,32},{48,40},{56,48},{64,56},{72,6... | collective-permute-start | bytes 442376 | tf_op jit(solution)/shard_map/ppermute | solution.py:428
  52.5 3.0 %collective-permute-start.10 = (f32[72,128]{1,0:T(8,128)S(1)}, f32[72,128]{1,0:T(8,128)S(1)}, u32[]{:S(2)}, u32[]{:S(2)}) collective-permute-start(f32[72,128]{1,0:T(8,128)S(1)} %get-tuple-element.63), channel_id=1, source_target_pairs={{0,1},{1,2},{2,3},{3,4},{4,5},{5,6},{6,7},{7,0},{8,9},{9,10},{10,1... | collective-permute-start | bytes 110600 | tf_op jit(solution)/shard_map/ppermute | solution.py:428
  55.5 3.8 %collective-permute-start.11 = (f32[72,128]{1,0:T(8,128)S(1)}, f32[72,128]{1,0:T(8,128)S(1)}, u32[]{:S(2)}, u32[]{:S(2)}) collective-permute-start(f32[72,128]{1,0:T(8,128)S(1)} %get-tuple-element.64), channel_id=1, source_target_pairs={{0,7},{1,0},{2,1},{3,2},{4,3},{5,4},{6,5},{7,6},{8,15},{9,8},{10,9... | collective-permute-start | bytes 110600 | tf_op jit(solution)/shard_map/ppermute | solution.py:428
  60.4 1.9 %shard_map.134 = (f32[32,128]{1,0:T(8,128)S(1)}, f32[16,128]{1,0:T(8,128)S(1)}, f32[8,32,128]{2,1,0:T(8,128)S(1)}, f32[8,32,128]{2,1,0:T(8,128)S(1)}, f32[256,12...) custom-call(s32[1]{0:T(128)S(6)} %copy.14.source, ...), custom_call_target="tpu_custom_call" | custom-call | tf_op jit(solution)/shard_map/pallas_call | solution.py:414
  62.3 3.2 %collective-permute-start.14 = (f32[88,128]{1,0:T(8,128)S(1)}, f32[88,128]{1,0:T(8,128)S(1)}, u32[]{:S(2)}, u32[]{:S(2)}) collective-permute-start(f32[88,128]{1,0:T(8,128)S(1)} %get-tuple-element.71), channel_id=1, source_target_pairs={{0,1},{1,2},{2,3},{3,4},{4,5},{5,6},{6,7},{7,0},{8,9},{9,10},{10,1... | collective-permute-start | bytes 135176 | tf_op jit(solution)/shard_map/ppermute | solution.py:428
  65.5 3.6 %collective-permute-start.15 = (f32[88,128]{1,0:T(8,128)S(1)}, f32[88,128]{1,0:T(8,128)S(1)}, u32[]{:S(2)}, u32[]{:S(2)}) collective-permute-start(f32[88,128]{1,0:T(8,128)S(1)} %get-tuple-element.72), channel_id=1, source_target_pairs={{0,7},{1,0},{2,1},{3,2},{4,3},{5,4},{6,5},{7,6},{8,15},{9,8},{10,9... | collective-permute-start | bytes 135176 | tf_op jit(solution)/shard_map/ppermute | solution.py:428
  69.1 1.2 %collective-permute-done.15.mu = f32[88,128]{1,0:T(8,128)S(1)} collective-permute-done((f32[88,128]{1,0:T(8,128)S(1)}, f32[88,128]{1,0:T(8,128)S(1)}, u32[]{:S(2)}, u32[]{:S(2)}) %collective-permute-start.15) | collective-permute-done | bytes 45088 | tf_op jit(solution)/shard_map/ppermute | solution.py:428
  71.1 4.4 %all-to-all-start = ((f32[16,32,128]{2,1,0:T(8,128)}), f32[16,32,128]{2,1,0:T(8,128)S(1)}, u32[]{:S(2)}, u32[]{:S(2)}) async-start(f32[16,32,128]{2,1,0:T(8,128)} %shard_map.135), calls=%async_computation | async-start | bytes 524288 | tf_op jit(solution)/shard_map/all_to_all | solution.py:487
  75.5 3.1 %collective-permute-start.12 = (f32[256,128]{1,0:T(8,128)S(1)}, f32[256,128]{1,0:T(8,128)S(1)}, u32[]{:S(2)}, u32[]{:S(2)}) collective-permute-start(f32[256,128]{1,0:T(8,128)S(1)} %get-tuple-element.69), channel_id=1, source_target_pairs={{0,8},{8,16},{16,24},{24,32},{32,40},{40,48},{48,56},{56,64},{64,7... | collective-permute-start | bytes 393224 | tf_op jit(solution)/shard_map/ppermute | solution.py:428
  78.6 4.9 %collective-permute-start.13 = (f32[256,128]{1,0:T(8,128)S(1)}, f32[256,128]{1,0:T(8,128)S(1)}, u32[]{:S(2)}, u32[]{:S(2)}) collective-permute-start(f32[256,128]{1,0:T(8,128)S(1)} %get-tuple-element.70), channel_id=1, source_target_pairs={{8,0},{16,8},{24,16},{32,24},{40,32},{48,40},{56,48},{64,56},{72,6... | collective-permute-start | bytes 393224 | tf_op jit(solution)/shard_map/ppermute | solution.py:428
  84.7 6.8 %shard_map.137 = (f32[32,128]{1,0:T(8,128)S(1)}, f32[32,128]{1,0:T(8,128)S(1)}) custom-call(f32[16,32,128]{2,1,0:T(8,128)S(1)} %all-to-all-done.got, f32[64,128]{1,0:T(8,128)S(1)} %get-tuple-element.77.keyx, f32[64,128]{1,0:T(8,128)S(1)} %get-tuple-element.78.keyy, f32[128,64]{1,0:T(8,128)S(1)} %get-tuple-element.79.count, ...), custom_call_target="tpu_custom_call" | custom-call | tf_op jit(solution)/shard_map/pallas_call | solution.py:414
  92.6 11.1 %collective-permute-start.16 = (f32[8,32,128]{2,1,0:T(8,128)S(1)}, f32[8,32,128]{2,1,0:T(8,128)S(1)}, u32[]{:S(2)}, u32[]{:S(2)}) collective-permute-start(f32[8,32,128]{2,1,0:T(8,128)S(1)} %get-tuple-element.88), channel_id=1, source_target_pairs={{0,128},{128,0},{256,384},{384,256},{1,129},{129,1},{257,385},{385... | collective-permute-start | bytes 393224 | tf_op jit(solution)/shard_map/ppermute | solution.py:515
  104.8 15.4 %all-gather = f32[1280,128]{1,0:T(8,128)S(1)} all-gather(f32[320,128]{1,0:T(8,128)S(1)} %shard_map.139), channel_id=2, replica_groups=mesh['shot'=4,'gx'=16,'gy'=8] {'shot'}, dimensions={0}, use_global_device_ids=true | all-gather | bytes 819200 | tf_op jit(solution)/shard_map/all_gather | solution.py:517
  (43 shorter events, 9.7 us)
Async XLA Ops:
  2.7 22.2 %copy-start.1 = (f32[1,8,32,128]{3,2,1,0:T(8,128)S(1)}, f32[1,8,32,128]{3,2,1,0:T(8,128)}, u32[]{:S(2)}) copy-start(f32[1,8,32,128]{3,2,1,0:T(8,128)} %param.18) | copy-start | bytes 393220
  2.7 22.2 %copy-start.4 = (f32[1,8,32,128]{3,2,1,0:T(8,128)S(1)}, f32[1,8,32,128]{3,2,1,0:T(8,128)}, u32[]{:S(2)}) copy-start(f32[1,8,32,128]{3,2,1,0:T(8,128)} %param.15) | copy-start | bytes 393220
  2.7 22.2 %copy-start.5 = (f32[1,8,32,128]{3,2,1,0:T(8,128)S(1)}, f32[1,8,32,128]{3,2,1,0:T(8,128)}, u32[]{:S(2)}) copy-start(f32[1,8,32,128]{3,2,1,0:T(8,128)} %param.17) | copy-start | bytes 393220
  2.8 22.0 %collective-permute-start = (f32[256,128]{1,0:T(8,128)S(1)}, f32[256,128]{1,0:T(8,128)S(1)}, u32[]{:S(2)}, u32[]{:S(2)}) collective-permute-start(f32[256,128]{1,0:T(8,128)S(1)} %get-tuple-element.46), channel_id=1, source_target_pairs={{0,8},{8,16},{16,24},{24,32},{32,40},{40,48},{48,56},{56,64},{64,7... | collective-permute-start | bytes 393224 | tf_op jit(solution)/shard_map/ppermute | solution.py:428
  6.1 18.7 %collective-permute-start.1 = (f32[256,128]{1,0:T(8,128)S(1)}, f32[256,128]{1,0:T(8,128)S(1)}, u32[]{:S(2)}, u32[]{:S(2)}) collective-permute-start(f32[256,128]{1,0:T(8,128)S(1)} %get-tuple-element.47), channel_id=1, source_target_pairs={{8,0},{16,8},{24,16},{32,24},{40,32},{48,40},{56,48},{64,56},{72,6... | collective-permute-start | bytes 393224 | tf_op jit(solution)/shard_map/ppermute | solution.py:428
  10.9 13.9 %collective-permute-start.2 = (f32[88,128]{1,0:T(8,128)S(1)}, f32[88,128]{1,0:T(8,128)S(1)}, u32[]{:S(2)}, u32[]{:S(2)}) collective-permute-start(f32[88,128]{1,0:T(8,128)S(1)} %get-tuple-element.48), channel_id=1, source_target_pairs={{0,1},{1,2},{2,3},{3,4},{4,5},{5,6},{6,7},{7,0},{8,9},{9,10},{10,1... | collective-permute-start | bytes 135176 | tf_op jit(solution)/shard_map/ppermute | solution.py:428
  14.9 9.9 %collective-permute-start.3 = (f32[88,128]{1,0:T(8,128)S(1)}, f32[88,128]{1,0:T(8,128)S(1)}, u32[]{:S(2)}, u32[]{:S(2)}) collective-permute-start(f32[88,128]{1,0:T(8,128)S(1)} %get-tuple-element.49), channel_id=1, source_target_pairs={{0,7},{1,0},{2,1},{3,2},{4,3},{5,4},{6,5},{7,6},{8,15},{9,8},{10,9... | collective-permute-start | bytes 135176 | tf_op jit(solution)/shard_map/ppermute | solution.py:428
  27.2 15.6 %collective-permute-start.4 = (f32[320,128]{1,0:T(8,128)S(1)}, f32[320,128]{1,0:T(8,128)S(1)}, u32[]{:S(2)}, u32[]{:S(2)}) collective-permute-start(f32[320,128]{1,0:T(8,128)S(1)} %get-tuple-element.53), channel_id=1, source_target_pairs={{0,8},{8,16},{16,24},{24,32},{32,40},{40,48},{48,56},{56,64},{64,7... | collective-permute-start | bytes 491528 | tf_op jit(solution)/shard_map/ppermute | solution.py:428
  29.2 13.7 %collective-permute-start.5 = (f32[320,128]{1,0:T(8,128)S(1)}, f32[320,128]{1,0:T(8,128)S(1)}, u32[]{:S(2)}, u32[]{:S(2)}) collective-permute-start(f32[320,128]{1,0:T(8,128)S(1)} %get-tuple-element.54), channel_id=1, source_target_pairs={{8,0},{16,8},{24,16},{32,24},{40,32},{48,40},{56,48},{64,56},{72,6... | collective-permute-start | bytes 491528 | tf_op jit(solution)/shard_map/ppermute | solution.py:428
  35.2 6.6 %collective-permute-start.6 = (f32[72,128]{1,0:T(8,128)S(1)}, f32[72,128]{1,0:T(8,128)S(1)}, u32[]{:S(2)}, u32[]{:S(2)}) collective-permute-start(f32[72,128]{1,0:T(8,128)S(1)} %get-tuple-element.55), channel_id=1, source_target_pairs={{0,1},{1,2},{2,3},{3,4},{4,5},{5,6},{6,7},{7,0},{8,9},{9,10},{10,1... | collective-permute-start | bytes 110600 | tf_op jit(solution)/shard_map/ppermute | solution.py:428
  37.1 5.7 %collective-permute-start.7 = (f32[72,128]{1,0:T(8,128)S(1)}, f32[72,128]{1,0:T(8,128)S(1)}, u32[]{:S(2)}, u32[]{:S(2)}) collective-permute-start(f32[72,128]{1,0:T(8,128)S(1)} %get-tuple-element.56), channel_id=1, source_target_pairs={{0,7},{1,0},{2,1},{3,2},{4,3},{5,4},{6,5},{7,6},{8,15},{9,8},{10,9... | collective-permute-start | bytes 110600 | tf_op jit(solution)/shard_map/ppermute | solution.py:428
  44.5 15.8 %collective-permute-start.8 = (f32[288,128]{1,0:T(8,128)S(1)}, f32[288,128]{1,0:T(8,128)S(1)}, u32[]{:S(2)}, u32[]{:S(2)}) collective-permute-start(f32[288,128]{1,0:T(8,128)S(1)} %get-tuple-element.61), channel_id=1, source_target_pairs={{0,8},{8,16},{16,24},{24,32},{32,40},{40,48},{48,56},{56,64},{64,7... | collective-permute-start | bytes 442376 | tf_op jit(solution)/shard_map/ppermute | solution.py:428
  46.4 13.9 %collective-permute-start.9 = (f32[288,128]{1,0:T(8,128)S(1)}, f32[288,128]{1,0:T(8,128)S(1)}, u32[]{:S(2)}, u32[]{:S(2)}) collective-permute-start(f32[288,128]{1,0:T(8,128)S(1)} %get-tuple-element.62), channel_id=1, source_target_pairs={{8,0},{16,8},{24,16},{32,24},{40,32},{48,40},{56,48},{64,56},{72,6... | collective-permute-start | bytes 442376 | tf_op jit(solution)/shard_map/ppermute | solution.py:428
  52.5 6.8 %collective-permute-start.10 = (f32[72,128]{1,0:T(8,128)S(1)}, f32[72,128]{1,0:T(8,128)S(1)}, u32[]{:S(2)}, u32[]{:S(2)}) collective-permute-start(f32[72,128]{1,0:T(8,128)S(1)} %get-tuple-element.63), channel_id=1, source_target_pairs={{0,1},{1,2},{2,3},{3,4},{4,5},{5,6},{6,7},{7,0},{8,9},{9,10},{10,1... | collective-permute-start | bytes 110600 | tf_op jit(solution)/shard_map/ppermute | solution.py:428
  55.5 4.8 %collective-permute-start.11 = (f32[72,128]{1,0:T(8,128)S(1)}, f32[72,128]{1,0:T(8,128)S(1)}, u32[]{:S(2)}, u32[]{:S(2)}) collective-permute-start(f32[72,128]{1,0:T(8,128)S(1)} %get-tuple-element.64), channel_id=1, source_target_pairs={{0,7},{1,0},{2,1},{3,2},{4,3},{5,4},{6,5},{7,6},{8,15},{9,8},{10,9... | collective-permute-start | bytes 110600 | tf_op jit(solution)/shard_map/ppermute | solution.py:428
  62.3 6.8 %collective-permute-start.14 = (f32[88,128]{1,0:T(8,128)S(1)}, f32[88,128]{1,0:T(8,128)S(1)}, u32[]{:S(2)}, u32[]{:S(2)}) collective-permute-start(f32[88,128]{1,0:T(8,128)S(1)} %get-tuple-element.71), channel_id=1, source_target_pairs={{0,1},{1,2},{2,3},{3,4},{4,5},{5,6},{6,7},{7,0},{8,9},{9,10},{10,1... | collective-permute-start | bytes 135176 | tf_op jit(solution)/shard_map/ppermute | solution.py:428
  65.5 4.8 %collective-permute-start.15 = (f32[88,128]{1,0:T(8,128)S(1)}, f32[88,128]{1,0:T(8,128)S(1)}, u32[]{:S(2)}, u32[]{:S(2)}) collective-permute-start(f32[88,128]{1,0:T(8,128)S(1)} %get-tuple-element.72), channel_id=1, source_target_pairs={{0,7},{1,0},{2,1},{3,2},{4,3},{5,4},{6,5},{7,6},{8,15},{9,8},{10,9... | collective-permute-start | bytes 135176 | tf_op jit(solution)/shard_map/ppermute | solution.py:428
  71.1 12.4 %copy-start.2 = (f32[1,8,32,128]{3,2,1,0:T(8,128)S(1)}, f32[1,8,32,128]{3,2,1,0:T(8,128)}, u32[]{:S(2)}) copy-start(f32[1,8,32,128]{3,2,1,0:T(8,128)} %param.14) | copy-start | bytes 393220
  71.1 12.4 %copy-start.6 = (s32[1,8192]{1,0:T(1,128)S(1)}, s32[1,8192]{1,0:T(1,128)}, u32[]{:S(2)}) copy-start(s32[1,8192]{1,0:T(1,128)} %param.21) | copy-start | bytes 98308
  71.1 13.6 %all-to-all-start = ((f32[16,32,128]{2,1,0:T(8,128)}), f32[16,32,128]{2,1,0:T(8,128)S(1)}, u32[]{:S(2)}, u32[]{:S(2)}) async-start(f32[16,32,128]{2,1,0:T(8,128)} %shard_map.135), calls=%async_computation | async-start | bytes 524288 | tf_op jit(solution)/shard_map/all_to_all | solution.py:487
  75.5 16.0 %collective-permute-start.12 = (f32[256,128]{1,0:T(8,128)S(1)}, f32[256,128]{1,0:T(8,128)S(1)}, u32[]{:S(2)}, u32[]{:S(2)}) collective-permute-start(f32[256,128]{1,0:T(8,128)S(1)} %get-tuple-element.69), channel_id=1, source_target_pairs={{0,8},{8,16},{16,24},{24,32},{32,40},{40,48},{48,56},{56,64},{64,7... | collective-permute-start | bytes 393224 | tf_op jit(solution)/shard_map/ppermute | solution.py:428
  78.6 12.9 %collective-permute-start.13 = (f32[256,128]{1,0:T(8,128)S(1)}, f32[256,128]{1,0:T(8,128)S(1)}, u32[]{:S(2)}, u32[]{:S(2)}) collective-permute-start(f32[256,128]{1,0:T(8,128)S(1)} %get-tuple-element.70), channel_id=1, source_target_pairs={{8,0},{16,8},{24,16},{32,24},{40,32},{48,40},{56,48},{64,56},{72,6... | collective-permute-start | bytes 393224 | tf_op jit(solution)/shard_map/ppermute | solution.py:428
  92.6 12.1 %collective-permute-start.16 = (f32[8,32,128]{2,1,0:T(8,128)S(1)}, f32[8,32,128]{2,1,0:T(8,128)S(1)}, u32[]{:S(2)}, u32[]{:S(2)}) collective-permute-start(f32[8,32,128]{2,1,0:T(8,128)S(1)} %get-tuple-element.88), channel_id=1, source_target_pairs={{0,128},{128,0},{256,384},{384,256},{1,129},{129,1},{257,385},{385... | collective-permute-start | bytes 393224 | tf_op jit(solution)/shard_map/ppermute | solution.py:515
  104.7 15.5 %copy-start.3 = (f32[8,32,128]{2,1,0:T(8,128)S(1)}, f32[8,32,128]{2,1,0:T(8,128)}, u32[]{:S(2)}) copy-start(f32[8,32,128]{2,1,0:T(8,128)} %logs.1) | copy-start | bytes 393220
  (3 other events, 2.4 us)

commit v9 on v8

--- a/solution.py
+++ b/solution.py
@@ -217,7 +217,7 @@
     part[NY : 2 * NY] = grad * zpk[...]
 
 
-def chunk_kernel(mat, md, mu, oc, out, traces):
+def chunk_kernel(mat, md, mu, oc, _, out, traces):
     keep_d, keep_u = edges()
     collect(3, md, mu, oc, traces)
     packed = jnp.where(keep_d, md[72:88], 0.0) + roll(jnp.where(keep_u, mu[72:88], 0.0), 96)
@@ -268,7 +268,7 @@
         keyy[g : g + 1] = key
         hoty[:, 128 * g : 128 * (g + 1)] = jnp.where(coly == key.astype(bf), one, none)
     count[...] = lax.dot_general(
-        hot[...], hoty[...], (((1,), (1,)), ((), ())), preferred_element_type=f32
+        hoty[...], hot[...], (((1,), (1,)), ((), ())), preferred_element_type=f32
     )
     vpk[...] = pack([vel[i] for i in range(NX)])
     zpk[...] = pack([noise[i] for i in range(NX)])
@@ -302,12 +302,12 @@
                 table[128 * part : 128 * (part + 1), at] = jnp.where(here, v128, none)
         at = pl.ds(pl.multiple_of(g * 512, 512), 512)
         return carry + lax.dot_general(
-            table[:, at], hoty[:, at], (((1,), (1,)), ((), ())), preferred_element_type=f32
+            hoty[:, at], table[:, at], (((1,), (1,)), ((), ())), preferred_element_type=f32
         )
 
-    sums = lax.fori_loop(0, ngx, build, jnp.zeros((384, 64), f32), unroll=ngx)
-    seen = sums[0:128] + sums[128:256] + sums[256:384]
-    tr = jnp.concatenate([seen, count[...]], 1).T
+    sums = lax.fori_loop(0, ngx, build, jnp.zeros((64, 384), f32), unroll=ngx)
+    seen = sums[:, 0:128] + sums[:, 128:256] + sums[:, 256:384]
+    counts = count[...]
 
     k_in = lax.broadcasted_iota(jnp.int32, (128, 512), 0)
     k_out = lax.broadcasted_iota(jnp.int32, (128, 512), 1)
@@ -321,8 +321,8 @@
         blk = got[jnp.clip(src, 0, ngx - 1), 16:32, :]
         m = jnp.concatenate([roll(blk, -32 * t) for t in range(4)], 0)
         m = jnp.where(ok, m, 0.0)
-        s_g = roll(tr[:64], 16 - 32 * g)
-        n_g = roll(tr[64:], 16 - 32 * g)
+        s_g = roll(seen, 16 - 32 * g)
+        n_g = roll(counts, 16 - 32 * g)
         dense.append(jnp.where(lane % 4 == 3, 0.0, n_g * m) - s_g)
         raw.append(jnp.where(lane % 4 == 0, n_g, m))
     inj[...] = jnp.dot(
@@ -483,8 +483,6 @@
         p_prev, p = p, p_next
         q_later, q = q, q_next
 
-    chunk = call(chunk_kernel, sds(ngx, 32, 128), (pltpu.VMEM((16, 128), f32),))(mat, md, mu, oc)
-    got = lax.all_to_all(chunk, "gx", 0, 0)
     nrec = receiver_column.shape[1]
     bf = jnp.bfloat16
     keyx, keyy, count, vpk, zpk = call(
@@ -492,7 +490,7 @@
         (
             sds(nrec // 128, 128),
             sds(nrec // 128, 128),
-            sds(128, 64),
+            sds(64, 128),
             sds(NY, NZ),
             sds(NY, NZ),
         ),
@@ -500,6 +498,10 @@
         + [pltpu.VMEM((128, nrec), bf), pltpu.VMEM((64, nrec), bf)],
         mib=12,
     )(receiver_column.reshape(-1, 128), vel, noise)
+    chunk = call(chunk_kernel, sds(ngx, 32, 128), (pltpu.VMEM((16, 128), f32),))(
+        mat, md, mu, oc, count
+    )
+    got = lax.all_to_all(chunk, "gx", 0, 0)
     g5 = pltpu.VMEM((5, 64, 128), f32)
     g48 = pltpu.VMEM((5, 48, 128), f32)
     image_in, driven = call(

time: 122 us -> 120 us (0.984)
  the two profiles are of different devices: /device:TPU:3 before, /device:TPU:49 now
where the time goes in v9:
time: 120 us; the launch traced here: 119 us
  starting transfers between devices  78.7 us (66%)
  blocking collectives  15.6 us (13%)
  Pallas kernels  15.1 us (13%)
  waiting for transfers between devices  5.1 us (4%)
  between operations  2.26 us (2%)
  local copies, waits for them, and re-layouts  1.52 us (1%)
    ppermute x16, starting transfers between devices, shift(): lax.ppermute(x, axis, [(i, (i + k) % n) for i in range(n) if wrap or 0 <=...  56.9 us
    all_gather x1, blocking collectives, local(): every = lax.all_gather(part, 'shot', axis=0)  15.6 us
    pallas_call x10, Pallas kernels, go(): pl.pallas_call(kernel, out_shape=outs, in_specs=[SM] * smem + [VM] * (len...  15.1 us
    ppermute x1, starting transfers between devices, local(): other = lax.ppermute(sent, 'shot', [(i, i ^ 1) for i in range(nshot)])  11.7 us
    all_to_all x1, starting transfers between devices, local(): got = lax.all_to_all(chunk, 'gx', 0, 0)  10 us
    ppermute x16, waiting for transfers between devices, shift(): lax.ppermute(x, axis, [(i, (i + k) % n) for i in range(n) if wrap or 0 <=...  3.11 us
  transfers between devices with their start and end apart: 18, of which 6 were waited for; matrix products, arithmetic and copies ran while one was open for 0% of the time, Pallas kernels for 6%

profile of v9, /device:TPU:49, one launch (start us, length us, event | category | flops | bytes accessed | tf_op | source)
XLA Modules:
  0.0 119.4 jit_solution(11199456206053239643)
XLA Ops:
  2.8 2.4 %collective-permute-start = (f32[256,128]{1,0:T(8,128)S(1)}, f32[256,128]{1,0:T(8,128)S(1)}, u32[]{:S(2)}, u32[]{:S(2)}) collective-permute-start(f32[256,128]{1,0:T(8,128)S(1)} %get-tuple-element.46), channel_id=1, source_target_pairs={{0,8},{8,16},{16,24},{24,32},{32,40},{40,48},{48,56},{56,64},{64,7... | collective-permute-start | bytes 393224 | tf_op jit(solution)/shard_map/ppermute | solution.py:428
  5.2 3.0 %collective-permute-start.1 = (f32[256,128]{1,0:T(8,128)S(1)}, f32[256,128]{1,0:T(8,128)S(1)}, u32[]{:S(2)}, u32[]{:S(2)}) collective-permute-start(f32[256,128]{1,0:T(8,128)S(1)} %get-tuple-element.47), channel_id=1, source_target_pairs={{8,0},{16,8},{24,16},{32,24},{40,32},{48,40},{56,48},{64,56},{72,6... | collective-permute-start | bytes 393224 | tf_op jit(solution)/shard_map/ppermute | solution.py:428
  8.2 4.0 %collective-permute-start.2 = (f32[88,128]{1,0:T(8,128)S(1)}, f32[88,128]{1,0:T(8,128)S(1)}, u32[]{:S(2)}, u32[]{:S(2)}) collective-permute-start(f32[88,128]{1,0:T(8,128)S(1)} %get-tuple-element.48), channel_id=1, source_target_pairs={{0,1},{1,2},{2,3},{3,4},{4,5},{5,6},{6,7},{7,0},{8,9},{9,10},{10,1... | collective-permute-start | bytes 135176 | tf_op jit(solution)/shard_map/ppermute | solution.py:428
  12.2 8.6 %collective-permute-start.3 = (f32[88,128]{1,0:T(8,128)S(1)}, f32[88,128]{1,0:T(8,128)S(1)}, u32[]{:S(2)}, u32[]{:S(2)}) collective-permute-start(f32[88,128]{1,0:T(8,128)S(1)} %get-tuple-element.49), channel_id=1, source_target_pairs={{0,7},{1,0},{2,1},{3,2},{4,3},{5,4},{6,5},{7,6},{8,15},{9,8},{10,9... | collective-permute-start | bytes 135176 | tf_op jit(solution)/shard_map/ppermute | solution.py:428
  22.8 1.7 %shard_map.132 = (f32[32,128]{1,0:T(8,128)S(1)}, f32[16,128]{1,0:T(8,128)S(1)}, f32[8,32,128]{2,1,0:T(8,128)S(1)}, f32[8,32,128]{2,1,0:T(8,128)S(1)}, f32[320,12...) custom-call(s32[1]{0:T(128)S(6)} %copy.14.source, ...), custom_call_target="tpu_custom_call" | custom-call | tf_op jit(solution)/shard_map/pallas_call | solution.py:414
  24.5 4.4 %collective-permute-start.4 = (f32[320,128]{1,0:T(8,128)S(1)}, f32[320,128]{1,0:T(8,128)S(1)}, u32[]{:S(2)}, u32[]{:S(2)}) collective-permute-start(f32[320,128]{1,0:T(8,128)S(1)} %get-tuple-element.53), channel_id=1, source_target_pairs={{0,8},{8,16},{16,24},{24,32},{32,40},{40,48},{48,56},{56,64},{64,7... | collective-permute-start | bytes 491528 | tf_op jit(solution)/shard_map/ppermute | solution.py:428
  29.0 1.9 %collective-permute-start.5 = (f32[320,128]{1,0:T(8,128)S(1)}, f32[320,128]{1,0:T(8,128)S(1)}, u32[]{:S(2)}, u32[]{:S(2)}) collective-permute-start(f32[320,128]{1,0:T(8,128)S(1)} %get-tuple-element.54), channel_id=1, source_target_pairs={{8,0},{16,8},{24,16},{32,24},{40,32},{48,40},{56,48},{64,56},{72,6... | collective-permute-start | bytes 491528 | tf_op jit(solution)/shard_map/ppermute | solution.py:428
  30.9 1.9 %collective-permute-start.6 = (f32[72,128]{1,0:T(8,128)S(1)}, f32[72,128]{1,0:T(8,128)S(1)}, u32[]{:S(2)}, u32[]{:S(2)}) collective-permute-start(f32[72,128]{1,0:T(8,128)S(1)} %get-tuple-element.55), channel_id=1, source_target_pairs={{0,1},{1,2},{2,3},{3,4},{4,5},{5,6},{6,7},{7,0},{8,9},{9,10},{10,1... | collective-permute-start | bytes 110600 | tf_op jit(solution)/shard_map/ppermute | solution.py:428
  32.8 4.9 %collective-permute-start.7 = (f32[72,128]{1,0:T(8,128)S(1)}, f32[72,128]{1,0:T(8,128)S(1)}, u32[]{:S(2)}, u32[]{:S(2)}) collective-permute-start(f32[72,128]{1,0:T(8,128)S(1)} %get-tuple-element.56), channel_id=1, source_target_pairs={{0,7},{1,0},{2,1},{3,2},{4,3},{5,4},{6,5},{7,6},{8,15},{9,8},{10,9... | collective-permute-start | bytes 110600 | tf_op jit(solution)/shard_map/ppermute | solution.py:428
  39.4 1.6 %shard_map.133 = (f32[32,128]{1,0:T(8,128)S(1)}, f32[16,128]{1,0:T(8,128)S(1)}, f32[8,32,128]{2,1,0:T(8,128)S(1)}, f32[8,32,128]{2,1,0:T(8,128)S(1)}, f32[288,12...) custom-call(s32[1]{0:T(128)S(6)} %copy.14.source, ...), custom_call_target="tpu_custom_call" | custom-call | tf_op jit(solution)/shard_map/pallas_call | solution.py:414
  41.1 5.1 %collective-permute-start.8 = (f32[288,128]{1,0:T(8,128)S(1)}, f32[288,128]{1,0:T(8,128)S(1)}, u32[]{:S(2)}, u32[]{:S(2)}) collective-permute-start(f32[288,128]{1,0:T(8,128)S(1)} %get-tuple-element.61), channel_id=1, source_target_pairs={{0,8},{8,16},{16,24},{24,32},{32,40},{40,48},{48,56},{56,64},{64,7... | collective-permute-start | bytes 442376 | tf_op jit(solution)/shard_map/ppermute | solution.py:428
  46.2 1.9 %collective-permute-start.9 = (f32[288,128]{1,0:T(8,128)S(1)}, f32[288,128]{1,0:T(8,128)S(1)}, u32[]{:S(2)}, u32[]{:S(2)}) collective-permute-start(f32[288,128]{1,0:T(8,128)S(1)} %get-tuple-element.62), channel_id=1, source_target_pairs={{8,0},{16,8},{24,16},{32,24},{40,32},{48,40},{56,48},{64,56},{72,6... | collective-permute-start | bytes 442376 | tf_op jit(solution)/shard_map/ppermute | solution.py:428
  48.2 3.0 %collective-permute-start.10 = (f32[72,128]{1,0:T(8,128)S(1)}, f32[72,128]{1,0:T(8,128)S(1)}, u32[]{:S(2)}, u32[]{:S(2)}) collective-permute-start(f32[72,128]{1,0:T(8,128)S(1)} %get-tuple-element.63), channel_id=1, source_target_pairs={{0,1},{1,2},{2,3},{3,4},{4,5},{5,6},{6,7},{7,0},{8,9},{9,10},{10,1... | collective-permute-start | bytes 110600 | tf_op jit(solution)/shard_map/ppermute | solution.py:428
  51.2 3.8 %collective-permute-start.11 = (f32[72,128]{1,0:T(8,128)S(1)}, f32[72,128]{1,0:T(8,128)S(1)}, u32[]{:S(2)}, u32[]{:S(2)}) collective-permute-start(f32[72,128]{1,0:T(8,128)S(1)} %get-tuple-element.64), channel_id=1, source_target_pairs={{0,7},{1,0},{2,1},{3,2},{4,3},{5,4},{6,5},{7,6},{8,15},{9,8},{10,9... | collective-permute-start | bytes 110600 | tf_op jit(solution)/shard_map/ppermute | solution.py:428
  56.2 2.0 %shard_map.134 = (f32[32,128]{1,0:T(8,128)S(1)}, f32[16,128]{1,0:T(8,128)S(1)}, f32[8,32,128]{2,1,0:T(8,128)S(1)}, f32[8,32,128]{2,1,0:T(8,128)S(1)}, f32[256,12...) custom-call(s32[1]{0:T(128)S(6)} %copy.14.source, ...), custom_call_target="tpu_custom_call" | custom-call | tf_op jit(solution)/shard_map/pallas_call | solution.py:414
  58.2 3.4 %collective-permute-start.14 = (f32[88,128]{1,0:T(8,128)S(1)}, f32[88,128]{1,0:T(8,128)S(1)}, u32[]{:S(2)}, u32[]{:S(2)}) collective-permute-start(f32[88,128]{1,0:T(8,128)S(1)} %get-tuple-element.71), channel_id=1, source_target_pairs={{0,1},{1,2},{2,3},{3,4},{4,5},{5,6},{6,7},{7,0},{8,9},{9,10},{10,1... | collective-permute-start | bytes 135176 | tf_op jit(solution)/shard_map/ppermute | solution.py:428
  61.5 3.3 %collective-permute-start.15 = (f32[88,128]{1,0:T(8,128)S(1)}, f32[88,128]{1,0:T(8,128)S(1)}, u32[]{:S(2)}, u32[]{:S(2)}) collective-permute-start(f32[88,128]{1,0:T(8,128)S(1)} %get-tuple-element.72), channel_id=1, source_target_pairs={{0,7},{1,0},{2,1},{3,2},{4,3},{5,4},{6,5},{7,6},{8,15},{9,8},{10,9... | collective-permute-start | bytes 135176 | tf_op jit(solution)/shard_map/ppermute | solution.py:428
  64.8 1.3 %shard_map.135 = (f32[64,128]{1,0:T(8,128)S(1)}, f32[64,128]{1,0:T(8,128)S(1)}, f32[64,128]{1,0:T(8,128)S(1)}, f32[32,128]{1,0:T(8,128)S(1)}, f32[32,128]{1,0:T(8,128)S(1)}) custom-call(s32[64,128]{1,0:T(8,128)S(1)} %bitcast.21, f32[8,32,128]{2,1,0:T(8,128)S(1)} %get-tuple-element.91.vel, f32[8,32,128]{2,1,0:T(8,128)S(1)} %bitcast.17), custom_call_target="tpu_custom_call" | custom-call | tf_op jit(solution)/shard_map/pallas_call | solution.py:414
  67.1 10.0 %all-to-all-start = ((f32[16,32,128]{2,1,0:T(8,128)}), f32[16,32,128]{2,1,0:T(8,128)S(1)}, u32[]{:S(2)}, u32[]{:S(2)}) async-start(f32[16,32,128]{2,1,0:T(8,128)} %shard_map.136), calls=%async_computation | async-start | bytes 524288 | tf_op jit(solution)/shard_map/all_to_all | solution.py:504
  77.1 3.1 %collective-permute-start.12 = (f32[256,128]{1,0:T(8,128)S(1)}, f32[256,128]{1,0:T(8,128)S(1)}, u32[]{:S(2)}, u32[]{:S(2)}) collective-permute-start(f32[256,128]{1,0:T(8,128)S(1)} %get-tuple-element.69), channel_id=1, source_target_pairs={{0,8},{8,16},{16,24},{24,32},{32,40},{40,48},{48,56},{56,64},{64,7... | collective-permute-start | bytes 393224 | tf_op jit(solution)/shard_map/ppermute | solution.py:428
  80.2 2.2 %collective-permute-start.13 = (f32[256,128]{1,0:T(8,128)S(1)}, f32[256,128]{1,0:T(8,128)S(1)}, u32[]{:S(2)}, u32[]{:S(2)}) collective-permute-start(f32[256,128]{1,0:T(8,128)S(1)} %get-tuple-element.70), channel_id=1, source_target_pairs={{8,0},{16,8},{24,16},{32,24},{40,32},{48,40},{56,48},{64,56},{72,6... | collective-permute-start | bytes 393224 | tf_op jit(solution)/shard_map/ppermute | solution.py:428
  83.5 5.7 %shard_map.137 = (f32[32,128]{1,0:T(8,128)S(1)}, f32[32,128]{1,0:T(8,128)S(1)}) custom-call(f32[16,32,128]{2,1,0:T(8,128)S(1)} %all-to-all-done.got, f32[64,128]{1,0:T(8,128)S(1)} %get-tuple-element.78.keyx, f32[64,128]{1,0:T(8,128)S(1)} %get-tuple-element.79.keyy, f32[64,128]{1,0:T(8,128)S(1)} %get-tuple-element.77._.count, ...), custom_call_target="tpu_custom_call" | custom-call | tf_op jit(solution)/shard_map/pallas_call | solution.py:414
  90.3 11.7 %collective-permute-start.16 = (f32[8,32,128]{2,1,0:T(8,128)S(1)}, f32[8,32,128]{2,1,0:T(8,128)S(1)}, u32[]{:S(2)}, u32[]{:S(2)}) collective-permute-start(f32[8,32,128]{2,1,0:T(8,128)S(1)} %get-tuple-element.88), channel_id=1, source_target_pairs={{0,128},{128,0},{256,384},{384,256},{1,129},{129,1},{257,385},{385... | collective-permute-start | bytes 393224 | tf_op jit(solution)/shard_map/ppermute | solution.py:517
  103.1 15.6 %all-gather = f32[1280,128]{1,0:T(8,128)S(1)} all-gather(f32[320,128]{1,0:T(8,128)S(1)} %shard_map.139), channel_id=2, replica_groups=mesh['shot'=4,'gx'=16,'gy'=8] {'shot'}, dimensions={0}, use_global_device_ids=true | all-gather | bytes 819200 | tf_op jit(solution)/shard_map/all_gather | solution.py:519
  (43 shorter events, 10.6 us)
Async XLA Ops:
  2.7 19.5 %copy-start.1 = (f32[1,8,32,128]{3,2,1,0:T(8,128)S(1)}, f32[1,8,32,128]{3,2,1,0:T(8,128)}, u32[]{:S(2)}) copy-start(f32[1,8,32,128]{3,2,1,0:T(8,128)} %param.18) | copy-start | bytes 393220
  2.7 19.5 %copy-start.4 = (f32[1,8,32,128]{3,2,1,0:T(8,128)S(1)}, f32[1,8,32,128]{3,2,1,0:T(8,128)}, u32[]{:S(2)}) copy-start(f32[1,8,32,128]{3,2,1,0:T(8,128)} %param.15) | copy-start | bytes 393220
  2.7 19.5 %copy-start.5 = (f32[1,8,32,128]{3,2,1,0:T(8,128)S(1)}, f32[1,8,32,128]{3,2,1,0:T(8,128)}, u32[]{:S(2)}) copy-start(f32[1,8,32,128]{3,2,1,0:T(8,128)} %param.17) | copy-start | bytes 393220
  2.8 19.3 %collective-permute-start = (f32[256,128]{1,0:T(8,128)S(1)}, f32[256,128]{1,0:T(8,128)S(1)}, u32[]{:S(2)}, u32[]{:S(2)}) collective-permute-start(f32[256,128]{1,0:T(8,128)S(1)} %get-tuple-element.46), channel_id=1, source_target_pairs={{0,8},{8,16},{16,24},{24,32},{32,40},{40,48},{48,56},{56,64},{64,7... | collective-permute-start | bytes 393224 | tf_op jit(solution)/shard_map/ppermute | solution.py:428
  5.2 16.9 %collective-permute-start.1 = (f32[256,128]{1,0:T(8,128)S(1)}, f32[256,128]{1,0:T(8,128)S(1)}, u32[]{:S(2)}, u32[]{:S(2)}) collective-permute-start(f32[256,128]{1,0:T(8,128)S(1)} %get-tuple-element.47), channel_id=1, source_target_pairs={{8,0},{16,8},{24,16},{32,24},{40,32},{48,40},{56,48},{64,56},{72,6... | collective-permute-start | bytes 393224 | tf_op jit(solution)/shard_map/ppermute | solution.py:428
  8.2 13.9 %collective-permute-start.2 = (f32[88,128]{1,0:T(8,128)S(1)}, f32[88,128]{1,0:T(8,128)S(1)}, u32[]{:S(2)}, u32[]{:S(2)}) collective-permute-start(f32[88,128]{1,0:T(8,128)S(1)} %get-tuple-element.48), channel_id=1, source_target_pairs={{0,1},{1,2},{2,3},{3,4},{4,5},{5,6},{6,7},{7,0},{8,9},{9,10},{10,1... | collective-permute-start | bytes 135176 | tf_op jit(solution)/shard_map/ppermute | solution.py:428
  12.2 9.9 %collective-permute-start.3 = (f32[88,128]{1,0:T(8,128)S(1)}, f32[88,128]{1,0:T(8,128)S(1)}, u32[]{:S(2)}, u32[]{:S(2)}) collective-permute-start(f32[88,128]{1,0:T(8,128)S(1)} %get-tuple-element.49), channel_id=1, source_target_pairs={{0,7},{1,0},{2,1},{3,2},{4,3},{5,4},{6,5},{7,6},{8,15},{9,8},{10,9... | collective-permute-start | bytes 135176 | tf_op jit(solution)/shard_map/ppermute | solution.py:428
  24.5 14.3 %collective-permute-start.4 = (f32[320,128]{1,0:T(8,128)S(1)}, f32[320,128]{1,0:T(8,128)S(1)}, u32[]{:S(2)}, u32[]{:S(2)}) collective-permute-start(f32[320,128]{1,0:T(8,128)S(1)} %get-tuple-element.53), channel_id=1, source_target_pairs={{0,8},{8,16},{16,24},{24,32},{32,40},{40,48},{48,56},{56,64},{64,7... | collective-permute-start | bytes 491528 | tf_op jit(solution)/shard_map/ppermute | solution.py:428
  29.0 10.5 %collective-permute-start.5 = (f32[320,128]{1,0:T(8,128)S(1)}, f32[320,128]{1,0:T(8,128)S(1)}, u32[]{:S(2)}, u32[]{:S(2)}) collective-permute-start(f32[320,128]{1,0:T(8,128)S(1)} %get-tuple-element.54), channel_id=1, source_target_pairs={{8,0},{16,8},{24,16},{32,24},{40,32},{48,40},{56,48},{64,56},{72,6... | collective-permute-start | bytes 491528 | tf_op jit(solution)/shard_map/ppermute | solution.py:428
  30.9 6.9 %collective-permute-start.6 = (f32[72,128]{1,0:T(8,128)S(1)}, f32[72,128]{1,0:T(8,128)S(1)}, u32[]{:S(2)}, u32[]{:S(2)}) collective-permute-start(f32[72,128]{1,0:T(8,128)S(1)} %get-tuple-element.55), channel_id=1, source_target_pairs={{0,1},{1,2},{2,3},{3,4},{4,5},{5,6},{6,7},{7,0},{8,9},{9,10},{10,1... | collective-permute-start | bytes 110600 | tf_op jit(solution)/shard_map/ppermute | solution.py:428
  32.8 6.0 %collective-permute-start.7 = (f32[72,128]{1,0:T(8,128)S(1)}, f32[72,128]{1,0:T(8,128)S(1)}, u32[]{:S(2)}, u32[]{:S(2)}) collective-permute-start(f32[72,128]{1,0:T(8,128)S(1)} %get-tuple-element.56), channel_id=1, source_target_pairs={{0,7},{1,0},{2,1},{3,2},{4,3},{5,4},{6,5},{7,6},{8,15},{9,8},{10,9... | collective-permute-start | bytes 110600 | tf_op jit(solution)/shard_map/ppermute | solution.py:428
  41.1 15.1 %collective-permute-start.8 = (f32[288,128]{1,0:T(8,128)S(1)}, f32[288,128]{1,0:T(8,128)S(1)}, u32[]{:S(2)}, u32[]{:S(2)}) collective-permute-start(f32[288,128]{1,0:T(8,128)S(1)} %get-tuple-element.61), channel_id=1, source_target_pairs={{0,8},{8,16},{16,24},{24,32},{32,40},{40,48},{48,56},{56,64},{64,7... | collective-permute-start | bytes 442376 | tf_op jit(solution)/shard_map/ppermute | solution.py:428
  46.2 9.9 %collective-permute-start.9 = (f32[288,128]{1,0:T(8,128)S(1)}, f32[288,128]{1,0:T(8,128)S(1)}, u32[]{:S(2)}, u32[]{:S(2)}) collective-permute-start(f32[288,128]{1,0:T(8,128)S(1)} %get-tuple-element.62), channel_id=1, source_target_pairs={{8,0},{16,8},{24,16},{32,24},{40,32},{48,40},{56,48},{64,56},{72,6... | collective-permute-start | bytes 442376 | tf_op jit(solution)/shard_map/ppermute | solution.py:428
  48.2 6.8 %collective-permute-start.10 = (f32[72,128]{1,0:T(8,128)S(1)}, f32[72,128]{1,0:T(8,128)S(1)}, u32[]{:S(2)}, u32[]{:S(2)}) collective-permute-start(f32[72,128]{1,0:T(8,128)S(1)} %get-tuple-element.63), channel_id=1, source_target_pairs={{0,1},{1,2},{2,3},{3,4},{4,5},{5,6},{6,7},{7,0},{8,9},{9,10},{10,1... | collective-permute-start | bytes 110600 | tf_op jit(solution)/shard_map/ppermute | solution.py:428
  51.2 5.0 %collective-permute-start.11 = (f32[72,128]{1,0:T(8,128)S(1)}, f32[72,128]{1,0:T(8,128)S(1)}, u32[]{:S(2)}, u32[]{:S(2)}) collective-permute-start(f32[72,128]{1,0:T(8,128)S(1)} %get-tuple-element.64), channel_id=1, source_target_pairs={{0,7},{1,0},{2,1},{3,2},{4,3},{5,4},{6,5},{7,6},{8,15},{9,8},{10,9... | collective-permute-start | bytes 110600 | tf_op jit(solution)/shard_map/ppermute | solution.py:428
  56.2 8.6 %copy-start.2 = (f32[1,8,32,128]{3,2,1,0:T(8,128)S(1)}, f32[1,8,32,128]{3,2,1,0:T(8,128)}, u32[]{:S(2)}) copy-start(f32[1,8,32,128]{3,2,1,0:T(8,128)} %param.14) | copy-start | bytes 393220
  56.2 8.6 %copy-start.6 = (s32[1,8192]{1,0:T(1,128)S(1)}, s32[1,8192]{1,0:T(1,128)}, u32[]{:S(2)}) copy-start(s32[1,8192]{1,0:T(1,128)} %param.21) | copy-start | bytes 98308
  58.2 8.0 %collective-permute-start.14 = (f32[88,128]{1,0:T(8,128)S(1)}, f32[88,128]{1,0:T(8,128)S(1)}, u32[]{:S(2)}, u32[]{:S(2)}) collective-permute-start(f32[88,128]{1,0:T(8,128)S(1)} %get-tuple-element.71), channel_id=1, source_target_pairs={{0,1},{1,2},{2,3},{3,4},{4,5},{5,6},{6,7},{7,0},{8,9},{9,10},{10,1... | collective-permute-start | bytes 135176 | tf_op jit(solution)/shard_map/ppermute | solution.py:428
  61.5 4.8 %collective-permute-start.15 = (f32[88,128]{1,0:T(8,128)S(1)}, f32[88,128]{1,0:T(8,128)S(1)}, u32[]{:S(2)}, u32[]{:S(2)}) collective-permute-start(f32[88,128]{1,0:T(8,128)S(1)} %get-tuple-element.72), channel_id=1, source_target_pairs={{0,7},{1,0},{2,1},{3,2},{4,3},{5,4},{6,5},{7,6},{8,15},{9,8},{10,9... | collective-permute-start | bytes 135176 | tf_op jit(solution)/shard_map/ppermute | solution.py:428
  67.1 16.4 %all-to-all-start = ((f32[16,32,128]{2,1,0:T(8,128)}), f32[16,32,128]{2,1,0:T(8,128)S(1)}, u32[]{:S(2)}, u32[]{:S(2)}) async-start(f32[16,32,128]{2,1,0:T(8,128)} %shard_map.136), calls=%async_computation | async-start | bytes 524288 | tf_op jit(solution)/shard_map/all_to_all | solution.py:504
  77.1 12.1 %collective-permute-start.12 = (f32[256,128]{1,0:T(8,128)S(1)}, f32[256,128]{1,0:T(8,128)S(1)}, u32[]{:S(2)}, u32[]{:S(2)}) collective-permute-start(f32[256,128]{1,0:T(8,128)S(1)} %get-tuple-element.69), channel_id=1, source_target_pairs={{0,8},{8,16},{16,24},{24,32},{32,40},{40,48},{48,56},{56,64},{64,7... | collective-permute-start | bytes 393224 | tf_op jit(solution)/shard_map/ppermute | solution.py:428
  80.2 9.0 %collective-permute-start.13 = (f32[256,128]{1,0:T(8,128)S(1)}, f32[256,128]{1,0:T(8,128)S(1)}, u32[]{:S(2)}, u32[]{:S(2)}) collective-permute-start(f32[256,128]{1,0:T(8,128)S(1)} %get-tuple-element.70), channel_id=1, source_target_pairs={{8,0},{16,8},{24,16},{32,24},{40,32},{48,40},{56,48},{64,56},{72,6... | collective-permute-start | bytes 393224 | tf_op jit(solution)/shard_map/ppermute | solution.py:428
  90.3 12.7 %collective-permute-start.16 = (f32[8,32,128]{2,1,0:T(8,128)S(1)}, f32[8,32,128]{2,1,0:T(8,128)S(1)}, u32[]{:S(2)}, u32[]{:S(2)}) collective-permute-start(f32[8,32,128]{2,1,0:T(8,128)S(1)} %get-tuple-element.88), channel_id=1, source_target_pairs={{0,128},{128,0},{256,384},{384,256},{1,129},{129,1},{257,385},{385... | collective-permute-start | bytes 393224 | tf_op jit(solution)/shard_map/ppermute | solution.py:517
  103.0 15.6 %copy-start.3 = (f32[8,32,128]{2,1,0:T(8,128)S(1)}, f32[8,32,128]{2,1,0:T(8,128)}, u32[]{:S(2)}) copy-start(f32[8,32,128]{2,1,0:T(8,128)} %logs.1) | copy-start | bytes 393220
  (3 other events, 2.4 us)

commit v10 on v9

--- a/solution.py
+++ b/solution.py
@@ -325,9 +325,16 @@
         n_g = roll(counts, 16 - 32 * g)
         dense.append(jnp.where(lane % 4 == 3, 0.0, n_g * m) - s_g)
         raw.append(jnp.where(lane % 4 == 0, n_g, m))
-    inj[...] = jnp.dot(
-        jnp.concatenate(dense + raw, 0), spread_to,
-        precision=lax.Precision.HIGHEST, preferred_element_type=f32,
+    whole = jnp.concatenate(dense + raw, 0)
+    hi = whole.astype(bf)
+    rest = whole - hi.astype(f32)
+    mid = rest.astype(bf)
+    low = (rest - mid.astype(f32)).astype(bf)
+    to = spread_to.astype(bf)
+    inj[...] = (
+        jnp.dot(hi, to, preferred_element_type=f32)
+        + jnp.dot(mid, to, preferred_element_type=f32)
+        + jnp.dot(low, to, preferred_element_type=f32)
     )
 
     def j(n, g, lo, hi):

time: 120 us -> 120 us (level)
  transfers between devices with their start and end apart: 18 -> 18, of which waited for: 6 -> 6; matrix products, arithmetic and copies ran while one was open for 0% -> 0% of each run, Pallas kernels for 6% -> 5%
where the time goes in v10:
time: 120 us; the launch traced here: 119 us
  starting transfers between devices  78.7 us (66%)
  blocking collectives  15.6 us (13%)
  Pallas kernels  14.6 us (12%)
  waiting for transfers between devices  5.1 us (4%)
  between operations  2.26 us (2%)
  local copies, waits for them, and re-layouts  1.52 us (1%)
    ppermute x16, starting transfers between devices, shift(): lax.ppermute(x, axis, [(i, (i + k) % n) for i in range(n) if wrap or 0 <=...  56.9 us
    all_gather x1, blocking collectives, local(): every = lax.all_gather(part, 'shot', axis=0)  15.6 us
    pallas_call x10, Pallas kernels, go(): pl.pallas_call(kernel, out_shape=outs, in_specs=[SM] * smem + [VM] * (len...  14.6 us
    ppermute x1, starting transfers between devices, local(): other = lax.ppermute(sent, 'shot', [(i, i ^ 1) for i in range(nshot)])  11.7 us
    all_to_all x1, starting transfers between devices, local(): got = lax.all_to_all(chunk, 'gx', 0, 0)  10 us
    ppermute x16, waiting for transfers between devices, shift(): lax.ppermute(x, axis, [(i, (i + k) % n) for i in range(n) if wrap or 0 <=...  3.11 us
  transfers between devices with their start and end apart: 18, of which 6 were waited for; matrix products, arithmetic and copies ran while one was open for 0% of the time, Pallas kernels for 5%

profile of v10, /device:TPU:49, one launch (start us, length us, event | category | flops | bytes accessed | tf_op | source)
XLA Modules:
  0.0 118.9 jit_solution(10551159730412284035)
XLA Ops:
  2.8 2.4 %collective-permute-start = (f32[256,128]{1,0:T(8,128)S(1)}, f32[256,128]{1,0:T(8,128)S(1)}, u32[]{:S(2)}, u32[]{:S(2)}) collective-permute-start(f32[256,128]{1,0:T(8,128)S(1)} %get-tuple-element.46), channel_id=1, source_target_pairs={{0,8},{8,16},{16,24},{24,32},{32,40},{40,48},{48,56},{56,64},{64,7... | collective-permute-start | bytes 393224 | tf_op jit(solution)/shard_map/ppermute | solution.py:435
  5.2 3.0 %collective-permute-start.1 = (f32[256,128]{1,0:T(8,128)S(1)}, f32[256,128]{1,0:T(8,128)S(1)}, u32[]{:S(2)}, u32[]{:S(2)}) collective-permute-start(f32[256,128]{1,0:T(8,128)S(1)} %get-tuple-element.47), channel_id=1, source_target_pairs={{8,0},{16,8},{24,16},{32,24},{40,32},{48,40},{56,48},{64,56},{72,6... | collective-permute-start | bytes 393224 | tf_op jit(solution)/shard_map/ppermute | solution.py:435
  8.2 4.0 %collective-permute-start.2 = (f32[88,128]{1,0:T(8,128)S(1)}, f32[88,128]{1,0:T(8,128)S(1)}, u32[]{:S(2)}, u32[]{:S(2)}) collective-permute-start(f32[88,128]{1,0:T(8,128)S(1)} %get-tuple-element.48), channel_id=1, source_target_pairs={{0,1},{1,2},{2,3},{3,4},{4,5},{5,6},{6,7},{7,0},{8,9},{9,10},{10,1... | collective-permute-start | bytes 135176 | tf_op jit(solution)/shard_map/ppermute | solution.py:435
  12.2 8.6 %collective-permute-start.3 = (f32[88,128]{1,0:T(8,128)S(1)}, f32[88,128]{1,0:T(8,128)S(1)}, u32[]{:S(2)}, u32[]{:S(2)}) collective-permute-start(f32[88,128]{1,0:T(8,128)S(1)} %get-tuple-element.49), channel_id=1, source_target_pairs={{0,7},{1,0},{2,1},{3,2},{4,3},{5,4},{6,5},{7,6},{8,15},{9,8},{10,9... | collective-permute-start | bytes 135176 | tf_op jit(solution)/shard_map/ppermute | solution.py:435
  22.8 1.7 %shard_map.132 = (f32[32,128]{1,0:T(8,128)S(1)}, f32[16,128]{1,0:T(8,128)S(1)}, f32[8,32,128]{2,1,0:T(8,128)S(1)}, f32[8,32,128]{2,1,0:T(8,128)S(1)}, f32[320,12...) custom-call(s32[1]{0:T(128)S(6)} %copy.14.source, ...), custom_call_target="tpu_custom_call" | custom-call | tf_op jit(solution)/shard_map/pallas_call | solution.py:421
  24.5 4.4 %collective-permute-start.4 = (f32[320,128]{1,0:T(8,128)S(1)}, f32[320,128]{1,0:T(8,128)S(1)}, u32[]{:S(2)}, u32[]{:S(2)}) collective-permute-start(f32[320,128]{1,0:T(8,128)S(1)} %get-tuple-element.53), channel_id=1, source_target_pairs={{0,8},{8,16},{16,24},{24,32},{32,40},{40,48},{48,56},{56,64},{64,7... | collective-permute-start | bytes 491528 | tf_op jit(solution)/shard_map/ppermute | solution.py:435
  29.0 1.9 %collective-permute-start.5 = (f32[320,128]{1,0:T(8,128)S(1)}, f32[320,128]{1,0:T(8,128)S(1)}, u32[]{:S(2)}, u32[]{:S(2)}) collective-permute-start(f32[320,128]{1,0:T(8,128)S(1)} %get-tuple-element.54), channel_id=1, source_target_pairs={{8,0},{16,8},{24,16},{32,24},{40,32},{48,40},{56,48},{64,56},{72,6... | collective-permute-start | bytes 491528 | tf_op jit(solution)/shard_map/ppermute | solution.py:435
  30.9 1.9 %collective-permute-start.6 = (f32[72,128]{1,0:T(8,128)S(1)}, f32[72,128]{1,0:T(8,128)S(1)}, u32[]{:S(2)}, u32[]{:S(2)}) collective-permute-start(f32[72,128]{1,0:T(8,128)S(1)} %get-tuple-element.55), channel_id=1, source_target_pairs={{0,1},{1,2},{2,3},{3,4},{4,5},{5,6},{6,7},{7,0},{8,9},{9,10},{10,1... | collective-permute-start | bytes 110600 | tf_op jit(solution)/shard_map/ppermute | solution.py:435
  32.8 4.9 %collective-permute-start.7 = (f32[72,128]{1,0:T(8,128)S(1)}, f32[72,128]{1,0:T(8,128)S(1)}, u32[]{:S(2)}, u32[]{:S(2)}) collective-permute-start(f32[72,128]{1,0:T(8,128)S(1)} %get-tuple-element.56), channel_id=1, source_target_pairs={{0,7},{1,0},{2,1},{3,2},{4,3},{5,4},{6,5},{7,6},{8,15},{9,8},{10,9... | collective-permute-start | bytes 110600 | tf_op jit(solution)/shard_map/ppermute | solution.py:435
  39.4 1.6 %shard_map.133 = (f32[32,128]{1,0:T(8,128)S(1)}, f32[16,128]{1,0:T(8,128)S(1)}, f32[8,32,128]{2,1,0:T(8,128)S(1)}, f32[8,32,128]{2,1,0:T(8,128)S(1)}, f32[288,12...) custom-call(s32[1]{0:T(128)S(6)} %copy.14.source, ...), custom_call_target="tpu_custom_call" | custom-call | tf_op jit(solution)/shard_map/pallas_call | solution.py:421
  41.1 5.1 %collective-permute-start.8 = (f32[288,128]{1,0:T(8,128)S(1)}, f32[288,128]{1,0:T(8,128)S(1)}, u32[]{:S(2)}, u32[]{:S(2)}) collective-permute-start(f32[288,128]{1,0:T(8,128)S(1)} %get-tuple-element.61), channel_id=1, source_target_pairs={{0,8},{8,16},{16,24},{24,32},{32,40},{40,48},{48,56},{56,64},{64,7... | collective-permute-start | bytes 442376 | tf_op jit(solution)/shard_map/ppermute | solution.py:435
  46.2 1.9 %collective-permute-start.9 = (f32[288,128]{1,0:T(8,128)S(1)}, f32[288,128]{1,0:T(8,128)S(1)}, u32[]{:S(2)}, u32[]{:S(2)}) collective-permute-start(f32[288,128]{1,0:T(8,128)S(1)} %get-tuple-element.62), channel_id=1, source_target_pairs={{8,0},{16,8},{24,16},{32,24},{40,32},{48,40},{56,48},{64,56},{72,6... | collective-permute-start | bytes 442376 | tf_op jit(solution)/shard_map/ppermute | solution.py:435
  48.2 3.0 %collective-permute-start.10 = (f32[72,128]{1,0:T(8,128)S(1)}, f32[72,128]{1,0:T(8,128)S(1)}, u32[]{:S(2)}, u32[]{:S(2)}) collective-permute-start(f32[72,128]{1,0:T(8,128)S(1)} %get-tuple-element.63), channel_id=1, source_target_pairs={{0,1},{1,2},{2,3},{3,4},{4,5},{5,6},{6,7},{7,0},{8,9},{9,10},{10,1... | collective-permute-start | bytes 110600 | tf_op jit(solution)/shard_map/ppermute | solution.py:435
  51.2 3.8 %collective-permute-start.11 = (f32[72,128]{1,0:T(8,128)S(1)}, f32[72,128]{1,0:T(8,128)S(1)}, u32[]{:S(2)}, u32[]{:S(2)}) collective-permute-start(f32[72,128]{1,0:T(8,128)S(1)} %get-tuple-element.64), channel_id=1, source_target_pairs={{0,7},{1,0},{2,1},{3,2},{4,3},{5,4},{6,5},{7,6},{8,15},{9,8},{10,9... | collective-permute-start | bytes 110600 | tf_op jit(solution)/shard_map/ppermute | solution.py:435
  56.2 2.0 %shard_map.134 = (f32[32,128]{1,0:T(8,128)S(1)}, f32[16,128]{1,0:T(8,128)S(1)}, f32[8,32,128]{2,1,0:T(8,128)S(1)}, f32[8,32,128]{2,1,0:T(8,128)S(1)}, f32[256,12...) custom-call(s32[1]{0:T(128)S(6)} %copy.14.source, ...), custom_call_target="tpu_custom_call" | custom-call | tf_op jit(solution)/shard_map/pallas_call | solution.py:421
  58.2 3.4 %collective-permute-start.14 = (f32[88,128]{1,0:T(8,128)S(1)}, f32[88,128]{1,0:T(8,128)S(1)}, u32[]{:S(2)}, u32[]{:S(2)}) collective-permute-start(f32[88,128]{1,0:T(8,128)S(1)} %get-tuple-element.71), channel_id=1, source_target_pairs={{0,1},{1,2},{2,3},{3,4},{4,5},{5,6},{6,7},{7,0},{8,9},{9,10},{10,1... | collective-permute-start | bytes 135176 | tf_op jit(solution)/shard_map/ppermute | solution.py:435
  61.5 3.3 %collective-permute-start.15 = (f32[88,128]{1,0:T(8,128)S(1)}, f32[88,128]{1,0:T(8,128)S(1)}, u32[]{:S(2)}, u32[]{:S(2)}) collective-permute-start(f32[88,128]{1,0:T(8,128)S(1)} %get-tuple-element.72), channel_id=1, source_target_pairs={{0,7},{1,0},{2,1},{3,2},{4,3},{5,4},{6,5},{7,6},{8,15},{9,8},{10,9... | collective-permute-start | bytes 135176 | tf_op jit(solution)/shard_map/ppermute | solution.py:435
  64.8 1.3 %shard_map.135 = (f32[64,128]{1,0:T(8,128)S(1)}, f32[64,128]{1,0:T(8,128)S(1)}, f32[64,128]{1,0:T(8,128)S(1)}, f32[32,128]{1,0:T(8,128)S(1)}, f32[32,128]{1,0:T(8,128)S(1)}) custom-call(s32[64,128]{1,0:T(8,128)S(1)} %bitcast.21, f32[8,32,128]{2,1,0:T(8,128)S(1)} %get-tuple-element.91.vel, f32[8,32,128]{2,1,0:T(8,128)S(1)} %bitcast.17), custom_call_target="tpu_custom_call" | custom-call | tf_op jit(solution)/shard_map/pallas_call | solution.py:421
  67.1 10.0 %all-to-all-start = ((f32[16,32,128]{2,1,0:T(8,128)}), f32[16,32,128]{2,1,0:T(8,128)S(1)}, u32[]{:S(2)}, u32[]{:S(2)}) async-start(f32[16,32,128]{2,1,0:T(8,128)} %shard_map.136), calls=%async_computation | async-start | bytes 524288 | tf_op jit(solution)/shard_map/all_to_all | solution.py:511
  77.1 3.1 %collective-permute-start.12 = (f32[256,128]{1,0:T(8,128)S(1)}, f32[256,128]{1,0:T(8,128)S(1)}, u32[]{:S(2)}, u32[]{:S(2)}) collective-permute-start(f32[256,128]{1,0:T(8,128)S(1)} %get-tuple-element.69), channel_id=1, source_target_pairs={{0,8},{8,16},{16,24},{24,32},{32,40},{40,48},{48,56},{56,64},{64,7... | collective-permute-start | bytes 393224 | tf_op jit(solution)/shard_map/ppermute | solution.py:435
  80.2 2.2 %collective-permute-start.13 = (f32[256,128]{1,0:T(8,128)S(1)}, f32[256,128]{1,0:T(8,128)S(1)}, u32[]{:S(2)}, u32[]{:S(2)}) collective-permute-start(f32[256,128]{1,0:T(8,128)S(1)} %get-tuple-element.70), channel_id=1, source_target_pairs={{8,0},{16,8},{24,16},{32,24},{40,32},{48,40},{56,48},{64,56},{72,6... | collective-permute-start | bytes 393224 | tf_op jit(solution)/shard_map/ppermute | solution.py:435
  83.5 5.2 %shard_map.137 = (f32[32,128]{1,0:T(8,128)S(1)}, f32[32,128]{1,0:T(8,128)S(1)}) custom-call(f32[16,32,128]{2,1,0:T(8,128)S(1)} %all-to-all-done.got, f32[64,128]{1,0:T(8,128)S(1)} %get-tuple-element.78.keyx, f32[64,128]{1,0:T(8,128)S(1)} %get-tuple-element.79.keyy, f32[64,128]{1,0:T(8,128)S(1)} %get-tuple-element.77._.count, ...), custom_call_target="tpu_custom_call" | custom-call | tf_op jit(solution)/shard_map/pallas_call | solution.py:421
  89.8 11.7 %collective-permute-start.16 = (f32[8,32,128]{2,1,0:T(8,128)S(1)}, f32[8,32,128]{2,1,0:T(8,128)S(1)}, u32[]{:S(2)}, u32[]{:S(2)}) collective-permute-start(f32[8,32,128]{2,1,0:T(8,128)S(1)} %get-tuple-element.88), channel_id=1, source_target_pairs={{0,128},{128,0},{256,384},{384,256},{1,129},{129,1},{257,385},{385... | collective-permute-start | bytes 393224 | tf_op jit(solution)/shard_map/ppermute | solution.py:524
  102.6 15.6 %all-gather = f32[1280,128]{1,0:T(8,128)S(1)} all-gather(f32[320,128]{1,0:T(8,128)S(1)} %shard_map.139), channel_id=2, replica_groups=mesh['shot'=4,'gx'=16,'gy'=8] {'shot'}, dimensions={0}, use_global_device_ids=true | all-gather | bytes 819200 | tf_op jit(solution)/shard_map/all_gather | solution.py:526
  (43 shorter events, 10.6 us)
Async XLA Ops:
  2.7 19.5 %copy-start.1 = (f32[1,8,32,128]{3,2,1,0:T(8,128)S(1)}, f32[1,8,32,128]{3,2,1,0:T(8,128)}, u32[]{:S(2)}) copy-start(f32[1,8,32,128]{3,2,1,0:T(8,128)} %param.18) | copy-start | bytes 393220
  2.7 19.5 %copy-start.4 = (f32[1,8,32,128]{3,2,1,0:T(8,128)S(1)}, f32[1,8,32,128]{3,2,1,0:T(8,128)}, u32[]{:S(2)}) copy-start(f32[1,8,32,128]{3,2,1,0:T(8,128)} %param.15) | copy-start | bytes 393220
  2.7 19.5 %copy-start.5 = (f32[1,8,32,128]{3,2,1,0:T(8,128)S(1)}, f32[1,8,32,128]{3,2,1,0:T(8,128)}, u32[]{:S(2)}) copy-start(f32[1,8,32,128]{3,2,1,0:T(8,128)} %param.17) | copy-start | bytes 393220
  2.8 19.3 %collective-permute-start = (f32[256,128]{1,0:T(8,128)S(1)}, f32[256,128]{1,0:T(8,128)S(1)}, u32[]{:S(2)}, u32[]{:S(2)}) collective-permute-start(f32[256,128]{1,0:T(8,128)S(1)} %get-tuple-element.46), channel_id=1, source_target_pairs={{0,8},{8,16},{16,24},{24,32},{32,40},{40,48},{48,56},{56,64},{64,7... | collective-permute-start | bytes 393224 | tf_op jit(solution)/shard_map/ppermute | solution.py:435
  5.2 16.9 %collective-permute-start.1 = (f32[256,128]{1,0:T(8,128)S(1)}, f32[256,128]{1,0:T(8,128)S(1)}, u32[]{:S(2)}, u32[]{:S(2)}) collective-permute-start(f32[256,128]{1,0:T(8,128)S(1)} %get-tuple-element.47), channel_id=1, source_target_pairs={{8,0},{16,8},{24,16},{32,24},{40,32},{48,40},{56,48},{64,56},{72,6... | collective-permute-start | bytes 393224 | tf_op jit(solution)/shard_map/ppermute | solution.py:435
  8.2 13.9 %collective-permute-start.2 = (f32[88,128]{1,0:T(8,128)S(1)}, f32[88,128]{1,0:T(8,128)S(1)}, u32[]{:S(2)}, u32[]{:S(2)}) collective-permute-start(f32[88,128]{1,0:T(8,128)S(1)} %get-tuple-element.48), channel_id=1, source_target_pairs={{0,1},{1,2},{2,3},{3,4},{4,5},{5,6},{6,7},{7,0},{8,9},{9,10},{10,1... | collective-permute-start | bytes 135176 | tf_op jit(solution)/shard_map/ppermute | solution.py:435
  12.2 9.9 %collective-permute-start.3 = (f32[88,128]{1,0:T(8,128)S(1)}, f32[88,128]{1,0:T(8,128)S(1)}, u32[]{:S(2)}, u32[]{:S(2)}) collective-permute-start(f32[88,128]{1,0:T(8,128)S(1)} %get-tuple-element.49), channel_id=1, source_target_pairs={{0,7},{1,0},{2,1},{3,2},{4,3},{5,4},{6,5},{7,6},{8,15},{9,8},{10,9... | collective-permute-start | bytes 135176 | tf_op jit(solution)/shard_map/ppermute | solution.py:435
  24.5 14.3 %collective-permute-start.4 = (f32[320,128]{1,0:T(8,128)S(1)}, f32[320,128]{1,0:T(8,128)S(1)}, u32[]{:S(2)}, u32[]{:S(2)}) collective-permute-start(f32[320,128]{1,0:T(8,128)S(1)} %get-tuple-element.53), channel_id=1, source_target_pairs={{0,8},{8,16},{16,24},{24,32},{32,40},{40,48},{48,56},{56,64},{64,7... | collective-permute-start | bytes 491528 | tf_op jit(solution)/shard_map/ppermute | solution.py:435
  29.0 10.5 %collective-permute-start.5 = (f32[320,128]{1,0:T(8,128)S(1)}, f32[320,128]{1,0:T(8,128)S(1)}, u32[]{:S(2)}, u32[]{:S(2)}) collective-permute-start(f32[320,128]{1,0:T(8,128)S(1)} %get-tuple-element.54), channel_id=1, source_target_pairs={{8,0},{16,8},{24,16},{32,24},{40,32},{48,40},{56,48},{64,56},{72,6... | collective-permute-start | bytes 491528 | tf_op jit(solution)/shard_map/ppermute | solution.py:435
  30.9 6.9 %collective-permute-start.6 = (f32[72,128]{1,0:T(8,128)S(1)}, f32[72,128]{1,0:T(8,128)S(1)}, u32[]{:S(2)}, u32[]{:S(2)}) collective-permute-start(f32[72,128]{1,0:T(8,128)S(1)} %get-tuple-element.55), channel_id=1, source_target_pairs={{0,1},{1,2},{2,3},{3,4},{4,5},{5,6},{6,7},{7,0},{8,9},{9,10},{10,1... | collective-permute-start | bytes 110600 | tf_op jit(solution)/shard_map/ppermute | solution.py:435
  32.8 6.0 %collective-permute-start.7 = (f32[72,128]{1,0:T(8,128)S(1)}, f32[72,128]{1,0:T(8,128)S(1)}, u32[]{:S(2)}, u32[]{:S(2)}) collective-permute-start(f32[72,128]{1,0:T(8,128)S(1)} %get-tuple-element.56), channel_id=1, source_target_pairs={{0,7},{1,0},{2,1},{3,2},{4,3},{5,4},{6,5},{7,6},{8,15},{9,8},{10,9... | collective-permute-start | bytes 110600 | tf_op jit(solution)/shard_map/ppermute | solution.py:435
  41.1 15.1 %collective-permute-start.8 = (f32[288,128]{1,0:T(8,128)S(1)}, f32[288,128]{1,0:T(8,128)S(1)}, u32[]{:S(2)}, u32[]{:S(2)}) collective-permute-start(f32[288,128]{1,0:T(8,128)S(1)} %get-tuple-element.61), channel_id=1, source_target_pairs={{0,8},{8,16},{16,24},{24,32},{32,40},{40,48},{48,56},{56,64},{64,7... | collective-permute-start | bytes 442376 | tf_op jit(solution)/shard_map/ppermute | solution.py:435
  46.2 9.9 %collective-permute-start.9 = (f32[288,128]{1,0:T(8,128)S(1)}, f32[288,128]{1,0:T(8,128)S(1)}, u32[]{:S(2)}, u32[]{:S(2)}) collective-permute-start(f32[288,128]{1,0:T(8,128)S(1)} %get-tuple-element.62), channel_id=1, source_target_pairs={{8,0},{16,8},{24,16},{32,24},{40,32},{48,40},{56,48},{64,56},{72,6... | collective-permute-start | bytes 442376 | tf_op jit(solution)/shard_map/ppermute | solution.py:435
  48.2 6.8 %collective-permute-start.10 = (f32[72,128]{1,0:T(8,128)S(1)}, f32[72,128]{1,0:T(8,128)S(1)}, u32[]{:S(2)}, u32[]{:S(2)}) collective-permute-start(f32[72,128]{1,0:T(8,128)S(1)} %get-tuple-element.63), channel_id=1, source_target_pairs={{0,1},{1,2},{2,3},{3,4},{4,5},{5,6},{6,7},{7,0},{8,9},{9,10},{10,1... | collective-permute-start | bytes 110600 | tf_op jit(solution)/shard_map/ppermute | solution.py:435
  51.2 5.0 %collective-permute-start.11 = (f32[72,128]{1,0:T(8,128)S(1)}, f32[72,128]{1,0:T(8,128)S(1)}, u32[]{:S(2)}, u32[]{:S(2)}) collective-permute-start(f32[72,128]{1,0:T(8,128)S(1)} %get-tuple-element.64), channel_id=1, source_target_pairs={{0,7},{1,0},{2,1},{3,2},{4,3},{5,4},{6,5},{7,6},{8,15},{9,8},{10,9... | collective-permute-start | bytes 110600 | tf_op jit(solution)/shard_map/ppermute | solution.py:435
  56.2 8.6 %copy-start.2 = (f32[1,8,32,128]{3,2,1,0:T(8,128)S(1)}, f32[1,8,32,128]{3,2,1,0:T(8,128)}, u32[]{:S(2)}) copy-start(f32[1,8,32,128]{3,2,1,0:T(8,128)} %param.14) | copy-start | bytes 393220
  56.2 8.6 %copy-start.6 = (s32[1,8192]{1,0:T(1,128)S(1)}, s32[1,8192]{1,0:T(1,128)}, u32[]{:S(2)}) copy-start(s32[1,8192]{1,0:T(1,128)} %param.21) | copy-start | bytes 98308
  58.2 8.0 %collective-permute-start.14 = (f32[88,128]{1,0:T(8,128)S(1)}, f32[88,128]{1,0:T(8,128)S(1)}, u32[]{:S(2)}, u32[]{:S(2)}) collective-permute-start(f32[88,128]{1,0:T(8,128)S(1)} %get-tuple-element.71), channel_id=1, source_target_pairs={{0,1},{1,2},{2,3},{3,4},{4,5},{5,6},{6,7},{7,0},{8,9},{9,10},{10,1... | collective-permute-start | bytes 135176 | tf_op jit(solution)/shard_map/ppermute | solution.py:435
  61.5 4.8 %collective-permute-start.15 = (f32[88,128]{1,0:T(8,128)S(1)}, f32[88,128]{1,0:T(8,128)S(1)}, u32[]{:S(2)}, u32[]{:S(2)}) collective-permute-start(f32[88,128]{1,0:T(8,128)S(1)} %get-tuple-element.72), channel_id=1, source_target_pairs={{0,7},{1,0},{2,1},{3,2},{4,3},{5,4},{6,5},{7,6},{8,15},{9,8},{10,9... | collective-permute-start | bytes 135176 | tf_op jit(solution)/shard_map/ppermute | solution.py:435
  67.1 16.4 %all-to-all-start = ((f32[16,32,128]{2,1,0:T(8,128)}), f32[16,32,128]{2,1,0:T(8,128)S(1)}, u32[]{:S(2)}, u32[]{:S(2)}) async-start(f32[16,32,128]{2,1,0:T(8,128)} %shard_map.136), calls=%async_computation | async-start | bytes 524288 | tf_op jit(solution)/shard_map/all_to_all | solution.py:511
  77.1 11.6 %collective-permute-start.12 = (f32[256,128]{1,0:T(8,128)S(1)}, f32[256,128]{1,0:T(8,128)S(1)}, u32[]{:S(2)}, u32[]{:S(2)}) collective-permute-start(f32[256,128]{1,0:T(8,128)S(1)} %get-tuple-element.69), channel_id=1, source_target_pairs={{0,8},{8,16},{16,24},{24,32},{32,40},{40,48},{48,56},{56,64},{64,7... | collective-permute-start | bytes 393224 | tf_op jit(solution)/shard_map/ppermute | solution.py:435
  80.2 8.5 %collective-permute-start.13 = (f32[256,128]{1,0:T(8,128)S(1)}, f32[256,128]{1,0:T(8,128)S(1)}, u32[]{:S(2)}, u32[]{:S(2)}) collective-permute-start(f32[256,128]{1,0:T(8,128)S(1)} %get-tuple-element.70), channel_id=1, source_target_pairs={{8,0},{16,8},{24,16},{32,24},{40,32},{48,40},{56,48},{64,56},{72,6... | collective-permute-start | bytes 393224 | tf_op jit(solution)/shard_map/ppermute | solution.py:435
  89.8 12.7 %collective-permute-start.16 = (f32[8,32,128]{2,1,0:T(8,128)S(1)}, f32[8,32,128]{2,1,0:T(8,128)S(1)}, u32[]{:S(2)}, u32[]{:S(2)}) collective-permute-start(f32[8,32,128]{2,1,0:T(8,128)S(1)} %get-tuple-element.88), channel_id=1, source_target_pairs={{0,128},{128,0},{256,384},{384,256},{1,129},{129,1},{257,385},{385... | collective-permute-start | bytes 393224 | tf_op jit(solution)/shard_map/ppermute | solution.py:524
  102.5 15.6 %copy-start.3 = (f32[8,32,128]{2,1,0:T(8,128)S(1)}, f32[8,32,128]{2,1,0:T(8,128)}, u32[]{:S(2)}) copy-start(f32[8,32,128]{2,1,0:T(8,128)} %logs.1) | copy-start | bytes 393220
  (3 other events, 2.4 us)
